TPU v7x, 32 devices: a whole 2x2x4 slice. The times are simulated.
32 devices in a mesh: groups: 2 (over x), ep: 16 (over z, y, core).
Axes of the slice: x: 2, y: 2, z: 4, core: 2. Of those that a mesh axis runs over, the one named last changes fastest.
Arguments:
- queries: bfloat16 [256, 4096], P('groups', 'ep'), parts along dimension 0, may hold values from -35 to 35
- key_values: bfloat16 [256, 256, 512], P(('groups', 'ep')), parts along dimension 0, may hold values from -12 to 12
- lengths: int32 [256], P(('groups', 'ep')), parts along dimension 0, may hold values from 2 to 256
- residual: bfloat16 [256, 3584], P(('groups', 'ep')), parts along dimension 0, may hold values from -25 to 25
- routes: int32 [256, 3], P(('groups', 'ep')), parts along dimension 0, may hold values from 0 to 7, as said below
- gate_weights: bfloat16 [256, 3], P(('groups', 'ep')), parts along dimension 0, may hold values from 0.19921875 to 1
- output_weight: bfloat16 [4096, 3584], P('ep'), may hold values from -0.09375 to 0.09375
- norm_gain: float32 [3584], replicated, may hold values from 0.1 to 1.9
- gate_weight: bfloat16 [24576, 3584], P('ep'), may hold values from -0.09375 to 0.09375
- up_weight: bfloat16 [24576, 3584], P('ep'), may hold values from -0.09375 to 0.09375
- down_weight: bfloat16 [24576, 3584], P('ep'), may hold values from -0.109375 to 0.109375
Outputs:
- layer_output: bfloat16 [256, 3584], P(('groups', 'ep')), parts along dimension 0
There are 2 independent parts, one for each index of `groups`. A program takes and returns all parts, laid end to end along the dimension named above; an argument that names none is the same for every part. Nothing has to cross between parts.
Inputs may be any that keep to these rules, and one draw needn't show every extreme that they name: `routes`: each row names 3 different experts. Among the rows of one index of ep no expert is named by more than 6 rows; one expert, the same for every index, is named by exactly 6 rows of each index, and there the other experts' counts differ by at most one.
All inputs are finite; a program needn't handle non-finite values.
Results may differ from a plain program's by a relative error of at most 0.0056.
Values may be sent and summed in bfloat16 or wider, within the bound.
No kernel may reach another device: no remote copies, remote signals or barrier semaphores. Data moves between devices by JAX's collectives and lax.ppermute only.
A program may use at most 128 MiB of HBM per device.

v0:
```python
import jax
import jax.numpy as jnp
from jax import lax
from jax.sharding import PartitionSpec as P

EXPERTS = 8
CAP = 6


EPSILON = 1e-05


def attend(query_rows, key_values, lengths):
    row_count = key_values.shape[0]
    head_dim = key_values.shape[2] // 2
    head_count = query_rows.shape[1] // head_dim
    query_heads = query_rows.reshape(row_count, head_count, head_dim)
    key_rows = key_values[:, :, :head_dim]
    value_rows = key_values[:, :, head_dim:]
    scores = jnp.einsum(
        "rhd,rtd->rht", query_heads, key_rows, preferred_element_type=jnp.float32
    ) * head_dim ** (-0.5)
    positions = lax.broadcasted_iota(jnp.int32, (row_count, 1, key_values.shape[1]), 2)
    scores = jnp.where(positions < lengths[:, None, None], scores, -1e30)
    row_max = jnp.max(scores, axis=2, keepdims=True)
    weights = jnp.exp(scores - row_max)
    prob_rows = (weights / jnp.sum(weights, axis=2, keepdims=True)).astype(jnp.bfloat16)
    attended = jnp.einsum("rht,rtd->rhd", prob_rows, value_rows, preferred_element_type=jnp.float32)
    return attended.astype(jnp.bfloat16).reshape(row_count, head_count * head_dim)


def normalize(middle, norm_gain):
    inverse_root = lax.rsqrt(jnp.mean(middle * middle, axis=1, keepdims=True) + EPSILON)
    return (middle * inverse_root * norm_gain).astype(jnp.bfloat16)


def expert_slice(slot_rows, gate_weight, up_weight, down_weight):
    source_count, slot_count, feature_count = slot_rows.shape
    flat_slots = slot_rows.reshape(source_count * slot_count, feature_count)
    contract = (((1,), (1,)), ((), ()))
    gate_pre = lax.dot_general(
        flat_slots, gate_weight, contract, preferred_element_type=jnp.float32
    )
    up_pre = lax.dot_general(flat_slots, up_weight, contract, preferred_element_type=jnp.float32)
    hidden = (jax.nn.silu(gate_pre) * up_pre).astype(jnp.bfloat16)
    partial_value = jnp.dot(hidden, down_weight, preferred_element_type=jnp.float32)
    return partial_value.astype(jnp.bfloat16).reshape(source_count, slot_count, feature_count)


def own_slots(routes, gate_weights):
    expert_ids = lax.broadcasted_iota(jnp.int32, (1, 1, EXPERTS), 2)
    matches = routes[:, :, None] == expert_ids
    hit_count = jnp.sum(matches.astype(jnp.int32), axis=1)
    before = jnp.cumsum(hit_count, axis=0) - hit_count
    slot_ids = lax.broadcasted_iota(jnp.int32, (1, CAP, 1), 1)
    selector = (hit_count.T[:, None, :] > 0) & (before.T[:, None, :] == slot_ids)
    gate_by_expert = jnp.sum(
        jnp.where(matches, gate_weights.astype(jnp.float32)[:, :, None], 0.0), axis=1
    )
    return (selector.astype(jnp.bfloat16), gate_by_expert)


def owner_combine(returned, selector, gate_by_expert, expert_span):
    feature_count = returned.shape[2]
    summed = jnp.sum(
        returned.reshape(EXPERTS, expert_span, CAP, feature_count).astype(jnp.float32), axis=1
    )
    weight_table = selector.astype(jnp.float32) * gate_by_expert.T[:, None, :]
    return jnp.einsum("ecr,ecd->rd", weight_table, summed, precision=lax.Precision.HIGHEST)


def local(
    queries,
    key_values,
    lengths,
    residual,
    routes,
    gate_weights,
    output_weight,
    norm_gain,
    gate_weight,
    up_weight,
    down_weight,
):
    tok_dev = key_values.shape[0]
    device_count = lax.axis_size("ep")
    expert_span = device_count // EXPERTS
    query_rows = lax.all_to_all(queries, "ep", split_axis=0, concat_axis=1, tiled=True)
    attended = attend(query_rows, key_values, lengths)
    head_rows = lax.all_to_all(attended, "ep", split_axis=1, concat_axis=0, tiled=True)
    residual_wide = residual.astype(jnp.float32)
    terms = jnp.dot(head_rows, output_weight, preferred_element_type=jnp.float32)
    terms = terms.reshape(device_count, tok_dev, terms.shape[1])
    arrived = lax.all_to_all(terms, "ep", split_axis=0, concat_axis=0, tiled=True)
    middle = residual_wide + jnp.sum(arrived, axis=0)
    normed = normalize(middle, norm_gain)
    selector, gate_by_expert = own_slots(routes, gate_weights)
    outgoing = jnp.einsum(
        "ecr,rd->ecd", selector, normed, preferred_element_type=jnp.float32
    ).astype(jnp.bfloat16)
    feature_count = outgoing.shape[2]
    outgoing = jnp.broadcast_to(
        outgoing[:, None], (EXPERTS, expert_span, CAP, feature_count)
    ).reshape(device_count, CAP, feature_count)
    partial_value = expert_slice(
        lax.all_to_all(outgoing, "ep", split_axis=0, concat_axis=0, tiled=True),
        gate_weight,
        up_weight,
        down_weight,
    )
    returned = lax.all_to_all(partial_value, "ep", split_axis=0, concat_axis=0, tiled=True)
    combined = owner_combine(returned, selector, gate_by_expert, expert_span)
    return (middle + combined).astype(jnp.bfloat16)


def solution(mesh):
    in_specs = (
        P("groups", "ep"),
        P(("groups", "ep"), None, None),
        P(("groups", "ep")),
        P(("groups", "ep"), None),
        P(("groups", "ep"), None),
        P(("groups", "ep"), None),
        P("ep", None),
        P(),
        P("ep", None),
        P("ep", None),
        P("ep", None),
    )
    out_specs = P(("groups", "ep"), None)
    return jax.shard_map(local, mesh=mesh, in_specs=in_specs, out_specs=out_specs, check_vma=False)
```

profile of v0, /device:TPU:0, one launch (start us, length us, event | category | flops | bytes accessed | tf_op | source)
XLA Modules:
  0.0 154.9 jit_solution(11312060726559935100)
XLA Ops:
  0.0 0.0 copy-start
  0.0 7.5 %all-to-all-start = ((bf16[16,8,256]{2,1,0:T(8,128)(2,1)}), bf16[16,8,256]{2,1,0:T(8,128)(2,1)S(1)}, u32[]{:S(2)}, u32[]{:S(2)}) async-start(bf16[16,8,256]{2,1,0:T(8,128)(2,1)} %bitcast.36), calls=%async_computation | async-start | bytes 131072 | tf_op jit(solution)/shard_map/all_to_all | solution.py:88
  7.5 0.7 iota_compare_fusion.2
  8.3 6.2 %all-to-all-done = bf16[16,8,256]{2,1,0:T(8,128)(2,1)S(1)} async-done(((bf16[16,8,256]{2,1,0:T(8,128)(2,1)}), bf16[16,8,256]{2,1,0:T(8,128)(2,1)S(1)}, u32[]{:S(2)}, u32[]{:S(2)}) %all-to-all-start) | async-done | bytes 65568 | tf_op jit(solution)/shard_map/all_to_all | solution.py:88
  14.4 1.6 %fusion.8 = f32[8,16,256]{2,1,0:T(8,128)S(1)} fusion(bf16[8,256,512]{2,1,0:T(8,128)(2,1)} %param.12, bf16[16,8,256]{2,1,0:T(8,128)(2,1)S(1)} %all-to-all-done, pred[8,256]{1,0:T(8,128)(4,1)S(1)} %iota_compare_fusion.2), kind=kOutput, calls=%fused_computation.14 | convolution fusion | flops 16842752 | bytes 1247232 | tf_op jit(solution)/shard_map/rhd,rtd->rht/dot_general | solution.py:20
  16.0 0.2 fusion.34
  16.2 1.5 convolution_convert_fusion.2
  17.8 9.5 %all_to_all.44 = bf16[8,16,256]{2,0,1:T(8,128)(2,1)S(1)} all-to-all(bf16[8,16,256]{2,0,1:T(8,128)(2,1)S(1)} %copy.36), channel_id=1, replica_groups=mesh['groups'=2,'ep'=16] {'ep'}, dimensions={1} | all-to-all | bytes 131072 | tf_op jit(solution)/shard_map/all_to_all | solution.py:90
  27.3 0.0 copy-done
  27.3 1.6 %fusion.4 = f32[16,8,3584]{2,1,0:T(8,128)} fusion(bf16[256,3584]{1,0:T(8,128)(2,1)S(1)} %copy-done, bf16[8,16,256]{2,0,1:T(8,128)(2,1)S(1)} %all_to_all.44), kind=kOutput, calls=%fused_computation.9 | convolution fusion | flops 234881024 | bytes 3735552 | tf_op jit(solution)/shard_map/dot_general | solution.py:92
  28.9 0.0 copy-start.8
  28.9 0.0 copy-start.1
  28.9 0.0 copy-start.5
  28.9 4.5 %all-to-all-start.2 = ((f32[16,8,3584]{2,1,0:T(8,128)}), f32[16,8,3584]{2,1,0:T(8,128)}, u32[]{:S(2)}, u32[]{:S(2)}) async-start(f32[16,8,3584]{2,1,0:T(8,128)} %fusion.4), calls=%async_computation.2 | async-start | bytes 3670016 | tf_op jit(solution)/shard_map/all_to_all | solution.py:94
  33.5 0.0 copy-done.8
  33.5 0.1 convert_reduce_fusion.1
  33.6 0.0 copy-start.6
  33.6 0.0 copy-start.3
  33.6 36.4 %all-to-all-done.2 = f32[16,8,3584]{2,1,0:T(8,128)} async-done(((f32[16,8,3584]{2,1,0:T(8,128)}), f32[16,8,3584]{2,1,0:T(8,128)}, u32[]{:S(2)}, u32[]{:S(2)}) %all-to-all-start.2) | async-done | bytes 1835040 | tf_op jit(solution)/shard_map/all_to_all | solution.py:94
  70.0 1.6 %reduce_sum.55 = f32[8,3584]{1,0:T(8,128)S(1)} reduce(f32[16,8,3584]{2,1,0:T(8,128)} %all-to-all-done.2, f32[]{:T(128)} %constant.5.clone.1), dimensions={0}, to_apply=%region_2.3 | reduce | flops 430080 | bytes 1949700 | tf_op jit(solution)/shard_map/reduce_sum | solution.py:95
  71.6 0.0 copy-done.1
  71.6 0.1 multiply_reduce_fusion
  71.8 0.0 copy-done.5
  71.8 0.3 convolution_convert_fusion.1
  72.1 0.1 copy.38
  72.2 0.1 broadcast_in_dim.44
  72.3 0.0 copy-done.6
  72.3 0.0 copy-done.3
  72.3 32.5 %all_to_all.45 = bf16[16,6,3584]{2,1,0:T(8,128)(2,1)S(1)} all-to-all(bf16[16,6,3584]{2,1,0:T(8,128)(2,1)S(1)} %bitcast.35), channel_id=1, replica_groups=mesh['groups'=2,'ep'=16] {'ep'}, dimensions={0} | all-to-all | bytes 1376256 | tf_op jit(solution)/shard_map/all_to_all | solution.py:106
  104.8 0.2 reshape.62
  105.0 8.4 %fusion.35 = f32[96,1536]{1,0:T(8,128)} fusion(bf16[96,3584]{1,0:T(8,128)(2,1)S(1)} %reshape.62, bf16[1536,3584]{1,0:T(8,128)(2,1)} %param.19), kind=kOutput, calls=%fused_computation.51 | convolution fusion | flops 1056964608 | bytes 12288000 | tf_op jit(solution)/shard_map/dot_general | solution.py:41
  113.4 12.7 %convolution_convert_fusion = bf16[96,3584]{1,0:T(8,128)(2,1)S(1)} fusion(bf16[1536,3584]{1,0:T(8,128)(2,1)} %param.21, bf16[96,3584]{1,0:T(8,128)(2,1)S(1)} %reshape.62, bf16[1536,3584]{1,0:T(8,128)(2,1)} %param.20, f32[96,1536]{1,0:T(8,128)} %fusion.35), kind=kOutput, calls=%fused_computation.1 | convolution fusion | flops 2115158016 | bytes 23986176 | tf_op jit(solution)/shard_map/dot_general | solution.py:46
  126.0 0.0 copy-start.10
  126.0 0.0 copy-start.9
  126.0 1.2 reshape.63
  127.2 0.0 copy-start.2
  127.2 0.0 copy-start.4
  127.2 0.0 copy-start.7
  127.2 4.6 %all-to-all-start.4 = ((bf16[16,6,3584]{2,1,0:T(8,128)(2,1)}), bf16[16,6,3584]{2,1,0:T(8,128)(2,1)S(1)}, u32[]{:S(2)}, u32[]{:S(2)}) async-start(bf16[16,6,3584]{2,1,0:T(8,128)(2,1)} %reshape.63), calls=%async_computation.4 | async-start | bytes 1835008 | tf_op jit(solution)/shard_map/all_to_all | solution.py:111
  131.8 0.0 copy-done.10
  131.8 0.0 copy-done.9
  131.8 0.1 select_reduce_fusion
  131.9 20.7 %all-to-all-done.4 = bf16[16,6,3584]{2,1,0:T(8,128)(2,1)S(1)} async-done(((bf16[16,6,3584]{2,1,0:T(8,128)(2,1)}), bf16[16,6,3584]{2,1,0:T(8,128)(2,1)S(1)}, u32[]{:S(2)}, u32[]{:S(2)}) %all-to-all-start.4) | async-done | bytes 688160 | tf_op jit(solution)/shard_map/all_to_all | solution.py:111
  152.6 0.2 convert_reduce_fusion
  152.8 0.0 copy-done.2
  152.8 0.0 copy-done.4
  152.9 0.0 copy-done.7
  152.9 2.1 %fusion.2 = bf16[8,3584]{1,0:T(8,128)(2,1)} fusion(f32[8,6,3584]{2,1,0:T(8,128)S(1)} %convert_reduce_fusion, f32[8,3584]{1,0:T(8,128)S(1)} %reduce_sum.55, bf16[8,3584]{1,0:T(8,128)(2,1)S(1)} %copy-done.2, f32[8,8]{0,1:T(8,128)S(1)} %bitcast.37, s32[8,8]{0,1:T(8,128)S(1)} %copy-done.4, pred[8,8]{0,1:T(8,128)(4,1)S(1)} %copy-done.7), kind=kOutput, calls=%fused_computation.5 | convolution fusion | flops 16631680 | bytes 918080 | tf_op jit(solution)/shard_map/ecr,ecd->rd/dot_general | solution.py:69
  (6 shorter events, 0.1 us)
Async XLA Ops:
  0.0 27.3 %copy-start = (bf16[256,3584]{1,0:T(8,128)(2,1)S(1)}, bf16[256,3584]{1,0:T(8,128)(2,1)}, u32[]{:S(2)}) copy-start(bf16[256,3584]{1,0:T(8,128)(2,1)} %param.17) | copy-start | bytes 5505028
  0.0 14.4 %all-to-all-start = ((bf16[16,8,256]{2,1,0:T(8,128)(2,1)}), bf16[16,8,256]{2,1,0:T(8,128)(2,1)S(1)}, u32[]{:S(2)}, u32[]{:S(2)}) async-start(bf16[16,8,256]{2,1,0:T(8,128)(2,1)} %bitcast.36), calls=%async_computation | async-start | bytes 131072 | tf_op jit(solution)/shard_map/all_to_all | solution.py:88
  28.9 4.6 %copy-start.8 = (s32[8,3]{0,1:T(4,128)S(1)}, s32[8,3]{0,1:T(4,128)}, u32[]{:S(2)}) copy-start(s32[8,3]{0,1:T(4,128)} %param.15) | copy-start | bytes 292
  28.9 42.7 %copy-start.1 = (bf16[8,3584]{1,0:T(8,128)(2,1)S(1)}, bf16[8,3584]{1,0:T(8,128)(2,1)}, u32[]{:S(2)}) copy-start(bf16[8,3584]{1,0:T(8,128)(2,1)} %param.14) | copy-start | bytes 172036
  28.9 42.8 %copy-start.5 = (f32[3584]{0:T(1024)S(1)}, f32[3584]{0:T(1024)}, u32[]{:S(2)}) copy-start(f32[3584]{0:T(1024)} %param.18) | copy-start | bytes 43012
  28.9 41.1 %all-to-all-start.2 = ((f32[16,8,3584]{2,1,0:T(8,128)}), f32[16,8,3584]{2,1,0:T(8,128)}, u32[]{:S(2)}, u32[]{:S(2)}) async-start(f32[16,8,3584]{2,1,0:T(8,128)} %fusion.4), calls=%async_computation.2 | async-start | bytes 3670016 | tf_op jit(solution)/shard_map/all_to_all | solution.py:94
  33.6 38.7 %copy-start.6 = (pred[8,8]{0,1:T(8,128)(4,1)}, pred[8,8]{0,1:T(8,128)(4,1)S(1)}, u32[]{:S(2)}) copy-start(pred[8,8]{0,1:T(8,128)(4,1)S(1)} %compare_bitcast_fusion) | copy-start | bytes 196
  33.6 38.7 %copy-start.3 = (s32[8,8]{0,1:T(8,128)}, s32[8,8]{0,1:T(8,128)S(1)}, u32[]{:S(2)}) copy-start(s32[8,8]{0,1:T(8,128)S(1)} %subtract_bitcast_fusion) | copy-start | bytes 772
  126.0 5.8 %copy-start.10 = (bf16[8,3]{0,1:T(4,128)(2,1)S(1)}, bf16[8,3]{0,1:T(4,128)(2,1)}, u32[]{:S(2)}) copy-start(bf16[8,3]{0,1:T(4,128)(2,1)} %param.16) | copy-start | bytes 148
  126.0 5.8 %copy-start.9 = (s32[8,3]{0,1:T(4,128)S(1)}, s32[8,3]{0,1:T(4,128)}, u32[]{:S(2)}) copy-start(s32[8,3]{0,1:T(4,128)} %param.15) | copy-start | bytes 292
  127.2 25.6 %copy-start.2 = (bf16[8,3584]{1,0:T(8,128)(2,1)S(1)}, bf16[8,3584]{1,0:T(8,128)(2,1)}, u32[]{:S(2)}) copy-start(bf16[8,3584]{1,0:T(8,128)(2,1)} %param.14) | copy-start | bytes 172036
  127.2 25.6 %copy-start.4 = (s32[8,8]{0,1:T(8,128)S(1)}, s32[8,8]{0,1:T(8,128)}, u32[]{:S(2)}) copy-start(s32[8,8]{0,1:T(8,128)} %copy-done.3) | copy-start | bytes 772
  127.2 25.6 %copy-start.7 = (pred[8,8]{0,1:T(8,128)(4,1)S(1)}, pred[8,8]{0,1:T(8,128)(4,1)}, u32[]{:S(2)}) copy-start(pred[8,8]{0,1:T(8,128)(4,1)} %copy-done.6) | copy-start | bytes 196
  127.2 25.4 %all-to-all-start.4 = ((bf16[16,6,3584]{2,1,0:T(8,128)(2,1)}), bf16[16,6,3584]{2,1,0:T(8,128)(2,1)S(1)}, u32[]{:S(2)}, u32[]{:S(2)}) async-start(bf16[16,6,3584]{2,1,0:T(8,128)(2,1)} %reshape.63), calls=%async_computation.4 | async-start | bytes 1835008 | tf_op jit(solution)/shard_map/all_to_all | solution.py:111
where the time goes:
time: 156 us; the launch traced here: 155 us
  waiting for transfers between devices  63.2 us (41%)
  blocking collectives  42 us (27%)
  matrix products  28.2 us (18%)
  starting transfers between devices  16.7 us (11%)
  other arithmetic  3.06 us (2%)
  local copies, waits for them, and re-layouts  1.63 us (1%)
    all_to_all x1, waiting for transfers between devices, local(): lax.all_to_all(terms, 'ep', split_axis=0, concat_axis=0, tiled=True)  36.4 us
    all_to_all x1, blocking collectives, local(): lax.all_to_all(outgoing, 'ep', split_axis=0, concat_axis=0, tiled=True)  32.5 us
    all_to_all x1, waiting for transfers between devices, local(): lax.all_to_all(partial_value, 'ep', split_axis=0, concat_axis=0, tiled=True)  20.7 us
    dot_general x1, matrix products, expert_slice(): jnp.dot(hidden, down_weight, preferred_element_type=jnp.float32)  12.7 us
    all_to_all x1, blocking collectives, local(): lax.all_to_all(attended, 'ep', split_axis=1, concat_axis=0, tiled=True)  9.48 us
    dot_general x1, matrix products, expert_slice(): lax.dot_general(flat_slots, gate_weight, contract, preferred_element_type...  8.36 us
    all_to_all x1, starting transfers between devices, local(): lax.all_to_all(queries, 'ep', split_axis=0, concat_axis=1, tiled=True)  7.52 us
    all_to_all x1, waiting for transfers between devices, local(): lax.all_to_all(queries, 'ep', split_axis=0, concat_axis=1, tiled=True)  6.17 us
  transfers between devices with their start and end apart: 3, of which 3 were waited for; matrix products, arithmetic and copies ran while one was open for 1% of the time, Pallas kernels for 0%

commit v1 on v0

v1 whole, which is shorter than its diff:
```python
import jax
import jax.numpy as jnp
from jax import lax
from jax.sharding import PartitionSpec as P

EXPERTS = 8
EPSILON = 1e-05
F32 = jnp.float32
BF16 = jnp.bfloat16


def attend(query_rows, key_values, lengths):
    row_count, context, width = key_values.shape
    head_dim = width // 2
    key_rows = key_values[:, :, :head_dim]
    value_rows = key_values[:, :, head_dim:]
    scores = jnp.einsum(
        "hrd,rtd->rht", query_rows, key_rows, preferred_element_type=F32
    ) * head_dim ** (-0.5)
    positions = lax.broadcasted_iota(jnp.int32, (row_count, 1, context), 2)
    scores = jnp.where(positions < lengths[:, None, None], scores, -1e30)
    row_max = jnp.max(scores, axis=2, keepdims=True)
    weights = jnp.exp(scores - row_max)
    prob_rows = (weights / jnp.sum(weights, axis=2, keepdims=True)).astype(BF16)
    attended = jnp.einsum("rht,rtd->hrd", prob_rows, value_rows, preferred_element_type=F32)
    return attended.astype(BF16)


def swap(x, bit, size):
    return lax.ppermute(x, "ep", [(i, i ^ bit) for i in range(size)])


def rank_bits(size):
    bits, bit = [], 1
    while bit < size:
        bits.append(bit)
        bit *= 2
    return bits


def order_of(bits):
    order = [0]
    for bit in reversed(bits):
        order = order + [o ^ bit for o in order]
    return order


def scatter_sum(parts, bits, size):
    for bit in bits:
        half = parts.shape[0] // 2
        sent = parts[half:].astype(BF16)
        parts = parts[:half].astype(F32) + swap(sent, bit, size).astype(F32)
    return parts[0]


def gather_rows(rows, bits, size):
    gathered = rows[None]
    for bit in reversed(bits):
        gathered = jnp.concatenate([gathered, swap(gathered, bit, size)], axis=0)
    return gathered


def local(
    queries,
    key_values,
    lengths,
    residual,
    routes,
    gate_weights,
    output_weight,
    norm_gain,
    gate_weight,
    up_weight,
    down_weight,
):
    tok = key_values.shape[0]
    head_dim = key_values.shape[2] // 2
    size = lax.axis_size("ep")
    me = lax.axis_index("ep")
    bits = rank_bits(size)
    order = jnp.array(order_of(bits), jnp.int32)
    span = size // EXPERTS
    feature = residual.shape[1]

    expert_ids = jnp.arange(size, dtype=jnp.int32) // span
    matches = routes[:, :, None] == expert_ids[None, None, :]
    gate_by_device = jnp.sum(
        jnp.where(matches, gate_weights.astype(F32)[:, :, None], 0.0), axis=1
    ).astype(BF16)
    gate_payload = jnp.broadcast_to(gate_by_device.T[:, :, None], (size, tok, 128))

    query_rows = lax.all_to_all(
        queries.reshape(size, tok, head_dim), "ep", split_axis=0, concat_axis=0, tiled=True
    )
    attended = attend(query_rows, key_values, lengths)
    head_rows = lax.all_to_all(
        jnp.concatenate([attended, gate_payload], axis=2),
        "ep", split_axis=0, concat_axis=0, tiled=True,
    )
    head_rows = jnp.take(head_rows, me ^ order, axis=0)
    gates = head_rows[:, :, head_dim].reshape(size * tok, 1).astype(F32)
    head_rows = head_rows[:, :, :head_dim].reshape(size * tok, head_dim)
    terms = jnp.dot(head_rows, output_weight, preferred_element_type=F32)
    arrived = scatter_sum(terms.reshape(size, tok, feature), bits, size)
    middle = residual.astype(F32) + arrived
    inverse_root = lax.rsqrt(jnp.mean(middle * middle, axis=1, keepdims=True) + EPSILON)
    normed = (middle * inverse_root * norm_gain).astype(BF16)
    rows = gather_rows(normed, bits, size).reshape(size * tok, feature)
    contract = (((1,), (1,)), ((), ()))
    gate_pre = lax.dot_general(rows, gate_weight, contract, preferred_element_type=F32)
    up_pre = lax.dot_general(rows, up_weight, contract, preferred_element_type=F32)
    hidden = (jax.nn.silu(gate_pre) * up_pre * gates).astype(BF16)
    partial_value = jnp.dot(hidden, down_weight, preferred_element_type=F32)
    combined = scatter_sum(partial_value.reshape(size, tok, feature), bits, size)
    return (middle + combined).astype(BF16)


def solution(mesh):
    in_specs = (
        P("groups", "ep"),
        P(("groups", "ep"), None, None),
        P(("groups", "ep")),
        P(("groups", "ep"), None),
        P(("groups", "ep"), None),
        P(("groups", "ep"), None),
        P("ep", None),
        P(),
        P("ep", None),
        P("ep", None),
        P("ep", None),
    )
    out_specs = P(("groups", "ep"), None)
    return jax.shard_map(local, mesh=mesh, in_specs=in_specs, out_specs=out_specs, check_vma=False)
```

time: 156 us -> 114 us (0.73)
  blocking collectives: 42 us -> 0 us
  waiting for transfers between devices: 63.2 us -> 66.7 us
  matrix products: 28.2 us -> 24.8 us
  starting transfers between devices: 16.7 us -> 13.9 us
  other arithmetic: 3.06 us -> 5.02 us
    ppermute x0 -> x12, waiting for transfers between devices: none -> 54.6 us  [swap(): return lax.ppermute(x, 'ep', [(i, i ^ bit) for i in range(size)])]
    all_to_all x3 -> x2, waiting for transfers between devices: 63.2 us -> 12.1 us  [the longest x1 7.33 us: local(): lax.all_to_all(jnp.concatenate([attended, gate_payload], axis=2), 'ep', s...]
    all_to_all x2 -> x0, blocking collectives: 42 us -> none  [the longest x1 32.5 us: local(): lax.all_to_all(outgoing, 'ep', split_axis=0, concat_axis=0, tiled=True)]
    all_to_all x3 -> x2, starting transfers between devices: 16.7 us -> 11 us  [the longest x1 7.52 us: local(): lax.all_to_all(queries.reshape(size, tok, head_dim), 'ep', split_axis=0,...]
    dot_general x7 -> x5, matrix products: 28.2 us -> 24.8 us  [the longest x1 13.6 us: local(): partial_value = jnp.dot(hidden, down_weight, preferred_element_type=F32)]
    ppermute x0 -> x12, starting transfers between devices: none -> 2.92 us  [swap(): return lax.ppermute(x, 'ep', [(i, i ^ bit) for i in range(size)])]
  transfers between devices with their start and end apart: 3 -> 14, of which waited for: 3 -> 14; matrix products, arithmetic and copies ran while one was open for 1% -> 2% of each run, Pallas kernels for 0% -> 0%
where the time goes in v1:
time: 114 us
  waiting for transfers between devices  66.7 us (59%)
  matrix products  24.8 us (22%)
  starting transfers between devices  13.9 us (12%)
  other arithmetic  5.02 us (4%)
  local copies, waits for them, and re-layouts  2.89 us (3%)
    ppermute x12, waiting for transfers between devices, swap(): return lax.ppermute(x, 'ep', [(i, i ^ bit) for i in range(size)])  54.6 us
    dot_general x1, matrix products, local(): partial_value = jnp.dot(hidden, down_weight, preferred_element_type=F32)  13.6 us
    dot_general x1, matrix products, local(): lax.dot_general(rows, up_weight, contract, preferred_element_type=F32)  7.71 us
    all_to_all x1, starting transfers between devices, local(): lax.all_to_all(queries.reshape(size, tok, head_dim), 'ep', split_axis=0,...  7.52 us
    all_to_all x1, waiting for transfers between devices, local(): lax.all_to_all(jnp.concatenate([attended, gate_payload], axis=2), 'ep', s...  7.33 us
    all_to_all x1, waiting for transfers between devices, local(): lax.all_to_all(queries.reshape(size, tok, head_dim), 'ep', split_axis=0,...  4.73 us
    all_to_all x1, starting transfers between devices, local(): lax.all_to_all(jnp.concatenate([attended, gate_payload], axis=2), 'ep', s...  3.51 us
    ppermute x12, starting transfers between devices, swap(): return lax.ppermute(x, 'ep', [(i, i ^ bit) for i in range(size)])  2.92 us
  transfers between devices with their start and end apart: 14, of which 14 were waited for; matrix products, arithmetic and copies ran while one was open for 2% of the time, Pallas kernels for 0%

profile of v1, /device:TPU:0, one launch (start us, length us, event | category | flops | bytes accessed | tf_op | source)
XLA Modules:
  0.0 113.7 jit_solution(15740132726531634788)
XLA Ops:
  0.0 7.5 %all-to-all-start = ((bf16[16,8,256]{2,1,0:T(8,128)(2,1)}), bf16[16,8,256]{2,1,0:T(8,128)(2,1)S(1)}, u32[]{:S(2)}, u32[]{:S(2)}) async-start(bf16[16,8,256]{2,1,0:T(8,128)(2,1)} %bitcast.56), calls=%async_computation | async-start | bytes 131072 | tf_op jit(solution)/shard_map/all_to_all | solution.py:92
  7.5 0.7 iota_compare_fusion
  8.3 0.7 convert_element_type.84
  8.9 0.8 select_reduce_fusion
  9.7 4.7 %all-to-all-done = bf16[16,8,256]{2,1,0:T(8,128)(2,1)S(1)} async-done(((bf16[16,8,256]{2,1,0:T(8,128)(2,1)}), bf16[16,8,256]{2,1,0:T(8,128)(2,1)S(1)}, u32[]{:S(2)}, u32[]{:S(2)}) %all-to-all-start) | async-done | bytes 65568 | tf_op jit(solution)/shard_map/all_to_all | solution.py:92
  14.4 1.6 %fusion.3 = f32[8,16,256]{2,1,0:T(8,128)S(1)} fusion(bf16[8,256,512]{2,1,0:T(8,128)(2,1)} %param.13, bf16[16,8,256]{2,1,0:T(8,128)(2,1)S(1)} %all-to-all-done, pred[8,256]{1,0:T(8,128)(4,1)S(1)} %iota_compare_fusion), kind=kOutput, calls=%fused_computation.5 | convolution fusion | flops 16842752 | bytes 1247232 | tf_op jit(solution)/shard_map/hrd,rtd->rht/dot_general | solution.py:17
  16.0 0.2 fusion.34
  16.2 1.5 %fusion.4 = bf16[16,8,256]{2,0,1:T(8,128)(2,1)S(1)} fusion(bf16[8,256,512]{2,1,0:T(8,128)(2,1)} %param.13, f32[8,16]{1,0:T(8,128)S(1)} %fusion.34, f32[8,16,256]{2,1,0:T(8,128)S(1)} %fusion.3), kind=kOutput, calls=%fused_computation.7 | convolution fusion | flops 16908672 | bytes 1380352 | tf_op jit(solution)/shard_map/rht,rtd->hrd/dot_general | solution.py:25
  17.8 0.1 broadcast_in_dim.58
  17.9 0.7 copy.25
  18.5 3.5 %all-to-all-start.1 = ((bf16[16,8,384]{2,1,0:T(8,128)(2,1)}), bf16[16,8,384]{2,1,0:T(8,128)(2,1)S(1)}, u32[]{:S(2)}, u32[]{:S(2)}) async-start(bf16[16,8,384]{2,1,0:T(8,128)(2,1)} %copy.25), calls=%async_computation.1 | async-start | bytes 196608 | tf_op jit(solution)/shard_map/all_to_all | solution.py:96
  22.1 7.3 %all-to-all-done.1 = bf16[16,8,384]{2,1,0:T(8,128)(2,1)S(1)} async-done(((bf16[16,8,384]{2,1,0:T(8,128)(2,1)}), bf16[16,8,384]{2,1,0:T(8,128)(2,1)S(1)}, u32[]{:S(2)}, u32[]{:S(2)}) %all-to-all-start.1) | async-done | bytes 98336 | tf_op jit(solution)/shard_map/all_to_all | solution.py:96
  29.4 0.6 gather_fusion
  30.0 0.1 broadcast_select_fusion
  30.1 0.4 fusion.27
  30.6 0.1 collective-permute-start
  30.7 1.8 %collective-permute-done = bf16[8,8,3584]{2,1,0:T(8,128)(2,1)S(1)} collective-permute-done((bf16[8,8,3584]{2,1,0:T(8,128)(2,1)S(1)}, bf16[8,8,3584]{2,1,0:T(8,128)(2,1)S(1)}, u32[]{:S(2)}, u32[]{:S(2)}) %collective-permute-start) | collective-permute-done | bytes 458784 | tf_op jit(solution)/shard_map/ppermute | solution.py:30
  32.5 0.1 fusion.8
  32.7 7.6 %collective-permute-done.1 = bf16[4,8,3584]{2,1,0:T(8,128)(2,1)S(1)} collective-permute-done((bf16[4,8,3584]{2,1,0:T(8,128)(2,1)S(1)}, bf16[4,8,3584]{2,1,0:T(8,128)(2,1)S(1)}, u32[]{:S(2)}, u32[]{:S(2)}) %collective-permute-start.1) | collective-permute-done | bytes 229408 | tf_op jit(solution)/shard_map/ppermute | solution.py:30
  40.4 0.1 collective-permute-start.2
  40.4 4.8 %collective-permute-done.2 = bf16[2,8,3584]{2,1,0:T(8,128)(2,1)S(1)} collective-permute-done((bf16[2,8,3584]{2,1,0:T(8,128)(2,1)S(1)}, bf16[2,8,3584]{2,1,0:T(8,128)(2,1)S(1)}, u32[]{:S(2)}, u32[]{:S(2)}) %collective-permute-start.2) | collective-permute-done | bytes 114720 | tf_op jit(solution)/shard_map/ppermute | solution.py:30
  45.3 0.2 collective-permute-start.3
  45.5 5.0 %collective-permute-done.3 = bf16[1,8,3584]{2,1,0:T(8,128)(2,1)S(1)} collective-permute-done((bf16[1,8,3584]{2,1,0:T(8,128)(2,1)S(1)}, bf16[1,8,3584]{2,1,0:T(8,128)(2,1)S(1)}, u32[]{:S(2)}, u32[]{:S(2)}) %collective-permute-start.3) | collective-permute-done | bytes 57376 | tf_op jit(solution)/shard_map/ppermute | solution.py:30
  50.5 0.1 multiply_reduce_fusion
  50.7 0.1 constant_dynamic-update-slice_fusion.4
  50.7 0.3 collective-permute-start.4
  51.0 5.3 %collective-permute-done.4 = bf16[1,8,3584]{2,1,0:T(8,128)(2,1)S(1)} collective-permute-done((bf16[1,8,3584]{2,1,0:T(8,128)(2,1)S(1)}, bf16[1,8,3584]{2,1,0:T(8,128)(2,1)S(1)}, u32[]{:S(2)}, u32[]{:S(2)}) %collective-permute-start.4) | collective-permute-done | bytes 57376 | tf_op jit(solution)/shard_map/ppermute | solution.py:30
  56.3 0.2 collective-permute-start.5
  56.5 0.1 convert_reduce_fusion
  56.6 0.1 reshape.79
  56.7 4.5 %collective-permute-done.5 = bf16[2,8,3584]{2,1,0:T(8,128)(2,1)S(1)} collective-permute-done((bf16[2,8,3584]{2,1,0:T(8,128)(2,1)S(1)}, bf16[2,8,3584]{2,1,0:T(8,128)(2,1)S(1)}, u32[]{:S(2)}, u32[]{:S(2)}) %collective-permute-start.5) | collective-permute-done | bytes 114720 | tf_op jit(solution)/shard_map/ppermute | solution.py:30
  61.2 0.7 collective-permute-start.6
  62.0 5.3 %collective-permute-done.6 = bf16[4,8,3584]{2,1,0:T(8,128)(2,1)S(1)} collective-permute-done((bf16[4,8,3584]{2,1,0:T(8,128)(2,1)S(1)}, bf16[4,8,3584]{2,1,0:T(8,128)(2,1)S(1)}, u32[]{:S(2)}, u32[]{:S(2)}) %collective-permute-start.6) | collective-permute-done | bytes 229408 | tf_op jit(solution)/shard_map/ppermute | solution.py:30
  67.3 0.1 collective-permute-start.7
  67.5 1.8 %collective-permute-done.7 = bf16[8,8,3584]{2,1,0:T(8,128)(2,1)S(1)} collective-permute-done((bf16[8,8,3584]{2,1,0:T(8,128)(2,1)S(1)}, bf16[8,8,3584]{2,1,0:T(8,128)(2,1)S(1)}, u32[]{:S(2)}, u32[]{:S(2)}) %collective-permute-start.7) | collective-permute-done | bytes 458784 | tf_op jit(solution)/shard_map/ppermute | solution.py:30
  69.3 7.7 %fusion.9 = f32[128,1536]{1,0:T(8,128)S(1)} fusion(bf16[1536,3584]{1,0:T(8,128)(2,1)} %param.21, bf16[16,8,3584]{2,1,0:T(8,128)(2,1)S(1)} %constant_dynamic-update-slice_fusion), kind=kOutput, calls=%fused_computation.16 | convolution fusion | flops 1409286144 | bytes 12713984 | tf_op jit(solution)/shard_map/dot_general | solution.py:111
  77.0 13.6 %fusion.15 = f32[128,3584]{1,0:T(8,128)} fusion(bf16[1536,3584]{1,0:T(8,128)(2,1)} %param.22, f32[128,1536]{1,0:T(8,128)S(1)} %fusion.9, bf16[1536,3584]{1,0:T(8,128)(2,1)} %param.20, bf16[16,8,3584]{2,1,0:T(8,128)(2,1)S(1)} %constant_dynamic-update-slice_fusion, f32[128]{0:T(128)S(1)} %reshape.79), kind=kOutput, calls=%fused_computation.28 | convolution fusion | flops 2819948544 | bytes 25559552 | tf_op jit(solution)/shard_map/dot_general | solution.py:113
  90.6 1.2 %fusion.14 = bf16[8,8,3584]{2,1,0:T(8,128)(2,1)S(1)} fusion(f32[128,3584]{1,0:T(8,128)} %fusion.15), kind=kLoop, calls=%fused_computation.22 | loop fusion | bytes 917504 | tf_op jit(solution)/shard_map/convert_element_type | solution.py:51
  91.8 0.2 collective-permute-start.8
  92.0 1.7 %collective-permute-done.8 = bf16[8,8,3584]{2,1,0:T(8,128)(2,1)S(1)} collective-permute-done((bf16[8,8,3584]{2,1,0:T(8,128)(2,1)S(1)}, bf16[8,8,3584]{2,1,0:T(8,128)(2,1)S(1)}, u32[]{:S(2)}, u32[]{:S(2)}) %collective-permute-start.8) | collective-permute-done | bytes 458784 | tf_op jit(solution)/shard_map/ppermute | solution.py:30
  93.7 1.3 %fusion.7 = f32[8,8,3584]{2,1,0:T(8,128)S(1)} fusion(f32[128,3584]{1,0:T(8,128)} %fusion.15, bf16[8,8,3584]{2,1,0:T(8,128)(2,1)S(1)} %collective-permute-done.8), kind=kLoop, calls=%fused_computation.12 | loop fusion | flops 458752 | bytes 2293760 | tf_op jit(solution)/shard_map/add | solution.py:52
  95.0 0.7 collective-permute-start.9
  95.7 7.0 %collective-permute-done.9 = bf16[4,8,3584]{2,1,0:T(8,128)(2,1)S(1)} collective-permute-done((bf16[4,8,3584]{2,1,0:T(8,128)(2,1)S(1)}, bf16[4,8,3584]{2,1,0:T(8,128)(2,1)S(1)}, u32[]{:S(2)}, u32[]{:S(2)}) %collective-permute-start.9) | collective-permute-done | bytes 229408 | tf_op jit(solution)/shard_map/ppermute | solution.py:30
  102.8 0.2 collective-permute-start.10
  103.0 4.6 %collective-permute-done.10 = bf16[2,8,3584]{2,1,0:T(8,128)(2,1)S(1)} collective-permute-done((bf16[2,8,3584]{2,1,0:T(8,128)(2,1)S(1)}, bf16[2,8,3584]{2,1,0:T(8,128)(2,1)S(1)}, u32[]{:S(2)}, u32[]{:S(2)}) %collective-permute-start.10) | collective-permute-done | bytes 114720 | tf_op jit(solution)/shard_map/ppermute | solution.py:30
  107.7 0.1 collective-permute-start.11
  107.8 5.3 %collective-permute-done.11 = bf16[1,8,3584]{2,1,0:T(8,128)(2,1)S(1)} collective-permute-done((bf16[1,8,3584]{2,1,0:T(8,128)(2,1)S(1)}, bf16[1,8,3584]{2,1,0:T(8,128)(2,1)S(1)}, u32[]{:S(2)}, u32[]{:S(2)}) %collective-permute-start.11) | collective-permute-done | bytes 57376 | tf_op jit(solution)/shard_map/ppermute | solution.py:30
  113.0 0.7 fusion.24
  (42 shorter events, 0.6 us)
Async XLA Ops:
  0.0 30.1 %copy-start = (bf16[256,3584]{1,0:T(8,128)(2,1)S(1)}, bf16[256,3584]{1,0:T(8,128)(2,1)}, u32[]{:S(2)}) copy-start(bf16[256,3584]{1,0:T(8,128)(2,1)} %param.18) | copy-start | bytes 5505028
  0.0 22.0 %copy-start.8 = (s32[16]{0:T(128)S(1)}, s32[16]{0:T(128)}, u32[]{:S(2)}) copy-start(s32[16]{0:T(128)} %constant.53.clone) | copy-start | bytes 196
  0.0 14.4 %all-to-all-start = ((bf16[16,8,256]{2,1,0:T(8,128)(2,1)}), bf16[16,8,256]{2,1,0:T(8,128)(2,1)S(1)}, u32[]{:S(2)}, u32[]{:S(2)}) async-start(bf16[16,8,256]{2,1,0:T(8,128)(2,1)} %bitcast.56), calls=%async_computation | async-start | bytes 131072 | tf_op jit(solution)/shard_map/all_to_all | solution.py:92
  18.5 10.9 %all-to-all-start.1 = ((bf16[16,8,384]{2,1,0:T(8,128)(2,1)}), bf16[16,8,384]{2,1,0:T(8,128)(2,1)S(1)}, u32[]{:S(2)}, u32[]{:S(2)}) async-start(bf16[16,8,384]{2,1,0:T(8,128)(2,1)} %copy.25), calls=%async_computation.1 | async-start | bytes 196608 | tf_op jit(solution)/shard_map/all_to_all | solution.py:96
  30.6 19.9 %copy-start.3 = (bf16[8,3584]{1,0:T(8,128)(2,1)S(1)}, bf16[8,3584]{1,0:T(8,128)(2,1)}, u32[]{:S(2)}) copy-start(bf16[8,3584]{1,0:T(8,128)(2,1)} %param.15) | copy-start | bytes 172036
  30.6 20.1 %copy-start.7 = (f32[3584]{0:T(1024)S(1)}, f32[3584]{0:T(1024)}, u32[]{:S(2)}) copy-start(f32[3584]{0:T(1024)} %param.19) | copy-start | bytes 43012
  30.6 1.9 %collective-permute-start = (bf16[8,8,3584]{2,1,0:T(8,128)(2,1)S(1)}, bf16[8,8,3584]{2,1,0:T(8,128)(2,1)S(1)}, u32[]{:S(2)}, u32[]{:S(2)}) collective-permute-start(bf16[8,8,3584]{2,1,0:T(8,128)(2,1)S(1)} %fusion.13), channel_id=1, source_target_pairs={{0,1},{1,0},{2,3},{3,2},{4,5},{5,4},{6,7},{7,6},{8,9},{9,8},{10,11... | collective-permute-start | bytes 1376264 | tf_op jit(solution)/shard_map/ppermute | solution.py:30
  32.6 7.7 %collective-permute-start.1 = (bf16[4,8,3584]{2,1,0:T(8,128)(2,1)S(1)}, bf16[4,8,3584]{2,1,0:T(8,128)(2,1)S(1)}, u32[]{:S(2)}, u32[]{:S(2)}) collective-permute-start(bf16[4,8,3584]{2,1,0:T(8,128)(2,1)S(1)} %slice.166), channel_id=1, source_target_pairs={{0,2},{1,3},{2,0},{3,1},{4,6},{5,7},{6,4},{7,5},{8,10},{9,11},{10,... | collective-permute-start | bytes 688136 | tf_op jit(solution)/shard_map/ppermute | solution.py:30
  40.4 4.9 %collective-permute-start.2 = (bf16[2,8,3584]{2,1,0:T(8,128)(2,1)S(1)}, bf16[2,8,3584]{2,1,0:T(8,128)(2,1)S(1)}, u32[]{:S(2)}, u32[]{:S(2)}) collective-permute-start(bf16[2,8,3584]{2,1,0:T(8,128)(2,1)S(1)} %slice.168), channel_id=1, source_target_pairs={{0,4},{1,5},{2,6},{3,7},{4,0},{5,1},{6,2},{7,3},{8,12},{9,13},{10,... | collective-permute-start | bytes 344072 | tf_op jit(solution)/shard_map/ppermute | solution.py:30
  45.2 5.4 %copy-start.1 = (f32[2,8,3584]{2,1,0:T(8,128)}, f32[2,8,3584]{2,1,0:T(8,128)S(1)}, u32[]{:S(2)}) copy-start(f32[2,8,3584]{2,1,0:T(8,128)S(1)} %slice_add_fusion.3) | copy-start | bytes 688132
  45.3 5.2 %collective-permute-start.3 = (bf16[1,8,3584]{2,1,0:T(8,128)(2,1)S(1)}, bf16[1,8,3584]{2,1,0:T(8,128)(2,1)S(1)}, u32[]{:S(2)}, u32[]{:S(2)}) collective-permute-start(bf16[1,8,3584]{2,1,0:T(8,128)(2,1)S(1)} %slice.170), channel_id=1, source_target_pairs={{0,8},{1,9},{2,10},{3,11},{4,12},{5,13},{6,14},{7,15},{8,0},{9,1},... | collective-permute-start | bytes 172040 | tf_op jit(solution)/shard_map/ppermute | solution.py:30
  50.5 5.8 %copy-start.5 = (bf16[1,8,3584]{2,1,0:T(8,128)(2,1)}, bf16[1,8,3584]{2,1,0:T(8,128)(2,1)S(1)}, u32[]{:S(2)}) copy-start(bf16[1,8,3584]{2,1,0:T(8,128)(2,1)S(1)} %collective-permute-done.3) | copy-start | bytes 172036
  50.7 5.6 %collective-permute-start.4 = (bf16[1,8,3584]{2,1,0:T(8,128)(2,1)S(1)}, bf16[1,8,3584]{2,1,0:T(8,128)(2,1)S(1)}, u32[]{:S(2)}, u32[]{:S(2)}) collective-permute-start(bf16[1,8,3584]{2,1,0:T(8,128)(2,1)S(1)} %get-tuple-element.6), channel_id=1, source_target_pairs={{0,8},{1,9},{2,10},{3,11},{4,12},{5,13},{6,14},{7,15},{8,0},{9,1},... | collective-permute-start | bytes 172040 | tf_op jit(solution)/shard_map/ppermute | solution.py:30
  56.3 4.9 %collective-permute-start.5 = (bf16[2,8,3584]{2,1,0:T(8,128)(2,1)S(1)}, bf16[2,8,3584]{2,1,0:T(8,128)(2,1)S(1)}, u32[]{:S(2)}, u32[]{:S(2)}) collective-permute-start(bf16[2,8,3584]{2,1,0:T(8,128)(2,1)S(1)} %pad_maximum_fusion.2), channel_id=1, source_target_pairs={{0,4},{1,5},{2,6},{3,7},{4,0},{5,1},{6,2},{7,3},{8,12},{9,13},{10,... | collective-permute-start | bytes 344072 | tf_op jit(solution)/shard_map/ppermute | solution.py:30
  61.2 6.1 %collective-permute-start.6 = (bf16[4,8,3584]{2,1,0:T(8,128)(2,1)S(1)}, bf16[4,8,3584]{2,1,0:T(8,128)(2,1)S(1)}, u32[]{:S(2)}, u32[]{:S(2)}) collective-permute-start(bf16[4,8,3584]{2,1,0:T(8,128)(2,1)S(1)} %pad_maximum_fusion.1), channel_id=1, source_target_pairs={{0,2},{1,3},{2,0},{3,1},{4,6},{5,7},{6,4},{7,5},{8,10},{9,11},{10,... | collective-permute-start | bytes 688136 | tf_op jit(solution)/shard_map/ppermute | solution.py:30
  67.3 1.9 %collective-permute-start.7 = (bf16[8,8,3584]{2,1,0:T(8,128)(2,1)S(1)}, bf16[8,8,3584]{2,1,0:T(8,128)(2,1)S(1)}, u32[]{:S(2)}, u32[]{:S(2)}) collective-permute-start(bf16[8,8,3584]{2,1,0:T(8,128)(2,1)S(1)} %pad_maximum_fusion), channel_id=1, source_target_pairs={{0,1},{1,0},{2,3},{3,2},{4,5},{5,4},{6,7},{7,6},{8,9},{9,8},{10,11... | collective-permute-start | bytes 1376264 | tf_op jit(solution)/shard_map/ppermute | solution.py:30
  91.8 21.2 %copy-start.2 = (f32[2,8,3584]{2,1,0:T(8,128)S(1)}, f32[2,8,3584]{2,1,0:T(8,128)}, u32[]{:S(2)}) copy-start(f32[2,8,3584]{2,1,0:T(8,128)} %copy-done.1) | copy-start | bytes 688132
  91.8 21.2 %copy-start.4 = (bf16[8,3584]{1,0:T(8,128)(2,1)S(1)}, bf16[8,3584]{1,0:T(8,128)(2,1)}, u32[]{:S(2)}) copy-start(bf16[8,3584]{1,0:T(8,128)(2,1)} %param.15) | copy-start | bytes 172036
  91.8 21.2 %copy-start.6 = (bf16[1,8,3584]{2,1,0:T(8,128)(2,1)S(1)}, bf16[1,8,3584]{2,1,0:T(8,128)(2,1)}, u32[]{:S(2)}) copy-start(bf16[1,8,3584]{2,1,0:T(8,128)(2,1)} %copy-done.5) | copy-start | bytes 172036
  91.8 1.9 %collective-permute-start.8 = (bf16[8,8,3584]{2,1,0:T(8,128)(2,1)S(1)}, bf16[8,8,3584]{2,1,0:T(8,128)(2,1)S(1)}, u32[]{:S(2)}, u32[]{:S(2)}) collective-permute-start(bf16[8,8,3584]{2,1,0:T(8,128)(2,1)S(1)} %fusion.14), channel_id=1, source_target_pairs={{0,1},{1,0},{2,3},{3,2},{4,5},{5,4},{6,7},{7,6},{8,9},{9,8},{10,11... | collective-permute-start | bytes 1376264 | tf_op jit(solution)/shard_map/ppermute | solution.py:30
  95.0 7.7 %collective-permute-start.9 = (bf16[4,8,3584]{2,1,0:T(8,128)(2,1)S(1)}, bf16[4,8,3584]{2,1,0:T(8,128)(2,1)S(1)}, u32[]{:S(2)}, u32[]{:S(2)}) collective-permute-start(bf16[4,8,3584]{2,1,0:T(8,128)(2,1)S(1)} %slice.165), channel_id=1, source_target_pairs={{0,2},{1,3},{2,0},{3,1},{4,6},{5,7},{6,4},{7,5},{8,10},{9,11},{10,... | collective-permute-start | bytes 688136 | tf_op jit(solution)/shard_map/ppermute | solution.py:30
  102.8 4.9 %collective-permute-start.10 = (bf16[2,8,3584]{2,1,0:T(8,128)(2,1)S(1)}, bf16[2,8,3584]{2,1,0:T(8,128)(2,1)S(1)}, u32[]{:S(2)}, u32[]{:S(2)}) collective-permute-start(bf16[2,8,3584]{2,1,0:T(8,128)(2,1)S(1)} %slice.167), channel_id=1, source_target_pairs={{0,4},{1,5},{2,6},{3,7},{4,0},{5,1},{6,2},{7,3},{8,12},{9,13},{10,... | collective-permute-start | bytes 344072 | tf_op jit(solution)/shard_map/ppermute | solution.py:30
  107.7 5.3 %collective-permute-start.11 = (bf16[1,8,3584]{2,1,0:T(8,128)(2,1)S(1)}, bf16[1,8,3584]{2,1,0:T(8,128)(2,1)S(1)}, u32[]{:S(2)}, u32[]{:S(2)}) collective-permute-start(bf16[1,8,3584]{2,1,0:T(8,128)(2,1)S(1)} %slice.169), channel_id=1, source_target_pairs={{0,8},{1,9},{2,10},{3,11},{4,12},{5,13},{6,14},{7,15},{8,0},{9,1},... | collective-permute-start | bytes 172040 | tf_op jit(solution)/shard_map/ppermute | solution.py:30

commit v2 on v1

v2 whole, which is shorter than its diff:
```python
import functools

import jax
import jax.numpy as jnp
from jax import lax
from jax.experimental import pallas as pl
from jax.experimental.pallas import tpu as pltpu
from jax.sharding import PartitionSpec as P

EXPERTS = 8
EPSILON = 1e-05
LANES = 128
F32 = jnp.float32
BF16 = jnp.bfloat16
VMEM_SPEC = pl.BlockSpec(memory_space=pltpu.VMEM)
HBM_SPEC = pl.BlockSpec(memory_space=pltpu.HBM)
SMEM_SPEC = pl.BlockSpec(memory_space=pltpu.SMEM)


def tile_of(extent, most):
    return max(t for t in range(LANES, most + 1, LANES) if extent % t == 0)


def attend_kernel(lengths_ref, routes_ref, shares_ref, query_ref, source_ref, out_ref, cache_ref, sems):
    heads, tok, head_dim = query_ref.shape
    context = cache_ref.shape[1]
    span = heads // EXPERTS
    copies = [
        pltpu.make_async_copy(source_ref.at[row], cache_ref.at[row], sems.at[row])
        for row in range(tok)
    ]
    for copy in copies:
        copy.start()
    rows = heads * tok
    turned = query_ref[...].reshape(rows, head_dim).T
    lane_row = lax.broadcasted_iota(jnp.int32, (context, rows), 1) % tok
    position = lax.broadcasted_iota(jnp.int32, (context, rows), 0)
    scores = jnp.zeros((context, rows), F32)
    live = jnp.zeros((context, rows), jnp.int32)
    for row in range(tok):
        copies[row].wait()
        found = jnp.dot(cache_ref[row, :, :head_dim], turned, preferred_element_type=F32)
        scores = jnp.where(lane_row == row, found, scores)
        live = jnp.where(lane_row == row, lengths_ref[row], live)
    scores = jnp.where(position < live, scores * head_dim ** (-0.5), -1e30)
    weights = jnp.exp(scores - jnp.max(scores, axis=0, keepdims=True))
    prob = (weights / jnp.sum(weights, axis=0, keepdims=True)).T.astype(BF16)
    out_row = lax.broadcasted_iota(jnp.int32, (rows, head_dim), 0) % tok
    attended = jnp.zeros((rows, head_dim), F32)
    for row in range(tok):
        found = jnp.dot(prob, cache_ref[row, :, head_dim:], preferred_element_type=F32)
        attended = jnp.where(out_row == row, found, attended)
    out_ref[:, :, :head_dim] = attended.astype(BF16).reshape(heads, tok, head_dim)
    place = lax.broadcasted_iota(jnp.int32, (rows, LANES), 0)
    expert = place // (tok * span)
    gates = jnp.zeros((rows, LANES), F32)
    for row in range(tok):
        for k in range(routes_ref.shape[1]):
            named = (place % tok == row) & (expert == routes_ref[row, k])
            gates = gates + jnp.where(named, shares_ref[row, k], 0.0)
    out_ref[:, :, head_dim:] = gates.astype(BF16).reshape(heads, tok, LANES)


def attend(lengths, routes, shares, query_rows, cache):
    heads, tok, head_dim = query_rows.shape
    return pl.pallas_call(
        attend_kernel,
        out_shape=jax.ShapeDtypeStruct((heads, tok, head_dim + LANES), BF16),
        in_specs=[SMEM_SPEC] * 3 + [VMEM_SPEC, HBM_SPEC],
        out_specs=VMEM_SPEC,
        scratch_shapes=[
            pltpu.VMEM(cache.shape, cache.dtype),
            pltpu.SemaphoreType.DMA((tok,)),
        ],
        compiler_params=pltpu.CompilerParams(vmem_limit_bytes=8 << 20),
    )(lengths, routes, shares, query_rows, pltpu.with_memory_space_constraint(cache, pltpu.HBM))


def project_kernel(core_ref, rows_ref, weight_ref, kept_ref, sent_ref, gates_ref):
    chips, _, tok, _ = rows_ref.shape
    head_dim = weight_ref.shape[0]
    half = chips * tok
    mine = core_ref[0]
    for place, core, out_ref in ((1, 1 - mine, sent_ref), (0, mine, kept_ref)):
        block = rows_ref[:, pl.ds(core, 1)].reshape(half, head_dim + LANES)
        out_ref[...] = jnp.dot(
            block[:, :head_dim], weight_ref[...], preferred_element_type=F32
        ).astype(out_ref.dtype)
        gates_ref[pl.ds(place * half, half), :] = block[:, head_dim:]


def project(core, rows, weight):
    chips, _, tok, _ = rows.shape
    half = chips * tok
    feature = weight.shape[1]
    return pl.pallas_call(
        project_kernel,
        out_shape=(
            jax.ShapeDtypeStruct((half, feature), F32),
            jax.ShapeDtypeStruct((half, feature), BF16),
            jax.ShapeDtypeStruct((2 * half, LANES), BF16),
        ),
        in_specs=[SMEM_SPEC, VMEM_SPEC, VMEM_SPEC],
        out_specs=(VMEM_SPEC, VMEM_SPEC, VMEM_SPEC),
        compiler_params=pltpu.CompilerParams(vmem_limit_bytes=8 << 20),
    )(core, rows, weight)


def expert_kernel(
    own_ref, other_ref, gates_ref, gate_source, up_source, down_source, kept_ref, sent_ref,
    turned, hidden, gate_ref, up_ref, down_ref, sems,
):
    half = own_ref.shape[0]
    units, feature = gate_ref.shape
    step = tile_of(units, 384)
    wide = tile_of(feature, 896)

    def unit_copies(at):
        rows = pl.ds(at, step)
        return [
            pltpu.make_async_copy(source.at[rows], target.at[rows], sems.at[which, at // step])
            for which, (source, target) in enumerate(((gate_source, gate_ref), (up_source, up_ref)))
        ]

    def down_copy(at):
        columns = pl.ds(at, wide)
        return pltpu.make_async_copy(
            down_source.at[:, columns], down_ref.at[:, columns], sems.at[2, at // wide]
        )

    for at in range(0, units, step):
        for copy in unit_copies(at):
            copy.start()
    for at in range(0, feature, wide):
        down_copy(at).start()
    turned[:, :half] = own_ref[...].T
    turned[:, half:] = other_ref[...].T
    gates = gates_ref[:, :1].astype(F32)
    for at in range(0, units, step):
        for copy in unit_copies(at):
            copy.wait()
        rows = pl.ds(at, step)
        gate_pre = jnp.dot(gate_ref[rows, :], turned[...], preferred_element_type=F32)
        up_pre = jnp.dot(up_ref[rows, :], turned[...], preferred_element_type=F32)
        product = gate_pre / (1.0 + jnp.exp(-gate_pre)) * up_pre
        hidden[:, rows] = (product.T * gates).astype(BF16)
    for at in range(0, feature, wide):
        down_copy(at).wait()
        columns = pl.ds(at, wide)
        part = jnp.dot(hidden[...], down_ref[:, columns], preferred_element_type=F32)
        kept_ref[:, columns] = part[:half]
        sent_ref[:, columns] = part[half:].astype(BF16)


def experts(own, other, gates, gate_weight, up_weight, down_weight):
    half, feature = own.shape
    units = gate_weight.shape[0]
    weights = (gate_weight, up_weight, down_weight)
    return pl.pallas_call(
        expert_kernel,
        out_shape=(
            jax.ShapeDtypeStruct((half, feature), F32),
            jax.ShapeDtypeStruct((half, feature), BF16),
        ),
        in_specs=[VMEM_SPEC] * 3 + [HBM_SPEC] * 3,
        out_specs=(VMEM_SPEC, VMEM_SPEC),
        scratch_shapes=[
            pltpu.VMEM((feature, 2 * half), BF16),
            pltpu.VMEM((2 * half, units), BF16),
        ]
        + [pltpu.VMEM((units, feature), BF16)] * 3
        + [pltpu.SemaphoreType.DMA((3, 8))],
        compiler_params=pltpu.CompilerParams(vmem_limit_bytes=44 << 20),
        cost_estimate=pl.CostEstimate(
            flops=12 * half * feature * units,
            bytes_accessed=6 * units * feature,
            transcendentals=2 * half * units,
        ),
    )(own, other, gates, *[pltpu.with_memory_space_constraint(w, pltpu.HBM) for w in weights])


def local(
    queries,
    key_values,
    lengths,
    residual,
    routes,
    gate_weights,
    output_weight,
    norm_gain,
    gate_weight,
    up_weight,
    down_weight,
):
    tok = key_values.shape[0]
    head_dim = key_values.shape[2] // 2
    size = lax.axis_size("ep")
    chips = size // 2
    core = lax.rem(lax.axis_index("ep"), 2).astype(jnp.int32).reshape(1)
    same_core = [[2 * chip + c for chip in range(chips)] for c in range(2)]
    feature = residual.shape[1]

    def swap_cores(x):
        return lax.ppermute(x, "ep", [(i, i ^ 1) for i in range(size)])

    def sum_over_chips(kept, arrived):
        summed = (kept + arrived.astype(F32)).astype(BF16).reshape(chips, tok, feature)
        blocks = lax.all_to_all(
            summed, "ep", split_axis=0, concat_axis=0, tiled=True, axis_index_groups=same_core
        )
        return jnp.sum(blocks.astype(F32), axis=0)

    query_rows = lax.all_to_all(
        queries.reshape(size, tok, head_dim), "ep", split_axis=0, concat_axis=0, tiled=True
    )
    attended = attend(lengths, routes, gate_weights.astype(F32), query_rows, key_values)
    head_rows = lax.all_to_all(attended, "ep", split_axis=0, concat_axis=0, tiled=True)
    kept, sent, gates = project(
        core, head_rows.reshape(chips, 2, tok, head_dim + LANES), output_weight
    )
    middle = residual.astype(F32) + sum_over_chips(kept, swap_cores(sent))
    inverse_root = lax.rsqrt(jnp.mean(middle * middle, axis=1, keepdims=True) + EPSILON)
    normed = (middle * inverse_root * norm_gain).astype(BF16)
    own = lax.all_to_all(
        jnp.broadcast_to(normed[None], (chips, tok, feature)),
        "ep", split_axis=0, concat_axis=0, tiled=True, axis_index_groups=same_core,
    ).reshape(chips * tok, feature)
    kept, sent = experts(own, swap_cores(own), gates, gate_weight, up_weight, down_weight)
    combined = sum_over_chips(kept, swap_cores(sent))
    return (middle + combined).astype(BF16)


def solution(mesh):
    in_specs = (
        P("groups", "ep"),
        P(("groups", "ep"), None, None),
        P(("groups", "ep")),
        P(("groups", "ep"), None),
        P(("groups", "ep"), None),
        P(("groups", "ep"), None),
        P("ep", None),
        P(),
        P("ep", None),
        P("ep", None),
        P("ep", None),
    )
    out_specs = P(("groups", "ep"), None)
    return jax.shard_map(local, mesh=mesh, in_specs=in_specs, out_specs=out_specs, check_vma=False)
```

time: 114 us -> 103 us (0.904)
  blocking collectives: 0 us -> 49.7 us
  waiting for transfers between devices: 66.7 us -> 18 us
  matrix products: 24.8 us -> 0 us
  Pallas kernels: 0 us -> 17.2 us
  starting transfers between devices: 13.9 us -> 11.2 us
  other arithmetic: 5.02 us -> 2.83 us
    all_to_all x0 -> x3, blocking collectives: none -> 49.7 us  [the longest x2 33 us: sum_over_chips(): lax.all_to_all(summed, 'ep', split_axis=0, concat_axis=0, tiled=True, axi...]
    ppermute x12 -> x3, waiting for transfers between devices: 54.6 us -> 5.29 us  [swap_cores(): return lax.ppermute(x, 'ep', [(i, i ^ 1) for i in range(size)])]
    dot_general x5 -> x0, matrix products: 24.8 us -> none  [the longest x1 13.6 us: local(): partial_value = jnp.dot(hidden, down_weight, preferred_element_type=F32)]
    pallas_call x0 -> x3, Pallas kernels: none -> 17.2 us  [the longest x1 11.9 us: experts(): pl.pallas_call(expert_kernel, out_shape=(jax.ShapeDtypeStruct((half, feat...]
    unnamed x21 -> x8, local copies, waits for them, and re-layouts: 0.08 us -> 3.68 us
    ppermute x12 -> x3, starting transfers between devices: 2.92 us -> 0.28 us  [swap_cores(): return lax.ppermute(x, 'ep', [(i, i ^ 1) for i in range(size)])]
    add x6 -> x0, other arithmetic: 1.47 us -> none  [scatter_sum(): parts = parts[:half].astype(F32) + swap(sent, bit, size).astype(F32)]
    convert_element_type x3 -> x0, local copies, waits for them, and re-layouts: 1.36 us -> none  [the longest x2 1.27 us: scatter_sum(): sent = parts[half:].astype(BF16)]
  transfers between devices with their start and end apart: 14 -> 5, of which waited for: 14 -> 5; matrix products, arithmetic and copies ran while one was open for 2% -> 1% of each run, Pallas kernels for 0% -> 0%
where the time goes in v2:
time: 103 us
  blocking collectives  49.7 us (48%)
  waiting for transfers between devices  18 us (17%)
  Pallas kernels  17.2 us (17%)
  starting transfers between devices  11.2 us (11%)
  local copies, waits for them, and re-layouts  3.71 us (4%)
  other arithmetic  2.83 us (3%)
    all_to_all x2, blocking collectives, sum_over_chips(): lax.all_to_all(summed, 'ep', split_axis=0, concat_axis=0, tiled=True, axi...  33 us
    all_to_all x1, blocking collectives, local(): lax.all_to_all(jnp.broadcast_to(normed[None], (chips, tok, feature)), 'ep...  16.7 us
    pallas_call x1, Pallas kernels, experts(): pl.pallas_call(expert_kernel, out_shape=(jax.ShapeDtypeStruct((half, feat...  11.9 us
    all_to_all x1, starting transfers between devices, local(): lax.all_to_all(queries.reshape(size, tok, head_dim), 'ep', split_axis=0,...  7.39 us
    all_to_all x1, waiting for transfers between devices, local(): lax.all_to_all(attended, 'ep', split_axis=0, concat_axis=0, tiled=True)  7.37 us
    all_to_all x1, waiting for transfers between devices, local(): lax.all_to_all(queries.reshape(size, tok, head_dim), 'ep', split_axis=0,...  5.36 us
    ppermute x3, waiting for transfers between devices, swap_cores(): return lax.ppermute(x, 'ep', [(i, i ^ 1) for i in range(size)])  5.29 us
    pallas_call x1, Pallas kernels, attend(): pl.pallas_call(attend_kernel, out_shape=jax.ShapeDtypeStruct((heads, tok,...  4.53 us
  transfers between devices with their start and end apart: 5, of which 5 were waited for; matrix products, arithmetic and copies ran while one was open for 1% of the time, Pallas kernels for 0%

profile of v2, /device:TPU:0, one launch (start us, length us, event | category | flops | bytes accessed | tf_op | source)
XLA Modules:
  0.0 102.7 jit_solution(13857561886985006897)
XLA Ops:
  0.0 7.4 %all-to-all-start = ((bf16[16,8,256]{2,1,0:T(8,128)(2,1)}), bf16[16,8,256]{2,1,0:T(8,128)(2,1)S(1)}, u32[]{:S(2)}, u32[]{:S(2)}) async-start(bf16[16,8,256]{2,1,0:T(8,128)(2,1)} %bitcast.11), calls=%async_computation | async-start | bytes 131072 | tf_op jit(solution)/shard_map/all_to_all | solution.py:213
  7.4 0.8 copy.12
  8.2 0.8 copy.13.routes_ref
  8.9 5.4 %all-to-all-done.query_ref = bf16[16,8,256]{2,1,0:T(8,128)(2,1)S(1)} async-done(((bf16[16,8,256]{2,1,0:T(8,128)(2,1)}), bf16[16,8,256]{2,1,0:T(8,128)(2,1)S(1)}, u32[]{:S(2)}, u32[]{:S(2)}) %all-to-all-start) | async-done | bytes 65568 | tf_op jit(solution)/shard_map/all_to_all | solution.py:213
  14.3 0.0 copy-start.1
  14.3 0.7 copy-done.1
  14.9 4.5 %shard_map.109 = bf16[16,8,384]{2,1,0:T(8,128)(2,1)} custom-call(s32[8]{0:T(128)S(1)} %copy-done.1, s32[8,3]{1,0:T(8,128)S(1)} %copy.13.routes_ref, f32[8,3]{1,0:T(8,128)S(1)} %convert_element_type.31.shares_ref, bf16[16,8,256]{2,1,0:T(8,128)(2,1)S(1)} %all-to-all-done.query_ref, bf16[8,256,512]{2,1,0:T(8,128)(2,1)} %source_ref.1), custom_call_target="tpu_custom_call" | custom-call | tf_op jit(solution)/shard_map/pallas_call | solution.py:66
  19.5 3.5 %all-to-all-start.1 = ((bf16[16,8,384]{2,1,0:T(8,128)(2,1)}), bf16[16,8,384]{2,1,0:T(8,128)(2,1)S(1)}, u32[]{:S(2)}, u32[]{:S(2)}) async-start(bf16[16,8,384]{2,1,0:T(8,128)(2,1)} %shard_map.109), calls=%async_computation.1 | async-start | bytes 196608 | tf_op jit(solution)/shard_map/all_to_all | solution.py:217
  23.0 7.4 %all-to-all-done.1 = bf16[16,8,384]{2,1,0:T(8,128)(2,1)S(1)} async-done(((bf16[16,8,384]{2,1,0:T(8,128)(2,1)}), bf16[16,8,384]{2,1,0:T(8,128)(2,1)S(1)}, u32[]{:S(2)}, u32[]{:S(2)}) %all-to-all-start.1) | async-done | bytes 98336 | tf_op jit(solution)/shard_map/all_to_all | solution.py:217
  30.4 0.0 copy-start
  30.4 1.5 %copy-done = bf16[256,3584]{1,0:T(8,128)(2,1)S(1)} copy-done((bf16[256,3584]{1,0:T(8,128)(2,1)S(1)}, bf16[256,3584]{1,0:T(8,128)(2,1)}, u32[]{:S(2)}) %copy-start) | copy-done | bytes 1835032
  31.9 0.8 shard_map.110
  32.6 0.1 collective-permute-start
  32.7 1.8 %collective-permute-done = bf16[64,3584]{1,0:T(8,128)(2,1)S(1)} collective-permute-done((bf16[64,3584]{1,0:T(8,128)(2,1)S(1)}, bf16[64,3584]{1,0:T(8,128)(2,1)S(1)}, u32[]{:S(2)}, u32[]{:S(2)}) %collective-permute-start) | collective-permute-done | bytes 458784 | tf_op jit(solution)/shard_map/ppermute | solution.py:204
  34.5 0.1 fusion
  34.6 16.2 %all_to_all.25 = bf16[8,8,3584]{2,1,0:T(8,128)(2,1)S(1)} all-to-all(bf16[8,8,3584]{2,1,0:T(8,128)(2,1)S(1)} %fusion), channel_id=1, replica_groups={{0,2,4,6,8,10,12,14},{1,3,5,7,9,11,13,15},{16,18,20,22,24,26,28,30},{17..., dimensions={0} | all-to-all | bytes 917504 | tf_op jit(solution)/shard_map/all_to_all | solution.py:208
  50.8 0.1 convert_reduce_fusion.1
  50.8 1.0 multiply_reduce_fusion
  51.8 0.9 multiply_convert_fusion
  52.8 16.7 %all_to_all.26 = bf16[8,8,3584]{2,1,0:T(8,128)(2,1)S(1)} all-to-all(bf16[8,8,3584]{2,1,0:T(8,128)(2,1)S(1)} %broadcast_in_dim.2), channel_id=1, replica_groups={{0,2,4,6,8,10,12,14},{1,3,5,7,9,11,13,15},{16,18,20,22,24,26,28,30},{17..., dimensions={0} | all-to-all | bytes 917504 | tf_op jit(solution)/shard_map/all_to_all | solution.py:224
  69.4 0.0 collective-permute-start.1
  69.4 1.8 %collective-permute-done.1.other_ref = bf16[64,3584]{1,0:T(8,128)(2,1)S(1)} collective-permute-done((bf16[64,3584]{1,0:T(8,128)(2,1)S(1)}, bf16[64,3584]{1,0:T(8,128)(2,1)S(1)}, u32[]{:S(2)}, u32[]{:S(2)}) %collective-permute-start.1) | collective-permute-done | bytes 458784 | tf_op jit(solution)/shard_map/ppermute | solution.py:204
  71.3 0.0 copy-start.2
  71.3 11.9 %shard_map.111 = (f32[64,3584]{1,0:T(8,128)S(1)}, bf16[64,3584]{1,0:T(8,128)(2,1)S(1)}) custom-call(bf16[64,3584]{1,0:T(8,128)(2,1)S(1)} %bitcast.9, bf16[64,3584]{1,0:T(8,128)(2,1)S(1)} %collective-permute-done.1.other_ref, bf16[128,128]{1,0:T(8,128)(2,1)S(1)} %get-tuple-element.12.gates_ref, bf16[1536,3584]{1,0:T(8,128)(2,1)} %gate_source.1, ...), custom_call_target="tpu_custom_call" | custom-call | flops 4227858432 | bytes 33030144 | tf_op jit(solution)/shard_map/pallas_call | solution.py:159
  83.2 0.2 collective-permute-start.2
  83.4 1.7 %collective-permute-done.2 = bf16[64,3584]{1,0:T(8,128)(2,1)S(1)} collective-permute-done((bf16[64,3584]{1,0:T(8,128)(2,1)S(1)}, bf16[64,3584]{1,0:T(8,128)(2,1)S(1)}, u32[]{:S(2)}, u32[]{:S(2)}) %collective-permute-start.2) | collective-permute-done | bytes 458784 | tf_op jit(solution)/shard_map/ppermute | solution.py:204
  85.1 0.1 fusion.1
  85.1 16.8 %all_to_all.27 = bf16[8,8,3584]{2,1,0:T(8,128)(2,1)S(1)} all-to-all(bf16[8,8,3584]{2,1,0:T(8,128)(2,1)S(1)} %fusion.1), channel_id=1, replica_groups={{0,2,4,6,8,10,12,14},{1,3,5,7,9,11,13,15},{16,18,20,22,24,26,28,30},{17..., dimensions={0} | all-to-all | bytes 917504 | tf_op jit(solution)/shard_map/all_to_all | solution.py:208
  102.0 0.1 convert_reduce_fusion
  102.0 0.0 copy-done.2
  102.0 0.6 add_convert_fusion.2
  (3 shorter events, 0.0 us)
Async XLA Ops:
  0.0 14.3 %all-to-all-start = ((bf16[16,8,256]{2,1,0:T(8,128)(2,1)}), bf16[16,8,256]{2,1,0:T(8,128)(2,1)S(1)}, u32[]{:S(2)}, u32[]{:S(2)}) async-start(bf16[16,8,256]{2,1,0:T(8,128)(2,1)} %bitcast.11), calls=%async_computation | async-start | bytes 131072 | tf_op jit(solution)/shard_map/all_to_all | solution.py:213
  14.3 0.7 copy-start.1
  19.5 10.9 %all-to-all-start.1 = ((bf16[16,8,384]{2,1,0:T(8,128)(2,1)}), bf16[16,8,384]{2,1,0:T(8,128)(2,1)S(1)}, u32[]{:S(2)}, u32[]{:S(2)}) async-start(bf16[16,8,384]{2,1,0:T(8,128)(2,1)} %shard_map.109), calls=%async_computation.1 | async-start | bytes 196608 | tf_op jit(solution)/shard_map/all_to_all | solution.py:217
  30.4 1.5 %copy-start = (bf16[256,3584]{1,0:T(8,128)(2,1)S(1)}, bf16[256,3584]{1,0:T(8,128)(2,1)}, u32[]{:S(2)}) copy-start(bf16[256,3584]{1,0:T(8,128)(2,1)} %weight_ref.1) | copy-start | bytes 5505028
  32.6 1.9 %collective-permute-start = (bf16[64,3584]{1,0:T(8,128)(2,1)S(1)}, bf16[64,3584]{1,0:T(8,128)(2,1)S(1)}, u32[]{:S(2)}, u32[]{:S(2)}) collective-permute-start(bf16[64,3584]{1,0:T(8,128)(2,1)S(1)} %get-tuple-element.11), channel_id=1, source_target_pairs={{0,1},{1,0},{2,3},{3,2},{4,5},{5,4},{6,7},{7,6},{8,9},{9,8},{10,11... | collective-permute-start | bytes 1376264 | tf_op jit(solution)/shard_map/ppermute | solution.py:204
  69.4 1.8 %collective-permute-start.1 = (bf16[64,3584]{1,0:T(8,128)(2,1)S(1)}, bf16[64,3584]{1,0:T(8,128)(2,1)S(1)}, u32[]{:S(2)}, u32[]{:S(2)}) collective-permute-start(bf16[64,3584]{1,0:T(8,128)(2,1)S(1)} %bitcast.8), channel_id=1, source_target_pairs={{0,1},{1,0},{2,3},{3,2},{4,5},{5,4},{6,7},{7,6},{8,9},{9,8},{10,11... | collective-permute-start | bytes 1376264 | tf_op jit(solution)/shard_map/ppermute | solution.py:204
  71.3 30.8 %copy-start.2 = (bf16[8,3584]{1,0:T(8,128)(2,1)S(1)}, bf16[8,3584]{1,0:T(8,128)(2,1)}, u32[]{:S(2)}) copy-start(bf16[8,3584]{1,0:T(8,128)(2,1)} %param.14) | copy-start | bytes 172036
  83.2 1.9 %collective-permute-start.2 = (bf16[64,3584]{1,0:T(8,128)(2,1)S(1)}, bf16[64,3584]{1,0:T(8,128)(2,1)S(1)}, u32[]{:S(2)}, u32[]{:S(2)}) collective-permute-start(bf16[64,3584]{1,0:T(8,128)(2,1)S(1)} %get-tuple-element.14), channel_id=1, source_target_pairs={{0,1},{1,0},{2,3},{3,2},{4,5},{5,4},{6,7},{7,6},{8,9},{9,8},{10,11... | collective-permute-start | bytes 1376264 | tf_op jit(solution)/shard_map/ppermute | solution.py:204

commit v3 on v2

v3 whole, which is shorter than its diff:
```python
import functools

import jax
import jax.numpy as jnp
from jax import lax
from jax.experimental import pallas as pl
from jax.experimental.pallas import tpu as pltpu
from jax.sharding import PartitionSpec as P

EXPERTS = 8
EPSILON = 1e-05
LANES = 128
F32 = jnp.float32
BF16 = jnp.bfloat16
VMEM_SPEC = pl.BlockSpec(memory_space=pltpu.VMEM)
HBM_SPEC = pl.BlockSpec(memory_space=pltpu.HBM)
SMEM_SPEC = pl.BlockSpec(memory_space=pltpu.SMEM)


def tile_of(extent, most):
    return max(t for t in range(LANES, most + 1, LANES) if extent % t == 0)


def fetch_kernel(count, *refs):
    sources, held, sems = refs[:count], refs[-count - 1 : -1], refs[-1]
    copies = [
        pltpu.make_async_copy(source, target, sems.at[at])
        for at, (source, target) in enumerate(zip(sources, held))
    ]
    for copy in copies:
        copy.start()
    for copy in copies:
        copy.wait()


def fetch(*arrays, after=()):
    count = len(arrays)
    return pl.pallas_call(
        functools.partial(fetch_kernel, count),
        out_shape=tuple(pltpu.VMEM(a.shape, a.dtype) for a in arrays),
        in_specs=[HBM_SPEC] * count + [pl.BlockSpec(memory_space=pl.ANY)] * len(after),
        out_specs=(VMEM_SPEC,) * count,
        scratch_shapes=[pltpu.SemaphoreType.DMA((count,))],
        compiler_params=pltpu.CompilerParams(vmem_limit_bytes=1 << 20),
        cost_estimate=pl.CostEstimate(
            flops=0, bytes_accessed=sum(2 * a.size for a in arrays), transcendentals=0
        ),
    )(*[pltpu.with_memory_space_constraint(a, pltpu.HBM) for a in arrays], *after)


def attend_kernel(meta_ref, shares_ref, query_ref, cache_ref, out_ref):
    heads, tok, head_dim = query_ref.shape
    context = cache_ref.shape[1]
    span = heads // EXPERTS
    rows = heads * tok
    turned = query_ref[...].reshape(rows, head_dim).T
    lane_row = lax.rem(lax.broadcasted_iota(jnp.int32, (1, rows), 1), tok)
    position = lax.broadcasted_iota(jnp.int32, (context, rows), 0)
    scores = jnp.zeros((context, rows), F32)
    live = jnp.zeros((1, rows), jnp.int32)
    for row in range(tok):
        found = jnp.dot(cache_ref[row, :, :head_dim], turned, preferred_element_type=F32)
        scores = jnp.where(lane_row == row, found, scores)
        live = jnp.where(lane_row == row, meta_ref[row, 0], live)
    scores = jnp.where(position < live, scores * head_dim ** (-0.5), -1e30)
    weights = jnp.exp(scores - jnp.max(scores, axis=0, keepdims=True))
    prob = (weights / jnp.sum(weights, axis=0, keepdims=True)).T.astype(BF16)
    place = lax.broadcasted_iota(jnp.int32, (rows, 1), 0)
    place_row = lax.rem(place, tok)
    attended = jnp.zeros((rows, head_dim), F32)
    for row in range(tok):
        found = jnp.dot(prob, cache_ref[row, :, head_dim:], preferred_element_type=F32)
        attended = jnp.where(place_row == row, found, attended)
    out_ref[:, :, :head_dim] = attended.astype(BF16).reshape(heads, tok, head_dim)
    expert = place // (tok * span)
    gates = jnp.zeros((rows, 1), F32)
    for row in range(tok):
        for k in range(shares_ref.shape[1]):
            named = (place_row == row) & (expert == meta_ref[row, 1 + k])
            gates = gates + jnp.where(named, shares_ref[row, k], 0.0)
    out_ref[:, :, head_dim:] = (
        jnp.broadcast_to(gates, (rows, LANES)).astype(BF16).reshape(heads, tok, LANES)
    )


def attend(meta, shares, query_rows, cache):
    heads, tok, head_dim = query_rows.shape
    return pl.pallas_call(
        attend_kernel,
        out_shape=jax.ShapeDtypeStruct((heads, tok, head_dim + LANES), BF16),
        in_specs=[SMEM_SPEC] * 2 + [VMEM_SPEC] * 2,
        out_specs=VMEM_SPEC,
        compiler_params=pltpu.CompilerParams(vmem_limit_bytes=8 << 20),
    )(meta, shares, query_rows, cache)


def relative_order(chips):
    order, bit = [0], chips // 2
    while bit:
        order = order + [o ^ bit for o in order]
        bit //= 2
    return order


def project_kernel(place_ref, rows_ref, weight_ref, kept_ref, sent_ref, gates_ref, ordered):
    chips, _, tok, _ = rows_ref.shape
    head_dim = weight_ref.shape[0]
    half = chips * tok
    mine, core = place_ref[0], place_ref[1]
    for part, core_at, out_ref in ((1, 1 - core, sent_ref), (0, core, kept_ref)):
        for at, bits in enumerate(relative_order(chips)):
            ordered[at] = rows_ref[mine ^ bits, core_at]
        block = ordered[...].reshape(half, head_dim + LANES)
        out_ref[...] = jnp.dot(
            block[:, :head_dim], weight_ref[...], preferred_element_type=F32
        ).astype(out_ref.dtype)
        gates_ref[pl.ds(part * half, half), :] = block[:, head_dim:]


def project(place, rows, weight):
    chips, _, tok, width = rows.shape
    half = chips * tok
    feature = weight.shape[1]
    return pl.pallas_call(
        project_kernel,
        out_shape=(
            jax.ShapeDtypeStruct((half, feature), F32),
            jax.ShapeDtypeStruct((half, feature), BF16),
            jax.ShapeDtypeStruct((2 * half, LANES), BF16),
        ),
        in_specs=[SMEM_SPEC, VMEM_SPEC, VMEM_SPEC],
        out_specs=(VMEM_SPEC, VMEM_SPEC, VMEM_SPEC),
        scratch_shapes=[pltpu.VMEM((chips, tok, width), BF16)],
        compiler_params=pltpu.CompilerParams(vmem_limit_bytes=8 << 20),
    )(place, rows, weight)


def norm_kernel(kept_ref, arrived_ref, gain_ref, middle_ref, normed_ref):
    tok = kept_ref.shape[0] // 2
    for block in range(2):
        mine = pl.ds(block * tok, tok)
        total = kept_ref[mine, :].astype(F32) + arrived_ref[1 - block].astype(F32)
        if block == 0:
            middle_ref[...] = total
        scale = lax.rsqrt(jnp.mean(total * total, axis=1, keepdims=True) + EPSILON)
        normed_ref[block] = (total * scale * gain_ref[...]).astype(BF16)


def norm(kept, arrived, gain):
    rows, feature = kept.shape
    tok = rows // 2
    return pl.pallas_call(
        norm_kernel,
        out_shape=(
            jax.ShapeDtypeStruct((tok, feature), F32),
            jax.ShapeDtypeStruct((2, tok, feature), BF16),
        ),
        in_specs=[VMEM_SPEC] * 3,
        out_specs=(VMEM_SPEC, VMEM_SPEC),
        compiler_params=pltpu.CompilerParams(vmem_limit_bytes=4 << 20),
    )(kept, arrived.reshape(2, tok, feature), gain)


def expert_kernel(
    place_ref, own_ref, other_ref, gates_ref, gate_source, up_source, down_source, kept_ref, sent_ref,
    turned, hidden, gate_ref, up_ref, down_ref, sems,
):
    half = own_ref.shape[0]
    units, feature = gate_ref.shape
    step = tile_of(units, 384)
    wide = tile_of(feature, 896)

    def unit_copies(at):
        rows = pl.ds(at, step)
        return [
            pltpu.make_async_copy(source.at[rows], target.at[rows], sems.at[which, at // step])
            for which, (source, target) in enumerate(((gate_source, gate_ref), (up_source, up_ref)))
        ]

    def down_copy(at):
        columns = pl.ds(at, wide)
        return pltpu.make_async_copy(
            down_source.at[:, columns], down_ref.at[:, columns], sems.at[2, at // wide]
        )

    for at in range(0, units, step):
        for copy in unit_copies(at):
            copy.start()
    for at in range(0, feature, wide):
        down_copy(at).start()
    turned[:, :half] = own_ref[...].T
    turned[:, half:] = other_ref[...].T
    gates = gates_ref[:, :1].astype(F32)
    for at in range(0, units, step):
        for copy in unit_copies(at):
            copy.wait()
        rows = pl.ds(at, step)
        gate_pre = jnp.dot(gate_ref[rows, :], turned[...], preferred_element_type=F32)
        up_pre = jnp.dot(up_ref[rows, :], turned[...], preferred_element_type=F32)
        product = gate_pre / (1.0 + jnp.exp(-gate_pre)) * up_pre
        hidden[:, rows] = (product.T * gates).astype(BF16)
    for at in range(0, feature, wide):
        down_copy(at).wait()
        columns = pl.ds(at, wide)
        part = jnp.dot(hidden[...], down_ref[:, columns], preferred_element_type=F32)
        chips, tok, _ = kept_ref.shape
        for at_block, bits in enumerate(relative_order(chips)):
            chip, low = place_ref[0] ^ bits, at_block * tok
            kept_ref[chip, :, columns] = part[low : low + tok]
            sent_ref[chip, :, columns] = part[half + low : half + low + tok].astype(BF16)


def experts(place, chips, own, other, gates, gate_weight, up_weight, down_weight):
    half, feature = own.shape
    units = gate_weight.shape[0]
    weights = (gate_weight, up_weight, down_weight)
    return pl.pallas_call(
        expert_kernel,
        out_shape=(
            jax.ShapeDtypeStruct((chips, half // chips, feature), F32),
            jax.ShapeDtypeStruct((chips, half // chips, feature), BF16),
        ),
        in_specs=[SMEM_SPEC] + [VMEM_SPEC] * 3 + [HBM_SPEC] * 3,
        out_specs=(VMEM_SPEC, VMEM_SPEC),
        scratch_shapes=[
            pltpu.VMEM((feature, 2 * half), BF16),
            pltpu.VMEM((2 * half, units), BF16),
        ]
        + [pltpu.VMEM((units, feature), BF16)] * 3
        + [pltpu.SemaphoreType.DMA((3, 8))],
        compiler_params=pltpu.CompilerParams(vmem_limit_bytes=44 << 20),
        cost_estimate=pl.CostEstimate(
            flops=12 * half * feature * units,
            bytes_accessed=6 * units * feature,
            transcendentals=2 * half * units,
        ),
    )(place, own, other, gates, *[pltpu.with_memory_space_constraint(w, pltpu.HBM) for w in weights])


def local(
    queries,
    key_values,
    lengths,
    residual,
    routes,
    gate_weights,
    output_weight,
    norm_gain,
    gate_weight,
    up_weight,
    down_weight,
):
    tok = key_values.shape[0]
    head_dim = key_values.shape[2] // 2
    size = lax.axis_size("ep")
    chips = size // 2
    me = lax.axis_index("ep").astype(jnp.int32)
    place = jnp.stack([me // 2, me % 2])
    same_core = [[2 * chip + c for chip in range(chips)] for c in range(2)]
    feature = residual.shape[1]

    def swap(x, bit):
        return lax.ppermute(x, "ep", [(i, i ^ bit) for i in range(size)])

    meta = jnp.concatenate([lengths[:, None], routes], axis=1)
    cache, residual_held, gain_held = fetch(
        key_values, residual, norm_gain.reshape(1, feature)
    )
    query_rows = lax.all_to_all(
        queries.reshape(size, tok, head_dim), "ep", split_axis=0, concat_axis=0, tiled=True
    )
    attended = attend(meta, gate_weights.astype(F32), query_rows, cache)
    (output_held,) = fetch(output_weight, after=(attended,))
    head_rows = lax.all_to_all(attended, "ep", split_axis=0, concat_axis=0, tiled=True)
    kept, sent, gates = project(
        place, head_rows.reshape(chips, 2, tok, head_dim + LANES), output_held
    )
    arrived = swap(sent, 1)
    bit = 2
    while bit < chips:
        half = kept.shape[0] // 2
        sent = (kept[half:] + arrived[half:].astype(F32)).astype(BF16)
        kept = kept[:half] + arrived[:half].astype(F32)
        arrived = swap(sent, bit)
        bit *= 2
    summed = kept + arrived.astype(F32)
    summed = summed.at[:tok].add(residual_held.astype(F32)).astype(BF16)
    middle, own = norm(summed, swap(summed, bit), gain_held)
    own = own.reshape(2 * tok, feature)
    bit //= 2
    while bit > 1:
        own = jnp.concatenate([own, swap(own, bit)], axis=0)
        bit //= 2
    kept, sent = experts(
        place, chips, own, swap(own, 1), gates, gate_weight, up_weight, down_weight
    )
    summed = (kept + swap(sent, 1).astype(F32)).astype(BF16)
    blocks = lax.all_to_all(
        summed, "ep", split_axis=0, concat_axis=0, tiled=True, axis_index_groups=same_core
    )
    return (middle + jnp.sum(blocks.astype(F32), axis=0)).astype(BF16)


def solution(mesh):
    in_specs = (
        P("groups", "ep"),
        P(("groups", "ep"), None, None),
        P(("groups", "ep")),
        P(("groups", "ep"), None),
        P(("groups", "ep"), None),
        P(("groups", "ep"), None),
        P("ep", None),
        P(),
        P("ep", None),
        P("ep", None),
        P("ep", None),
    )
    out_specs = P(("groups", "ep"), None)
    return jax.shard_map(local, mesh=mesh, in_specs=in_specs, out_specs=out_specs, check_vma=False)
```

time: 103 us -> 95.5 us (0.927)
  blocking collectives: 49.7 us -> 16.2 us
  waiting for transfers between devices: 18 us -> 41.4 us
  starting transfers between devices: 11.2 us -> 13.3 us
  Pallas kernels: 17.2 us -> 19.2 us
  other arithmetic: 2.83 us -> 1.14 us
    all_to_all x3 -> x1, blocking collectives: 49.7 us -> 16.2 us  [local(): lax.all_to_all(summed, 'ep', split_axis=0, concat_axis=0, tiled=True, axi...]
    ppermute x3 -> x8, waiting for transfers between devices: 5.29 us -> 34 us  [swap(): return lax.ppermute(x, 'ep', [(i, i ^ bit) for i in range(size)])]
    pallas_call x1 -> x4, Pallas kernels: 11.9 us -> 15.7 us  [the longest x1 12.4 us: experts(): pl.pallas_call(expert_kernel, out_shape=(jax.ShapeDtypeStruct((chips, hal...]
    all_to_all x1, waiting for transfers between devices: 5.36 us -> 1.6 us  [local(): lax.all_to_all(queries.reshape(size, tok, head_dim), 'ep', split_axis=0,...]
    pallas_call x1, Pallas kernels: 4.53 us -> 2.23 us  [attend(): pl.pallas_call(attend_kernel, out_shape=jax.ShapeDtypeStruct((heads, tok,...]
    unnamed x8 -> x2, local copies, waits for them, and re-layouts: 3.68 us -> 1.52 us
    all_to_all x1, waiting for transfers between devices: 7.37 us -> 5.8 us  [local(): lax.all_to_all(attended, 'ep', split_axis=0, concat_axis=0, tiled=True)]
    reshape x0 -> x1, local copies, waits for them, and re-layouts: none -> 1.33 us  [local(): norm_gain.reshape(1, feature)]
  transfers between devices with their start and end apart: 5 -> 10, of which waited for: 5 -> 10; matrix products, arithmetic and copies ran while one was open for 1% -> 4% of each run, Pallas kernels for 0% -> 3%
where the time goes in v3:
time: 95.5 us; the launch traced here: 95.1 us
  waiting for transfers between devices  41.4 us (43%)
  Pallas kernels  19.2 us (20%)
  blocking collectives  16.2 us (17%)
  starting transfers between devices  13.3 us (14%)
  local copies, waits for them, and re-layouts  3.58 us (4%)
  other arithmetic  1.14 us (1%)
    ppermute x8, waiting for transfers between devices, swap(): return lax.ppermute(x, 'ep', [(i, i ^ bit) for i in range(size)])  34 us
    all_to_all x1, blocking collectives, local(): lax.all_to_all(summed, 'ep', split_axis=0, concat_axis=0, tiled=True, axi...  16.2 us
    pallas_call x1, Pallas kernels, experts(): pl.pallas_call(expert_kernel, out_shape=(jax.ShapeDtypeStruct((chips, hal...  12.4 us
    all_to_all x1, starting transfers between devices, local(): lax.all_to_all(queries.reshape(size, tok, head_dim), 'ep', split_axis=0,...  7.39 us
    all_to_all x1, waiting for transfers between devices, local(): lax.all_to_all(attended, 'ep', split_axis=0, concat_axis=0, tiled=True)  5.8 us
    all_to_all x1, starting transfers between devices, local(): lax.all_to_all(attended, 'ep', split_axis=0, concat_axis=0, tiled=True)  4.4 us
    pallas_call x2, Pallas kernels, fetch(): pl.pallas_call(functools.partial(fetch_kernel, count), out_shape=tuple((p...  3.13 us
    pallas_call x1, Pallas kernels, attend(): pl.pallas_call(attend_kernel, out_shape=jax.ShapeDtypeStruct((heads, tok,...  2.23 us
  transfers between devices with their start and end apart: 10, of which 10 were waited for; matrix products, arithmetic and copies ran while one was open for 4% of the time, Pallas kernels for 3%

profile of v3, /device:TPU:0, one launch (start us, length us, event | category | flops | bytes accessed | tf_op | source)
XLA Modules:
  0.0 95.1 jit_solution(4635846167013519725)
XLA Ops:
  0.0 7.4 %all-to-all-start = ((bf16[16,8,256]{2,1,0:T(8,128)(2,1)}), bf16[16,8,256]{2,1,0:T(8,128)(2,1)S(1)}, u32[]{:S(2)}, u32[]{:S(2)}) async-start(bf16[16,8,256]{2,1,0:T(8,128)(2,1)} %bitcast.12), calls=%async_computation | async-start | bytes 131072 | tf_op jit(solution)/shard_map/all_to_all | solution.py:269
  7.4 0.8 copy.14
  8.2 0.7 copy.12
  8.9 0.8 copy.13
  9.7 1.3 %reshape.42.refs_2_ = f32[1,3584]{1,0:T(1,128)} reshape(f32[3584]{0:T(1024)} %param.20) | data formatting | bytes 28672 | tf_op jit(solution)/shard_map/reshape | solution.py:267
  11.0 1.6 %shard_map.109 = (bf16[8,256,512]{2,1,0:T(8,128)(2,1)S(1)}, bf16[8,3584]{1,0:T(8,128)(2,1)S(1)}, f32[1,3584]{1,0:T(1,128)S(1)}) custom-call(bf16[8,256,512]{2,1,0:T(8,128)(2,1)} %refs_0_.2, bf16[8,3584]{1,0:T(8,128)(2,1)} %refs_1_.1, f32[1,3584]{1,0:T(1,128)} %reshape.42.refs_2_), custom_call_target="tpu_custom_call" | custom-call | bytes 2161664 | tf_op jit(solution)/shard_map/pallas_call | solution.py:38
  12.6 0.1 pad_add_fusion.meta_ref
  12.7 1.6 %all-to-all-done.query_ref = bf16[16,8,256]{2,1,0:T(8,128)(2,1)S(1)} async-done(((bf16[16,8,256]{2,1,0:T(8,128)(2,1)}), bf16[16,8,256]{2,1,0:T(8,128)(2,1)S(1)}, u32[]{:S(2)}, u32[]{:S(2)}) %all-to-all-start) | async-done | bytes 65568 | tf_op jit(solution)/shard_map/all_to_all | solution.py:269
  14.3 2.2 %shard_map.110.refs_1_ = bf16[16,8,384]{2,1,0:T(8,128)(2,1)} custom-call(s32[8,4]{1,0:T(8,128)S(1)} %pad_add_fusion.meta_ref, f32[8,3]{1,0:T(8,128)S(1)} %convert_element_type.42.shares_ref, bf16[16,8,256]{2,1,0:T(8,128)(2,1)S(1)} %all-to-all-done.query_ref, bf16[8,256,512]{2,1,0:T(8,128)(2,1)S(1)} %get-tuple-element.27.cache_ref), custom_call_target="tpu_custom_call" | custom-call | tf_op jit(solution)/shard_map/pallas_call | solution.py:88
  16.5 4.4 %all-to-all-start.1 = ((bf16[16,8,384]{2,1,0:T(8,128)(2,1)}), bf16[16,8,384]{2,1,0:T(8,128)(2,1)S(1)}, u32[]{:S(2)}, u32[]{:S(2)}) async-start(bf16[16,8,384]{2,1,0:T(8,128)(2,1)} %shard_map.110.refs_1_), calls=%async_computation.1 | async-start | bytes 196608 | tf_op jit(solution)/shard_map/all_to_all | solution.py:274
  20.9 0.1 pad_add_fusion.1.place_ref
  21.0 1.5 %shard_map.111.weight_ref = bf16[256,3584]{1,0:T(8,128)(2,1)S(1)} custom-call(bf16[256,3584]{1,0:T(8,128)(2,1)} %refs_0_.3, bf16[16,8,384]{2,1,0:T(8,128)(2,1)} %shard_map.110.refs_1_), custom_call_target="tpu_custom_call" | custom-call | bytes 1835008 | tf_op jit(solution)/shard_map/pallas_call | solution.py:38
  22.5 5.8 %all-to-all-done.1 = bf16[16,8,384]{2,1,0:T(8,128)(2,1)S(1)} async-done(((bf16[16,8,384]{2,1,0:T(8,128)(2,1)}), bf16[16,8,384]{2,1,0:T(8,128)(2,1)S(1)}, u32[]{:S(2)}, u32[]{:S(2)}) %all-to-all-start.1) | async-done | bytes 98336 | tf_op jit(solution)/shard_map/all_to_all | solution.py:274
  28.3 1.3 %shard_map.112 = (f32[64,3584]{1,0:T(8,128)S(1)}, bf16[64,3584]{1,0:T(8,128)(2,1)S(1)}, bf16[128,128]{1,0:T(8,128)(2,1)S(1)}) custom-call(s32[2]{0:T(128)S(1)} %pad_add_fusion.1.place_ref, bf16[8,2,8,384]{3,2,1,0:T(8,128)(2,1)S(1)} %bitcast.10, bf16[256,3584]{1,0:T(8,128)(2,1)S(1)} %shard_map.111.weight_ref), custom_call_target="tpu_custom_call" | custom-call | tf_op jit(solution)/shard_map/pallas_call | solution.py:124
  29.6 0.1 collective-permute-start
  29.7 1.8 %collective-permute-done = bf16[64,3584]{1,0:T(8,128)(2,1)S(1)} collective-permute-done((bf16[64,3584]{1,0:T(8,128)(2,1)S(1)}, bf16[64,3584]{1,0:T(8,128)(2,1)S(1)}, u32[]{:S(2)}, u32[]{:S(2)}) %collective-permute-start) | collective-permute-done | bytes 458784 | tf_op jit(solution)/shard_map/ppermute | solution.py:263
  31.5 0.1 add_convert_fusion.1
  31.6 0.1 collective-permute-start.1
  31.7 7.6 %collective-permute-done.1 = bf16[32,3584]{1,0:T(8,128)(2,1)S(1)} collective-permute-done((bf16[32,3584]{1,0:T(8,128)(2,1)S(1)}, bf16[32,3584]{1,0:T(8,128)(2,1)S(1)}, u32[]{:S(2)}, u32[]{:S(2)}) %collective-permute-start.1) | collective-permute-done | bytes 229408 | tf_op jit(solution)/shard_map/ppermute | solution.py:263
  39.3 0.1 collective-permute-start.2
  39.4 4.8 %collective-permute-done.2 = bf16[16,3584]{1,0:T(8,128)(2,1)S(1)} collective-permute-done((bf16[16,3584]{1,0:T(8,128)(2,1)S(1)}, bf16[16,3584]{1,0:T(8,128)(2,1)S(1)}, u32[]{:S(2)}, u32[]{:S(2)}) %collective-permute-start.2) | collective-permute-done | bytes 114720 | tf_op jit(solution)/shard_map/ppermute | solution.py:263
  44.3 0.2 collective-permute-start.3
  44.5 6.2 %collective-permute-done.3 = bf16[16,3584]{1,0:T(8,128)(2,1)S(1)} collective-permute-done((bf16[16,3584]{1,0:T(8,128)(2,1)S(1)}, bf16[16,3584]{1,0:T(8,128)(2,1)S(1)}, u32[]{:S(2)}, u32[]{:S(2)}) %collective-permute-start.3) | collective-permute-done | bytes 114720 | tf_op jit(solution)/shard_map/ppermute | solution.py:263
  50.7 0.1 shard_map.113
  50.9 0.1 collective-permute-start.4
  50.9 4.8 %collective-permute-done.4 = bf16[16,3584]{1,0:T(8,128)(2,1)S(1)} collective-permute-done((bf16[16,3584]{1,0:T(8,128)(2,1)S(1)}, bf16[16,3584]{1,0:T(8,128)(2,1)S(1)}, u32[]{:S(2)}, u32[]{:S(2)}) %collective-permute-start.4) | collective-permute-done | bytes 114720 | tf_op jit(solution)/shard_map/ppermute | solution.py:263
  55.7 0.7 collective-permute-start.5
  56.5 5.4 %collective-permute-done.5 = bf16[32,3584]{1,0:T(8,128)(2,1)S(1)} collective-permute-done((bf16[32,3584]{1,0:T(8,128)(2,1)S(1)}, bf16[32,3584]{1,0:T(8,128)(2,1)S(1)}, u32[]{:S(2)}, u32[]{:S(2)}) %collective-permute-start.5) | collective-permute-done | bytes 229408 | tf_op jit(solution)/shard_map/ppermute | solution.py:263
  61.9 0.1 collective-permute-start.6
  61.9 1.8 %collective-permute-done.6.other_ref = bf16[64,3584]{1,0:T(8,128)(2,1)S(1)} collective-permute-done((bf16[64,3584]{1,0:T(8,128)(2,1)S(1)}, bf16[64,3584]{1,0:T(8,128)(2,1)S(1)}, u32[]{:S(2)}, u32[]{:S(2)}) %collective-permute-start.6) | collective-permute-done | bytes 458784 | tf_op jit(solution)/shard_map/ppermute | solution.py:263
  63.7 12.4 %shard_map.114 = (f32[8,8,3584]{2,1,0:T(8,128)S(1)}, bf16[8,8,3584]{2,1,0:T(8,128)(2,1)S(1)}) custom-call(s32[2]{0:T(128)S(1)} %pad_add_fusion.1.place_ref, bf16[64,3584]{1,0:T(8,128)(2,1)S(1)} %pad_maximum_fusion.own_ref, bf16[64,3584]{1,0:T(8,128)(2,1)S(1)} %collective-permute-done.6.other_ref, bf16[128,128]{1,0:T(8,128)(2,1)S(1)} %get-tuple-element.34.gates_ref, ...), custom_call_target="tpu_custom_call" | custom-call | flops 4227858432 | bytes 33030144 | tf_op jit(solution)/shard_map/pallas_call | solution.py:217
  76.2 0.2 collective-permute-start.7
  76.4 1.7 %collective-permute-done.7 = bf16[8,8,3584]{2,1,0:T(8,128)(2,1)S(1)} collective-permute-done((bf16[8,8,3584]{2,1,0:T(8,128)(2,1)S(1)}, bf16[8,8,3584]{2,1,0:T(8,128)(2,1)S(1)}, u32[]{:S(2)}, u32[]{:S(2)}) %collective-permute-start.7) | collective-permute-done | bytes 458784 | tf_op jit(solution)/shard_map/ppermute | solution.py:263
  78.1 0.1 add_convert_fusion
  78.2 16.2 %all_to_all.15 = bf16[8,8,3584]{2,1,0:T(8,128)(2,1)S(1)} all-to-all(bf16[8,8,3584]{2,1,0:T(8,128)(2,1)S(1)} %add_convert_fusion), channel_id=1, replica_groups={{0,2,4,6,8,10,12,14},{1,3,5,7,9,11,13,15},{16,18,20,22,24,26,28,30},{17..., dimensions={0} | all-to-all | bytes 917504 | tf_op jit(solution)/shard_map/all_to_all | solution.py:298
  94.3 0.1 convert_reduce_fusion
  94.4 0.6 add_convert_fusion.2
  (7 shorter events, 0.1 us)
Async XLA Ops:
  0.0 14.3 %all-to-all-start = ((bf16[16,8,256]{2,1,0:T(8,128)(2,1)}), bf16[16,8,256]{2,1,0:T(8,128)(2,1)S(1)}, u32[]{:S(2)}, u32[]{:S(2)}) async-start(bf16[16,8,256]{2,1,0:T(8,128)(2,1)} %bitcast.12), calls=%async_computation | async-start | bytes 131072 | tf_op jit(solution)/shard_map/all_to_all | solution.py:269
  16.5 11.8 %all-to-all-start.1 = ((bf16[16,8,384]{2,1,0:T(8,128)(2,1)}), bf16[16,8,384]{2,1,0:T(8,128)(2,1)S(1)}, u32[]{:S(2)}, u32[]{:S(2)}) async-start(bf16[16,8,384]{2,1,0:T(8,128)(2,1)} %shard_map.110.refs_1_), calls=%async_computation.1 | async-start | bytes 196608 | tf_op jit(solution)/shard_map/all_to_all | solution.py:274
  29.6 1.9 %collective-permute-start = (bf16[64,3584]{1,0:T(8,128)(2,1)S(1)}, bf16[64,3584]{1,0:T(8,128)(2,1)S(1)}, u32[]{:S(2)}, u32[]{:S(2)}) collective-permute-start(bf16[64,3584]{1,0:T(8,128)(2,1)S(1)} %get-tuple-element.29), channel_id=1, source_target_pairs={{0,1},{1,0},{2,3},{3,2},{4,5},{5,4},{6,7},{7,6},{8,9},{9,8},{10,11... | collective-permute-start | bytes 1376264 | tf_op jit(solution)/shard_map/ppermute | solution.py:263
  31.6 7.7 %collective-permute-start.1 = (bf16[32,3584]{1,0:T(8,128)(2,1)S(1)}, bf16[32,3584]{1,0:T(8,128)(2,1)S(1)}, u32[]{:S(2)}, u32[]{:S(2)}) collective-permute-start(bf16[32,3584]{1,0:T(8,128)(2,1)S(1)} %get-tuple-element.37), channel_id=1, source_target_pairs={{0,2},{1,3},{2,0},{3,1},{4,6},{5,7},{6,4},{7,5},{8,10},{9,11},{10,... | collective-permute-start | bytes 688136 | tf_op jit(solution)/shard_map/ppermute | solution.py:263
  39.3 4.9 %collective-permute-start.2 = (bf16[16,3584]{1,0:T(8,128)(2,1)S(1)}, bf16[16,3584]{1,0:T(8,128)(2,1)S(1)}, u32[]{:S(2)}, u32[]{:S(2)}) collective-permute-start(bf16[16,3584]{1,0:T(8,128)(2,1)S(1)} %fusion), channel_id=1, source_target_pairs={{0,4},{1,5},{2,6},{3,7},{4,0},{5,1},{6,2},{7,3},{8,12},{9,13},{10,... | collective-permute-start | bytes 344072 | tf_op jit(solution)/shard_map/ppermute | solution.py:263
  44.3 6.4 %collective-permute-start.3 = (bf16[16,3584]{1,0:T(8,128)(2,1)S(1)}, bf16[16,3584]{1,0:T(8,128)(2,1)S(1)}, u32[]{:S(2)}, u32[]{:S(2)}) collective-permute-start(bf16[16,3584]{1,0:T(8,128)(2,1)S(1)} %convert_element_type.51.kept_ref), channel_id=1, source_target_pairs={{0,8},{1,9},{2,10},{3,11},{4,12},{5,13},{6,14},{7,15},{8,0},{9,1},... | collective-permute-start | bytes 344072 | tf_op jit(solution)/shard_map/ppermute | solution.py:263
  50.9 4.9 %collective-permute-start.4 = (bf16[16,3584]{1,0:T(8,128)(2,1)S(1)}, bf16[16,3584]{1,0:T(8,128)(2,1)S(1)}, u32[]{:S(2)}, u32[]{:S(2)}) collective-permute-start(bf16[16,3584]{1,0:T(8,128)(2,1)S(1)} %bitcast.7), channel_id=1, source_target_pairs={{0,4},{1,5},{2,6},{3,7},{4,0},{5,1},{6,2},{7,3},{8,12},{9,13},{10,... | collective-permute-start | bytes 344072 | tf_op jit(solution)/shard_map/ppermute | solution.py:263
  55.7 6.1 %collective-permute-start.5 = (bf16[32,3584]{1,0:T(8,128)(2,1)S(1)}, bf16[32,3584]{1,0:T(8,128)(2,1)S(1)}, u32[]{:S(2)}, u32[]{:S(2)}) collective-permute-start(bf16[32,3584]{1,0:T(8,128)(2,1)S(1)} %pad_maximum_fusion.1), channel_id=1, source_target_pairs={{0,2},{1,3},{2,0},{3,1},{4,6},{5,7},{6,4},{7,5},{8,10},{9,11},{10,... | collective-permute-start | bytes 688136 | tf_op jit(solution)/shard_map/ppermute | solution.py:263
  61.9 1.9 %collective-permute-start.6 = (bf16[64,3584]{1,0:T(8,128)(2,1)S(1)}, bf16[64,3584]{1,0:T(8,128)(2,1)S(1)}, u32[]{:S(2)}, u32[]{:S(2)}) collective-permute-start(bf16[64,3584]{1,0:T(8,128)(2,1)S(1)} %pad_maximum_fusion.own_ref), channel_id=1, source_target_pairs={{0,1},{1,0},{2,3},{3,2},{4,5},{5,4},{6,7},{7,6},{8,9},{9,8},{10,11... | collective-permute-start | bytes 1376264 | tf_op jit(solution)/shard_map/ppermute | solution.py:263
  76.2 1.9 %collective-permute-start.7 = (bf16[8,8,3584]{2,1,0:T(8,128)(2,1)S(1)}, bf16[8,8,3584]{2,1,0:T(8,128)(2,1)S(1)}, u32[]{:S(2)}, u32[]{:S(2)}) collective-permute-start(bf16[8,8,3584]{2,1,0:T(8,128)(2,1)S(1)} %get-tuple-element.36), channel_id=1, source_target_pairs={{0,1},{1,0},{2,3},{3,2},{4,5},{5,4},{6,7},{7,6},{8,9},{9,8},{10,11... | collective-permute-start | bytes 1376264 | tf_op jit(solution)/shard_map/ppermute | solution.py:263

commit v4 on v3

--- a/solution.py
+++ b/solution.py
@@ -21,34 +21,40 @@
     return max(t for t in range(LANES, most + 1, LANES) if extent % t == 0)
 
 
-def fetch_kernel(count, *refs):
-    sources, held, sems = refs[:count], refs[-count - 1 : -1], refs[-1]
+def fetch_kernel(count, carried, *refs):
+    sources, held, sems = refs[:count], refs[-count - 1 - carried : -1 - carried], refs[-1]
     copies = [
         pltpu.make_async_copy(source, target, sems.at[at])
         for at, (source, target) in enumerate(zip(sources, held))
     ]
     for copy in copies:
         copy.start()
+    if carried:
+        refs[-2][...] = refs[count][...]
     for copy in copies:
         copy.wait()
 
 
-def fetch(*arrays, after=()):
-    count = len(arrays)
-    return pl.pallas_call(
-        functools.partial(fetch_kernel, count),
-        out_shape=tuple(pltpu.VMEM(a.shape, a.dtype) for a in arrays),
-        in_specs=[HBM_SPEC] * count + [pl.BlockSpec(memory_space=pl.ANY)] * len(after),
-        out_specs=(VMEM_SPEC,) * count,
+def fetch(*arrays, after=(), carry=None):
+    count, carried = len(arrays), int(carry is not None)
+    carries = (carry,) * carried
+    return pl.pallas_call(
+        functools.partial(fetch_kernel, count, carried),
+        out_shape=tuple(pltpu.VMEM(a.shape, a.dtype) for a in arrays)
+        + tuple(jax.ShapeDtypeStruct(c.shape, c.dtype) for c in carries),
+        in_specs=[HBM_SPEC] * count
+        + [VMEM_SPEC] * carried
+        + [pl.BlockSpec(memory_space=pl.ANY)] * len(after),
+        out_specs=(VMEM_SPEC,) * (count + carried),
         scratch_shapes=[pltpu.SemaphoreType.DMA((count,))],
-        compiler_params=pltpu.CompilerParams(vmem_limit_bytes=1 << 20),
+        compiler_params=pltpu.CompilerParams(vmem_limit_bytes=4 << 20),
         cost_estimate=pl.CostEstimate(
             flops=0, bytes_accessed=sum(2 * a.size for a in arrays), transcendentals=0
         ),
-    )(*[pltpu.with_memory_space_constraint(a, pltpu.HBM) for a in arrays], *after)
-
-
-def attend_kernel(meta_ref, shares_ref, query_ref, cache_ref, out_ref):
+    )(*[pltpu.with_memory_space_constraint(a, pltpu.HBM) for a in arrays], *carries, *after)
+
+
+def attend_kernel(lengths_ref, routes_ref, shares_ref, query_ref, cache_ref, out_ref):
     heads, tok, head_dim = query_ref.shape
     context = cache_ref.shape[1]
     span = heads // EXPERTS
@@ -61,7 +67,7 @@
     for row in range(tok):
         found = jnp.dot(cache_ref[row, :, :head_dim], turned, preferred_element_type=F32)
         scores = jnp.where(lane_row == row, found, scores)
-        live = jnp.where(lane_row == row, meta_ref[row, 0], live)
+        live = jnp.where(lane_row == row, lengths_ref[row], live)
     scores = jnp.where(position < live, scores * head_dim ** (-0.5), -1e30)
     weights = jnp.exp(scores - jnp.max(scores, axis=0, keepdims=True))
     prob = (weights / jnp.sum(weights, axis=0, keepdims=True)).T.astype(BF16)
@@ -75,23 +81,23 @@
     expert = place // (tok * span)
     gates = jnp.zeros((rows, 1), F32)
     for row in range(tok):
-        for k in range(shares_ref.shape[1]):
-            named = (place_row == row) & (expert == meta_ref[row, 1 + k])
-            gates = gates + jnp.where(named, shares_ref[row, k], 0.0)
+        for k in range(shares_ref.shape[0]):
+            named = (place_row == row) & (expert == routes_ref[k, row])
+            gates = gates + jnp.where(named, shares_ref[k, row], 0.0)
     out_ref[:, :, head_dim:] = (
         jnp.broadcast_to(gates, (rows, LANES)).astype(BF16).reshape(heads, tok, LANES)
     )
 
 
-def attend(meta, shares, query_rows, cache):
+def attend(lengths, routes, shares, query_rows, cache):
     heads, tok, head_dim = query_rows.shape
     return pl.pallas_call(
         attend_kernel,
         out_shape=jax.ShapeDtypeStruct((heads, tok, head_dim + LANES), BF16),
-        in_specs=[SMEM_SPEC] * 2 + [VMEM_SPEC] * 2,
+        in_specs=[SMEM_SPEC] * 3 + [VMEM_SPEC] * 2,
         out_specs=VMEM_SPEC,
         compiler_params=pltpu.CompilerParams(vmem_limit_bytes=8 << 20),
-    )(meta, shares, query_rows, cache)
+    )(lengths, routes, shares, query_rows, cache)
 
 
 def relative_order(chips):
@@ -143,7 +149,7 @@
         if block == 0:
             middle_ref[...] = total
         scale = lax.rsqrt(jnp.mean(total * total, axis=1, keepdims=True) + EPSILON)
-        normed_ref[block] = (total * scale * gain_ref[...]).astype(BF16)
+        normed_ref[block] = (total * scale * gain_ref[...].reshape(1, -1)).astype(BF16)
 
 
 def norm(kept, arrived, gain):
@@ -162,40 +168,35 @@
 
 
 def expert_kernel(
-    place_ref, own_ref, other_ref, gates_ref, gate_source, up_source, down_source, kept_ref, sent_ref,
-    turned, hidden, gate_ref, up_ref, down_ref, sems,
+    place_ref, near_ref, far_ref, near_other_ref, far_other_ref, gates_ref, gate_ref, up_source, down_source,
+    kept_ref, sent_ref, turned, hidden, up_ref, down_ref, sems,
 ):
-    half = own_ref.shape[0]
+    half = 2 * near_ref.shape[0]
     units, feature = gate_ref.shape
     step = tile_of(units, 384)
     wide = tile_of(feature, 896)
 
-    def unit_copies(at):
+    def up_copy(at):
         rows = pl.ds(at, step)
-        return [
-            pltpu.make_async_copy(source.at[rows], target.at[rows], sems.at[which, at // step])
-            for which, (source, target) in enumerate(((gate_source, gate_ref), (up_source, up_ref)))
-        ]
+        return pltpu.make_async_copy(up_source.at[rows], up_ref.at[rows], sems.at[0, at // step])
 
     def down_copy(at):
         columns = pl.ds(at, wide)
         return pltpu.make_async_copy(
-            down_source.at[:, columns], down_ref.at[:, columns], sems.at[2, at // wide]
+            down_source.at[:, columns], down_ref.at[:, columns], sems.at[1, at // wide]
         )
 
     for at in range(0, units, step):
-        for copy in unit_copies(at):
-            copy.start()
+        up_copy(at).start()
     for at in range(0, feature, wide):
         down_copy(at).start()
-    turned[:, :half] = own_ref[...].T
-    turned[:, half:] = other_ref[...].T
+    pieces = (near_ref, far_ref, near_other_ref, far_other_ref)
+    turned[...] = jnp.concatenate([piece[...] for piece in pieces], axis=0).T
     gates = gates_ref[:, :1].astype(F32)
     for at in range(0, units, step):
-        for copy in unit_copies(at):
-            copy.wait()
         rows = pl.ds(at, step)
         gate_pre = jnp.dot(gate_ref[rows, :], turned[...], preferred_element_type=F32)
+        up_copy(at).wait()
         up_pre = jnp.dot(up_ref[rows, :], turned[...], preferred_element_type=F32)
         product = gate_pre / (1.0 + jnp.exp(-gate_pre)) * up_pre
         hidden[:, rows] = (product.T * gates).astype(BF16)
@@ -210,31 +211,31 @@
             sent_ref[chip, :, columns] = part[half + low : half + low + tok].astype(BF16)
 
 
-def experts(place, chips, own, other, gates, gate_weight, up_weight, down_weight):
-    half, feature = own.shape
+def experts(place, chips, pieces, gates, gate_weight, up_weight, down_weight):
+    half, feature = 2 * pieces[0].shape[0], pieces[0].shape[1]
     units = gate_weight.shape[0]
-    weights = (gate_weight, up_weight, down_weight)
+    weights = (up_weight, down_weight)
     return pl.pallas_call(
         expert_kernel,
         out_shape=(
             jax.ShapeDtypeStruct((chips, half // chips, feature), F32),
             jax.ShapeDtypeStruct((chips, half // chips, feature), BF16),
         ),
-        in_specs=[SMEM_SPEC] + [VMEM_SPEC] * 3 + [HBM_SPEC] * 3,
+        in_specs=[SMEM_SPEC] + [VMEM_SPEC] * 6 + [HBM_SPEC] * 2,
         out_specs=(VMEM_SPEC, VMEM_SPEC),
         scratch_shapes=[
             pltpu.VMEM((feature, 2 * half), BF16),
             pltpu.VMEM((2 * half, units), BF16),
         ]
-        + [pltpu.VMEM((units, feature), BF16)] * 3
-        + [pltpu.SemaphoreType.DMA((3, 8))],
-        compiler_params=pltpu.CompilerParams(vmem_limit_bytes=44 << 20),
+        + [pltpu.VMEM((units, feature), BF16)] * 2
+        + [pltpu.SemaphoreType.DMA((2, 8))],
+        compiler_params=pltpu.CompilerParams(vmem_limit_bytes=32 << 20),
         cost_estimate=pl.CostEstimate(
             flops=12 * half * feature * units,
             bytes_accessed=6 * units * feature,
             transcendentals=2 * half * units,
         ),
-    )(place, own, other, gates, *[pltpu.with_memory_space_constraint(w, pltpu.HBM) for w in weights])
+    )(place, *pieces, gates, gate_weight, *[pltpu.with_memory_space_constraint(w, pltpu.HBM) for w in weights])
 
 
 def local(
@@ -257,19 +258,17 @@
     me = lax.axis_index("ep").astype(jnp.int32)
     place = jnp.stack([me // 2, me % 2])
     same_core = [[2 * chip + c for chip in range(chips)] for c in range(2)]
-    feature = residual.shape[1]
 
     def swap(x, bit):
         return lax.ppermute(x, "ep", [(i, i ^ bit) for i in range(size)])
 
-    meta = jnp.concatenate([lengths[:, None], routes], axis=1)
-    cache, residual_held, gain_held = fetch(
-        key_values, residual, norm_gain.reshape(1, feature)
+    cache, residual_held, gain_held, lengths_held, routes_held = fetch(
+        key_values, residual, norm_gain, lengths, routes.T
     )
     query_rows = lax.all_to_all(
         queries.reshape(size, tok, head_dim), "ep", split_axis=0, concat_axis=0, tiled=True
     )
-    attended = attend(meta, gate_weights.astype(F32), query_rows, cache)
+    attended = attend(lengths_held, routes_held, gate_weights.astype(F32).T, query_rows, cache)
     (output_held,) = fetch(output_weight, after=(attended,))
     head_rows = lax.all_to_all(attended, "ep", split_axis=0, concat_axis=0, tiled=True)
     kept, sent, gates = project(
@@ -286,14 +285,15 @@
     summed = kept + arrived.astype(F32)
     summed = summed.at[:tok].add(residual_held.astype(F32)).astype(BF16)
     middle, own = norm(summed, swap(summed, bit), gain_held)
-    own = own.reshape(2 * tok, feature)
+    own = own.reshape(2 * tok, -1)
     bit //= 2
-    while bit > 1:
+    while bit > 2:
         own = jnp.concatenate([own, swap(own, bit)], axis=0)
         bit //= 2
-    kept, sent = experts(
-        place, chips, own, swap(own, 1), gates, gate_weight, up_weight, down_weight
-    )
+    far = swap(own, bit)
+    gate_held, near = fetch(gate_weight, carry=own)
+    pieces = (near, far, swap(near, 1), swap(far, 1))
+    kept, sent = experts(place, chips, pieces, gates, gate_held, up_weight, down_weight)
     summed = (kept + swap(sent, 1).astype(F32)).astype(BF16)
     blocks = lax.all_to_all(
         summed, "ep", split_axis=0, concat_axis=0, tiled=True, axis_index_groups=same_core

time: 95.5 us -> 93.1 us (0.975)
  local copies, waits for them, and re-layouts: 3.58 us -> 0 us
  Pallas kernels: 19.2 us -> 22.4 us
  waiting for transfers between devices: 41.4 us -> 39.8 us
    ppermute x8 -> x9, waiting for transfers between devices: 34 us -> 29.5 us  [swap(): return lax.ppermute(x, 'ep', [(i, i ^ bit) for i in range(size)])]
    pallas_call x2 -> x3, Pallas kernels: 3.13 us -> 7.29 us  [fetch(): pl.pallas_call(functools.partial(fetch_kernel, count, carried), out_shape...]
    all_to_all x1, waiting for transfers between devices: 1.6 us -> 4.56 us  [local(): lax.all_to_all(queries.reshape(size, tok, head_dim), 'ep', split_axis=0,...]
    unnamed x2 -> x0, local copies, waits for them, and re-layouts: 1.52 us -> none
    reshape x1 -> x0, local copies, waits for them, and re-layouts: 1.33 us -> none  [local(): norm_gain.reshape(1, feature)]
  transfers between devices with their start and end apart: 10 -> 11, of which waited for: 10 -> 11; matrix products, arithmetic and copies ran while one was open for 4% -> 1% of each run, Pallas kernels for 3% -> 8%
where the time goes in v4:
time: 93.1 us; the launch traced here: 92.7 us
  waiting for transfers between devices  39.8 us (43%)
  Pallas kernels  22.4 us (24%)
  blocking collectives  16.2 us (17%)
  starting transfers between devices  12.4 us (13%)
  other arithmetic  1.74 us (2%)
    ppermute x9, waiting for transfers between devices, swap(): return lax.ppermute(x, 'ep', [(i, i ^ bit) for i in range(size)])  29.5 us
    all_to_all x1, blocking collectives, local(): lax.all_to_all(summed, 'ep', split_axis=0, concat_axis=0, tiled=True, axi...  16.2 us
    pallas_call x1, Pallas kernels, experts(): pl.pallas_call(expert_kernel, out_shape=(jax.ShapeDtypeStruct((chips, hal...  11.5 us
    all_to_all x1, starting transfers between devices, local(): lax.all_to_all(queries.reshape(size, tok, head_dim), 'ep', split_axis=0,...  7.38 us
    pallas_call x3, Pallas kernels, fetch(): pl.pallas_call(functools.partial(fetch_kernel, count, carried), out_shape...  7.29 us
    all_to_all x1, waiting for transfers between devices, local(): lax.all_to_all(attended, 'ep', split_axis=0, concat_axis=0, tiled=True)  5.76 us
    all_to_all x1, waiting for transfers between devices, local(): lax.all_to_all(queries.reshape(size, tok, head_dim), 'ep', split_axis=0,...  4.56 us
    all_to_all x1, starting transfers between devices, local(): lax.all_to_all(attended, 'ep', split_axis=0, concat_axis=0, tiled=True)  3.51 us
  transfers between devices with their start and end apart: 11, of which 11 were waited for; matrix products, arithmetic and copies ran while one was open for 1% of the time, Pallas kernels for 8%

profile of v4, /device:TPU:0, one launch (start us, length us, event | category | flops | bytes accessed | tf_op | source)
XLA Modules:
  0.0 92.7 jit_solution(7716478898997294518)
XLA Ops:
  0.0 7.4 %all-to-all-start = ((bf16[16,8,256]{2,1,0:T(8,128)(2,1)}), bf16[16,8,256]{2,1,0:T(8,128)(2,1)S(1)}, u32[]{:S(2)}, u32[]{:S(2)}) async-start(bf16[16,8,256]{2,1,0:T(8,128)(2,1)} %bitcast.13), calls=%async_computation | async-start | bytes 131072 | tf_op jit(solution)/shard_map/all_to_all | solution.py:268
  7.4 1.6 %shard_map.109 = (bf16[8,256,512]{2,1,0:T(8,128)(2,1)S(1)}, bf16[8,3584]{1,0:T(8,128)(2,1)S(1)}, f32[3584]{0:T(1024)S(1)}, s32[8]{0:T(128)S(1)}, s32[3,8]{1,0:T(4,128)S(1)}) custom-call(bf16[8,256,512]{2,1,0:T(8,128)(2,1)} %refs_0_.3, bf16[8,3584]{1,0:T(8,128)(2,1)} %refs_1_.1, f32[3584]{0:T(1024)} %refs_2_.1, s32[8]{0:T(128)} %refs_3_.1, s32[3,8]{1,0:T(4,128)} %bitcast.14), custom_call_target="tpu_custom_call" | custom-call | bytes 2161728 | tf_op jit(solution)/shard_map/pallas_call | solution.py:41
  9.0 0.7 convert_bitcast_fusion.shares_ref
  9.7 4.6 %all-to-all-done.query_ref = bf16[16,8,256]{2,1,0:T(8,128)(2,1)S(1)} async-done(((bf16[16,8,256]{2,1,0:T(8,128)(2,1)}), bf16[16,8,256]{2,1,0:T(8,128)(2,1)S(1)}, u32[]{:S(2)}, u32[]{:S(2)}) %all-to-all-start) | async-done | bytes 65568 | tf_op jit(solution)/shard_map/all_to_all | solution.py:268
  14.3 2.2 %shard_map.110.refs_1_ = bf16[16,8,384]{2,1,0:T(8,128)(2,1)} custom-call(s32[8]{0:T(128)S(1)} %get-tuple-element.31.lengths_ref, s32[3,8]{1,0:T(4,128)S(1)} %get-tuple-element.32.routes_ref, f32[3,8]{1,0:T(4,128)S(1)} %convert_bitcast_fusion.shares_ref, bf16[16,8,256]{2,1,0:T(8,128)(2,1)S(1)} %all-to-all-done.query_ref, ...), custom_call_target="tpu_custom_call" | custom-call | tf_op jit(solution)/shard_map/pallas_call | solution.py:94
  16.5 3.5 %all-to-all-start.1 = ((bf16[16,8,384]{2,1,0:T(8,128)(2,1)}), bf16[16,8,384]{2,1,0:T(8,128)(2,1)S(1)}, u32[]{:S(2)}, u32[]{:S(2)}) async-start(bf16[16,8,384]{2,1,0:T(8,128)(2,1)} %shard_map.110.refs_1_), calls=%async_computation.1 | async-start | bytes 196608 | tf_op jit(solution)/shard_map/all_to_all | solution.py:273
  20.0 0.1 pad_add_fusion.place_ref
  20.1 1.5 %shard_map.111.weight_ref = bf16[256,3584]{1,0:T(8,128)(2,1)S(1)} custom-call(bf16[256,3584]{1,0:T(8,128)(2,1)} %refs_0_.4, bf16[16,8,384]{2,1,0:T(8,128)(2,1)} %shard_map.110.refs_1_), custom_call_target="tpu_custom_call" | custom-call | bytes 1835008 | tf_op jit(solution)/shard_map/pallas_call | solution.py:41
  21.6 5.8 %all-to-all-done.1 = bf16[16,8,384]{2,1,0:T(8,128)(2,1)S(1)} async-done(((bf16[16,8,384]{2,1,0:T(8,128)(2,1)}), bf16[16,8,384]{2,1,0:T(8,128)(2,1)S(1)}, u32[]{:S(2)}, u32[]{:S(2)}) %all-to-all-start.1) | async-done | bytes 98336 | tf_op jit(solution)/shard_map/all_to_all | solution.py:273
  27.3 1.3 %shard_map.112 = (f32[64,3584]{1,0:T(8,128)S(1)}, bf16[64,3584]{1,0:T(8,128)(2,1)S(1)}, bf16[128,128]{1,0:T(8,128)(2,1)S(1)}) custom-call(s32[2]{0:T(128)S(1)} %pad_add_fusion.place_ref, bf16[8,2,8,384]{3,2,1,0:T(8,128)(2,1)S(1)} %bitcast.9, bf16[256,3584]{1,0:T(8,128)(2,1)S(1)} %shard_map.111.weight_ref), custom_call_target="tpu_custom_call" | custom-call | tf_op jit(solution)/shard_map/pallas_call | solution.py:130
  28.6 0.1 collective-permute-start
  28.7 1.8 %collective-permute-done = bf16[64,3584]{1,0:T(8,128)(2,1)S(1)} collective-permute-done((bf16[64,3584]{1,0:T(8,128)(2,1)S(1)}, bf16[64,3584]{1,0:T(8,128)(2,1)S(1)}, u32[]{:S(2)}, u32[]{:S(2)}) %collective-permute-start) | collective-permute-done | bytes 458784 | tf_op jit(solution)/shard_map/ppermute | solution.py:263
  30.5 0.1 add_convert_fusion.1
  30.6 0.1 collective-permute-start.1
  30.7 7.6 %collective-permute-done.1 = bf16[32,3584]{1,0:T(8,128)(2,1)S(1)} collective-permute-done((bf16[32,3584]{1,0:T(8,128)(2,1)S(1)}, bf16[32,3584]{1,0:T(8,128)(2,1)S(1)}, u32[]{:S(2)}, u32[]{:S(2)}) %collective-permute-start.1) | collective-permute-done | bytes 229408 | tf_op jit(solution)/shard_map/ppermute | solution.py:263
  38.3 0.1 collective-permute-start.2
  38.4 4.8 %collective-permute-done.2 = bf16[16,3584]{1,0:T(8,128)(2,1)S(1)} collective-permute-done((bf16[16,3584]{1,0:T(8,128)(2,1)S(1)}, bf16[16,3584]{1,0:T(8,128)(2,1)S(1)}, u32[]{:S(2)}, u32[]{:S(2)}) %collective-permute-start.2) | collective-permute-done | bytes 114720 | tf_op jit(solution)/shard_map/ppermute | solution.py:263
  43.3 0.2 collective-permute-start.3
  43.5 6.2 %collective-permute-done.3 = bf16[16,3584]{1,0:T(8,128)(2,1)S(1)} collective-permute-done((bf16[16,3584]{1,0:T(8,128)(2,1)S(1)}, bf16[16,3584]{1,0:T(8,128)(2,1)S(1)}, u32[]{:S(2)}, u32[]{:S(2)}) %collective-permute-start.3) | collective-permute-done | bytes 114720 | tf_op jit(solution)/shard_map/ppermute | solution.py:263
  49.7 0.1 shard_map.113
  49.9 0.1 collective-permute-start.4
  50.0 4.8 %collective-permute-done.4 = bf16[16,3584]{1,0:T(8,128)(2,1)S(1)} collective-permute-done((bf16[16,3584]{1,0:T(8,128)(2,1)S(1)}, bf16[16,3584]{1,0:T(8,128)(2,1)S(1)}, u32[]{:S(2)}, u32[]{:S(2)}) %collective-permute-start.4) | collective-permute-done | bytes 114720 | tf_op jit(solution)/shard_map/ppermute | solution.py:263
  54.8 0.7 collective-permute-start.5
  55.5 4.1 %shard_map.114 = (bf16[1536,3584]{1,0:T(8,128)(2,1)S(1)}, bf16[32,3584]{1,0:T(8,128)(2,1)S(1)}) custom-call(bf16[1536,3584]{1,0:T(8,128)(2,1)} %refs_0_.5, bf16[32,3584]{1,0:T(8,128)(2,1)S(1)} %pad_maximum_fusion.refs_1_), custom_call_target="tpu_custom_call" | custom-call | bytes 11010048 | tf_op jit(solution)/shard_map/pallas_call | solution.py:41
  59.6 0.1 collective-permute-start.6
  59.7 1.1 %collective-permute-done.5.far_ref = bf16[32,3584]{1,0:T(8,128)(2,1)S(1)} collective-permute-done((bf16[32,3584]{1,0:T(8,128)(2,1)S(1)}, bf16[32,3584]{1,0:T(8,128)(2,1)S(1)}, u32[]{:S(2)}, u32[]{:S(2)}) %collective-permute-start.5) | collective-permute-done | bytes 229408 | tf_op jit(solution)/shard_map/ppermute | solution.py:263
  60.8 0.0 collective-permute-start.7
  60.8 0.3 collective-permute-done.6.near_other_ref
  61.2 1.1 %collective-permute-done.7.far_other_ref = bf16[32,3584]{1,0:T(8,128)(2,1)S(1)} collective-permute-done((bf16[32,3584]{1,0:T(8,128)(2,1)S(1)}, bf16[32,3584]{1,0:T(8,128)(2,1)S(1)}, u32[]{:S(2)}, u32[]{:S(2)}) %collective-permute-start.7) | collective-permute-done | bytes 229408 | tf_op jit(solution)/shard_map/ppermute | solution.py:263
  62.3 11.5 %shard_map.115 = (f32[8,8,3584]{2,1,0:T(8,128)S(1)}, bf16[8,8,3584]{2,1,0:T(8,128)(2,1)S(1)}) custom-call(s32[2]{0:T(128)S(1)} %pad_add_fusion.place_ref, bf16[32,3584]{1,0:T(8,128)(2,1)S(1)} %get-tuple-element.40.near_ref, bf16[32,3584]{1,0:T(8,128)(2,1)S(1)} %collective-permute-done.5.far_ref, bf16[32,3584]{1,0:T(8,128)(2,1)S(1)} %collective-permute-done.6.near_other_ref, ...), custom_call_target="tpu_custom_call" | custom-call | flops 4227858432 | bytes 33030144 | tf_op jit(solution)/shard_map/pallas_call | solution.py:218
  73.9 0.2 collective-permute-start.8
  74.1 1.7 %collective-permute-done.8 = bf16[8,8,3584]{2,1,0:T(8,128)(2,1)S(1)} collective-permute-done((bf16[8,8,3584]{2,1,0:T(8,128)(2,1)S(1)}, bf16[8,8,3584]{2,1,0:T(8,128)(2,1)S(1)}, u32[]{:S(2)}, u32[]{:S(2)}) %collective-permute-start.8) | collective-permute-done | bytes 458784 | tf_op jit(solution)/shard_map/ppermute | solution.py:263
  75.7 0.1 add_convert_fusion
  75.8 16.2 %all_to_all.15 = bf16[8,8,3584]{2,1,0:T(8,128)(2,1)S(1)} all-to-all(bf16[8,8,3584]{2,1,0:T(8,128)(2,1)S(1)} %add_convert_fusion), channel_id=1, replica_groups={{0,2,4,6,8,10,12,14},{1,3,5,7,9,11,13,15},{16,18,20,22,24,26,28,30},{17..., dimensions={0} | all-to-all | bytes 917504 | tf_op jit(solution)/shard_map/all_to_all | solution.py:298
  92.0 0.1 convert_reduce_fusion
  92.1 0.6 add_convert_fusion.2
  (5 shorter events, 0.1 us)
Async XLA Ops:
  0.0 14.3 %all-to-all-start = ((bf16[16,8,256]{2,1,0:T(8,128)(2,1)}), bf16[16,8,256]{2,1,0:T(8,128)(2,1)S(1)}, u32[]{:S(2)}, u32[]{:S(2)}) async-start(bf16[16,8,256]{2,1,0:T(8,128)(2,1)} %bitcast.13), calls=%async_computation | async-start | bytes 131072 | tf_op jit(solution)/shard_map/all_to_all | solution.py:268
  16.5 10.9 %all-to-all-start.1 = ((bf16[16,8,384]{2,1,0:T(8,128)(2,1)}), bf16[16,8,384]{2,1,0:T(8,128)(2,1)S(1)}, u32[]{:S(2)}, u32[]{:S(2)}) async-start(bf16[16,8,384]{2,1,0:T(8,128)(2,1)} %shard_map.110.refs_1_), calls=%async_computation.1 | async-start | bytes 196608 | tf_op jit(solution)/shard_map/all_to_all | solution.py:273
  28.6 1.9 %collective-permute-start = (bf16[64,3584]{1,0:T(8,128)(2,1)S(1)}, bf16[64,3584]{1,0:T(8,128)(2,1)S(1)}, u32[]{:S(2)}, u32[]{:S(2)}) collective-permute-start(bf16[64,3584]{1,0:T(8,128)(2,1)S(1)} %get-tuple-element.35), channel_id=1, source_target_pairs={{0,1},{1,0},{2,3},{3,2},{4,5},{5,4},{6,7},{7,6},{8,9},{9,8},{10,11... | collective-permute-start | bytes 1376264 | tf_op jit(solution)/shard_map/ppermute | solution.py:263
  30.6 7.7 %collective-permute-start.1 = (bf16[32,3584]{1,0:T(8,128)(2,1)S(1)}, bf16[32,3584]{1,0:T(8,128)(2,1)S(1)}, u32[]{:S(2)}, u32[]{:S(2)}) collective-permute-start(bf16[32,3584]{1,0:T(8,128)(2,1)S(1)} %get-tuple-element.45), channel_id=1, source_target_pairs={{0,2},{1,3},{2,0},{3,1},{4,6},{5,7},{6,4},{7,5},{8,10},{9,11},{10,... | collective-permute-start | bytes 688136 | tf_op jit(solution)/shard_map/ppermute | solution.py:263
  38.3 4.9 %collective-permute-start.2 = (bf16[16,3584]{1,0:T(8,128)(2,1)S(1)}, bf16[16,3584]{1,0:T(8,128)(2,1)S(1)}, u32[]{:S(2)}, u32[]{:S(2)}) collective-permute-start(bf16[16,3584]{1,0:T(8,128)(2,1)S(1)} %fusion), channel_id=1, source_target_pairs={{0,4},{1,5},{2,6},{3,7},{4,0},{5,1},{6,2},{7,3},{8,12},{9,13},{10,... | collective-permute-start | bytes 344072 | tf_op jit(solution)/shard_map/ppermute | solution.py:263
  43.3 6.4 %collective-permute-start.3 = (bf16[16,3584]{1,0:T(8,128)(2,1)S(1)}, bf16[16,3584]{1,0:T(8,128)(2,1)S(1)}, u32[]{:S(2)}, u32[]{:S(2)}) collective-permute-start(bf16[16,3584]{1,0:T(8,128)(2,1)S(1)} %convert_element_type.48.kept_ref), channel_id=1, source_target_pairs={{0,8},{1,9},{2,10},{3,11},{4,12},{5,13},{6,14},{7,15},{8,0},{9,1},... | collective-permute-start | bytes 344072 | tf_op jit(solution)/shard_map/ppermute | solution.py:263
  49.9 4.9 %collective-permute-start.4 = (bf16[16,3584]{1,0:T(8,128)(2,1)S(1)}, bf16[16,3584]{1,0:T(8,128)(2,1)S(1)}, u32[]{:S(2)}, u32[]{:S(2)}) collective-permute-start(bf16[16,3584]{1,0:T(8,128)(2,1)S(1)} %bitcast.10), channel_id=1, source_target_pairs={{0,4},{1,5},{2,6},{3,7},{4,0},{5,1},{6,2},{7,3},{8,12},{9,13},{10,... | collective-permute-start | bytes 344072 | tf_op jit(solution)/shard_map/ppermute | solution.py:263
  54.8 6.1 %collective-permute-start.5 = (bf16[32,3584]{1,0:T(8,128)(2,1)S(1)}, bf16[32,3584]{1,0:T(8,128)(2,1)S(1)}, u32[]{:S(2)}, u32[]{:S(2)}) collective-permute-start(bf16[32,3584]{1,0:T(8,128)(2,1)S(1)} %pad_maximum_fusion.refs_1_), channel_id=1, source_target_pairs={{0,2},{1,3},{2,0},{3,1},{4,6},{5,7},{6,4},{7,5},{8,10},{9,11},{10,... | collective-permute-start | bytes 688136 | tf_op jit(solution)/shard_map/ppermute | solution.py:263
  59.6 1.6 %collective-permute-start.6 = (bf16[32,3584]{1,0:T(8,128)(2,1)S(1)}, bf16[32,3584]{1,0:T(8,128)(2,1)S(1)}, u32[]{:S(2)}, u32[]{:S(2)}) collective-permute-start(bf16[32,3584]{1,0:T(8,128)(2,1)S(1)} %get-tuple-element.40.near_ref), channel_id=1, source_target_pairs={{0,1},{1,0},{2,3},{3,2},{4,5},{5,4},{6,7},{7,6},{8,9},{9,8},{10,11... | collective-permute-start | bytes 688136 | tf_op jit(solution)/shard_map/ppermute | solution.py:263
  60.8 1.5 %collective-permute-start.7 = (bf16[32,3584]{1,0:T(8,128)(2,1)S(1)}, bf16[32,3584]{1,0:T(8,128)(2,1)S(1)}, u32[]{:S(2)}, u32[]{:S(2)}) collective-permute-start(bf16[32,3584]{1,0:T(8,128)(2,1)S(1)} %collective-permute-done.5.far_ref), channel_id=1, source_target_pairs={{0,1},{1,0},{2,3},{3,2},{4,5},{5,4},{6,7},{7,6},{8,9},{9,8},{10,11... | collective-permute-start | bytes 688136 | tf_op jit(solution)/shard_map/ppermute | solution.py:263
  73.9 1.9 %collective-permute-start.8 = (bf16[8,8,3584]{2,1,0:T(8,128)(2,1)S(1)}, bf16[8,8,3584]{2,1,0:T(8,128)(2,1)S(1)}, u32[]{:S(2)}, u32[]{:S(2)}) collective-permute-start(bf16[8,8,3584]{2,1,0:T(8,128)(2,1)S(1)} %get-tuple-element.44), channel_id=1, source_target_pairs={{0,1},{1,0},{2,3},{3,2},{4,5},{5,4},{6,7},{7,6},{8,9},{9,8},{10,11... | collective-permute-start | bytes 1376264 | tf_op jit(solution)/shard_map/ppermute | solution.py:263

commit v5 on v4

--- a/solution.py
+++ b/solution.py
@@ -168,10 +168,10 @@
 
 
 def expert_kernel(
-    place_ref, near_ref, far_ref, near_other_ref, far_other_ref, gates_ref, gate_ref, up_source, down_source,
-    kept_ref, sent_ref, turned, hidden, up_ref, down_ref, sems,
+    place_ref, gates_ref, gate_ref, up_source, down_source, *refs
 ):
-    half = 2 * near_ref.shape[0]
+    pieces, (kept_ref, sent_ref, turned, hidden, up_ref, down_ref, sems) = refs[:-7], refs[-7:]
+    half = turned.shape[1] // 2
     units, feature = gate_ref.shape
     step = tile_of(units, 384)
     wide = tile_of(feature, 896)
@@ -190,7 +190,6 @@
         up_copy(at).start()
     for at in range(0, feature, wide):
         down_copy(at).start()
-    pieces = (near_ref, far_ref, near_other_ref, far_other_ref)
     turned[...] = jnp.concatenate([piece[...] for piece in pieces], axis=0).T
     gates = gates_ref[:, :1].astype(F32)
     for at in range(0, units, step):
@@ -212,7 +211,8 @@
 
 
 def experts(place, chips, pieces, gates, gate_weight, up_weight, down_weight):
-    half, feature = 2 * pieces[0].shape[0], pieces[0].shape[1]
+    half = sum(piece.shape[0] for piece in pieces) // 2
+    feature = gate_weight.shape[1]
     units = gate_weight.shape[0]
     weights = (up_weight, down_weight)
     return pl.pallas_call(
@@ -221,7 +221,8 @@
             jax.ShapeDtypeStruct((chips, half // chips, feature), F32),
             jax.ShapeDtypeStruct((chips, half // chips, feature), BF16),
         ),
-        in_specs=[SMEM_SPEC] + [VMEM_SPEC] * 6 + [HBM_SPEC] * 2,
+        in_specs=[SMEM_SPEC, VMEM_SPEC, VMEM_SPEC, HBM_SPEC, HBM_SPEC]
+        + [VMEM_SPEC] * len(pieces),
         out_specs=(VMEM_SPEC, VMEM_SPEC),
         scratch_shapes=[
             pltpu.VMEM((feature, 2 * half), BF16),
@@ -235,7 +236,13 @@
             bytes_accessed=6 * units * feature,
             transcendentals=2 * half * units,
         ),
-    )(place, *pieces, gates, gate_weight, *[pltpu.with_memory_space_constraint(w, pltpu.HBM) for w in weights])
+    )(
+        place,
+        gates,
+        gate_weight,
+        *[pltpu.with_memory_space_constraint(w, pltpu.HBM) for w in weights],
+        *pieces,
+    )
 
 
 def local(
@@ -275,24 +282,31 @@
         place, head_rows.reshape(chips, 2, tok, head_dim + LANES), output_held
     )
     arrived = swap(sent, 1)
-    bit = 2
+    quarter = kept.shape[0] // 4
+    parts = [
+        kept[at : at + quarter] + arrived[at : at + quarter].astype(F32)
+        for at in range(0, 4 * quarter, quarter)
+    ]
+    kept = parts[0]
+    for bits, part in ((6, parts[3]), (2, parts[2]), (4, parts[1])):
+        kept = kept + swap(part.astype(BF16), bits).astype(F32)
+    bit = 8
     while bit < chips:
         half = kept.shape[0] // 2
-        sent = (kept[half:] + arrived[half:].astype(F32)).astype(BF16)
-        kept = kept[:half] + arrived[:half].astype(F32)
-        arrived = swap(sent, bit)
+        sent = kept[half:].astype(BF16)
+        kept = kept[:half] + swap(sent, bit).astype(F32)
         bit *= 2
-    summed = kept + arrived.astype(F32)
-    summed = summed.at[:tok].add(residual_held.astype(F32)).astype(BF16)
+    summed = kept.at[:tok].add(residual_held.astype(F32)).astype(BF16)
     middle, own = norm(summed, swap(summed, bit), gain_held)
     own = own.reshape(2 * tok, -1)
     bit //= 2
-    while bit > 2:
+    while bit > 4:
         own = jnp.concatenate([own, swap(own, bit)], axis=0)
         bit //= 2
-    far = swap(own, bit)
-    gate_held, near = fetch(gate_weight, carry=own)
-    pieces = (near, far, swap(near, 1), swap(far, 1))
+    others = [swap(own, bits) for bits in (4, 2, 6)]
+    gate_held, own = fetch(gate_weight, carry=own)
+    pieces = [own] + others
+    pieces = pieces + [swap(piece, 1) for piece in pieces]
     kept, sent = experts(place, chips, pieces, gates, gate_held, up_weight, down_weight)
     summed = (kept + swap(sent, 1).astype(F32)).astype(BF16)
     blocks = lax.all_to_all(

time: 93.1 us -> 87.9 us (0.944)
  waiting for transfers between devices: 39.8 us -> 27.3 us
  starting transfers between devices: 12.4 us -> 19.7 us
    ppermute x9 -> x13, waiting for transfers between devices: 29.5 us -> 17 us  [swap(): return lax.ppermute(x, 'ep', [(i, i ^ bit) for i in range(size)])]
    ppermute x9 -> x13, starting transfers between devices: 1.51 us -> 8.85 us  [swap(): return lax.ppermute(x, 'ep', [(i, i ^ bit) for i in range(size)])]
  transfers between devices with their start and end apart: 11 -> 15, of which waited for: 11 -> 12; matrix products, arithmetic and copies ran while one was open for 1% -> 1% of each run, Pallas kernels for 8% -> 8%
where the time goes in v5:
time: 87.9 us; the launch traced here: 87.5 us
  waiting for transfers between devices  27.3 us (31%)
  Pallas kernels  22.3 us (25%)
  starting transfers between devices  19.7 us (22%)
  blocking collectives  16.3 us (19%)
  other arithmetic  1.7 us (2%)
    ppermute x13, waiting for transfers between devices, swap(): return lax.ppermute(x, 'ep', [(i, i ^ bit) for i in range(size)])  17 us
    all_to_all x1, blocking collectives, local(): lax.all_to_all(summed, 'ep', split_axis=0, concat_axis=0, tiled=True, axi...  16.3 us
    pallas_call x1, Pallas kernels, experts(): pl.pallas_call(expert_kernel, out_shape=(jax.ShapeDtypeStruct((chips, hal...  11.4 us
    ppermute x13, starting transfers between devices, swap(): return lax.ppermute(x, 'ep', [(i, i ^ bit) for i in range(size)])  8.85 us
    all_to_all x1, starting transfers between devices, local(): lax.all_to_all(queries.reshape(size, tok, head_dim), 'ep', split_axis=0,...  7.38 us
    pallas_call x3, Pallas kernels, fetch(): pl.pallas_call(functools.partial(fetch_kernel, count, carried), out_shape...  7.29 us
    all_to_all x1, waiting for transfers between devices, local(): lax.all_to_all(attended, 'ep', split_axis=0, concat_axis=0, tiled=True)  5.76 us
    all_to_all x1, waiting for transfers between devices, local(): lax.all_to_all(queries.reshape(size, tok, head_dim), 'ep', split_axis=0,...  4.56 us
  transfers between devices with their start and end apart: 15, of which 12 were waited for; matrix products, arithmetic and copies ran while one was open for 1% of the time, Pallas kernels for 8%

profile of v5, /device:TPU:0, one launch (start us, length us, event | category | flops | bytes accessed | tf_op | source)
XLA Modules:
  0.0 87.5 jit_solution(12247692191413564522)
XLA Ops:
  0.0 7.4 %all-to-all-start = ((bf16[16,8,256]{2,1,0:T(8,128)(2,1)}), bf16[16,8,256]{2,1,0:T(8,128)(2,1)S(1)}, u32[]{:S(2)}, u32[]{:S(2)}) async-start(bf16[16,8,256]{2,1,0:T(8,128)(2,1)} %bitcast.15), calls=%async_computation | async-start | bytes 131072 | tf_op jit(solution)/shard_map/all_to_all | solution.py:275
  7.4 1.6 %shard_map.109 = (bf16[8,256,512]{2,1,0:T(8,128)(2,1)S(1)}, bf16[8,3584]{1,0:T(8,128)(2,1)S(1)}, f32[3584]{0:T(1024)S(1)}, s32[8]{0:T(128)S(1)}, s32[3,8]{1,0:T(4,128)S(1)}) custom-call(bf16[8,256,512]{2,1,0:T(8,128)(2,1)} %refs_0_.3, bf16[8,3584]{1,0:T(8,128)(2,1)} %refs_1_.1, f32[3584]{0:T(1024)} %refs_2_.1, s32[8]{0:T(128)} %refs_3_.1, s32[3,8]{1,0:T(4,128)} %bitcast.16), custom_call_target="tpu_custom_call" | custom-call | bytes 2161728 | tf_op jit(solution)/shard_map/pallas_call | solution.py:41
  9.0 0.7 convert_bitcast_fusion.shares_ref
  9.7 4.6 %all-to-all-done.query_ref = bf16[16,8,256]{2,1,0:T(8,128)(2,1)S(1)} async-done(((bf16[16,8,256]{2,1,0:T(8,128)(2,1)}), bf16[16,8,256]{2,1,0:T(8,128)(2,1)S(1)}, u32[]{:S(2)}, u32[]{:S(2)}) %all-to-all-start) | async-done | bytes 65568 | tf_op jit(solution)/shard_map/all_to_all | solution.py:275
  14.3 2.2 %shard_map.110.refs_1_ = bf16[16,8,384]{2,1,0:T(8,128)(2,1)} custom-call(s32[8]{0:T(128)S(1)} %get-tuple-element.31.lengths_ref, s32[3,8]{1,0:T(4,128)S(1)} %get-tuple-element.32.routes_ref, f32[3,8]{1,0:T(4,128)S(1)} %convert_bitcast_fusion.shares_ref, bf16[16,8,256]{2,1,0:T(8,128)(2,1)S(1)} %all-to-all-done.query_ref, ...), custom_call_target="tpu_custom_call" | custom-call | tf_op jit(solution)/shard_map/pallas_call | solution.py:94
  16.5 3.5 %all-to-all-start.1 = ((bf16[16,8,384]{2,1,0:T(8,128)(2,1)}), bf16[16,8,384]{2,1,0:T(8,128)(2,1)S(1)}, u32[]{:S(2)}, u32[]{:S(2)}) async-start(bf16[16,8,384]{2,1,0:T(8,128)(2,1)} %shard_map.110.refs_1_), calls=%async_computation.1 | async-start | bytes 196608 | tf_op jit(solution)/shard_map/all_to_all | solution.py:280
  20.0 0.1 pad_add_fusion.place_ref
  20.1 1.5 %shard_map.111.weight_ref = bf16[256,3584]{1,0:T(8,128)(2,1)S(1)} custom-call(bf16[256,3584]{1,0:T(8,128)(2,1)} %refs_0_.4, bf16[16,8,384]{2,1,0:T(8,128)(2,1)} %shard_map.110.refs_1_), custom_call_target="tpu_custom_call" | custom-call | bytes 1835008 | tf_op jit(solution)/shard_map/pallas_call | solution.py:41
  21.6 5.8 %all-to-all-done.1 = bf16[16,8,384]{2,1,0:T(8,128)(2,1)S(1)} async-done(((bf16[16,8,384]{2,1,0:T(8,128)(2,1)}), bf16[16,8,384]{2,1,0:T(8,128)(2,1)S(1)}, u32[]{:S(2)}, u32[]{:S(2)}) %all-to-all-start.1) | async-done | bytes 98336 | tf_op jit(solution)/shard_map/all_to_all | solution.py:280
  27.3 1.3 %shard_map.112 = (f32[64,3584]{1,0:T(8,128)S(1)}, bf16[64,3584]{1,0:T(8,128)(2,1)S(1)}, bf16[128,128]{1,0:T(8,128)(2,1)S(1)}) custom-call(s32[2]{0:T(128)S(1)} %pad_add_fusion.place_ref, bf16[8,2,8,384]{3,2,1,0:T(8,128)(2,1)S(1)} %bitcast.9, bf16[256,3584]{1,0:T(8,128)(2,1)S(1)} %shard_map.111.weight_ref), custom_call_target="tpu_custom_call" | custom-call | tf_op jit(solution)/shard_map/pallas_call | solution.py:130
  28.7 0.1 collective-permute-start
  28.7 1.8 %collective-permute-done = bf16[64,3584]{1,0:T(8,128)(2,1)S(1)} collective-permute-done((bf16[64,3584]{1,0:T(8,128)(2,1)S(1)}, bf16[64,3584]{1,0:T(8,128)(2,1)S(1)}, u32[]{:S(2)}, u32[]{:S(2)}) %collective-permute-start) | collective-permute-done | bytes 458784 | tf_op jit(solution)/shard_map/ppermute | solution.py:270
  30.5 0.1 add_convert_fusion.3
  30.6 0.1 collective-permute-start.1
  30.7 1.2 %collective-permute-start.3 = (bf16[16,3584]{1,0:T(8,128)(2,1)S(1)}, bf16[16,3584]{1,0:T(8,128)(2,1)S(1)}, u32[]{:S(2)}, u32[]{:S(2)}) collective-permute-start(bf16[16,3584]{1,0:T(8,128)(2,1)S(1)} %get-tuple-element.46), channel_id=1, source_target_pairs={{0,4},{1,5},{2,6},{3,7},{4,0},{5,1},{6,2},{7,3},{8,12},{9,13},{10,... | collective-permute-start | bytes 344072 | tf_op jit(solution)/shard_map/ppermute | solution.py:270
  31.9 2.3 %collective-permute-start.2 = (bf16[16,3584]{1,0:T(8,128)(2,1)S(1)}, bf16[16,3584]{1,0:T(8,128)(2,1)S(1)}, u32[]{:S(2)}, u32[]{:S(2)}) collective-permute-start(bf16[16,3584]{1,0:T(8,128)(2,1)S(1)} %get-tuple-element.47), channel_id=1, source_target_pairs={{0,2},{1,3},{2,0},{3,1},{4,6},{5,7},{6,4},{7,5},{8,10},{9,11},{10,... | collective-permute-start | bytes 344072 | tf_op jit(solution)/shard_map/ppermute | solution.py:270
  34.2 3.4 %collective-permute-done.1 = bf16[16,3584]{1,0:T(8,128)(2,1)S(1)} collective-permute-done((bf16[16,3584]{1,0:T(8,128)(2,1)S(1)}, bf16[16,3584]{1,0:T(8,128)(2,1)S(1)}, u32[]{:S(2)}, u32[]{:S(2)}) %collective-permute-start.1) | collective-permute-done | bytes 114720 | tf_op jit(solution)/shard_map/ppermute | solution.py:270
  37.6 0.2 collective-permute-done.3
  37.7 1.5 %collective-permute-done.2 = bf16[16,3584]{1,0:T(8,128)(2,1)S(1)} collective-permute-done((bf16[16,3584]{1,0:T(8,128)(2,1)S(1)}, bf16[16,3584]{1,0:T(8,128)(2,1)S(1)}, u32[]{:S(2)}, u32[]{:S(2)}) %collective-permute-start.2) | collective-permute-done | bytes 114720 | tf_op jit(solution)/shard_map/ppermute | solution.py:270
  39.2 0.1 convert_add_fusion
  39.3 0.2 collective-permute-start.4
  39.5 7.7 %collective-permute-done.4 = bf16[16,3584]{1,0:T(8,128)(2,1)S(1)} collective-permute-done((bf16[16,3584]{1,0:T(8,128)(2,1)S(1)}, bf16[16,3584]{1,0:T(8,128)(2,1)S(1)}, u32[]{:S(2)}, u32[]{:S(2)}) %collective-permute-start.4) | collective-permute-done | bytes 114720 | tf_op jit(solution)/shard_map/ppermute | solution.py:270
  47.2 0.1 shard_map.113
  47.4 0.1 collective-permute-start.7
  47.5 0.5 collective-permute-start.6
  48.0 3.0 %collective-permute-start.5 = (bf16[16,3584]{1,0:T(8,128)(2,1)S(1)}, bf16[16,3584]{1,0:T(8,128)(2,1)S(1)}, u32[]{:S(2)}, u32[]{:S(2)}) collective-permute-start(bf16[16,3584]{1,0:T(8,128)(2,1)S(1)} %bitcast.12), channel_id=1, source_target_pairs={{0,4},{1,5},{2,6},{3,7},{4,0},{5,1},{6,2},{7,3},{8,12},{9,13},{10,... | collective-permute-start | bytes 344072 | tf_op jit(solution)/shard_map/ppermute | solution.py:270
  50.9 4.1 %shard_map.114 = (bf16[1536,3584]{1,0:T(8,128)(2,1)S(1)}, bf16[16,3584]{1,0:T(8,128)(2,1)S(1)}) custom-call(bf16[1536,3584]{1,0:T(8,128)(2,1)} %refs_0_.5, bf16[16,3584]{1,0:T(8,128)(2,1)S(1)} %bitcast.13), custom_call_target="tpu_custom_call" | custom-call | bytes 11010048 | tf_op jit(solution)/shard_map/pallas_call | solution.py:41
  55.1 0.1 collective-permute-start.8
  55.2 0.0 collective-permute-done.7.refs_3_
  55.2 0.5 collective-permute-start.11
  55.7 0.0 collective-permute-done.6.refs_2_
  55.7 0.1 collective-permute-start.10
  55.7 0.0 collective-permute-done.5.refs_1_
  55.8 0.4 collective-permute-start.9
  56.2 0.3 collective-permute-done.8.refs_4_
  56.5 0.2 collective-permute-done.11.refs_7_
  56.6 0.4 collective-permute-done.10.refs_6_
  57.0 0.2 collective-permute-done.9.refs_5_
  57.2 11.4 %shard_map.115 = (f32[8,8,3584]{2,1,0:T(8,128)S(1)}, bf16[8,8,3584]{2,1,0:T(8,128)(2,1)S(1)}) custom-call(s32[2]{0:T(128)S(1)} %pad_add_fusion.place_ref, bf16[128,128]{1,0:T(8,128)(2,1)S(1)} %get-tuple-element.39.gates_ref, bf16[1536,3584]{1,0:T(8,128)(2,1)S(1)} %get-tuple-element.41.gate_ref, bf16[1536,3584]{1,0:T(8,128)(2,1)} %up_source.1, ...), custom_call_target="tpu_custom_call" | custom-call | flops 4227858432 | bytes 33030144 | tf_op jit(solution)/shard_map/pallas_call | solution.py:218
  68.6 0.4 collective-permute-start.12
  69.0 1.5 %collective-permute-done.12 = bf16[8,8,3584]{2,1,0:T(8,128)(2,1)S(1)} collective-permute-done((bf16[8,8,3584]{2,1,0:T(8,128)(2,1)S(1)}, bf16[8,8,3584]{2,1,0:T(8,128)(2,1)S(1)}, u32[]{:S(2)}, u32[]{:S(2)}) %collective-permute-start.12) | collective-permute-done | bytes 458784 | tf_op jit(solution)/shard_map/ppermute | solution.py:270
  70.4 0.1 add_convert_fusion
  70.5 16.3 %all_to_all.15 = bf16[8,8,3584]{2,1,0:T(8,128)(2,1)S(1)} all-to-all(bf16[8,8,3584]{2,1,0:T(8,128)(2,1)S(1)} %add_convert_fusion), channel_id=1, replica_groups={{0,2,4,6,8,10,12,14},{1,3,5,7,9,11,13,15},{16,18,20,22,24,26,28,30},{17..., dimensions={0} | all-to-all | bytes 917504 | tf_op jit(solution)/shard_map/all_to_all | solution.py:312
  86.8 0.1 convert_reduce_fusion
  86.9 0.6 add_convert_fusion.4
  (2 shorter events, 0.0 us)
Async XLA Ops:
  0.0 14.3 %all-to-all-start = ((bf16[16,8,256]{2,1,0:T(8,128)(2,1)}), bf16[16,8,256]{2,1,0:T(8,128)(2,1)S(1)}, u32[]{:S(2)}, u32[]{:S(2)}) async-start(bf16[16,8,256]{2,1,0:T(8,128)(2,1)} %bitcast.15), calls=%async_computation | async-start | bytes 131072 | tf_op jit(solution)/shard_map/all_to_all | solution.py:275
  16.5 10.9 %all-to-all-start.1 = ((bf16[16,8,384]{2,1,0:T(8,128)(2,1)}), bf16[16,8,384]{2,1,0:T(8,128)(2,1)S(1)}, u32[]{:S(2)}, u32[]{:S(2)}) async-start(bf16[16,8,384]{2,1,0:T(8,128)(2,1)} %shard_map.110.refs_1_), calls=%async_computation.1 | async-start | bytes 196608 | tf_op jit(solution)/shard_map/all_to_all | solution.py:280
  28.7 1.9 %collective-permute-start = (bf16[64,3584]{1,0:T(8,128)(2,1)S(1)}, bf16[64,3584]{1,0:T(8,128)(2,1)S(1)}, u32[]{:S(2)}, u32[]{:S(2)}) collective-permute-start(bf16[64,3584]{1,0:T(8,128)(2,1)S(1)} %get-tuple-element.35), channel_id=1, source_target_pairs={{0,1},{1,0},{2,3},{3,2},{4,5},{5,4},{6,7},{7,6},{8,9},{9,8},{10,11... | collective-permute-start | bytes 1376264 | tf_op jit(solution)/shard_map/ppermute | solution.py:270
  30.6 7.0 %collective-permute-start.1 = (bf16[16,3584]{1,0:T(8,128)(2,1)S(1)}, bf16[16,3584]{1,0:T(8,128)(2,1)S(1)}, u32[]{:S(2)}, u32[]{:S(2)}) collective-permute-start(bf16[16,3584]{1,0:T(8,128)(2,1)S(1)} %get-tuple-element.45), channel_id=1, source_target_pairs={{0,6},{1,7},{2,4},{3,5},{4,2},{5,3},{6,0},{7,1},{8,14},{9,15},{10,... | collective-permute-start | bytes 344072 | tf_op jit(solution)/shard_map/ppermute | solution.py:270
  30.7 7.0 %collective-permute-start.3 = (bf16[16,3584]{1,0:T(8,128)(2,1)S(1)}, bf16[16,3584]{1,0:T(8,128)(2,1)S(1)}, u32[]{:S(2)}, u32[]{:S(2)}) collective-permute-start(bf16[16,3584]{1,0:T(8,128)(2,1)S(1)} %get-tuple-element.46), channel_id=1, source_target_pairs={{0,4},{1,5},{2,6},{3,7},{4,0},{5,1},{6,2},{7,3},{8,12},{9,13},{10,... | collective-permute-start | bytes 344072 | tf_op jit(solution)/shard_map/ppermute | solution.py:270
  31.9 7.3 %collective-permute-start.2 = (bf16[16,3584]{1,0:T(8,128)(2,1)S(1)}, bf16[16,3584]{1,0:T(8,128)(2,1)S(1)}, u32[]{:S(2)}, u32[]{:S(2)}) collective-permute-start(bf16[16,3584]{1,0:T(8,128)(2,1)S(1)} %get-tuple-element.47), channel_id=1, source_target_pairs={{0,2},{1,3},{2,0},{3,1},{4,6},{5,7},{6,4},{7,5},{8,10},{9,11},{10,... | collective-permute-start | bytes 344072 | tf_op jit(solution)/shard_map/ppermute | solution.py:270
  39.3 7.9 %collective-permute-start.4 = (bf16[16,3584]{1,0:T(8,128)(2,1)S(1)}, bf16[16,3584]{1,0:T(8,128)(2,1)S(1)}, u32[]{:S(2)}, u32[]{:S(2)}) collective-permute-start(bf16[16,3584]{1,0:T(8,128)(2,1)S(1)} %convert_element_type.60.kept_ref), channel_id=1, source_target_pairs={{0,8},{1,9},{2,10},{3,11},{4,12},{5,13},{6,14},{7,15},{8,0},{9,1},... | collective-permute-start | bytes 344072 | tf_op jit(solution)/shard_map/ppermute | solution.py:270
  47.4 7.8 %collective-permute-start.7 = (bf16[16,3584]{1,0:T(8,128)(2,1)S(1)}, bf16[16,3584]{1,0:T(8,128)(2,1)S(1)}, u32[]{:S(2)}, u32[]{:S(2)}) collective-permute-start(bf16[16,3584]{1,0:T(8,128)(2,1)S(1)} %bitcast.10), channel_id=1, source_target_pairs={{0,6},{1,7},{2,4},{3,5},{4,2},{5,3},{6,0},{7,1},{8,14},{9,15},{10,... | collective-permute-start | bytes 344072 | tf_op jit(solution)/shard_map/ppermute | solution.py:270
  47.5 8.2 %collective-permute-start.6 = (bf16[16,3584]{1,0:T(8,128)(2,1)S(1)}, bf16[16,3584]{1,0:T(8,128)(2,1)S(1)}, u32[]{:S(2)}, u32[]{:S(2)}) collective-permute-start(bf16[16,3584]{1,0:T(8,128)(2,1)S(1)} %bitcast.11), channel_id=1, source_target_pairs={{0,2},{1,3},{2,0},{3,1},{4,6},{5,7},{6,4},{7,5},{8,10},{9,11},{10,... | collective-permute-start | bytes 344072 | tf_op jit(solution)/shard_map/ppermute | solution.py:270
  48.0 7.8 %collective-permute-start.5 = (bf16[16,3584]{1,0:T(8,128)(2,1)S(1)}, bf16[16,3584]{1,0:T(8,128)(2,1)S(1)}, u32[]{:S(2)}, u32[]{:S(2)}) collective-permute-start(bf16[16,3584]{1,0:T(8,128)(2,1)S(1)} %bitcast.12), channel_id=1, source_target_pairs={{0,4},{1,5},{2,6},{3,7},{4,0},{5,1},{6,2},{7,3},{8,12},{9,13},{10,... | collective-permute-start | bytes 344072 | tf_op jit(solution)/shard_map/ppermute | solution.py:270
  55.1 1.4 %collective-permute-start.8 = (bf16[16,3584]{1,0:T(8,128)(2,1)S(1)}, bf16[16,3584]{1,0:T(8,128)(2,1)S(1)}, u32[]{:S(2)}, u32[]{:S(2)}) collective-permute-start(bf16[16,3584]{1,0:T(8,128)(2,1)S(1)} %get-tuple-element.42.refs_0_), channel_id=1, source_target_pairs={{0,1},{1,0},{2,3},{3,2},{4,5},{5,4},{6,7},{7,6},{8,9},{9,8},{10,11... | collective-permute-start | bytes 344072 | tf_op jit(solution)/shard_map/ppermute | solution.py:270
  55.2 1.5 %collective-permute-start.11 = (bf16[16,3584]{1,0:T(8,128)(2,1)S(1)}, bf16[16,3584]{1,0:T(8,128)(2,1)S(1)}, u32[]{:S(2)}, u32[]{:S(2)}) collective-permute-start(bf16[16,3584]{1,0:T(8,128)(2,1)S(1)} %collective-permute-done.7.refs_3_), channel_id=1, source_target_pairs={{0,1},{1,0},{2,3},{3,2},{4,5},{5,4},{6,7},{7,6},{8,9},{9,8},{10,11... | collective-permute-start | bytes 344072 | tf_op jit(solution)/shard_map/ppermute | solution.py:270
  55.7 1.3 %collective-permute-start.10 = (bf16[16,3584]{1,0:T(8,128)(2,1)S(1)}, bf16[16,3584]{1,0:T(8,128)(2,1)S(1)}, u32[]{:S(2)}, u32[]{:S(2)}) collective-permute-start(bf16[16,3584]{1,0:T(8,128)(2,1)S(1)} %collective-permute-done.6.refs_2_), channel_id=1, source_target_pairs={{0,1},{1,0},{2,3},{3,2},{4,5},{5,4},{6,7},{7,6},{8,9},{9,8},{10,11... | collective-permute-start | bytes 344072 | tf_op jit(solution)/shard_map/ppermute | solution.py:270
  55.8 1.4 %collective-permute-start.9 = (bf16[16,3584]{1,0:T(8,128)(2,1)S(1)}, bf16[16,3584]{1,0:T(8,128)(2,1)S(1)}, u32[]{:S(2)}, u32[]{:S(2)}) collective-permute-start(bf16[16,3584]{1,0:T(8,128)(2,1)S(1)} %collective-permute-done.5.refs_1_), channel_id=1, source_target_pairs={{0,1},{1,0},{2,3},{3,2},{4,5},{5,4},{6,7},{7,6},{8,9},{9,8},{10,11... | collective-permute-start | bytes 344072 | tf_op jit(solution)/shard_map/ppermute | solution.py:270
  68.6 1.9 %collective-permute-start.12 = (bf16[8,8,3584]{2,1,0:T(8,128)(2,1)S(1)}, bf16[8,8,3584]{2,1,0:T(8,128)(2,1)S(1)}, u32[]{:S(2)}, u32[]{:S(2)}) collective-permute-start(bf16[8,8,3584]{2,1,0:T(8,128)(2,1)S(1)} %get-tuple-element.44), channel_id=1, source_target_pairs={{0,1},{1,0},{2,3},{3,2},{4,5},{5,4},{6,7},{7,6},{8,9},{9,8},{10,11... | collective-permute-start | bytes 1376264 | tf_op jit(solution)/shard_map/ppermute | solution.py:270

commit v6 on v5

--- a/solution.py
+++ b/solution.py
@@ -168,26 +168,20 @@
 
 
 def expert_kernel(
-    place_ref, gates_ref, gate_ref, up_source, down_source, *refs
+    gates_ref, gate_ref, up_ref, down_source, *refs
 ):
-    pieces, (kept_ref, sent_ref, turned, hidden, up_ref, down_ref, sems) = refs[:-7], refs[-7:]
+    pieces, (kept_ref, sent_ref, turned, hidden, down_ref, sems) = refs[:-6], refs[-6:]
     half = turned.shape[1] // 2
     units, feature = gate_ref.shape
     step = tile_of(units, 384)
     wide = tile_of(feature, 896)
 
-    def up_copy(at):
-        rows = pl.ds(at, step)
-        return pltpu.make_async_copy(up_source.at[rows], up_ref.at[rows], sems.at[0, at // step])
-
     def down_copy(at):
         columns = pl.ds(at, wide)
         return pltpu.make_async_copy(
-            down_source.at[:, columns], down_ref.at[:, columns], sems.at[1, at // wide]
+            down_source.at[:, columns], down_ref.at[:, columns], sems.at[at // wide]
         )
 
-    for at in range(0, units, step):
-        up_copy(at).start()
     for at in range(0, feature, wide):
         down_copy(at).start()
     turned[...] = jnp.concatenate([piece[...] for piece in pieces], axis=0).T
@@ -195,7 +189,6 @@
     for at in range(0, units, step):
         rows = pl.ds(at, step)
         gate_pre = jnp.dot(gate_ref[rows, :], turned[...], preferred_element_type=F32)
-        up_copy(at).wait()
         up_pre = jnp.dot(up_ref[rows, :], turned[...], preferred_element_type=F32)
         product = gate_pre / (1.0 + jnp.exp(-gate_pre)) * up_pre
         hidden[:, rows] = (product.T * gates).astype(BF16)
@@ -203,44 +196,39 @@
         down_copy(at).wait()
         columns = pl.ds(at, wide)
         part = jnp.dot(hidden[...], down_ref[:, columns], preferred_element_type=F32)
-        chips, tok, _ = kept_ref.shape
-        for at_block, bits in enumerate(relative_order(chips)):
-            chip, low = place_ref[0] ^ bits, at_block * tok
-            kept_ref[chip, :, columns] = part[low : low + tok]
-            sent_ref[chip, :, columns] = part[half + low : half + low + tok].astype(BF16)
-
-
-def experts(place, chips, pieces, gates, gate_weight, up_weight, down_weight):
+        kept_ref[:, columns] = part[:half]
+        sent_ref[:, columns] = part[half:].astype(BF16)
+
+
+def experts(pieces, gates, gate_weight, up_weight, down_weight):
     half = sum(piece.shape[0] for piece in pieces) // 2
     feature = gate_weight.shape[1]
     units = gate_weight.shape[0]
-    weights = (up_weight, down_weight)
     return pl.pallas_call(
         expert_kernel,
         out_shape=(
-            jax.ShapeDtypeStruct((chips, half // chips, feature), F32),
-            jax.ShapeDtypeStruct((chips, half // chips, feature), BF16),
-        ),
-        in_specs=[SMEM_SPEC, VMEM_SPEC, VMEM_SPEC, HBM_SPEC, HBM_SPEC]
-        + [VMEM_SPEC] * len(pieces),
+            jax.ShapeDtypeStruct((half, feature), F32),
+            jax.ShapeDtypeStruct((half, feature), BF16),
+        ),
+        in_specs=[VMEM_SPEC] * 3 + [HBM_SPEC] + [VMEM_SPEC] * len(pieces),
         out_specs=(VMEM_SPEC, VMEM_SPEC),
         scratch_shapes=[
             pltpu.VMEM((feature, 2 * half), BF16),
             pltpu.VMEM((2 * half, units), BF16),
-        ]
-        + [pltpu.VMEM((units, feature), BF16)] * 2
-        + [pltpu.SemaphoreType.DMA((2, 8))],
-        compiler_params=pltpu.CompilerParams(vmem_limit_bytes=32 << 20),
+            pltpu.VMEM((units, feature), BF16),
+            pltpu.SemaphoreType.DMA((8,)),
+        ],
+        compiler_params=pltpu.CompilerParams(vmem_limit_bytes=22 << 20),
         cost_estimate=pl.CostEstimate(
             flops=12 * half * feature * units,
             bytes_accessed=6 * units * feature,
             transcendentals=2 * half * units,
         ),
     )(
-        place,
         gates,
         gate_weight,
-        *[pltpu.with_memory_space_constraint(w, pltpu.HBM) for w in weights],
+        up_weight,
+        pltpu.with_memory_space_constraint(down_weight, pltpu.HBM),
         *pieces,
     )
 
@@ -264,10 +252,25 @@
     chips = size // 2
     me = lax.axis_index("ep").astype(jnp.int32)
     place = jnp.stack([me // 2, me % 2])
-    same_core = [[2 * chip + c for chip in range(chips)] for c in range(2)]
 
     def swap(x, bit):
         return lax.ppermute(x, "ep", [(i, i ^ bit) for i in range(size)])
+
+    def sum_nearest(kept, arrived):
+        quarter = kept.shape[0] // 4
+        parts = [
+            kept[at : at + quarter] + arrived[at : at + quarter].astype(F32)
+            for at in range(0, 4 * quarter, quarter)
+        ]
+        kept = parts[0]
+        for bits, part in ((6, parts[3]), (2, parts[2]), (4, parts[1])):
+            kept = kept + swap(part.astype(BF16), bits).astype(F32)
+        bit = 8
+        while bit < chips:
+            half = kept.shape[0] // 2
+            kept = kept[:half] + swap(kept[half:].astype(BF16), bit).astype(F32)
+            bit *= 2
+        return kept
 
     cache, residual_held, gain_held, lengths_held, routes_held = fetch(
         key_values, residual, norm_gain, lengths, routes.T
@@ -281,22 +284,10 @@
     kept, sent, gates = project(
         place, head_rows.reshape(chips, 2, tok, head_dim + LANES), output_held
     )
-    arrived = swap(sent, 1)
-    quarter = kept.shape[0] // 4
-    parts = [
-        kept[at : at + quarter] + arrived[at : at + quarter].astype(F32)
-        for at in range(0, 4 * quarter, quarter)
-    ]
-    kept = parts[0]
-    for bits, part in ((6, parts[3]), (2, parts[2]), (4, parts[1])):
-        kept = kept + swap(part.astype(BF16), bits).astype(F32)
-    bit = 8
-    while bit < chips:
-        half = kept.shape[0] // 2
-        sent = kept[half:].astype(BF16)
-        kept = kept[:half] + swap(sent, bit).astype(F32)
-        bit *= 2
+    kept = sum_nearest(kept, swap(sent, 1))
     summed = kept.at[:tok].add(residual_held.astype(F32)).astype(BF16)
+    bit = chips
+    up_held, gain_held = fetch(up_weight, after=(summed,), carry=gain_held)
     middle, own = norm(summed, swap(summed, bit), gain_held)
     own = own.reshape(2 * tok, -1)
     bit //= 2
@@ -307,12 +298,10 @@
     gate_held, own = fetch(gate_weight, carry=own)
     pieces = [own] + others
     pieces = pieces + [swap(piece, 1) for piece in pieces]
-    kept, sent = experts(place, chips, pieces, gates, gate_held, up_weight, down_weight)
-    summed = (kept + swap(sent, 1).astype(F32)).astype(BF16)
-    blocks = lax.all_to_all(
-        summed, "ep", split_axis=0, concat_axis=0, tiled=True, axis_index_groups=same_core
-    )
-    return (middle + jnp.sum(blocks.astype(F32), axis=0)).astype(BF16)
+    kept, sent = experts(pieces, gates, gate_held, up_held, down_weight)
+    kept = sum_nearest(kept, swap(sent, 1))
+    combined = kept[:tok] + swap(kept[tok:].astype(BF16), chips).astype(F32)
+    return (middle + combined).astype(BF16)
 
 
 def solution(mesh):

time: 87.9 us -> 85.2 us (0.969)
  blocking collectives: 16.3 us -> 0 us
  waiting for transfers between devices: 27.3 us -> 33.8 us
  starting transfers between devices: 19.7 us -> 23.4 us
  Pallas kernels: 22.3 us -> 25.7 us
    all_to_all x1 -> x0, blocking collectives: 16.3 us -> none  [local(): lax.all_to_all(summed, 'ep', split_axis=0, concat_axis=0, tiled=True, axi...]
    ppermute x13 -> x17, waiting for transfers between devices: 17 us -> 23.5 us  [swap(): return lax.ppermute(x, 'ep', [(i, i ^ bit) for i in range(size)])]
    pallas_call x3 -> x4, Pallas kernels: 7.29 us -> 11.4 us  [fetch(): pl.pallas_call(functools.partial(fetch_kernel, count, carried), out_shape...]
    ppermute x13 -> x17, starting transfers between devices: 8.85 us -> 12.5 us  [swap(): return lax.ppermute(x, 'ep', [(i, i ^ bit) for i in range(size)])]
  transfers between devices with their start and end apart: 15 -> 19, of which waited for: 12 -> 16; matrix products, arithmetic and copies ran while one was open for 1% -> 1% of each run, Pallas kernels for 8% -> 13%
where the time goes in v6:
time: 85.2 us; the launch traced here: 84.8 us
  waiting for transfers between devices  33.8 us (40%)
  Pallas kernels  25.7 us (30%)
  starting transfers between devices  23.4 us (27%)
  other arithmetic  1.72 us (2%)
    ppermute x17, waiting for transfers between devices, swap(): return lax.ppermute(x, 'ep', [(i, i ^ bit) for i in range(size)])  23.5 us
    ppermute x17, starting transfers between devices, swap(): return lax.ppermute(x, 'ep', [(i, i ^ bit) for i in range(size)])  12.5 us
    pallas_call x4, Pallas kernels, fetch(): pl.pallas_call(functools.partial(fetch_kernel, count, carried), out_shape...  11.4 us
    pallas_call x1, Pallas kernels, experts(): pl.pallas_call(expert_kernel, out_shape=(jax.ShapeDtypeStruct((half, feat...  10.7 us
    all_to_all x1, starting transfers between devices, local(): lax.all_to_all(queries.reshape(size, tok, head_dim), 'ep', split_axis=0,...  7.38 us
    all_to_all x1, waiting for transfers between devices, local(): lax.all_to_all(attended, 'ep', split_axis=0, concat_axis=0, tiled=True)  5.76 us
    all_to_all x1, waiting for transfers between devices, local(): lax.all_to_all(queries.reshape(size, tok, head_dim), 'ep', split_axis=0,...  4.56 us
    all_to_all x1, starting transfers between devices, local(): lax.all_to_all(attended, 'ep', split_axis=0, concat_axis=0, tiled=True)  3.51 us
  transfers between devices with their start and end apart: 19, of which 16 were waited for; matrix products, arithmetic and copies ran while one was open for 1% of the time, Pallas kernels for 13%

profile of v6, /device:TPU:0, one launch (start us, length us, event | category | flops | bytes accessed | tf_op | source)
XLA Modules:
  0.0 84.8 jit_solution(6323124121642766484)
XLA Ops:
  0.0 7.4 %all-to-all-start = ((bf16[16,8,256]{2,1,0:T(8,128)(2,1)}), bf16[16,8,256]{2,1,0:T(8,128)(2,1)S(1)}, u32[]{:S(2)}, u32[]{:S(2)}) async-start(bf16[16,8,256]{2,1,0:T(8,128)(2,1)} %bitcast.15), calls=%async_computation | async-start | bytes 131072 | tf_op jit(solution)/shard_map/all_to_all | solution.py:278
  7.4 1.6 %shard_map.109 = (bf16[8,256,512]{2,1,0:T(8,128)(2,1)S(1)}, bf16[8,3584]{1,0:T(8,128)(2,1)S(1)}, f32[3584]{0:T(1024)S(1)}, s32[8]{0:T(128)S(1)}, s32[3,8]{1,0:T(4,128)S(1)}) custom-call(bf16[8,256,512]{2,1,0:T(8,128)(2,1)} %refs_0_.4, bf16[8,3584]{1,0:T(8,128)(2,1)} %refs_1_.1, f32[3584]{0:T(1024)} %refs_2_.1, s32[8]{0:T(128)} %refs_3_.1, s32[3,8]{1,0:T(4,128)} %bitcast.16), custom_call_target="tpu_custom_call" | custom-call | bytes 2161728 | tf_op jit(solution)/shard_map/pallas_call | solution.py:41
  9.0 0.7 convert_bitcast_fusion.shares_ref
  9.7 4.6 %all-to-all-done.query_ref = bf16[16,8,256]{2,1,0:T(8,128)(2,1)S(1)} async-done(((bf16[16,8,256]{2,1,0:T(8,128)(2,1)}), bf16[16,8,256]{2,1,0:T(8,128)(2,1)S(1)}, u32[]{:S(2)}, u32[]{:S(2)}) %all-to-all-start) | async-done | bytes 65568 | tf_op jit(solution)/shard_map/all_to_all | solution.py:278
  14.3 2.2 %shard_map.110.refs_1_ = bf16[16,8,384]{2,1,0:T(8,128)(2,1)} custom-call(s32[8]{0:T(128)S(1)} %get-tuple-element.33.lengths_ref, s32[3,8]{1,0:T(4,128)S(1)} %get-tuple-element.34.routes_ref, f32[3,8]{1,0:T(4,128)S(1)} %convert_bitcast_fusion.shares_ref, bf16[16,8,256]{2,1,0:T(8,128)(2,1)S(1)} %all-to-all-done.query_ref, ...), custom_call_target="tpu_custom_call" | custom-call | tf_op jit(solution)/shard_map/pallas_call | solution.py:94
  16.5 3.5 %all-to-all-start.1 = ((bf16[16,8,384]{2,1,0:T(8,128)(2,1)}), bf16[16,8,384]{2,1,0:T(8,128)(2,1)S(1)}, u32[]{:S(2)}, u32[]{:S(2)}) async-start(bf16[16,8,384]{2,1,0:T(8,128)(2,1)} %shard_map.110.refs_1_), calls=%async_computation.1 | async-start | bytes 196608 | tf_op jit(solution)/shard_map/all_to_all | solution.py:283
  20.0 0.1 pad_add_fusion.place_ref
  20.1 1.5 %shard_map.111.weight_ref = bf16[256,3584]{1,0:T(8,128)(2,1)S(1)} custom-call(bf16[256,3584]{1,0:T(8,128)(2,1)} %refs_0_.5, bf16[16,8,384]{2,1,0:T(8,128)(2,1)} %shard_map.110.refs_1_), custom_call_target="tpu_custom_call" | custom-call | bytes 1835008 | tf_op jit(solution)/shard_map/pallas_call | solution.py:41
  21.6 5.8 %all-to-all-done.1 = bf16[16,8,384]{2,1,0:T(8,128)(2,1)S(1)} async-done(((bf16[16,8,384]{2,1,0:T(8,128)(2,1)}), bf16[16,8,384]{2,1,0:T(8,128)(2,1)S(1)}, u32[]{:S(2)}, u32[]{:S(2)}) %all-to-all-start.1) | async-done | bytes 98336 | tf_op jit(solution)/shard_map/all_to_all | solution.py:283
  27.3 1.3 %shard_map.112 = (f32[64,3584]{1,0:T(8,128)S(1)}, bf16[64,3584]{1,0:T(8,128)(2,1)S(1)}, bf16[128,128]{1,0:T(8,128)(2,1)S(1)}) custom-call(s32[2]{0:T(128)S(1)} %pad_add_fusion.place_ref, bf16[8,2,8,384]{3,2,1,0:T(8,128)(2,1)S(1)} %bitcast.9, bf16[256,3584]{1,0:T(8,128)(2,1)S(1)} %shard_map.111.weight_ref), custom_call_target="tpu_custom_call" | custom-call | tf_op jit(solution)/shard_map/pallas_call | solution.py:130
  28.6 0.1 collective-permute-start
  28.7 1.8 %collective-permute-done = bf16[64,3584]{1,0:T(8,128)(2,1)S(1)} collective-permute-done((bf16[64,3584]{1,0:T(8,128)(2,1)S(1)}, bf16[64,3584]{1,0:T(8,128)(2,1)S(1)}, u32[]{:S(2)}, u32[]{:S(2)}) %collective-permute-start) | collective-permute-done | bytes 458784 | tf_op jit(solution)/shard_map/ppermute | solution.py:257
  30.6 0.1 collective-permute-start.1
  30.7 1.2 %collective-permute-start.3 = (bf16[16,3584]{1,0:T(8,128)(2,1)S(1)}, bf16[16,3584]{1,0:T(8,128)(2,1)S(1)}, u32[]{:S(2)}, u32[]{:S(2)}) collective-permute-start(bf16[16,3584]{1,0:T(8,128)(2,1)S(1)} %get-tuple-element.53), channel_id=1, source_target_pairs={{0,4},{1,5},{2,6},{3,7},{4,0},{5,1},{6,2},{7,3},{8,12},{9,13},{10,... | collective-permute-start | bytes 344072 | tf_op jit(solution)/shard_map/ppermute | solution.py:257
  31.9 2.3 %collective-permute-start.2 = (bf16[16,3584]{1,0:T(8,128)(2,1)S(1)}, bf16[16,3584]{1,0:T(8,128)(2,1)S(1)}, u32[]{:S(2)}, u32[]{:S(2)}) collective-permute-start(bf16[16,3584]{1,0:T(8,128)(2,1)S(1)} %get-tuple-element.54), channel_id=1, source_target_pairs={{0,2},{1,3},{2,0},{3,1},{4,6},{5,7},{6,4},{7,5},{8,10},{9,11},{10,... | collective-permute-start | bytes 344072 | tf_op jit(solution)/shard_map/ppermute | solution.py:257
  34.2 3.4 %collective-permute-done.1 = bf16[16,3584]{1,0:T(8,128)(2,1)S(1)} collective-permute-done((bf16[16,3584]{1,0:T(8,128)(2,1)S(1)}, bf16[16,3584]{1,0:T(8,128)(2,1)S(1)}, u32[]{:S(2)}, u32[]{:S(2)}) %collective-permute-start.1) | collective-permute-done | bytes 114720 | tf_op jit(solution)/shard_map/ppermute | solution.py:257
  37.5 0.2 collective-permute-done.3
  37.7 1.5 %collective-permute-done.2 = bf16[16,3584]{1,0:T(8,128)(2,1)S(1)} collective-permute-done((bf16[16,3584]{1,0:T(8,128)(2,1)S(1)}, bf16[16,3584]{1,0:T(8,128)(2,1)S(1)}, u32[]{:S(2)}, u32[]{:S(2)}) %collective-permute-start.2) | collective-permute-done | bytes 114720 | tf_op jit(solution)/shard_map/ppermute | solution.py:257
  39.3 0.2 collective-permute-start.4
  39.5 4.1 %shard_map.113 = (bf16[1536,3584]{1,0:T(8,128)(2,1)S(1)}, f32[3584]{0:T(1024)S(1)}) custom-call(bf16[1536,3584]{1,0:T(8,128)(2,1)} %refs_0_.6, f32[3584]{0:T(1024)S(1)} %get-tuple-element.39.refs_1_, bf16[16,3584]{1,0:T(8,128)(2,1)S(1)} %convert_element_type.85.refs_2_.kept_ref), custom_call_target="tpu_custom_call" | custom-call | bytes 11010048 | tf_op jit(solution)/shard_map/pallas_call | solution.py:41
  43.7 3.6 %collective-permute-done.4 = bf16[16,3584]{1,0:T(8,128)(2,1)S(1)} collective-permute-done((bf16[16,3584]{1,0:T(8,128)(2,1)S(1)}, bf16[16,3584]{1,0:T(8,128)(2,1)S(1)}, u32[]{:S(2)}, u32[]{:S(2)}) %collective-permute-start.4) | collective-permute-done | bytes 114720 | tf_op jit(solution)/shard_map/ppermute | solution.py:257
  47.2 0.1 shard_map.114
  47.4 0.1 collective-permute-start.7
  47.5 0.5 collective-permute-start.6
  48.0 3.0 %collective-permute-start.5 = (bf16[16,3584]{1,0:T(8,128)(2,1)S(1)}, bf16[16,3584]{1,0:T(8,128)(2,1)S(1)}, u32[]{:S(2)}, u32[]{:S(2)}) collective-permute-start(bf16[16,3584]{1,0:T(8,128)(2,1)S(1)} %bitcast.12), channel_id=1, source_target_pairs={{0,4},{1,5},{2,6},{3,7},{4,0},{5,1},{6,2},{7,3},{8,12},{9,13},{10,... | collective-permute-start | bytes 344072 | tf_op jit(solution)/shard_map/ppermute | solution.py:257
  50.9 4.1 %shard_map.115 = (bf16[1536,3584]{1,0:T(8,128)(2,1)S(1)}, bf16[16,3584]{1,0:T(8,128)(2,1)S(1)}) custom-call(bf16[1536,3584]{1,0:T(8,128)(2,1)} %refs_0_.7, bf16[16,3584]{1,0:T(8,128)(2,1)S(1)} %bitcast.13), custom_call_target="tpu_custom_call" | custom-call | bytes 11010048 | tf_op jit(solution)/shard_map/pallas_call | solution.py:41
  55.1 0.1 collective-permute-start.8
  55.2 0.5 collective-permute-start.11
  55.7 0.1 collective-permute-start.10
  55.8 0.4 collective-permute-start.9
  56.2 0.3 collective-permute-done.8.refs_4_
  56.5 0.2 collective-permute-done.11.refs_7_
  56.6 0.4 collective-permute-done.10.refs_6_
  57.0 0.2 collective-permute-done.9.refs_5_
  57.2 10.7 %shard_map.116 = (f32[64,3584]{1,0:T(8,128)S(1)}, bf16[64,3584]{1,0:T(8,128)(2,1)S(1)}) custom-call(bf16[128,128]{1,0:T(8,128)(2,1)S(1)} %get-tuple-element.42.gates_ref, bf16[1536,3584]{1,0:T(8,128)(2,1)S(1)} %get-tuple-element.44.gate_ref, bf16[1536,3584]{1,0:T(8,128)(2,1)S(1)} %get-tuple-element.45.up_ref, bf16[1536,3584]{1,0:T(8,128)(2,1)} %down_source.1, ...), custom_call_target="tpu_custom_call" | custom-call | flops 4227858432 | bytes 33030144 | tf_op jit(solution)/shard_map/pallas_call | solution.py:207
  67.8 0.4 collective-permute-start.12
  68.2 1.5 %collective-permute-done.12 = bf16[64,3584]{1,0:T(8,128)(2,1)S(1)} collective-permute-done((bf16[64,3584]{1,0:T(8,128)(2,1)S(1)}, bf16[64,3584]{1,0:T(8,128)(2,1)S(1)}, u32[]{:S(2)}, u32[]{:S(2)}) %collective-permute-start.12) | collective-permute-done | bytes 458784 | tf_op jit(solution)/shard_map/ppermute | solution.py:257
  69.7 0.1 add_convert_fusion.2
  69.8 0.6 collective-permute-start.13
  70.4 1.6 %collective-permute-start.15 = (bf16[16,3584]{1,0:T(8,128)(2,1)S(1)}, bf16[16,3584]{1,0:T(8,128)(2,1)S(1)}, u32[]{:S(2)}, u32[]{:S(2)}) collective-permute-start(bf16[16,3584]{1,0:T(8,128)(2,1)S(1)} %get-tuple-element.50), channel_id=1, source_target_pairs={{0,4},{1,5},{2,6},{3,7},{4,0},{5,1},{6,2},{7,3},{8,12},{9,13},{10,... | collective-permute-start | bytes 344072 | tf_op jit(solution)/shard_map/ppermute | solution.py:257
  72.0 1.4 %collective-permute-start.14 = (bf16[16,3584]{1,0:T(8,128)(2,1)S(1)}, bf16[16,3584]{1,0:T(8,128)(2,1)S(1)}, u32[]{:S(2)}, u32[]{:S(2)}) collective-permute-start(bf16[16,3584]{1,0:T(8,128)(2,1)S(1)} %get-tuple-element.51), channel_id=1, source_target_pairs={{0,2},{1,3},{2,0},{3,1},{4,6},{5,7},{6,4},{7,5},{8,10},{9,11},{10,... | collective-permute-start | bytes 344072 | tf_op jit(solution)/shard_map/ppermute | solution.py:257
  73.4 3.4 %collective-permute-done.13 = bf16[16,3584]{1,0:T(8,128)(2,1)S(1)} collective-permute-done((bf16[16,3584]{1,0:T(8,128)(2,1)S(1)}, bf16[16,3584]{1,0:T(8,128)(2,1)S(1)}, u32[]{:S(2)}, u32[]{:S(2)}) %collective-permute-start.13) | collective-permute-done | bytes 114720 | tf_op jit(solution)/shard_map/ppermute | solution.py:257
  76.7 0.9 %collective-permute-done.15 = bf16[16,3584]{1,0:T(8,128)(2,1)S(1)} collective-permute-done((bf16[16,3584]{1,0:T(8,128)(2,1)S(1)}, bf16[16,3584]{1,0:T(8,128)(2,1)S(1)}, u32[]{:S(2)}, u32[]{:S(2)}) %collective-permute-start.15) | collective-permute-done | bytes 114720 | tf_op jit(solution)/shard_map/ppermute | solution.py:257
  77.6 1.0 %collective-permute-done.14 = bf16[16,3584]{1,0:T(8,128)(2,1)S(1)} collective-permute-done((bf16[16,3584]{1,0:T(8,128)(2,1)S(1)}, bf16[16,3584]{1,0:T(8,128)(2,1)S(1)}, u32[]{:S(2)}, u32[]{:S(2)}) %collective-permute-start.14) | collective-permute-done | bytes 114720 | tf_op jit(solution)/shard_map/ppermute | solution.py:257
  78.6 0.1 convert_add_fusion
  78.7 0.1 collective-permute-start.16
  78.8 5.3 %collective-permute-done.16 = bf16[8,3584]{1,0:T(8,128)(2,1)S(1)} collective-permute-done((bf16[8,3584]{1,0:T(8,128)(2,1)S(1)}, bf16[8,3584]{1,0:T(8,128)(2,1)S(1)}, u32[]{:S(2)}, u32[]{:S(2)}) %collective-permute-start.16) | collective-permute-done | bytes 57376 | tf_op jit(solution)/shard_map/ppermute | solution.py:257
  84.1 0.6 fusion.1
  (8 shorter events, 0.2 us)
Async XLA Ops:
  0.0 14.3 %all-to-all-start = ((bf16[16,8,256]{2,1,0:T(8,128)(2,1)}), bf16[16,8,256]{2,1,0:T(8,128)(2,1)S(1)}, u32[]{:S(2)}, u32[]{:S(2)}) async-start(bf16[16,8,256]{2,1,0:T(8,128)(2,1)} %bitcast.15), calls=%async_computation | async-start | bytes 131072 | tf_op jit(solution)/shard_map/all_to_all | solution.py:278
  16.5 10.9 %all-to-all-start.1 = ((bf16[16,8,384]{2,1,0:T(8,128)(2,1)}), bf16[16,8,384]{2,1,0:T(8,128)(2,1)S(1)}, u32[]{:S(2)}, u32[]{:S(2)}) async-start(bf16[16,8,384]{2,1,0:T(8,128)(2,1)} %shard_map.110.refs_1_), calls=%async_computation.1 | async-start | bytes 196608 | tf_op jit(solution)/shard_map/all_to_all | solution.py:283
  28.6 1.9 %collective-permute-start = (bf16[64,3584]{1,0:T(8,128)(2,1)S(1)}, bf16[64,3584]{1,0:T(8,128)(2,1)S(1)}, u32[]{:S(2)}, u32[]{:S(2)}) collective-permute-start(bf16[64,3584]{1,0:T(8,128)(2,1)S(1)} %get-tuple-element.37), channel_id=1, source_target_pairs={{0,1},{1,0},{2,3},{3,2},{4,5},{5,4},{6,7},{7,6},{8,9},{9,8},{10,11... | collective-permute-start | bytes 1376264 | tf_op jit(solution)/shard_map/ppermute | solution.py:257
  30.6 7.0 %collective-permute-start.1 = (bf16[16,3584]{1,0:T(8,128)(2,1)S(1)}, bf16[16,3584]{1,0:T(8,128)(2,1)S(1)}, u32[]{:S(2)}, u32[]{:S(2)}) collective-permute-start(bf16[16,3584]{1,0:T(8,128)(2,1)S(1)} %get-tuple-element.52), channel_id=1, source_target_pairs={{0,6},{1,7},{2,4},{3,5},{4,2},{5,3},{6,0},{7,1},{8,14},{9,15},{10,... | collective-permute-start | bytes 344072 | tf_op jit(solution)/shard_map/ppermute | solution.py:257
  30.7 7.0 %collective-permute-start.3 = (bf16[16,3584]{1,0:T(8,128)(2,1)S(1)}, bf16[16,3584]{1,0:T(8,128)(2,1)S(1)}, u32[]{:S(2)}, u32[]{:S(2)}) collective-permute-start(bf16[16,3584]{1,0:T(8,128)(2,1)S(1)} %get-tuple-element.53), channel_id=1, source_target_pairs={{0,4},{1,5},{2,6},{3,7},{4,0},{5,1},{6,2},{7,3},{8,12},{9,13},{10,... | collective-permute-start | bytes 344072 | tf_op jit(solution)/shard_map/ppermute | solution.py:257
  31.9 7.3 %collective-permute-start.2 = (bf16[16,3584]{1,0:T(8,128)(2,1)S(1)}, bf16[16,3584]{1,0:T(8,128)(2,1)S(1)}, u32[]{:S(2)}, u32[]{:S(2)}) collective-permute-start(bf16[16,3584]{1,0:T(8,128)(2,1)S(1)} %get-tuple-element.54), channel_id=1, source_target_pairs={{0,2},{1,3},{2,0},{3,1},{4,6},{5,7},{6,4},{7,5},{8,10},{9,11},{10,... | collective-permute-start | bytes 344072 | tf_op jit(solution)/shard_map/ppermute | solution.py:257
  39.3 7.9 %collective-permute-start.4 = (bf16[16,3584]{1,0:T(8,128)(2,1)S(1)}, bf16[16,3584]{1,0:T(8,128)(2,1)S(1)}, u32[]{:S(2)}, u32[]{:S(2)}) collective-permute-start(bf16[16,3584]{1,0:T(8,128)(2,1)S(1)} %convert_element_type.85.refs_2_.kept_ref), channel_id=1, source_target_pairs={{0,8},{1,9},{2,10},{3,11},{4,12},{5,13},{6,14},{7,15},{8,0},{9,1},... | collective-permute-start | bytes 344072 | tf_op jit(solution)/shard_map/ppermute | solution.py:257
  47.4 7.8 %collective-permute-start.7 = (bf16[16,3584]{1,0:T(8,128)(2,1)S(1)}, bf16[16,3584]{1,0:T(8,128)(2,1)S(1)}, u32[]{:S(2)}, u32[]{:S(2)}) collective-permute-start(bf16[16,3584]{1,0:T(8,128)(2,1)S(1)} %bitcast.10), channel_id=1, source_target_pairs={{0,6},{1,7},{2,4},{3,5},{4,2},{5,3},{6,0},{7,1},{8,14},{9,15},{10,... | collective-permute-start | bytes 344072 | tf_op jit(solution)/shard_map/ppermute | solution.py:257
  47.5 8.2 %collective-permute-start.6 = (bf16[16,3584]{1,0:T(8,128)(2,1)S(1)}, bf16[16,3584]{1,0:T(8,128)(2,1)S(1)}, u32[]{:S(2)}, u32[]{:S(2)}) collective-permute-start(bf16[16,3584]{1,0:T(8,128)(2,1)S(1)} %bitcast.11), channel_id=1, source_target_pairs={{0,2},{1,3},{2,0},{3,1},{4,6},{5,7},{6,4},{7,5},{8,10},{9,11},{10,... | collective-permute-start | bytes 344072 | tf_op jit(solution)/shard_map/ppermute | solution.py:257
  48.0 7.8 %collective-permute-start.5 = (bf16[16,3584]{1,0:T(8,128)(2,1)S(1)}, bf16[16,3584]{1,0:T(8,128)(2,1)S(1)}, u32[]{:S(2)}, u32[]{:S(2)}) collective-permute-start(bf16[16,3584]{1,0:T(8,128)(2,1)S(1)} %bitcast.12), channel_id=1, source_target_pairs={{0,4},{1,5},{2,6},{3,7},{4,0},{5,1},{6,2},{7,3},{8,12},{9,13},{10,... | collective-permute-start | bytes 344072 | tf_op jit(solution)/shard_map/ppermute | solution.py:257
  55.1 1.4 %collective-permute-start.8 = (bf16[16,3584]{1,0:T(8,128)(2,1)S(1)}, bf16[16,3584]{1,0:T(8,128)(2,1)S(1)}, u32[]{:S(2)}, u32[]{:S(2)}) collective-permute-start(bf16[16,3584]{1,0:T(8,128)(2,1)S(1)} %get-tuple-element.46.refs_0_), channel_id=1, source_target_pairs={{0,1},{1,0},{2,3},{3,2},{4,5},{5,4},{6,7},{7,6},{8,9},{9,8},{10,11... | collective-permute-start | bytes 344072 | tf_op jit(solution)/shard_map/ppermute | solution.py:257
  55.2 1.5 %collective-permute-start.11 = (bf16[16,3584]{1,0:T(8,128)(2,1)S(1)}, bf16[16,3584]{1,0:T(8,128)(2,1)S(1)}, u32[]{:S(2)}, u32[]{:S(2)}) collective-permute-start(bf16[16,3584]{1,0:T(8,128)(2,1)S(1)} %collective-permute-done.7.refs_3_), channel_id=1, source_target_pairs={{0,1},{1,0},{2,3},{3,2},{4,5},{5,4},{6,7},{7,6},{8,9},{9,8},{10,11... | collective-permute-start | bytes 344072 | tf_op jit(solution)/shard_map/ppermute | solution.py:257
  55.7 1.3 %collective-permute-start.10 = (bf16[16,3584]{1,0:T(8,128)(2,1)S(1)}, bf16[16,3584]{1,0:T(8,128)(2,1)S(1)}, u32[]{:S(2)}, u32[]{:S(2)}) collective-permute-start(bf16[16,3584]{1,0:T(8,128)(2,1)S(1)} %collective-permute-done.6.refs_2_), channel_id=1, source_target_pairs={{0,1},{1,0},{2,3},{3,2},{4,5},{5,4},{6,7},{7,6},{8,9},{9,8},{10,11... | collective-permute-start | bytes 344072 | tf_op jit(solution)/shard_map/ppermute | solution.py:257
  55.8 1.4 %collective-permute-start.9 = (bf16[16,3584]{1,0:T(8,128)(2,1)S(1)}, bf16[16,3584]{1,0:T(8,128)(2,1)S(1)}, u32[]{:S(2)}, u32[]{:S(2)}) collective-permute-start(bf16[16,3584]{1,0:T(8,128)(2,1)S(1)} %collective-permute-done.5.refs_1_), channel_id=1, source_target_pairs={{0,1},{1,0},{2,3},{3,2},{4,5},{5,4},{6,7},{7,6},{8,9},{9,8},{10,11... | collective-permute-start | bytes 344072 | tf_op jit(solution)/shard_map/ppermute | solution.py:257
  67.8 1.9 %collective-permute-start.12 = (bf16[64,3584]{1,0:T(8,128)(2,1)S(1)}, bf16[64,3584]{1,0:T(8,128)(2,1)S(1)}, u32[]{:S(2)}, u32[]{:S(2)}) collective-permute-start(bf16[64,3584]{1,0:T(8,128)(2,1)S(1)} %get-tuple-element.48), channel_id=1, source_target_pairs={{0,1},{1,0},{2,3},{3,2},{4,5},{5,4},{6,7},{7,6},{8,9},{9,8},{10,11... | collective-permute-start | bytes 1376264 | tf_op jit(solution)/shard_map/ppermute | solution.py:257
  69.8 6.9 %collective-permute-start.13 = (bf16[16,3584]{1,0:T(8,128)(2,1)S(1)}, bf16[16,3584]{1,0:T(8,128)(2,1)S(1)}, u32[]{:S(2)}, u32[]{:S(2)}) collective-permute-start(bf16[16,3584]{1,0:T(8,128)(2,1)S(1)} %get-tuple-element.49), channel_id=1, source_target_pairs={{0,6},{1,7},{2,4},{3,5},{4,2},{5,3},{6,0},{7,1},{8,14},{9,15},{10,... | collective-permute-start | bytes 344072 | tf_op jit(solution)/shard_map/ppermute | solution.py:257
  70.4 7.3 %collective-permute-start.15 = (bf16[16,3584]{1,0:T(8,128)(2,1)S(1)}, bf16[16,3584]{1,0:T(8,128)(2,1)S(1)}, u32[]{:S(2)}, u32[]{:S(2)}) collective-permute-start(bf16[16,3584]{1,0:T(8,128)(2,1)S(1)} %get-tuple-element.50), channel_id=1, source_target_pairs={{0,4},{1,5},{2,6},{3,7},{4,0},{5,1},{6,2},{7,3},{8,12},{9,13},{10,... | collective-permute-start | bytes 344072 | tf_op jit(solution)/shard_map/ppermute | solution.py:257
  72.0 6.6 %collective-permute-start.14 = (bf16[16,3584]{1,0:T(8,128)(2,1)S(1)}, bf16[16,3584]{1,0:T(8,128)(2,1)S(1)}, u32[]{:S(2)}, u32[]{:S(2)}) collective-permute-start(bf16[16,3584]{1,0:T(8,128)(2,1)S(1)} %get-tuple-element.51), channel_id=1, source_target_pairs={{0,2},{1,3},{2,0},{3,1},{4,6},{5,7},{6,4},{7,5},{8,10},{9,11},{10,... | collective-permute-start | bytes 344072 | tf_op jit(solution)/shard_map/ppermute | solution.py:257
  78.7 5.4 %collective-permute-start.16 = (bf16[8,3584]{1,0:T(8,128)(2,1)S(1)}, bf16[8,3584]{1,0:T(8,128)(2,1)S(1)}, u32[]{:S(2)}, u32[]{:S(2)}) collective-permute-start(bf16[8,3584]{1,0:T(8,128)(2,1)S(1)} %slice.129), channel_id=1, source_target_pairs={{0,8},{1,9},{2,10},{3,11},{4,12},{5,13},{6,14},{7,15},{8,0},{9,1},... | collective-permute-start | bytes 172040 | tf_op jit(solution)/shard_map/ppermute | solution.py:257

commit v7 on v6

--- a/solution.py
+++ b/solution.py
@@ -1,4 +1,5 @@
 import functools
+import math
 
 import jax
 import jax.numpy as jnp
@@ -21,11 +22,11 @@
     return max(t for t in range(LANES, most + 1, LANES) if extent % t == 0)
 
 
-def fetch_kernel(count, carried, *refs):
+def fetch_kernel(count, carried, ranges, *refs):
     sources, held, sems = refs[:count], refs[-count - 1 - carried : -1 - carried], refs[-1]
     copies = [
-        pltpu.make_async_copy(source, target, sems.at[at])
-        for at, (source, target) in enumerate(zip(sources, held))
+        pltpu.make_async_copy(source if rows is None else source.at[pl.ds(*rows)], target, sems.at[at])
+        for at, (source, target, rows) in enumerate(zip(sources, held, ranges))
     ]
     for copy in copies:
         copy.start()
@@ -38,9 +39,14 @@
 def fetch(*arrays, after=(), carry=None):
     count, carried = len(arrays), int(carry is not None)
     carries = (carry,) * carried
-    return pl.pallas_call(
-        functools.partial(fetch_kernel, count, carried),
-        out_shape=tuple(pltpu.VMEM(a.shape, a.dtype) for a in arrays)
+    ranges = [a[1:] if isinstance(a, tuple) else None for a in arrays]
+    arrays = [a[0] if isinstance(a, tuple) else a for a in arrays]
+    shapes = [
+        a.shape if rows is None else (rows[1],) + a.shape[1:] for a, rows in zip(arrays, ranges)
+    ]
+    return pl.pallas_call(
+        functools.partial(fetch_kernel, count, carried, ranges),
+        out_shape=tuple(pltpu.VMEM(s, a.dtype) for s, a in zip(shapes, arrays))
         + tuple(jax.ShapeDtypeStruct(c.shape, c.dtype) for c in carries),
         in_specs=[HBM_SPEC] * count
         + [VMEM_SPEC] * carried
@@ -108,36 +114,37 @@
     return order
 
 
-def project_kernel(place_ref, rows_ref, weight_ref, kept_ref, sent_ref, gates_ref, ordered):
+def project_kernel(place_ref, rows_ref, weight_ref, terms_ref, gates_ref, ordered):
     chips, _, tok, _ = rows_ref.shape
     head_dim = weight_ref.shape[0]
-    half = chips * tok
-    mine, core = place_ref[0], place_ref[1]
-    for part, core_at, out_ref in ((1, 1 - core, sent_ref), (0, core, kept_ref)):
-        for at, bits in enumerate(relative_order(chips)):
-            ordered[at] = rows_ref[mine ^ bits, core_at]
-        block = ordered[...].reshape(half, head_dim + LANES)
-        out_ref[...] = jnp.dot(
-            block[:, :head_dim], weight_ref[...], preferred_element_type=F32
-        ).astype(out_ref.dtype)
-        gates_ref[pl.ds(part * half, half), :] = block[:, head_dim:]
-
-
-def project(place, rows, weight):
+    for at, bits in enumerate(relative_order(chips)):
+        ordered[at] = rows_ref[place_ref[0] ^ bits, place_ref[1]]
+    block = ordered[...].reshape(chips * tok, head_dim + LANES)
+    terms_ref[...] = jnp.dot(
+        block[:, :head_dim], weight_ref[...], preferred_element_type=F32
+    ).astype(terms_ref.dtype)
+    gates_ref[...] = block[:, head_dim:]
+
+
+def project(place, rows, weight, dtype):
     chips, _, tok, width = rows.shape
     half = chips * tok
     feature = weight.shape[1]
     return pl.pallas_call(
         project_kernel,
         out_shape=(
-            jax.ShapeDtypeStruct((half, feature), F32),
-            jax.ShapeDtypeStruct((half, feature), BF16),
-            jax.ShapeDtypeStruct((2 * half, LANES), BF16),
+            jax.ShapeDtypeStruct((half, feature), dtype),
+            jax.ShapeDtypeStruct((half, LANES), BF16),
         ),
         in_specs=[SMEM_SPEC, VMEM_SPEC, VMEM_SPEC],
-        out_specs=(VMEM_SPEC, VMEM_SPEC, VMEM_SPEC),
+        out_specs=(VMEM_SPEC, VMEM_SPEC),
         scratch_shapes=[pltpu.VMEM((chips, tok, width), BF16)],
         compiler_params=pltpu.CompilerParams(vmem_limit_bytes=8 << 20),
+        cost_estimate=pl.CostEstimate(
+            flops=2 * half * feature * weight.shape[0],
+            bytes_accessed=2 * weight.size,
+            transcendentals=0,
+        ),
     )(place, rows, weight)
 
 
@@ -167,13 +174,10 @@
     )(kept, arrived.reshape(2, tok, feature), gain)
 
 
-def expert_kernel(
-    gates_ref, gate_ref, up_ref, down_source, *refs
-):
+def expert_kernel(own_gates_ref, other_gates_ref, first_ref, second_ref, up_ref, down_source, *refs):
     pieces, (kept_ref, sent_ref, turned, hidden, down_ref, sems) = refs[:-6], refs[-6:]
     half = turned.shape[1] // 2
-    units, feature = gate_ref.shape
-    step = tile_of(units, 384)
+    units, feature = up_ref.shape
     wide = tile_of(feature, 896)
 
     def down_copy(at):
@@ -185,13 +189,19 @@
     for at in range(0, feature, wide):
         down_copy(at).start()
     turned[...] = jnp.concatenate([piece[...] for piece in pieces], axis=0).T
-    gates = gates_ref[:, :1].astype(F32)
+    gates = jnp.concatenate([own_gates_ref[...], other_gates_ref[...]], axis=0)
+    gates = gates.astype(F32).T[:1]
+    part = first_ref.shape[0]
+    step = tile_of(math.gcd(part, units - part), 384)
     for at in range(0, units, step):
+        gate_ref, low = (first_ref, at) if at < part else (second_ref, at - part)
         rows = pl.ds(at, step)
-        gate_pre = jnp.dot(gate_ref[rows, :], turned[...], preferred_element_type=F32)
+        gate_pre = jnp.dot(
+            gate_ref[pl.ds(low, step), :], turned[...], preferred_element_type=F32
+        )
         up_pre = jnp.dot(up_ref[rows, :], turned[...], preferred_element_type=F32)
-        product = gate_pre / (1.0 + jnp.exp(-gate_pre)) * up_pre
-        hidden[:, rows] = (product.T * gates).astype(BF16)
+        product = gate_pre / (1.0 + jnp.exp(-gate_pre)) * up_pre * gates
+        hidden[:, rows] = product.astype(BF16).T
     for at in range(0, feature, wide):
         down_copy(at).wait()
         columns = pl.ds(at, wide)
@@ -200,17 +210,16 @@
         sent_ref[:, columns] = part[half:].astype(BF16)
 
 
-def experts(pieces, gates, gate_weight, up_weight, down_weight):
-    half = sum(piece.shape[0] for piece in pieces) // 2
-    feature = gate_weight.shape[1]
-    units = gate_weight.shape[0]
+def experts(pieces, own_gates, other_gates, first_gate, second_gate, up_weight, down_weight):
+    half = own_gates.shape[0]
+    units, feature = up_weight.shape
     return pl.pallas_call(
         expert_kernel,
         out_shape=(
             jax.ShapeDtypeStruct((half, feature), F32),
             jax.ShapeDtypeStruct((half, feature), BF16),
         ),
-        in_specs=[VMEM_SPEC] * 3 + [HBM_SPEC] + [VMEM_SPEC] * len(pieces),
+        in_specs=[VMEM_SPEC] * 5 + [HBM_SPEC] + [VMEM_SPEC] * len(pieces),
         out_specs=(VMEM_SPEC, VMEM_SPEC),
         scratch_shapes=[
             pltpu.VMEM((feature, 2 * half), BF16),
@@ -225,8 +234,10 @@
             transcendentals=2 * half * units,
         ),
     )(
-        gates,
-        gate_weight,
+        own_gates,
+        other_gates,
+        first_gate,
+        second_gate,
         up_weight,
         pltpu.with_memory_space_constraint(down_weight, pltpu.HBM),
         *pieces,
@@ -252,6 +263,7 @@
     chips = size // 2
     me = lax.axis_index("ep").astype(jnp.int32)
     place = jnp.stack([me // 2, me % 2])
+    other_place = jnp.stack([me // 2, 1 - me % 2])
 
     def swap(x, bit):
         return lax.ppermute(x, "ep", [(i, i ^ bit) for i in range(size)])
@@ -281,13 +293,18 @@
     attended = attend(lengths_held, routes_held, gate_weights.astype(F32).T, query_rows, cache)
     (output_held,) = fetch(output_weight, after=(attended,))
     head_rows = lax.all_to_all(attended, "ep", split_axis=0, concat_axis=0, tiled=True)
-    kept, sent, gates = project(
-        place, head_rows.reshape(chips, 2, tok, head_dim + LANES), output_held
-    )
-    kept = sum_nearest(kept, swap(sent, 1))
+    head_rows = head_rows.reshape(chips, 2, tok, head_dim + LANES)
+    sent, other_gates = project(other_place, head_rows, output_held, BF16)
+    arrived = swap(sent, 1)
+    kept, own_gates = project(place, head_rows, output_held, F32)
+    kept = sum_nearest(kept, arrived)
     summed = kept.at[:tok].add(residual_held.astype(F32)).astype(BF16)
     bit = chips
-    up_held, gain_held = fetch(up_weight, after=(summed,), carry=gain_held)
+    units = gate_weight.shape[0]
+    part = units // LANES // 2 * LANES
+    up_held, first_held, gain_held = fetch(
+        up_weight, (gate_weight, 0, part), after=(summed,), carry=gain_held
+    )
     middle, own = norm(summed, swap(summed, bit), gain_held)
     own = own.reshape(2 * tok, -1)
     bit //= 2
@@ -295,10 +312,12 @@
         own = jnp.concatenate([own, swap(own, bit)], axis=0)
         bit //= 2
     others = [swap(own, bits) for bits in (4, 2, 6)]
-    gate_held, own = fetch(gate_weight, carry=own)
+    second_held, own = fetch((gate_weight, part, units - part), carry=own)
     pieces = [own] + others
     pieces = pieces + [swap(piece, 1) for piece in pieces]
-    kept, sent = experts(pieces, gates, gate_held, up_held, down_weight)
+    kept, sent = experts(
+        pieces, own_gates, other_gates, first_held, second_held, up_held, down_weight
+    )
     kept = sum_nearest(kept, swap(sent, 1))
     combined = kept[:tok] + swap(kept[tok:].astype(BF16), chips).astype(F32)
     return (middle + combined).astype(BF16)

time: 85.2 us -> 84.3 us (0.989)
  waiting for transfers between devices: 33.8 us -> 32.2 us
    ppermute x17, waiting for transfers between devices: 23.5 us -> 21.9 us  [swap(): return lax.ppermute(x, 'ep', [(i, i ^ bit) for i in range(size)])]
    pallas_call x1 -> x2, Pallas kernels: 1.3 us -> 1.97 us  [project(): pl.pallas_call(project_kernel, out_shape=(jax.ShapeDtypeStruct((half, fea...]
  transfers between devices with their start and end apart: 19 -> 19, of which waited for: 16 -> 17; matrix products, arithmetic and copies ran while one was open for 1% -> 1% of each run, Pallas kernels for 13% -> 15%
where the time goes in v7:
time: 84.3 us; the launch traced here: 83.9 us
  waiting for transfers between devices  32.2 us (38%)
  Pallas kernels  26.4 us (31%)
  starting transfers between devices  23.4 us (28%)
  other arithmetic  1.72 us (2%)
    ppermute x17, waiting for transfers between devices, swap(): return lax.ppermute(x, 'ep', [(i, i ^ bit) for i in range(size)])  21.9 us
    ppermute x17, starting transfers between devices, swap(): return lax.ppermute(x, 'ep', [(i, i ^ bit) for i in range(size)])  12.5 us
    pallas_call x4, Pallas kernels, fetch(): pl.pallas_call(functools.partial(fetch_kernel, count, carried, ranges), o...  11.4 us
    pallas_call x1, Pallas kernels, experts(): pl.pallas_call(expert_kernel, out_shape=(jax.ShapeDtypeStruct((half, feat...  10.6 us
    all_to_all x1, starting transfers between devices, local(): lax.all_to_all(queries.reshape(size, tok, head_dim), 'ep', split_axis=0,...  7.38 us
    all_to_all x1, waiting for transfers between devices, local(): lax.all_to_all(attended, 'ep', split_axis=0, concat_axis=0, tiled=True)  5.76 us
    all_to_all x1, waiting for transfers between devices, local(): lax.all_to_all(queries.reshape(size, tok, head_dim), 'ep', split_axis=0,...  4.56 us
    all_to_all x1, starting transfers between devices, local(): lax.all_to_all(attended, 'ep', split_axis=0, concat_axis=0, tiled=True)  3.51 us
  transfers between devices with their start and end apart: 19, of which 17 were waited for; matrix products, arithmetic and copies ran while one was open for 1% of the time, Pallas kernels for 15%

profile of v7, /device:TPU:0, one launch (start us, length us, event | category | flops | bytes accessed | tf_op | source)
XLA Modules:
  0.0 83.9 jit_solution(9712771596838735039)
XLA Ops:
  0.0 7.4 %all-to-all-start = ((bf16[16,8,256]{2,1,0:T(8,128)(2,1)}), bf16[16,8,256]{2,1,0:T(8,128)(2,1)S(1)}, u32[]{:S(2)}, u32[]{:S(2)}) async-start(bf16[16,8,256]{2,1,0:T(8,128)(2,1)} %bitcast.17), calls=%async_computation | async-start | bytes 131072 | tf_op jit(solution)/shard_map/all_to_all | solution.py:290
  7.4 1.6 %shard_map.109 = (bf16[8,256,512]{2,1,0:T(8,128)(2,1)S(1)}, bf16[8,3584]{1,0:T(8,128)(2,1)S(1)}, f32[3584]{0:T(1024)S(1)}, s32[8]{0:T(128)S(1)}, s32[3,8]{1,0:T(4,128)S(1)}) custom-call(bf16[8,256,512]{2,1,0:T(8,128)(2,1)} %refs_0_.4, bf16[8,3584]{1,0:T(8,128)(2,1)} %refs_1_.2, f32[3584]{0:T(1024)} %refs_2_.1, s32[8]{0:T(128)} %refs_3_.1, s32[3,8]{1,0:T(4,128)} %bitcast.18), custom_call_target="tpu_custom_call" | custom-call | bytes 2161728 | tf_op jit(solution)/shard_map/pallas_call | solution.py:47
  9.0 0.7 convert_bitcast_fusion.shares_ref
  9.7 4.6 %all-to-all-done.query_ref = bf16[16,8,256]{2,1,0:T(8,128)(2,1)S(1)} async-done(((bf16[16,8,256]{2,1,0:T(8,128)(2,1)}), bf16[16,8,256]{2,1,0:T(8,128)(2,1)S(1)}, u32[]{:S(2)}, u32[]{:S(2)}) %all-to-all-start) | async-done | bytes 65568 | tf_op jit(solution)/shard_map/all_to_all | solution.py:290
  14.3 2.2 %shard_map.110.refs_1_ = bf16[16,8,384]{2,1,0:T(8,128)(2,1)} custom-call(s32[8]{0:T(128)S(1)} %get-tuple-element.35.lengths_ref, s32[3,8]{1,0:T(4,128)S(1)} %get-tuple-element.36.routes_ref, f32[3,8]{1,0:T(4,128)S(1)} %convert_bitcast_fusion.shares_ref, bf16[16,8,256]{2,1,0:T(8,128)(2,1)S(1)} %all-to-all-done.query_ref, ...), custom_call_target="tpu_custom_call" | custom-call | tf_op jit(solution)/shard_map/pallas_call | solution.py:100
  16.5 3.5 %all-to-all-start.1 = ((bf16[16,8,384]{2,1,0:T(8,128)(2,1)}), bf16[16,8,384]{2,1,0:T(8,128)(2,1)S(1)}, u32[]{:S(2)}, u32[]{:S(2)}) async-start(bf16[16,8,384]{2,1,0:T(8,128)(2,1)} %shard_map.110.refs_1_), calls=%async_computation.1 | async-start | bytes 196608 | tf_op jit(solution)/shard_map/all_to_all | solution.py:295
  20.0 0.1 pad_add_fusion
  20.1 1.5 %shard_map.111.weight_ref = bf16[256,3584]{1,0:T(8,128)(2,1)S(1)} custom-call(bf16[256,3584]{1,0:T(8,128)(2,1)} %refs_0_.5, bf16[16,8,384]{2,1,0:T(8,128)(2,1)} %shard_map.110.refs_1_), custom_call_target="tpu_custom_call" | custom-call | bytes 1835008 | tf_op jit(solution)/shard_map/pallas_call | solution.py:47
  21.6 5.8 %all-to-all-done.1 = bf16[16,8,384]{2,1,0:T(8,128)(2,1)S(1)} async-done(((bf16[16,8,384]{2,1,0:T(8,128)(2,1)}), bf16[16,8,384]{2,1,0:T(8,128)(2,1)S(1)}, u32[]{:S(2)}, u32[]{:S(2)}) %all-to-all-start.1) | async-done | bytes 98336 | tf_op jit(solution)/shard_map/all_to_all | solution.py:295
  27.3 1.0 %shard_map.113 = (bf16[64,3584]{1,0:T(8,128)(2,1)S(1)}, bf16[64,128]{1,0:T(8,128)(2,1)S(1)}) custom-call(s32[2]{0:T(128)S(1)} %get-tuple-element.60.place_ref, bf16[8,2,8,384]{3,2,1,0:T(8,128)(2,1)S(1)} %bitcast.10, bf16[256,3584]{1,0:T(8,128)(2,1)S(1)} %shard_map.111.weight_ref), custom_call_target="tpu_custom_call" | custom-call | flops 117440512 | bytes 1835008 | tf_op jit(solution)/shard_map/pallas_call | solution.py:133
  28.3 0.1 collective-permute-start
  28.4 1.0 %shard_map.112 = (f32[64,3584]{1,0:T(8,128)S(1)}, bf16[64,128]{1,0:T(8,128)(2,1)S(1)}) custom-call(s32[2]{0:T(128)S(1)} %get-tuple-element.59.place_ref, bf16[8,2,8,384]{3,2,1,0:T(8,128)(2,1)S(1)} %bitcast.11, bf16[256,3584]{1,0:T(8,128)(2,1)S(1)} %shard_map.111.weight_ref), custom_call_target="tpu_custom_call" | custom-call | flops 117440512 | bytes 1835008 | tf_op jit(solution)/shard_map/pallas_call | solution.py:133
  29.4 0.8 collective-permute-done
  30.3 0.1 collective-permute-start.1
  30.4 1.2 %collective-permute-start.3 = (bf16[16,3584]{1,0:T(8,128)(2,1)S(1)}, bf16[16,3584]{1,0:T(8,128)(2,1)S(1)}, u32[]{:S(2)}, u32[]{:S(2)}) collective-permute-start(bf16[16,3584]{1,0:T(8,128)(2,1)S(1)} %get-tuple-element.57), channel_id=1, source_target_pairs={{0,4},{1,5},{2,6},{3,7},{4,0},{5,1},{6,2},{7,3},{8,12},{9,13},{10,... | collective-permute-start | bytes 344072 | tf_op jit(solution)/shard_map/ppermute | solution.py:269
  31.6 2.3 %collective-permute-start.2 = (bf16[16,3584]{1,0:T(8,128)(2,1)S(1)}, bf16[16,3584]{1,0:T(8,128)(2,1)S(1)}, u32[]{:S(2)}, u32[]{:S(2)}) collective-permute-start(bf16[16,3584]{1,0:T(8,128)(2,1)S(1)} %get-tuple-element.58), channel_id=1, source_target_pairs={{0,2},{1,3},{2,0},{3,1},{4,6},{5,7},{6,4},{7,5},{8,10},{9,11},{10,... | collective-permute-start | bytes 344072 | tf_op jit(solution)/shard_map/ppermute | solution.py:269
  33.8 3.4 %collective-permute-done.1 = bf16[16,3584]{1,0:T(8,128)(2,1)S(1)} collective-permute-done((bf16[16,3584]{1,0:T(8,128)(2,1)S(1)}, bf16[16,3584]{1,0:T(8,128)(2,1)S(1)}, u32[]{:S(2)}, u32[]{:S(2)}) %collective-permute-start.1) | collective-permute-done | bytes 114720 | tf_op jit(solution)/shard_map/ppermute | solution.py:269
  37.2 0.2 collective-permute-done.3
  37.4 1.5 %collective-permute-done.2 = bf16[16,3584]{1,0:T(8,128)(2,1)S(1)} collective-permute-done((bf16[16,3584]{1,0:T(8,128)(2,1)S(1)}, bf16[16,3584]{1,0:T(8,128)(2,1)S(1)}, u32[]{:S(2)}, u32[]{:S(2)}) %collective-permute-start.2) | collective-permute-done | bytes 114720 | tf_op jit(solution)/shard_map/ppermute | solution.py:269
  39.0 0.2 collective-permute-start.4
  39.2 5.7 %shard_map.114 = (bf16[1536,3584]{1,0:T(8,128)(2,1)S(1)}, bf16[768,3584]{1,0:T(8,128)(2,1)S(1)}, f32[3584]{0:T(1024)S(1)}) custom-call(bf16[1536,3584]{1,0:T(8,128)(2,1)} %refs_0_.6, bf16[1536,3584]{1,0:T(8,128)(2,1)} %refs_0_.7, f32[3584]{0:T(1024)S(1)} %get-tuple-element.41.refs_2_, bf16[16,3584]{1,0:T(8,128)(2,1)S(1)} %convert_element_type.85.refs_3_.kept_ref), custom_call_target="tpu_custom_call" | custom-call | bytes 22020096 | tf_op jit(solution)/shard_map/pallas_call | solution.py:47
  44.9 2.0 %collective-permute-done.4 = bf16[16,3584]{1,0:T(8,128)(2,1)S(1)} collective-permute-done((bf16[16,3584]{1,0:T(8,128)(2,1)S(1)}, bf16[16,3584]{1,0:T(8,128)(2,1)S(1)}, u32[]{:S(2)}, u32[]{:S(2)}) %collective-permute-start.4) | collective-permute-done | bytes 114720 | tf_op jit(solution)/shard_map/ppermute | solution.py:269
  46.9 0.1 shard_map.115
  47.1 0.1 collective-permute-start.7
  47.1 0.5 collective-permute-start.6
  47.6 3.0 %collective-permute-start.5 = (bf16[16,3584]{1,0:T(8,128)(2,1)S(1)}, bf16[16,3584]{1,0:T(8,128)(2,1)S(1)}, u32[]{:S(2)}, u32[]{:S(2)}) collective-permute-start(bf16[16,3584]{1,0:T(8,128)(2,1)S(1)} %bitcast.14), channel_id=1, source_target_pairs={{0,4},{1,5},{2,6},{3,7},{4,0},{5,1},{6,2},{7,3},{8,12},{9,13},{10,... | collective-permute-start | bytes 344072 | tf_op jit(solution)/shard_map/ppermute | solution.py:269
  50.6 2.6 %shard_map.116 = (bf16[768,3584]{1,0:T(8,128)(2,1)S(1)}, bf16[16,3584]{1,0:T(8,128)(2,1)S(1)}) custom-call(bf16[1536,3584]{1,0:T(8,128)(2,1)} %refs_0_.7, bf16[16,3584]{1,0:T(8,128)(2,1)S(1)} %bitcast.15), custom_call_target="tpu_custom_call" | custom-call | bytes 11010048 | tf_op jit(solution)/shard_map/pallas_call | solution.py:47
  53.2 0.1 collective-permute-start.8
  53.3 0.8 collective-permute-done.7.refs_3_
  54.1 0.7 collective-permute-done.6.refs_2_
  54.7 0.5 collective-permute-start.9
  55.3 0.1 collective-permute-done.11.refs_7_
  55.4 0.7 collective-permute-done.10.refs_6_
  56.1 0.2 collective-permute-done.9.refs_5_
  56.2 10.6 %shard_map.117 = (f32[64,3584]{1,0:T(8,128)S(1)}, bf16[64,3584]{1,0:T(8,128)(2,1)S(1)}) custom-call(bf16[64,128]{1,0:T(8,128)(2,1)S(1)} %get-tuple-element.44.own_gates_ref, bf16[64,128]{1,0:T(8,128)(2,1)S(1)} %get-tuple-element.45.other_gates_ref, bf16[768,3584]{1,0:T(8,128)(2,1)S(1)} %get-tuple-element.46.first_ref, ...), custom_call_target="tpu_custom_call" | custom-call | flops 4227858432 | bytes 33030144 | tf_op jit(solution)/shard_map/pallas_call | solution.py:216
  66.9 0.4 collective-permute-start.12
  67.3 1.5 %collective-permute-done.12 = bf16[64,3584]{1,0:T(8,128)(2,1)S(1)} collective-permute-done((bf16[64,3584]{1,0:T(8,128)(2,1)S(1)}, bf16[64,3584]{1,0:T(8,128)(2,1)S(1)}, u32[]{:S(2)}, u32[]{:S(2)}) %collective-permute-start.12) | collective-permute-done | bytes 458784 | tf_op jit(solution)/shard_map/ppermute | solution.py:269
  68.8 0.1 add_convert_fusion.2
  68.8 1.2 %collective-permute-start.13 = (bf16[16,3584]{1,0:T(8,128)(2,1)S(1)}, bf16[16,3584]{1,0:T(8,128)(2,1)S(1)}, u32[]{:S(2)}, u32[]{:S(2)}) collective-permute-start(bf16[16,3584]{1,0:T(8,128)(2,1)S(1)} %get-tuple-element.53), channel_id=1, source_target_pairs={{0,6},{1,7},{2,4},{3,5},{4,2},{5,3},{6,0},{7,1},{8,14},{9,15},{10,... | collective-permute-start | bytes 344072 | tf_op jit(solution)/shard_map/ppermute | solution.py:269
  70.0 1.6 %collective-permute-start.15 = (bf16[16,3584]{1,0:T(8,128)(2,1)S(1)}, bf16[16,3584]{1,0:T(8,128)(2,1)S(1)}, u32[]{:S(2)}, u32[]{:S(2)}) collective-permute-start(bf16[16,3584]{1,0:T(8,128)(2,1)S(1)} %get-tuple-element.54), channel_id=1, source_target_pairs={{0,4},{1,5},{2,6},{3,7},{4,0},{5,1},{6,2},{7,3},{8,12},{9,13},{10,... | collective-permute-start | bytes 344072 | tf_op jit(solution)/shard_map/ppermute | solution.py:269
  71.6 0.8 collective-permute-start.14
  72.4 3.4 %collective-permute-done.13 = bf16[16,3584]{1,0:T(8,128)(2,1)S(1)} collective-permute-done((bf16[16,3584]{1,0:T(8,128)(2,1)S(1)}, bf16[16,3584]{1,0:T(8,128)(2,1)S(1)}, u32[]{:S(2)}, u32[]{:S(2)}) %collective-permute-start.13) | collective-permute-done | bytes 114720 | tf_op jit(solution)/shard_map/ppermute | solution.py:269
  75.8 1.5 %collective-permute-done.15 = bf16[16,3584]{1,0:T(8,128)(2,1)S(1)} collective-permute-done((bf16[16,3584]{1,0:T(8,128)(2,1)S(1)}, bf16[16,3584]{1,0:T(8,128)(2,1)S(1)}, u32[]{:S(2)}, u32[]{:S(2)}) %collective-permute-start.15) | collective-permute-done | bytes 114720 | tf_op jit(solution)/shard_map/ppermute | solution.py:269
  77.3 0.4 collective-permute-done.14
  77.7 0.1 convert_add_fusion
  77.8 0.6 collective-permute-start.16
  78.4 4.9 %collective-permute-done.16 = bf16[8,3584]{1,0:T(8,128)(2,1)S(1)} collective-permute-done((bf16[8,3584]{1,0:T(8,128)(2,1)S(1)}, bf16[8,3584]{1,0:T(8,128)(2,1)S(1)}, u32[]{:S(2)}, u32[]{:S(2)}) %collective-permute-start.16) | collective-permute-done | bytes 57376 | tf_op jit(solution)/shard_map/ppermute | solution.py:269
  83.3 0.6 fusion.1
  (9 shorter events, 0.2 us)
Async XLA Ops:
  0.0 14.3 %all-to-all-start = ((bf16[16,8,256]{2,1,0:T(8,128)(2,1)}), bf16[16,8,256]{2,1,0:T(8,128)(2,1)S(1)}, u32[]{:S(2)}, u32[]{:S(2)}) async-start(bf16[16,8,256]{2,1,0:T(8,128)(2,1)} %bitcast.17), calls=%async_computation | async-start | bytes 131072 | tf_op jit(solution)/shard_map/all_to_all | solution.py:290
  16.5 10.9 %all-to-all-start.1 = ((bf16[16,8,384]{2,1,0:T(8,128)(2,1)}), bf16[16,8,384]{2,1,0:T(8,128)(2,1)S(1)}, u32[]{:S(2)}, u32[]{:S(2)}) async-start(bf16[16,8,384]{2,1,0:T(8,128)(2,1)} %shard_map.110.refs_1_), calls=%async_computation.1 | async-start | bytes 196608 | tf_op jit(solution)/shard_map/all_to_all | solution.py:295
  28.3 1.9 %collective-permute-start = (bf16[64,3584]{1,0:T(8,128)(2,1)S(1)}, bf16[64,3584]{1,0:T(8,128)(2,1)S(1)}, u32[]{:S(2)}, u32[]{:S(2)}) collective-permute-start(bf16[64,3584]{1,0:T(8,128)(2,1)S(1)} %get-tuple-element.39), channel_id=1, source_target_pairs={{0,1},{1,0},{2,3},{3,2},{4,5},{5,4},{6,7},{7,6},{8,9},{9,8},{10,11... | collective-permute-start | bytes 1376264 | tf_op jit(solution)/shard_map/ppermute | solution.py:269
  30.3 7.0 %collective-permute-start.1 = (bf16[16,3584]{1,0:T(8,128)(2,1)S(1)}, bf16[16,3584]{1,0:T(8,128)(2,1)S(1)}, u32[]{:S(2)}, u32[]{:S(2)}) collective-permute-start(bf16[16,3584]{1,0:T(8,128)(2,1)S(1)} %get-tuple-element.56), channel_id=1, source_target_pairs={{0,6},{1,7},{2,4},{3,5},{4,2},{5,3},{6,0},{7,1},{8,14},{9,15},{10,... | collective-permute-start | bytes 344072 | tf_op jit(solution)/shard_map/ppermute | solution.py:269
  30.4 7.0 %collective-permute-start.3 = (bf16[16,3584]{1,0:T(8,128)(2,1)S(1)}, bf16[16,3584]{1,0:T(8,128)(2,1)S(1)}, u32[]{:S(2)}, u32[]{:S(2)}) collective-permute-start(bf16[16,3584]{1,0:T(8,128)(2,1)S(1)} %get-tuple-element.57), channel_id=1, source_target_pairs={{0,4},{1,5},{2,6},{3,7},{4,0},{5,1},{6,2},{7,3},{8,12},{9,13},{10,... | collective-permute-start | bytes 344072 | tf_op jit(solution)/shard_map/ppermute | solution.py:269
  31.6 7.3 %collective-permute-start.2 = (bf16[16,3584]{1,0:T(8,128)(2,1)S(1)}, bf16[16,3584]{1,0:T(8,128)(2,1)S(1)}, u32[]{:S(2)}, u32[]{:S(2)}) collective-permute-start(bf16[16,3584]{1,0:T(8,128)(2,1)S(1)} %get-tuple-element.58), channel_id=1, source_target_pairs={{0,2},{1,3},{2,0},{3,1},{4,6},{5,7},{6,4},{7,5},{8,10},{9,11},{10,... | collective-permute-start | bytes 344072 | tf_op jit(solution)/shard_map/ppermute | solution.py:269
  39.0 7.9 %collective-permute-start.4 = (bf16[16,3584]{1,0:T(8,128)(2,1)S(1)}, bf16[16,3584]{1,0:T(8,128)(2,1)S(1)}, u32[]{:S(2)}, u32[]{:S(2)}) collective-permute-start(bf16[16,3584]{1,0:T(8,128)(2,1)S(1)} %convert_element_type.85.refs_3_.kept_ref), channel_id=1, source_target_pairs={{0,8},{1,9},{2,10},{3,11},{4,12},{5,13},{6,14},{7,15},{8,0},{9,1},... | collective-permute-start | bytes 344072 | tf_op jit(solution)/shard_map/ppermute | solution.py:269
  47.1 7.0 %collective-permute-start.7 = (bf16[16,3584]{1,0:T(8,128)(2,1)S(1)}, bf16[16,3584]{1,0:T(8,128)(2,1)S(1)}, u32[]{:S(2)}, u32[]{:S(2)}) collective-permute-start(bf16[16,3584]{1,0:T(8,128)(2,1)S(1)} %bitcast.12), channel_id=1, source_target_pairs={{0,6},{1,7},{2,4},{3,5},{4,2},{5,3},{6,0},{7,1},{8,14},{9,15},{10,... | collective-permute-start | bytes 344072 | tf_op jit(solution)/shard_map/ppermute | solution.py:269
  47.1 7.6 %collective-permute-start.6 = (bf16[16,3584]{1,0:T(8,128)(2,1)S(1)}, bf16[16,3584]{1,0:T(8,128)(2,1)S(1)}, u32[]{:S(2)}, u32[]{:S(2)}) collective-permute-start(bf16[16,3584]{1,0:T(8,128)(2,1)S(1)} %bitcast.13), channel_id=1, source_target_pairs={{0,2},{1,3},{2,0},{3,1},{4,6},{5,7},{6,4},{7,5},{8,10},{9,11},{10,... | collective-permute-start | bytes 344072 | tf_op jit(solution)/shard_map/ppermute | solution.py:269
  47.6 7.1 %collective-permute-start.5 = (bf16[16,3584]{1,0:T(8,128)(2,1)S(1)}, bf16[16,3584]{1,0:T(8,128)(2,1)S(1)}, u32[]{:S(2)}, u32[]{:S(2)}) collective-permute-start(bf16[16,3584]{1,0:T(8,128)(2,1)S(1)} %bitcast.14), channel_id=1, source_target_pairs={{0,4},{1,5},{2,6},{3,7},{4,0},{5,1},{6,2},{7,3},{8,12},{9,13},{10,... | collective-permute-start | bytes 344072 | tf_op jit(solution)/shard_map/ppermute | solution.py:269
  53.2 2.1 %collective-permute-start.8 = (bf16[16,3584]{1,0:T(8,128)(2,1)S(1)}, bf16[16,3584]{1,0:T(8,128)(2,1)S(1)}, u32[]{:S(2)}, u32[]{:S(2)}) collective-permute-start(bf16[16,3584]{1,0:T(8,128)(2,1)S(1)} %get-tuple-element.50.refs_0_), channel_id=1, source_target_pairs={{0,1},{1,0},{2,3},{3,2},{4,5},{5,4},{6,7},{7,6},{8,9},{9,8},{10,11... | collective-permute-start | bytes 344072 | tf_op jit(solution)/shard_map/ppermute | solution.py:269
  54.1 1.3 %collective-permute-start.11 = (bf16[16,3584]{1,0:T(8,128)(2,1)S(1)}, bf16[16,3584]{1,0:T(8,128)(2,1)S(1)}, u32[]{:S(2)}, u32[]{:S(2)}) collective-permute-start(bf16[16,3584]{1,0:T(8,128)(2,1)S(1)} %collective-permute-done.7.refs_3_), channel_id=1, source_target_pairs={{0,1},{1,0},{2,3},{3,2},{4,5},{5,4},{6,7},{7,6},{8,9},{9,8},{10,11... | collective-permute-start | bytes 344072 | tf_op jit(solution)/shard_map/ppermute | solution.py:269
  54.7 1.3 %collective-permute-start.10 = (bf16[16,3584]{1,0:T(8,128)(2,1)S(1)}, bf16[16,3584]{1,0:T(8,128)(2,1)S(1)}, u32[]{:S(2)}, u32[]{:S(2)}) collective-permute-start(bf16[16,3584]{1,0:T(8,128)(2,1)S(1)} %collective-permute-done.6.refs_2_), channel_id=1, source_target_pairs={{0,1},{1,0},{2,3},{3,2},{4,5},{5,4},{6,7},{7,6},{8,9},{9,8},{10,11... | collective-permute-start | bytes 344072 | tf_op jit(solution)/shard_map/ppermute | solution.py:269
  54.7 1.5 %collective-permute-start.9 = (bf16[16,3584]{1,0:T(8,128)(2,1)S(1)}, bf16[16,3584]{1,0:T(8,128)(2,1)S(1)}, u32[]{:S(2)}, u32[]{:S(2)}) collective-permute-start(bf16[16,3584]{1,0:T(8,128)(2,1)S(1)} %collective-permute-done.5.refs_1_), channel_id=1, source_target_pairs={{0,1},{1,0},{2,3},{3,2},{4,5},{5,4},{6,7},{7,6},{8,9},{9,8},{10,11... | collective-permute-start | bytes 344072 | tf_op jit(solution)/shard_map/ppermute | solution.py:269
  66.9 1.9 %collective-permute-start.12 = (bf16[64,3584]{1,0:T(8,128)(2,1)S(1)}, bf16[64,3584]{1,0:T(8,128)(2,1)S(1)}, u32[]{:S(2)}, u32[]{:S(2)}) collective-permute-start(bf16[64,3584]{1,0:T(8,128)(2,1)S(1)} %get-tuple-element.52), channel_id=1, source_target_pairs={{0,1},{1,0},{2,3},{3,2},{4,5},{5,4},{6,7},{7,6},{8,9},{9,8},{10,11... | collective-permute-start | bytes 1376264 | tf_op jit(solution)/shard_map/ppermute | solution.py:269
  68.8 6.9 %collective-permute-start.13 = (bf16[16,3584]{1,0:T(8,128)(2,1)S(1)}, bf16[16,3584]{1,0:T(8,128)(2,1)S(1)}, u32[]{:S(2)}, u32[]{:S(2)}) collective-permute-start(bf16[16,3584]{1,0:T(8,128)(2,1)S(1)} %get-tuple-element.53), channel_id=1, source_target_pairs={{0,6},{1,7},{2,4},{3,5},{4,2},{5,3},{6,0},{7,1},{8,14},{9,15},{10,... | collective-permute-start | bytes 344072 | tf_op jit(solution)/shard_map/ppermute | solution.py:269
  70.0 7.3 %collective-permute-start.15 = (bf16[16,3584]{1,0:T(8,128)(2,1)S(1)}, bf16[16,3584]{1,0:T(8,128)(2,1)S(1)}, u32[]{:S(2)}, u32[]{:S(2)}) collective-permute-start(bf16[16,3584]{1,0:T(8,128)(2,1)S(1)} %get-tuple-element.54), channel_id=1, source_target_pairs={{0,4},{1,5},{2,6},{3,7},{4,0},{5,1},{6,2},{7,3},{8,12},{9,13},{10,... | collective-permute-start | bytes 344072 | tf_op jit(solution)/shard_map/ppermute | solution.py:269
  71.6 6.0 %collective-permute-start.14 = (bf16[16,3584]{1,0:T(8,128)(2,1)S(1)}, bf16[16,3584]{1,0:T(8,128)(2,1)S(1)}, u32[]{:S(2)}, u32[]{:S(2)}) collective-permute-start(bf16[16,3584]{1,0:T(8,128)(2,1)S(1)} %get-tuple-element.55), channel_id=1, source_target_pairs={{0,2},{1,3},{2,0},{3,1},{4,6},{5,7},{6,4},{7,5},{8,10},{9,11},{10,... | collective-permute-start | bytes 344072 | tf_op jit(solution)/shard_map/ppermute | solution.py:269
  77.8 5.5 %collective-permute-start.16 = (bf16[8,3584]{1,0:T(8,128)(2,1)S(1)}, bf16[8,3584]{1,0:T(8,128)(2,1)S(1)}, u32[]{:S(2)}, u32[]{:S(2)}) collective-permute-start(bf16[8,3584]{1,0:T(8,128)(2,1)S(1)} %slice.129), channel_id=1, source_target_pairs={{0,8},{1,9},{2,10},{3,11},{4,12},{5,13},{6,14},{7,15},{8,0},{9,1},... | collective-permute-start | bytes 172040 | tf_op jit(solution)/shard_map/ppermute | solution.py:269

commit v8 on v7

--- a/solution.py
+++ b/solution.py
@@ -178,16 +178,17 @@
     pieces, (kept_ref, sent_ref, turned, hidden, down_ref, sems) = refs[:-6], refs[-6:]
     half = turned.shape[1] // 2
     units, feature = up_ref.shape
-    wide = tile_of(feature, 896)
-
-    def down_copy(at):
-        columns = pl.ds(at, wide)
-        return pltpu.make_async_copy(
-            down_source.at[:, columns], down_ref.at[:, columns], sems.at[at // wide]
+    wide = tile_of(feature, 1792)
+
+    deep = tile_of(units, 384)
+    copies = [
+        pltpu.make_async_copy(
+            down_source.at[pl.ds(at, deep)], down_ref.at[pl.ds(at, deep)], sems.at[at // deep]
         )
-
-    for at in range(0, feature, wide):
-        down_copy(at).start()
+        for at in range(0, units, deep)
+    ]
+    for copy in copies:
+        copy.start()
     turned[...] = jnp.concatenate([piece[...] for piece in pieces], axis=0).T
     gates = jnp.concatenate([own_gates_ref[...], other_gates_ref[...]], axis=0)
     gates = gates.astype(F32).T[:1]
@@ -202,8 +203,9 @@
         up_pre = jnp.dot(up_ref[rows, :], turned[...], preferred_element_type=F32)
         product = gate_pre / (1.0 + jnp.exp(-gate_pre)) * up_pre * gates
         hidden[:, rows] = product.astype(BF16).T
+    for copy in copies:
+        copy.wait()
     for at in range(0, feature, wide):
-        down_copy(at).wait()
         columns = pl.ds(at, wide)
         part = jnp.dot(hidden[...], down_ref[:, columns], preferred_element_type=F32)
         kept_ref[:, columns] = part[:half]

time: 84.3 us -> 85.3 us (1.012)
  Pallas kernels: 26.4 us -> 27.3 us
    pallas_call x1, Pallas kernels: 10.6 us -> 11.6 us  [experts(): pl.pallas_call(expert_kernel, out_shape=(jax.ShapeDtypeStruct((half, feat...]
where the time goes in v8:
time: 85.3 us; the launch traced here: 84.9 us
  waiting for transfers between devices  32.2 us (38%)
  Pallas kernels  27.3 us (32%)
  starting transfers between devices  23.4 us (27%)
  other arithmetic  1.72 us (2%)
    ppermute x17, waiting for transfers between devices, swap(): return lax.ppermute(x, 'ep', [(i, i ^ bit) for i in range(size)])  21.9 us
    ppermute x17, starting transfers between devices, swap(): return lax.ppermute(x, 'ep', [(i, i ^ bit) for i in range(size)])  12.5 us
    pallas_call x1, Pallas kernels, experts(): pl.pallas_call(expert_kernel, out_shape=(jax.ShapeDtypeStruct((half, feat...  11.6 us
    pallas_call x4, Pallas kernels, fetch(): pl.pallas_call(functools.partial(fetch_kernel, count, carried, ranges), o...  11.4 us
    all_to_all x1, starting transfers between devices, local(): lax.all_to_all(queries.reshape(size, tok, head_dim), 'ep', split_axis=0,...  7.38 us
    all_to_all x1, waiting for transfers between devices, local(): lax.all_to_all(attended, 'ep', split_axis=0, concat_axis=0, tiled=True)  5.76 us
    all_to_all x1, waiting for transfers between devices, local(): lax.all_to_all(queries.reshape(size, tok, head_dim), 'ep', split_axis=0,...  4.56 us
    all_to_all x1, starting transfers between devices, local(): lax.all_to_all(attended, 'ep', split_axis=0, concat_axis=0, tiled=True)  3.51 us
  transfers between devices with their start and end apart: 19, of which 17 were waited for; matrix products, arithmetic and copies ran while one was open for 1% of the time, Pallas kernels for 15%

profile of v8, /device:TPU:0, one launch (start us, length us, event | category | flops | bytes accessed | tf_op | source)
XLA Modules:
  0.0 84.9 jit_solution(844098841022711342)
XLA Ops:
  0.0 7.4 %all-to-all-start = ((bf16[16,8,256]{2,1,0:T(8,128)(2,1)}), bf16[16,8,256]{2,1,0:T(8,128)(2,1)S(1)}, u32[]{:S(2)}, u32[]{:S(2)}) async-start(bf16[16,8,256]{2,1,0:T(8,128)(2,1)} %bitcast.17), calls=%async_computation | async-start | bytes 131072 | tf_op jit(solution)/shard_map/all_to_all | solution.py:292
  7.4 1.6 %shard_map.109 = (bf16[8,256,512]{2,1,0:T(8,128)(2,1)S(1)}, bf16[8,3584]{1,0:T(8,128)(2,1)S(1)}, f32[3584]{0:T(1024)S(1)}, s32[8]{0:T(128)S(1)}, s32[3,8]{1,0:T(4,128)S(1)}) custom-call(bf16[8,256,512]{2,1,0:T(8,128)(2,1)} %refs_0_.4, bf16[8,3584]{1,0:T(8,128)(2,1)} %refs_1_.2, f32[3584]{0:T(1024)} %refs_2_.1, s32[8]{0:T(128)} %refs_3_.1, s32[3,8]{1,0:T(4,128)} %bitcast.18), custom_call_target="tpu_custom_call" | custom-call | bytes 2161728 | tf_op jit(solution)/shard_map/pallas_call | solution.py:47
  9.0 0.7 convert_bitcast_fusion.shares_ref
  9.7 4.6 %all-to-all-done.query_ref = bf16[16,8,256]{2,1,0:T(8,128)(2,1)S(1)} async-done(((bf16[16,8,256]{2,1,0:T(8,128)(2,1)}), bf16[16,8,256]{2,1,0:T(8,128)(2,1)S(1)}, u32[]{:S(2)}, u32[]{:S(2)}) %all-to-all-start) | async-done | bytes 65568 | tf_op jit(solution)/shard_map/all_to_all | solution.py:292
  14.3 2.2 %shard_map.110.refs_1_ = bf16[16,8,384]{2,1,0:T(8,128)(2,1)} custom-call(s32[8]{0:T(128)S(1)} %get-tuple-element.35.lengths_ref, s32[3,8]{1,0:T(4,128)S(1)} %get-tuple-element.36.routes_ref, f32[3,8]{1,0:T(4,128)S(1)} %convert_bitcast_fusion.shares_ref, bf16[16,8,256]{2,1,0:T(8,128)(2,1)S(1)} %all-to-all-done.query_ref, ...), custom_call_target="tpu_custom_call" | custom-call | tf_op jit(solution)/shard_map/pallas_call | solution.py:100
  16.5 3.5 %all-to-all-start.1 = ((bf16[16,8,384]{2,1,0:T(8,128)(2,1)}), bf16[16,8,384]{2,1,0:T(8,128)(2,1)S(1)}, u32[]{:S(2)}, u32[]{:S(2)}) async-start(bf16[16,8,384]{2,1,0:T(8,128)(2,1)} %shard_map.110.refs_1_), calls=%async_computation.1 | async-start | bytes 196608 | tf_op jit(solution)/shard_map/all_to_all | solution.py:297
  20.0 0.1 pad_add_fusion
  20.1 1.5 %shard_map.111.weight_ref = bf16[256,3584]{1,0:T(8,128)(2,1)S(1)} custom-call(bf16[256,3584]{1,0:T(8,128)(2,1)} %refs_0_.5, bf16[16,8,384]{2,1,0:T(8,128)(2,1)} %shard_map.110.refs_1_), custom_call_target="tpu_custom_call" | custom-call | bytes 1835008 | tf_op jit(solution)/shard_map/pallas_call | solution.py:47
  21.6 5.8 %all-to-all-done.1 = bf16[16,8,384]{2,1,0:T(8,128)(2,1)S(1)} async-done(((bf16[16,8,384]{2,1,0:T(8,128)(2,1)}), bf16[16,8,384]{2,1,0:T(8,128)(2,1)S(1)}, u32[]{:S(2)}, u32[]{:S(2)}) %all-to-all-start.1) | async-done | bytes 98336 | tf_op jit(solution)/shard_map/all_to_all | solution.py:297
  27.3 1.0 %shard_map.113 = (bf16[64,3584]{1,0:T(8,128)(2,1)S(1)}, bf16[64,128]{1,0:T(8,128)(2,1)S(1)}) custom-call(s32[2]{0:T(128)S(1)} %get-tuple-element.60.place_ref, bf16[8,2,8,384]{3,2,1,0:T(8,128)(2,1)S(1)} %bitcast.10, bf16[256,3584]{1,0:T(8,128)(2,1)S(1)} %shard_map.111.weight_ref), custom_call_target="tpu_custom_call" | custom-call | flops 117440512 | bytes 1835008 | tf_op jit(solution)/shard_map/pallas_call | solution.py:133
  28.3 0.1 collective-permute-start
  28.4 1.0 %shard_map.112 = (f32[64,3584]{1,0:T(8,128)S(1)}, bf16[64,128]{1,0:T(8,128)(2,1)S(1)}) custom-call(s32[2]{0:T(128)S(1)} %get-tuple-element.59.place_ref, bf16[8,2,8,384]{3,2,1,0:T(8,128)(2,1)S(1)} %bitcast.11, bf16[256,3584]{1,0:T(8,128)(2,1)S(1)} %shard_map.111.weight_ref), custom_call_target="tpu_custom_call" | custom-call | flops 117440512 | bytes 1835008 | tf_op jit(solution)/shard_map/pallas_call | solution.py:133
  29.4 0.8 collective-permute-done
  30.3 0.1 collective-permute-start.1
  30.4 1.2 %collective-permute-start.3 = (bf16[16,3584]{1,0:T(8,128)(2,1)S(1)}, bf16[16,3584]{1,0:T(8,128)(2,1)S(1)}, u32[]{:S(2)}, u32[]{:S(2)}) collective-permute-start(bf16[16,3584]{1,0:T(8,128)(2,1)S(1)} %get-tuple-element.57), channel_id=1, source_target_pairs={{0,4},{1,5},{2,6},{3,7},{4,0},{5,1},{6,2},{7,3},{8,12},{9,13},{10,... | collective-permute-start | bytes 344072 | tf_op jit(solution)/shard_map/ppermute | solution.py:271
  31.6 2.3 %collective-permute-start.2 = (bf16[16,3584]{1,0:T(8,128)(2,1)S(1)}, bf16[16,3584]{1,0:T(8,128)(2,1)S(1)}, u32[]{:S(2)}, u32[]{:S(2)}) collective-permute-start(bf16[16,3584]{1,0:T(8,128)(2,1)S(1)} %get-tuple-element.58), channel_id=1, source_target_pairs={{0,2},{1,3},{2,0},{3,1},{4,6},{5,7},{6,4},{7,5},{8,10},{9,11},{10,... | collective-permute-start | bytes 344072 | tf_op jit(solution)/shard_map/ppermute | solution.py:271
  33.8 3.4 %collective-permute-done.1 = bf16[16,3584]{1,0:T(8,128)(2,1)S(1)} collective-permute-done((bf16[16,3584]{1,0:T(8,128)(2,1)S(1)}, bf16[16,3584]{1,0:T(8,128)(2,1)S(1)}, u32[]{:S(2)}, u32[]{:S(2)}) %collective-permute-start.1) | collective-permute-done | bytes 114720 | tf_op jit(solution)/shard_map/ppermute | solution.py:271
  37.2 0.2 collective-permute-done.3
  37.4 1.5 %collective-permute-done.2 = bf16[16,3584]{1,0:T(8,128)(2,1)S(1)} collective-permute-done((bf16[16,3584]{1,0:T(8,128)(2,1)S(1)}, bf16[16,3584]{1,0:T(8,128)(2,1)S(1)}, u32[]{:S(2)}, u32[]{:S(2)}) %collective-permute-start.2) | collective-permute-done | bytes 114720 | tf_op jit(solution)/shard_map/ppermute | solution.py:271
  39.0 0.2 collective-permute-start.4
  39.2 5.7 %shard_map.114 = (bf16[1536,3584]{1,0:T(8,128)(2,1)S(1)}, bf16[768,3584]{1,0:T(8,128)(2,1)S(1)}, f32[3584]{0:T(1024)S(1)}) custom-call(bf16[1536,3584]{1,0:T(8,128)(2,1)} %refs_0_.6, bf16[1536,3584]{1,0:T(8,128)(2,1)} %refs_0_.7, f32[3584]{0:T(1024)S(1)} %get-tuple-element.41.refs_2_, bf16[16,3584]{1,0:T(8,128)(2,1)S(1)} %convert_element_type.85.refs_3_.kept_ref), custom_call_target="tpu_custom_call" | custom-call | bytes 22020096 | tf_op jit(solution)/shard_map/pallas_call | solution.py:47
  44.9 2.0 %collective-permute-done.4 = bf16[16,3584]{1,0:T(8,128)(2,1)S(1)} collective-permute-done((bf16[16,3584]{1,0:T(8,128)(2,1)S(1)}, bf16[16,3584]{1,0:T(8,128)(2,1)S(1)}, u32[]{:S(2)}, u32[]{:S(2)}) %collective-permute-start.4) | collective-permute-done | bytes 114720 | tf_op jit(solution)/shard_map/ppermute | solution.py:271
  46.9 0.1 shard_map.115
  47.1 0.1 collective-permute-start.7
  47.1 0.5 collective-permute-start.6
  47.6 3.0 %collective-permute-start.5 = (bf16[16,3584]{1,0:T(8,128)(2,1)S(1)}, bf16[16,3584]{1,0:T(8,128)(2,1)S(1)}, u32[]{:S(2)}, u32[]{:S(2)}) collective-permute-start(bf16[16,3584]{1,0:T(8,128)(2,1)S(1)} %bitcast.14), channel_id=1, source_target_pairs={{0,4},{1,5},{2,6},{3,7},{4,0},{5,1},{6,2},{7,3},{8,12},{9,13},{10,... | collective-permute-start | bytes 344072 | tf_op jit(solution)/shard_map/ppermute | solution.py:271
  50.6 2.6 %shard_map.116 = (bf16[768,3584]{1,0:T(8,128)(2,1)S(1)}, bf16[16,3584]{1,0:T(8,128)(2,1)S(1)}) custom-call(bf16[1536,3584]{1,0:T(8,128)(2,1)} %refs_0_.7, bf16[16,3584]{1,0:T(8,128)(2,1)S(1)} %bitcast.15), custom_call_target="tpu_custom_call" | custom-call | bytes 11010048 | tf_op jit(solution)/shard_map/pallas_call | solution.py:47
  53.2 0.1 collective-permute-start.8
  53.3 0.8 collective-permute-done.7.refs_3_
  54.1 0.7 collective-permute-done.6.refs_2_
  54.7 0.5 collective-permute-start.9
  55.3 0.1 collective-permute-done.11.refs_7_
  55.4 0.7 collective-permute-done.10.refs_6_
  56.1 0.2 collective-permute-done.9.refs_5_
  56.2 11.6 %shard_map.117 = (f32[64,3584]{1,0:T(8,128)S(1)}, bf16[64,3584]{1,0:T(8,128)(2,1)S(1)}) custom-call(bf16[64,128]{1,0:T(8,128)(2,1)S(1)} %get-tuple-element.44.own_gates_ref, bf16[64,128]{1,0:T(8,128)(2,1)S(1)} %get-tuple-element.45.other_gates_ref, bf16[768,3584]{1,0:T(8,128)(2,1)S(1)} %get-tuple-element.46.first_ref, ...), custom_call_target="tpu_custom_call" | custom-call | flops 4227858432 | bytes 33030144 | tf_op jit(solution)/shard_map/pallas_call | solution.py:218
  67.9 0.4 collective-permute-start.12
  68.3 1.5 %collective-permute-done.12 = bf16[64,3584]{1,0:T(8,128)(2,1)S(1)} collective-permute-done((bf16[64,3584]{1,0:T(8,128)(2,1)S(1)}, bf16[64,3584]{1,0:T(8,128)(2,1)S(1)}, u32[]{:S(2)}, u32[]{:S(2)}) %collective-permute-start.12) | collective-permute-done | bytes 458784 | tf_op jit(solution)/shard_map/ppermute | solution.py:271
  69.7 0.1 add_convert_fusion.2
  69.8 1.2 %collective-permute-start.13 = (bf16[16,3584]{1,0:T(8,128)(2,1)S(1)}, bf16[16,3584]{1,0:T(8,128)(2,1)S(1)}, u32[]{:S(2)}, u32[]{:S(2)}) collective-permute-start(bf16[16,3584]{1,0:T(8,128)(2,1)S(1)} %get-tuple-element.53), channel_id=1, source_target_pairs={{0,6},{1,7},{2,4},{3,5},{4,2},{5,3},{6,0},{7,1},{8,14},{9,15},{10,... | collective-permute-start | bytes 344072 | tf_op jit(solution)/shard_map/ppermute | solution.py:271
  71.0 1.6 %collective-permute-start.15 = (bf16[16,3584]{1,0:T(8,128)(2,1)S(1)}, bf16[16,3584]{1,0:T(8,128)(2,1)S(1)}, u32[]{:S(2)}, u32[]{:S(2)}) collective-permute-start(bf16[16,3584]{1,0:T(8,128)(2,1)S(1)} %get-tuple-element.54), channel_id=1, source_target_pairs={{0,4},{1,5},{2,6},{3,7},{4,0},{5,1},{6,2},{7,3},{8,12},{9,13},{10,... | collective-permute-start | bytes 344072 | tf_op jit(solution)/shard_map/ppermute | solution.py:271
  72.6 0.8 collective-permute-start.14
  73.4 3.4 %collective-permute-done.13 = bf16[16,3584]{1,0:T(8,128)(2,1)S(1)} collective-permute-done((bf16[16,3584]{1,0:T(8,128)(2,1)S(1)}, bf16[16,3584]{1,0:T(8,128)(2,1)S(1)}, u32[]{:S(2)}, u32[]{:S(2)}) %collective-permute-start.13) | collective-permute-done | bytes 114720 | tf_op jit(solution)/shard_map/ppermute | solution.py:271
  76.8 1.5 %collective-permute-done.15 = bf16[16,3584]{1,0:T(8,128)(2,1)S(1)} collective-permute-done((bf16[16,3584]{1,0:T(8,128)(2,1)S(1)}, bf16[16,3584]{1,0:T(8,128)(2,1)S(1)}, u32[]{:S(2)}, u32[]{:S(2)}) %collective-permute-start.15) | collective-permute-done | bytes 114720 | tf_op jit(solution)/shard_map/ppermute | solution.py:271
  78.3 0.4 collective-permute-done.14
  78.6 0.1 convert_add_fusion
  78.7 0.6 collective-permute-start.16
  79.3 4.9 %collective-permute-done.16 = bf16[8,3584]{1,0:T(8,128)(2,1)S(1)} collective-permute-done((bf16[8,3584]{1,0:T(8,128)(2,1)S(1)}, bf16[8,3584]{1,0:T(8,128)(2,1)S(1)}, u32[]{:S(2)}, u32[]{:S(2)}) %collective-permute-start.16) | collective-permute-done | bytes 57376 | tf_op jit(solution)/shard_map/ppermute | solution.py:271
  84.3 0.6 fusion.1
  (9 shorter events, 0.2 us)
Async XLA Ops:
  0.0 14.3 %all-to-all-start = ((bf16[16,8,256]{2,1,0:T(8,128)(2,1)}), bf16[16,8,256]{2,1,0:T(8,128)(2,1)S(1)}, u32[]{:S(2)}, u32[]{:S(2)}) async-start(bf16[16,8,256]{2,1,0:T(8,128)(2,1)} %bitcast.17), calls=%async_computation | async-start | bytes 131072 | tf_op jit(solution)/shard_map/all_to_all | solution.py:292
  16.5 10.9 %all-to-all-start.1 = ((bf16[16,8,384]{2,1,0:T(8,128)(2,1)}), bf16[16,8,384]{2,1,0:T(8,128)(2,1)S(1)}, u32[]{:S(2)}, u32[]{:S(2)}) async-start(bf16[16,8,384]{2,1,0:T(8,128)(2,1)} %shard_map.110.refs_1_), calls=%async_computation.1 | async-start | bytes 196608 | tf_op jit(solution)/shard_map/all_to_all | solution.py:297
  28.3 1.9 %collective-permute-start = (bf16[64,3584]{1,0:T(8,128)(2,1)S(1)}, bf16[64,3584]{1,0:T(8,128)(2,1)S(1)}, u32[]{:S(2)}, u32[]{:S(2)}) collective-permute-start(bf16[64,3584]{1,0:T(8,128)(2,1)S(1)} %get-tuple-element.39), channel_id=1, source_target_pairs={{0,1},{1,0},{2,3},{3,2},{4,5},{5,4},{6,7},{7,6},{8,9},{9,8},{10,11... | collective-permute-start | bytes 1376264 | tf_op jit(solution)/shard_map/ppermute | solution.py:271
  30.3 7.0 %collective-permute-start.1 = (bf16[16,3584]{1,0:T(8,128)(2,1)S(1)}, bf16[16,3584]{1,0:T(8,128)(2,1)S(1)}, u32[]{:S(2)}, u32[]{:S(2)}) collective-permute-start(bf16[16,3584]{1,0:T(8,128)(2,1)S(1)} %get-tuple-element.56), channel_id=1, source_target_pairs={{0,6},{1,7},{2,4},{3,5},{4,2},{5,3},{6,0},{7,1},{8,14},{9,15},{10,... | collective-permute-start | bytes 344072 | tf_op jit(solution)/shard_map/ppermute | solution.py:271
  30.4 7.0 %collective-permute-start.3 = (bf16[16,3584]{1,0:T(8,128)(2,1)S(1)}, bf16[16,3584]{1,0:T(8,128)(2,1)S(1)}, u32[]{:S(2)}, u32[]{:S(2)}) collective-permute-start(bf16[16,3584]{1,0:T(8,128)(2,1)S(1)} %get-tuple-element.57), channel_id=1, source_target_pairs={{0,4},{1,5},{2,6},{3,7},{4,0},{5,1},{6,2},{7,3},{8,12},{9,13},{10,... | collective-permute-start | bytes 344072 | tf_op jit(solution)/shard_map/ppermute | solution.py:271
  31.6 7.3 %collective-permute-start.2 = (bf16[16,3584]{1,0:T(8,128)(2,1)S(1)}, bf16[16,3584]{1,0:T(8,128)(2,1)S(1)}, u32[]{:S(2)}, u32[]{:S(2)}) collective-permute-start(bf16[16,3584]{1,0:T(8,128)(2,1)S(1)} %get-tuple-element.58), channel_id=1, source_target_pairs={{0,2},{1,3},{2,0},{3,1},{4,6},{5,7},{6,4},{7,5},{8,10},{9,11},{10,... | collective-permute-start | bytes 344072 | tf_op jit(solution)/shard_map/ppermute | solution.py:271
  39.0 7.9 %collective-permute-start.4 = (bf16[16,3584]{1,0:T(8,128)(2,1)S(1)}, bf16[16,3584]{1,0:T(8,128)(2,1)S(1)}, u32[]{:S(2)}, u32[]{:S(2)}) collective-permute-start(bf16[16,3584]{1,0:T(8,128)(2,1)S(1)} %convert_element_type.85.refs_3_.kept_ref), channel_id=1, source_target_pairs={{0,8},{1,9},{2,10},{3,11},{4,12},{5,13},{6,14},{7,15},{8,0},{9,1},... | collective-permute-start | bytes 344072 | tf_op jit(solution)/shard_map/ppermute | solution.py:271
  47.1 7.0 %collective-permute-start.7 = (bf16[16,3584]{1,0:T(8,128)(2,1)S(1)}, bf16[16,3584]{1,0:T(8,128)(2,1)S(1)}, u32[]{:S(2)}, u32[]{:S(2)}) collective-permute-start(bf16[16,3584]{1,0:T(8,128)(2,1)S(1)} %bitcast.12), channel_id=1, source_target_pairs={{0,6},{1,7},{2,4},{3,5},{4,2},{5,3},{6,0},{7,1},{8,14},{9,15},{10,... | collective-permute-start | bytes 344072 | tf_op jit(solution)/shard_map/ppermute | solution.py:271
  47.1 7.6 %collective-permute-start.6 = (bf16[16,3584]{1,0:T(8,128)(2,1)S(1)}, bf16[16,3584]{1,0:T(8,128)(2,1)S(1)}, u32[]{:S(2)}, u32[]{:S(2)}) collective-permute-start(bf16[16,3584]{1,0:T(8,128)(2,1)S(1)} %bitcast.13), channel_id=1, source_target_pairs={{0,2},{1,3},{2,0},{3,1},{4,6},{5,7},{6,4},{7,5},{8,10},{9,11},{10,... | collective-permute-start | bytes 344072 | tf_op jit(solution)/shard_map/ppermute | solution.py:271
  47.6 7.1 %collective-permute-start.5 = (bf16[16,3584]{1,0:T(8,128)(2,1)S(1)}, bf16[16,3584]{1,0:T(8,128)(2,1)S(1)}, u32[]{:S(2)}, u32[]{:S(2)}) collective-permute-start(bf16[16,3584]{1,0:T(8,128)(2,1)S(1)} %bitcast.14), channel_id=1, source_target_pairs={{0,4},{1,5},{2,6},{3,7},{4,0},{5,1},{6,2},{7,3},{8,12},{9,13},{10,... | collective-permute-start | bytes 344072 | tf_op jit(solution)/shard_map/ppermute | solution.py:271
  53.2 2.1 %collective-permute-start.8 = (bf16[16,3584]{1,0:T(8,128)(2,1)S(1)}, bf16[16,3584]{1,0:T(8,128)(2,1)S(1)}, u32[]{:S(2)}, u32[]{:S(2)}) collective-permute-start(bf16[16,3584]{1,0:T(8,128)(2,1)S(1)} %get-tuple-element.50.refs_0_), channel_id=1, source_target_pairs={{0,1},{1,0},{2,3},{3,2},{4,5},{5,4},{6,7},{7,6},{8,9},{9,8},{10,11... | collective-permute-start | bytes 344072 | tf_op jit(solution)/shard_map/ppermute | solution.py:271
  54.1 1.3 %collective-permute-start.11 = (bf16[16,3584]{1,0:T(8,128)(2,1)S(1)}, bf16[16,3584]{1,0:T(8,128)(2,1)S(1)}, u32[]{:S(2)}, u32[]{:S(2)}) collective-permute-start(bf16[16,3584]{1,0:T(8,128)(2,1)S(1)} %collective-permute-done.7.refs_3_), channel_id=1, source_target_pairs={{0,1},{1,0},{2,3},{3,2},{4,5},{5,4},{6,7},{7,6},{8,9},{9,8},{10,11... | collective-permute-start | bytes 344072 | tf_op jit(solution)/shard_map/ppermute | solution.py:271
  54.7 1.3 %collective-permute-start.10 = (bf16[16,3584]{1,0:T(8,128)(2,1)S(1)}, bf16[16,3584]{1,0:T(8,128)(2,1)S(1)}, u32[]{:S(2)}, u32[]{:S(2)}) collective-permute-start(bf16[16,3584]{1,0:T(8,128)(2,1)S(1)} %collective-permute-done.6.refs_2_), channel_id=1, source_target_pairs={{0,1},{1,0},{2,3},{3,2},{4,5},{5,4},{6,7},{7,6},{8,9},{9,8},{10,11... | collective-permute-start | bytes 344072 | tf_op jit(solution)/shard_map/ppermute | solution.py:271
  54.7 1.5 %collective-permute-start.9 = (bf16[16,3584]{1,0:T(8,128)(2,1)S(1)}, bf16[16,3584]{1,0:T(8,128)(2,1)S(1)}, u32[]{:S(2)}, u32[]{:S(2)}) collective-permute-start(bf16[16,3584]{1,0:T(8,128)(2,1)S(1)} %collective-permute-done.5.refs_1_), channel_id=1, source_target_pairs={{0,1},{1,0},{2,3},{3,2},{4,5},{5,4},{6,7},{7,6},{8,9},{9,8},{10,11... | collective-permute-start | bytes 344072 | tf_op jit(solution)/shard_map/ppermute | solution.py:271
  67.9 1.9 %collective-permute-start.12 = (bf16[64,3584]{1,0:T(8,128)(2,1)S(1)}, bf16[64,3584]{1,0:T(8,128)(2,1)S(1)}, u32[]{:S(2)}, u32[]{:S(2)}) collective-permute-start(bf16[64,3584]{1,0:T(8,128)(2,1)S(1)} %get-tuple-element.52), channel_id=1, source_target_pairs={{0,1},{1,0},{2,3},{3,2},{4,5},{5,4},{6,7},{7,6},{8,9},{9,8},{10,11... | collective-permute-start | bytes 1376264 | tf_op jit(solution)/shard_map/ppermute | solution.py:271
  69.8 6.9 %collective-permute-start.13 = (bf16[16,3584]{1,0:T(8,128)(2,1)S(1)}, bf16[16,3584]{1,0:T(8,128)(2,1)S(1)}, u32[]{:S(2)}, u32[]{:S(2)}) collective-permute-start(bf16[16,3584]{1,0:T(8,128)(2,1)S(1)} %get-tuple-element.53), channel_id=1, source_target_pairs={{0,6},{1,7},{2,4},{3,5},{4,2},{5,3},{6,0},{7,1},{8,14},{9,15},{10,... | collective-permute-start | bytes 344072 | tf_op jit(solution)/shard_map/ppermute | solution.py:271
  71.0 7.3 %collective-permute-start.15 = (bf16[16,3584]{1,0:T(8,128)(2,1)S(1)}, bf16[16,3584]{1,0:T(8,128)(2,1)S(1)}, u32[]{:S(2)}, u32[]{:S(2)}) collective-permute-start(bf16[16,3584]{1,0:T(8,128)(2,1)S(1)} %get-tuple-element.54), channel_id=1, source_target_pairs={{0,4},{1,5},{2,6},{3,7},{4,0},{5,1},{6,2},{7,3},{8,12},{9,13},{10,... | collective-permute-start | bytes 344072 | tf_op jit(solution)/shard_map/ppermute | solution.py:271
  72.6 6.0 %collective-permute-start.14 = (bf16[16,3584]{1,0:T(8,128)(2,1)S(1)}, bf16[16,3584]{1,0:T(8,128)(2,1)S(1)}, u32[]{:S(2)}, u32[]{:S(2)}) collective-permute-start(bf16[16,3584]{1,0:T(8,128)(2,1)S(1)} %get-tuple-element.55), channel_id=1, source_target_pairs={{0,2},{1,3},{2,0},{3,1},{4,6},{5,7},{6,4},{7,5},{8,10},{9,11},{10,... | collective-permute-start | bytes 344072 | tf_op jit(solution)/shard_map/ppermute | solution.py:271
  78.7 5.5 %collective-permute-start.16 = (bf16[8,3584]{1,0:T(8,128)(2,1)S(1)}, bf16[8,3584]{1,0:T(8,128)(2,1)S(1)}, u32[]{:S(2)}, u32[]{:S(2)}) collective-permute-start(bf16[8,3584]{1,0:T(8,128)(2,1)S(1)} %slice.129), channel_id=1, source_target_pairs={{0,8},{1,9},{2,10},{3,11},{4,12},{5,13},{6,14},{7,15},{8,0},{9,1},... | collective-permute-start | bytes 172040 | tf_op jit(solution)/shard_map/ppermute | solution.py:271

commit v9 on v8

--- a/solution.py
+++ b/solution.py
@@ -174,18 +174,19 @@
     )(kept, arrived.reshape(2, tok, feature), gain)
 
 
-def expert_kernel(own_gates_ref, other_gates_ref, first_ref, second_ref, up_ref, down_source, *refs):
+def expert_kernel(own_gates_ref, other_gates_ref, first_ref, second_ref, up_ref, low_ref, middle_ref, down_source, *refs):
     pieces, (kept_ref, sent_ref, turned, hidden, down_ref, sems) = refs[:-6], refs[-6:]
     half = turned.shape[1] // 2
     units, feature = up_ref.shape
     wide = tile_of(feature, 1792)
 
-    deep = tile_of(units, 384)
+    first_unit = units - down_ref.shape[0]
+    deep = tile_of(down_ref.shape[0], 128)
     copies = [
         pltpu.make_async_copy(
-            down_source.at[pl.ds(at, deep)], down_ref.at[pl.ds(at, deep)], sems.at[at // deep]
+            down_source.at[pl.ds(first_unit + at, deep)], down_ref.at[pl.ds(at, deep)], sems.at[at // deep]
         )
-        for at in range(0, units, deep)
+        for at in range(0, down_ref.shape[0], deep)
     ]
     for copy in copies:
         copy.start()
@@ -207,40 +208,43 @@
         copy.wait()
     for at in range(0, feature, wide):
         columns = pl.ds(at, wide)
-        part = jnp.dot(hidden[...], down_ref[:, columns], preferred_element_type=F32)
-        kept_ref[:, columns] = part[:half]
-        sent_ref[:, columns] = part[half:].astype(BF16)
-
-
-def experts(pieces, own_gates, other_gates, first_gate, second_gate, up_weight, down_weight):
-    half = own_gates.shape[0]
-    units, feature = up_weight.shape
+        total, low = None, 0
+        for ref in (low_ref, middle_ref, down_ref):
+            units_here = pl.ds(low, ref.shape[0])
+            term = jnp.dot(hidden[:, units_here], ref[:, columns], preferred_element_type=F32)
+            total = term if total is None else total + term
+            low += ref.shape[0]
+        kept_ref[:, columns] = total[:half]
+        sent_ref[:, columns] = total[half:].astype(BF16)
+
+
+def experts(pieces, gates, held, down_weight):
+    half = gates[0].shape[0]
+    units, feature = down_weight.shape
+    rest = units - held[3].shape[0] - held[4].shape[0]
     return pl.pallas_call(
         expert_kernel,
         out_shape=(
             jax.ShapeDtypeStruct((half, feature), F32),
             jax.ShapeDtypeStruct((half, feature), BF16),
         ),
-        in_specs=[VMEM_SPEC] * 5 + [HBM_SPEC] + [VMEM_SPEC] * len(pieces),
+        in_specs=[VMEM_SPEC] * 7 + [HBM_SPEC] + [VMEM_SPEC] * len(pieces),
         out_specs=(VMEM_SPEC, VMEM_SPEC),
         scratch_shapes=[
             pltpu.VMEM((feature, 2 * half), BF16),
             pltpu.VMEM((2 * half, units), BF16),
-            pltpu.VMEM((units, feature), BF16),
+            pltpu.VMEM((rest, feature), BF16),
             pltpu.SemaphoreType.DMA((8,)),
         ],
-        compiler_params=pltpu.CompilerParams(vmem_limit_bytes=22 << 20),
+        compiler_params=pltpu.CompilerParams(vmem_limit_bytes=16 << 20),
         cost_estimate=pl.CostEstimate(
             flops=12 * half * feature * units,
             bytes_accessed=6 * units * feature,
             transcendentals=2 * half * units,
         ),
     )(
-        own_gates,
-        other_gates,
-        first_gate,
-        second_gate,
-        up_weight,
+        *gates,
+        *held,
         pltpu.with_memory_space_constraint(down_weight, pltpu.HBM),
         *pieces,
     )
@@ -304,8 +308,9 @@
     bit = chips
     units = gate_weight.shape[0]
     part = units // LANES // 2 * LANES
-    up_held, first_held, gain_held = fetch(
-        up_weight, (gate_weight, 0, part), after=(summed,), carry=gain_held
+    third = units // LANES // 3 * LANES
+    up_held, first_held, low_held, gain_held = fetch(
+        up_weight, (gate_weight, 0, part), (down_weight, 0, third), after=(summed,), carry=gain_held
     )
     middle, own = norm(summed, swap(summed, bit), gain_held)
     own = own.reshape(2 * tok, -1)
@@ -314,12 +319,13 @@
         own = jnp.concatenate([own, swap(own, bit)], axis=0)
         bit //= 2
     others = [swap(own, bits) for bits in (4, 2, 6)]
-    second_held, own = fetch((gate_weight, part, units - part), carry=own)
+    second_held, middle_held, own = fetch(
+        (gate_weight, part, units - part), (down_weight, third, third), carry=own
+    )
     pieces = [own] + others
     pieces = pieces + [swap(piece, 1) for piece in pieces]
-    kept, sent = experts(
-        pieces, own_gates, other_gates, first_held, second_held, up_held, down_weight
-    )
+    held = (first_held, second_held, up_held, low_held, middle_held)
+    kept, sent = experts(pieces, (own_gates, other_gates), held, down_weight)
     kept = sum_nearest(kept, swap(sent, 1))
     combined = kept[:tok] + swap(kept[tok:].astype(BF16), chips).astype(F32)
     return (middle + combined).astype(BF16)

time: 85.3 us -> 83.6 us (0.980)
  waiting for transfers between devices: 32.2 us -> 28.6 us
  starting transfers between devices: 23.4 us -> 25.2 us
    ppermute x17, waiting for transfers between devices: 21.9 us -> 18.3 us  [swap(): return lax.ppermute(x, 'ep', [(i, i ^ bit) for i in range(size)])]
    pallas_call x4, Pallas kernels: 11.4 us -> 13.6 us  [fetch(): pl.pallas_call(functools.partial(fetch_kernel, count, carried, ranges), o...]
    pallas_call x1, Pallas kernels: 11.6 us -> 9.59 us  [experts(): pl.pallas_call(expert_kernel, out_shape=(jax.ShapeDtypeStruct((half, feat...]
    ppermute x17, starting transfers between devices: 12.5 us -> 14.3 us  [swap(): return lax.ppermute(x, 'ep', [(i, i ^ bit) for i in range(size)])]
  transfers between devices with their start and end apart: 19 -> 19, of which waited for: 17 -> 16; matrix products, arithmetic and copies ran while one was open for 1% -> 1% of each run, Pallas kernels for 15% -> 18%
where the time goes in v9:
time: 83.6 us; the launch traced here: 83.2 us
  waiting for transfers between devices  28.6 us (34%)
  Pallas kernels  27.5 us (33%)
  starting transfers between devices  25.2 us (30%)
  other arithmetic  1.72 us (2%)
    ppermute x17, waiting for transfers between devices, swap(): return lax.ppermute(x, 'ep', [(i, i ^ bit) for i in range(size)])  18.3 us
    ppermute x17, starting transfers between devices, swap(): return lax.ppermute(x, 'ep', [(i, i ^ bit) for i in range(size)])  14.3 us
    pallas_call x4, Pallas kernels, fetch(): pl.pallas_call(functools.partial(fetch_kernel, count, carried, ranges), o...  13.6 us
    pallas_call x1, Pallas kernels, experts(): pl.pallas_call(expert_kernel, out_shape=(jax.ShapeDtypeStruct((half, feat...  9.59 us
    all_to_all x1, starting transfers between devices, local(): lax.all_to_all(queries.reshape(size, tok, head_dim), 'ep', split_axis=0,...  7.38 us
    all_to_all x1, waiting for transfers between devices, local(): lax.all_to_all(attended, 'ep', split_axis=0, concat_axis=0, tiled=True)  5.76 us
    all_to_all x1, waiting for transfers between devices, local(): lax.all_to_all(queries.reshape(size, tok, head_dim), 'ep', split_axis=0,...  4.56 us
    all_to_all x1, starting transfers between devices, local(): lax.all_to_all(attended, 'ep', split_axis=0, concat_axis=0, tiled=True)  3.51 us
  transfers between devices with their start and end apart: 19, of which 16 were waited for; matrix products, arithmetic and copies ran while one was open for 1% of the time, Pallas kernels for 18%

profile of v9, /device:TPU:0, one launch (start us, length us, event | category | flops | bytes accessed | tf_op | source)
XLA Modules:
  0.0 83.2 jit_solution(12670657455686229495)
XLA Ops:
  0.0 7.4 %all-to-all-start = ((bf16[16,8,256]{2,1,0:T(8,128)(2,1)}), bf16[16,8,256]{2,1,0:T(8,128)(2,1)S(1)}, u32[]{:S(2)}, u32[]{:S(2)}) async-start(bf16[16,8,256]{2,1,0:T(8,128)(2,1)} %bitcast.17), calls=%async_computation | async-start | bytes 131072 | tf_op jit(solution)/shard_map/all_to_all | solution.py:296
  7.4 1.6 %shard_map.109 = (bf16[8,256,512]{2,1,0:T(8,128)(2,1)S(1)}, bf16[8,3584]{1,0:T(8,128)(2,1)S(1)}, f32[3584]{0:T(1024)S(1)}, s32[8]{0:T(128)S(1)}, s32[3,8]{1,0:T(4,128)S(1)}) custom-call(bf16[8,256,512]{2,1,0:T(8,128)(2,1)} %refs_0_.4, bf16[8,3584]{1,0:T(8,128)(2,1)} %refs_1_.3, f32[3584]{0:T(1024)} %refs_2_.2, s32[8]{0:T(128)} %refs_3_.1, s32[3,8]{1,0:T(4,128)} %bitcast.18), custom_call_target="tpu_custom_call" | custom-call | bytes 2161728 | tf_op jit(solution)/shard_map/pallas_call | solution.py:47
  9.0 0.7 convert_bitcast_fusion.shares_ref
  9.7 4.6 %all-to-all-done.query_ref = bf16[16,8,256]{2,1,0:T(8,128)(2,1)S(1)} async-done(((bf16[16,8,256]{2,1,0:T(8,128)(2,1)}), bf16[16,8,256]{2,1,0:T(8,128)(2,1)S(1)}, u32[]{:S(2)}, u32[]{:S(2)}) %all-to-all-start) | async-done | bytes 65568 | tf_op jit(solution)/shard_map/all_to_all | solution.py:296
  14.3 2.2 %shard_map.110.refs_1_ = bf16[16,8,384]{2,1,0:T(8,128)(2,1)} custom-call(s32[8]{0:T(128)S(1)} %get-tuple-element.37.lengths_ref, s32[3,8]{1,0:T(4,128)S(1)} %get-tuple-element.38.routes_ref, f32[3,8]{1,0:T(4,128)S(1)} %convert_bitcast_fusion.shares_ref, bf16[16,8,256]{2,1,0:T(8,128)(2,1)S(1)} %all-to-all-done.query_ref, ...), custom_call_target="tpu_custom_call" | custom-call | tf_op jit(solution)/shard_map/pallas_call | solution.py:100
  16.5 3.5 %all-to-all-start.1 = ((bf16[16,8,384]{2,1,0:T(8,128)(2,1)}), bf16[16,8,384]{2,1,0:T(8,128)(2,1)S(1)}, u32[]{:S(2)}, u32[]{:S(2)}) async-start(bf16[16,8,384]{2,1,0:T(8,128)(2,1)} %shard_map.110.refs_1_), calls=%async_computation.1 | async-start | bytes 196608 | tf_op jit(solution)/shard_map/all_to_all | solution.py:301
  20.0 0.1 pad_add_fusion
  20.1 1.5 %shard_map.111.weight_ref = bf16[256,3584]{1,0:T(8,128)(2,1)S(1)} custom-call(bf16[256,3584]{1,0:T(8,128)(2,1)} %refs_0_.5, bf16[16,8,384]{2,1,0:T(8,128)(2,1)} %shard_map.110.refs_1_), custom_call_target="tpu_custom_call" | custom-call | bytes 1835008 | tf_op jit(solution)/shard_map/pallas_call | solution.py:47
  21.6 5.8 %all-to-all-done.1 = bf16[16,8,384]{2,1,0:T(8,128)(2,1)S(1)} async-done(((bf16[16,8,384]{2,1,0:T(8,128)(2,1)}), bf16[16,8,384]{2,1,0:T(8,128)(2,1)S(1)}, u32[]{:S(2)}, u32[]{:S(2)}) %all-to-all-start.1) | async-done | bytes 98336 | tf_op jit(solution)/shard_map/all_to_all | solution.py:301
  27.3 1.0 %shard_map.113 = (bf16[64,3584]{1,0:T(8,128)(2,1)S(1)}, bf16[64,128]{1,0:T(8,128)(2,1)S(1)}) custom-call(s32[2]{0:T(128)S(1)} %get-tuple-element.64.place_ref, bf16[8,2,8,384]{3,2,1,0:T(8,128)(2,1)S(1)} %bitcast.10, bf16[256,3584]{1,0:T(8,128)(2,1)S(1)} %shard_map.111.weight_ref), custom_call_target="tpu_custom_call" | custom-call | flops 117440512 | bytes 1835008 | tf_op jit(solution)/shard_map/pallas_call | solution.py:133
  28.4 1.0 %shard_map.112 = (f32[64,3584]{1,0:T(8,128)S(1)}, bf16[64,128]{1,0:T(8,128)(2,1)S(1)}) custom-call(s32[2]{0:T(128)S(1)} %get-tuple-element.63.place_ref, bf16[8,2,8,384]{3,2,1,0:T(8,128)(2,1)S(1)} %bitcast.11, bf16[256,3584]{1,0:T(8,128)(2,1)S(1)} %shard_map.111.weight_ref), custom_call_target="tpu_custom_call" | custom-call | flops 117440512 | bytes 1835008 | tf_op jit(solution)/shard_map/pallas_call | solution.py:133
  29.4 0.8 collective-permute-done
  30.3 0.1 collective-permute-start.1
  30.4 1.2 %collective-permute-start.3 = (bf16[16,3584]{1,0:T(8,128)(2,1)S(1)}, bf16[16,3584]{1,0:T(8,128)(2,1)S(1)}, u32[]{:S(2)}, u32[]{:S(2)}) collective-permute-start(bf16[16,3584]{1,0:T(8,128)(2,1)S(1)} %get-tuple-element.61), channel_id=1, source_target_pairs={{0,4},{1,5},{2,6},{3,7},{4,0},{5,1},{6,2},{7,3},{8,12},{9,13},{10,... | collective-permute-start | bytes 344072 | tf_op jit(solution)/shard_map/ppermute | solution.py:275
  31.6 2.3 %collective-permute-start.2 = (bf16[16,3584]{1,0:T(8,128)(2,1)S(1)}, bf16[16,3584]{1,0:T(8,128)(2,1)S(1)}, u32[]{:S(2)}, u32[]{:S(2)}) collective-permute-start(bf16[16,3584]{1,0:T(8,128)(2,1)S(1)} %get-tuple-element.62), channel_id=1, source_target_pairs={{0,2},{1,3},{2,0},{3,1},{4,6},{5,7},{6,4},{7,5},{8,10},{9,11},{10,... | collective-permute-start | bytes 344072 | tf_op jit(solution)/shard_map/ppermute | solution.py:275
  33.8 3.4 %collective-permute-done.1 = bf16[16,3584]{1,0:T(8,128)(2,1)S(1)} collective-permute-done((bf16[16,3584]{1,0:T(8,128)(2,1)S(1)}, bf16[16,3584]{1,0:T(8,128)(2,1)S(1)}, u32[]{:S(2)}, u32[]{:S(2)}) %collective-permute-start.1) | collective-permute-done | bytes 114720 | tf_op jit(solution)/shard_map/ppermute | solution.py:275
  37.2 0.2 collective-permute-done.3
  37.4 1.5 %collective-permute-done.2 = bf16[16,3584]{1,0:T(8,128)(2,1)S(1)} collective-permute-done((bf16[16,3584]{1,0:T(8,128)(2,1)S(1)}, bf16[16,3584]{1,0:T(8,128)(2,1)S(1)}, u32[]{:S(2)}, u32[]{:S(2)}) %collective-permute-start.2) | collective-permute-done | bytes 114720 | tf_op jit(solution)/shard_map/ppermute | solution.py:275
  39.0 0.2 collective-permute-start.4
  39.2 6.8 %shard_map.114 = (bf16[1536,3584]{1,0:T(8,128)(2,1)S(1)}, bf16[768,3584]{1,0:T(8,128)(2,1)S(1)}, bf16[512,3584]{1,0:T(8,128)(2,1)S(1)}, f32[3584]{0:T(1024)S(1)}) custom-call(bf16[1536,3584]{1,0:T(8,128)(2,1)} %refs_0_.6, bf16[1536,3584]{1,0:T(8,128)(2,1)} %refs_0_.7, bf16[1536,3584]{1,0:T(8,128)(2,1)} %down_source.1, f32[3584]{0:T(1024)S(1)} %get-tuple-element.43.refs_3_, ...), custom_call_target="tpu_custom_call" | custom-call | bytes 33030144 | tf_op jit(solution)/shard_map/pallas_call | solution.py:47
  46.0 0.9 %collective-permute-done.4 = bf16[16,3584]{1,0:T(8,128)(2,1)S(1)} collective-permute-done((bf16[16,3584]{1,0:T(8,128)(2,1)S(1)}, bf16[16,3584]{1,0:T(8,128)(2,1)S(1)}, u32[]{:S(2)}, u32[]{:S(2)}) %collective-permute-start.4) | collective-permute-done | bytes 114720 | tf_op jit(solution)/shard_map/ppermute | solution.py:275
  46.9 0.1 shard_map.115
  47.1 0.3 collective-permute-start.7
  47.3 1.3 %collective-permute-start.6 = (bf16[16,3584]{1,0:T(8,128)(2,1)S(1)}, bf16[16,3584]{1,0:T(8,128)(2,1)S(1)}, u32[]{:S(2)}, u32[]{:S(2)}) collective-permute-start(bf16[16,3584]{1,0:T(8,128)(2,1)S(1)} %bitcast.13), channel_id=1, source_target_pairs={{0,2},{1,3},{2,0},{3,1},{4,6},{5,7},{6,4},{7,5},{8,10},{9,11},{10,... | collective-permute-start | bytes 344072 | tf_op jit(solution)/shard_map/ppermute | solution.py:275
  48.7 1.9 %collective-permute-start.5 = (bf16[16,3584]{1,0:T(8,128)(2,1)S(1)}, bf16[16,3584]{1,0:T(8,128)(2,1)S(1)}, u32[]{:S(2)}, u32[]{:S(2)}) collective-permute-start(bf16[16,3584]{1,0:T(8,128)(2,1)S(1)} %bitcast.14), channel_id=1, source_target_pairs={{0,4},{1,5},{2,6},{3,7},{4,0},{5,1},{6,2},{7,3},{8,12},{9,13},{10,... | collective-permute-start | bytes 344072 | tf_op jit(solution)/shard_map/ppermute | solution.py:275
  50.6 3.7 %shard_map.116 = (bf16[768,3584]{1,0:T(8,128)(2,1)S(1)}, bf16[512,3584]{1,0:T(8,128)(2,1)S(1)}, bf16[16,3584]{1,0:T(8,128)(2,1)S(1)}) custom-call(bf16[1536,3584]{1,0:T(8,128)(2,1)} %refs_0_.7, bf16[1536,3584]{1,0:T(8,128)(2,1)} %down_source.1, bf16[16,3584]{1,0:T(8,128)(2,1)S(1)} %bitcast.15), custom_call_target="tpu_custom_call" | custom-call | bytes 22020096 | tf_op jit(solution)/shard_map/pallas_call | solution.py:47
  54.3 0.1 collective-permute-start.8
  54.4 0.5 collective-permute-start.11
  54.9 0.1 collective-permute-start.10
  55.0 0.4 collective-permute-start.9
  55.4 0.3 collective-permute-done.8.refs_4_
  55.7 0.2 collective-permute-done.11.refs_7_
  55.9 0.4 collective-permute-done.10.refs_6_
  56.2 0.2 collective-permute-done.9.refs_5_
  56.4 9.6 %shard_map.117 = (f32[64,3584]{1,0:T(8,128)S(1)}, bf16[64,3584]{1,0:T(8,128)(2,1)S(1)}) custom-call(bf16[64,128]{1,0:T(8,128)(2,1)S(1)} %get-tuple-element.46.own_gates_ref, bf16[64,128]{1,0:T(8,128)(2,1)S(1)} %get-tuple-element.47.other_gates_ref, bf16[768,3584]{1,0:T(8,128)(2,1)S(1)} %get-tuple-element.48.first_ref, ...), custom_call_target="tpu_custom_call" | custom-call | flops 4227858432 | bytes 33030144 | tf_op jit(solution)/shard_map/pallas_call | solution.py:225
  66.0 0.4 collective-permute-start.12
  66.4 1.5 %collective-permute-done.12 = bf16[64,3584]{1,0:T(8,128)(2,1)S(1)} collective-permute-done((bf16[64,3584]{1,0:T(8,128)(2,1)S(1)}, bf16[64,3584]{1,0:T(8,128)(2,1)S(1)}, u32[]{:S(2)}, u32[]{:S(2)}) %collective-permute-start.12) | collective-permute-done | bytes 458784 | tf_op jit(solution)/shard_map/ppermute | solution.py:275
  67.9 0.1 add_convert_fusion.2
  67.9 1.0 %collective-permute-start.13 = (bf16[16,3584]{1,0:T(8,128)(2,1)S(1)}, bf16[16,3584]{1,0:T(8,128)(2,1)S(1)}, u32[]{:S(2)}, u32[]{:S(2)}) collective-permute-start(bf16[16,3584]{1,0:T(8,128)(2,1)S(1)} %get-tuple-element.57), channel_id=1, source_target_pairs={{0,6},{1,7},{2,4},{3,5},{4,2},{5,3},{6,0},{7,1},{8,14},{9,15},{10,... | collective-permute-start | bytes 344072 | tf_op jit(solution)/shard_map/ppermute | solution.py:275
  69.0 1.6 %collective-permute-start.15 = (bf16[16,3584]{1,0:T(8,128)(2,1)S(1)}, bf16[16,3584]{1,0:T(8,128)(2,1)S(1)}, u32[]{:S(2)}, u32[]{:S(2)}) collective-permute-start(bf16[16,3584]{1,0:T(8,128)(2,1)S(1)} %get-tuple-element.58), channel_id=1, source_target_pairs={{0,4},{1,5},{2,6},{3,7},{4,0},{5,1},{6,2},{7,3},{8,12},{9,13},{10,... | collective-permute-start | bytes 344072 | tf_op jit(solution)/shard_map/ppermute | solution.py:275
  70.6 0.9 %collective-permute-start.14 = (bf16[16,3584]{1,0:T(8,128)(2,1)S(1)}, bf16[16,3584]{1,0:T(8,128)(2,1)S(1)}, u32[]{:S(2)}, u32[]{:S(2)}) collective-permute-start(bf16[16,3584]{1,0:T(8,128)(2,1)S(1)} %get-tuple-element.59), channel_id=1, source_target_pairs={{0,2},{1,3},{2,0},{3,1},{4,6},{5,7},{6,4},{7,5},{8,10},{9,11},{10,... | collective-permute-start | bytes 344072 | tf_op jit(solution)/shard_map/ppermute | solution.py:275
  71.5 3.4 %collective-permute-done.13 = bf16[16,3584]{1,0:T(8,128)(2,1)S(1)} collective-permute-done((bf16[16,3584]{1,0:T(8,128)(2,1)S(1)}, bf16[16,3584]{1,0:T(8,128)(2,1)S(1)}, u32[]{:S(2)}, u32[]{:S(2)}) %collective-permute-start.13) | collective-permute-done | bytes 114720 | tf_op jit(solution)/shard_map/ppermute | solution.py:275
  74.9 1.3 %collective-permute-done.15 = bf16[16,3584]{1,0:T(8,128)(2,1)S(1)} collective-permute-done((bf16[16,3584]{1,0:T(8,128)(2,1)S(1)}, bf16[16,3584]{1,0:T(8,128)(2,1)S(1)}, u32[]{:S(2)}, u32[]{:S(2)}) %collective-permute-start.15) | collective-permute-done | bytes 114720 | tf_op jit(solution)/shard_map/ppermute | solution.py:275
  76.2 0.6 collective-permute-done.14
  76.8 0.1 convert_add_fusion
  76.9 1.9 %collective-permute-start.16 = (bf16[8,3584]{1,0:T(8,128)(2,1)S(1)}, bf16[8,3584]{1,0:T(8,128)(2,1)S(1)}, u32[]{:S(2)}, u32[]{:S(2)}) collective-permute-start(bf16[8,3584]{1,0:T(8,128)(2,1)S(1)} %slice.129), channel_id=1, source_target_pairs={{0,8},{1,9},{2,10},{3,11},{4,12},{5,13},{6,14},{7,15},{8,0},{9,1},... | collective-permute-start | bytes 172040 | tf_op jit(solution)/shard_map/ppermute | solution.py:275
  78.8 3.8 %collective-permute-done.16 = bf16[8,3584]{1,0:T(8,128)(2,1)S(1)} collective-permute-done((bf16[8,3584]{1,0:T(8,128)(2,1)S(1)}, bf16[8,3584]{1,0:T(8,128)(2,1)S(1)}, u32[]{:S(2)}, u32[]{:S(2)}) %collective-permute-start.16) | collective-permute-done | bytes 57376 | tf_op jit(solution)/shard_map/ppermute | solution.py:275
  82.6 0.6 fusion.1
  (9 shorter events, 0.2 us)
Async XLA Ops:
  0.0 14.3 %all-to-all-start = ((bf16[16,8,256]{2,1,0:T(8,128)(2,1)}), bf16[16,8,256]{2,1,0:T(8,128)(2,1)S(1)}, u32[]{:S(2)}, u32[]{:S(2)}) async-start(bf16[16,8,256]{2,1,0:T(8,128)(2,1)} %bitcast.17), calls=%async_computation | async-start | bytes 131072 | tf_op jit(solution)/shard_map/all_to_all | solution.py:296
  16.5 10.9 %all-to-all-start.1 = ((bf16[16,8,384]{2,1,0:T(8,128)(2,1)}), bf16[16,8,384]{2,1,0:T(8,128)(2,1)S(1)}, u32[]{:S(2)}, u32[]{:S(2)}) async-start(bf16[16,8,384]{2,1,0:T(8,128)(2,1)} %shard_map.110.refs_1_), calls=%async_computation.1 | async-start | bytes 196608 | tf_op jit(solution)/shard_map/all_to_all | solution.py:301
  28.3 1.9 %collective-permute-start = (bf16[64,3584]{1,0:T(8,128)(2,1)S(1)}, bf16[64,3584]{1,0:T(8,128)(2,1)S(1)}, u32[]{:S(2)}, u32[]{:S(2)}) collective-permute-start(bf16[64,3584]{1,0:T(8,128)(2,1)S(1)} %get-tuple-element.41), channel_id=1, source_target_pairs={{0,1},{1,0},{2,3},{3,2},{4,5},{5,4},{6,7},{7,6},{8,9},{9,8},{10,11... | collective-permute-start | bytes 1376264 | tf_op jit(solution)/shard_map/ppermute | solution.py:275
  30.3 7.0 %collective-permute-start.1 = (bf16[16,3584]{1,0:T(8,128)(2,1)S(1)}, bf16[16,3584]{1,0:T(8,128)(2,1)S(1)}, u32[]{:S(2)}, u32[]{:S(2)}) collective-permute-start(bf16[16,3584]{1,0:T(8,128)(2,1)S(1)} %get-tuple-element.60), channel_id=1, source_target_pairs={{0,6},{1,7},{2,4},{3,5},{4,2},{5,3},{6,0},{7,1},{8,14},{9,15},{10,... | collective-permute-start | bytes 344072 | tf_op jit(solution)/shard_map/ppermute | solution.py:275
  30.4 7.0 %collective-permute-start.3 = (bf16[16,3584]{1,0:T(8,128)(2,1)S(1)}, bf16[16,3584]{1,0:T(8,128)(2,1)S(1)}, u32[]{:S(2)}, u32[]{:S(2)}) collective-permute-start(bf16[16,3584]{1,0:T(8,128)(2,1)S(1)} %get-tuple-element.61), channel_id=1, source_target_pairs={{0,4},{1,5},{2,6},{3,7},{4,0},{5,1},{6,2},{7,3},{8,12},{9,13},{10,... | collective-permute-start | bytes 344072 | tf_op jit(solution)/shard_map/ppermute | solution.py:275
  31.6 7.3 %collective-permute-start.2 = (bf16[16,3584]{1,0:T(8,128)(2,1)S(1)}, bf16[16,3584]{1,0:T(8,128)(2,1)S(1)}, u32[]{:S(2)}, u32[]{:S(2)}) collective-permute-start(bf16[16,3584]{1,0:T(8,128)(2,1)S(1)} %get-tuple-element.62), channel_id=1, source_target_pairs={{0,2},{1,3},{2,0},{3,1},{4,6},{5,7},{6,4},{7,5},{8,10},{9,11},{10,... | collective-permute-start | bytes 344072 | tf_op jit(solution)/shard_map/ppermute | solution.py:275
  39.0 7.9 %collective-permute-start.4 = (bf16[16,3584]{1,0:T(8,128)(2,1)S(1)}, bf16[16,3584]{1,0:T(8,128)(2,1)S(1)}, u32[]{:S(2)}, u32[]{:S(2)}) collective-permute-start(bf16[16,3584]{1,0:T(8,128)(2,1)S(1)} %convert_element_type.85.refs_4_.kept_ref), channel_id=1, source_target_pairs={{0,8},{1,9},{2,10},{3,11},{4,12},{5,13},{6,14},{7,15},{8,0},{9,1},... | collective-permute-start | bytes 344072 | tf_op jit(solution)/shard_map/ppermute | solution.py:275
  47.1 7.3 %collective-permute-start.7 = (bf16[16,3584]{1,0:T(8,128)(2,1)S(1)}, bf16[16,3584]{1,0:T(8,128)(2,1)S(1)}, u32[]{:S(2)}, u32[]{:S(2)}) collective-permute-start(bf16[16,3584]{1,0:T(8,128)(2,1)S(1)} %bitcast.12), channel_id=1, source_target_pairs={{0,6},{1,7},{2,4},{3,5},{4,2},{5,3},{6,0},{7,1},{8,14},{9,15},{10,... | collective-permute-start | bytes 344072 | tf_op jit(solution)/shard_map/ppermute | solution.py:275
  47.3 7.6 %collective-permute-start.6 = (bf16[16,3584]{1,0:T(8,128)(2,1)S(1)}, bf16[16,3584]{1,0:T(8,128)(2,1)S(1)}, u32[]{:S(2)}, u32[]{:S(2)}) collective-permute-start(bf16[16,3584]{1,0:T(8,128)(2,1)S(1)} %bitcast.13), channel_id=1, source_target_pairs={{0,2},{1,3},{2,0},{3,1},{4,6},{5,7},{6,4},{7,5},{8,10},{9,11},{10,... | collective-permute-start | bytes 344072 | tf_op jit(solution)/shard_map/ppermute | solution.py:275
  48.7 6.3 %collective-permute-start.5 = (bf16[16,3584]{1,0:T(8,128)(2,1)S(1)}, bf16[16,3584]{1,0:T(8,128)(2,1)S(1)}, u32[]{:S(2)}, u32[]{:S(2)}) collective-permute-start(bf16[16,3584]{1,0:T(8,128)(2,1)S(1)} %bitcast.14), channel_id=1, source_target_pairs={{0,4},{1,5},{2,6},{3,7},{4,0},{5,1},{6,2},{7,3},{8,12},{9,13},{10,... | collective-permute-start | bytes 344072 | tf_op jit(solution)/shard_map/ppermute | solution.py:275
  54.3 1.4 %collective-permute-start.8 = (bf16[16,3584]{1,0:T(8,128)(2,1)S(1)}, bf16[16,3584]{1,0:T(8,128)(2,1)S(1)}, u32[]{:S(2)}, u32[]{:S(2)}) collective-permute-start(bf16[16,3584]{1,0:T(8,128)(2,1)S(1)} %get-tuple-element.54.refs_0_), channel_id=1, source_target_pairs={{0,1},{1,0},{2,3},{3,2},{4,5},{5,4},{6,7},{7,6},{8,9},{9,8},{10,11... | collective-permute-start | bytes 344072 | tf_op jit(solution)/shard_map/ppermute | solution.py:275
  54.4 1.5 %collective-permute-start.11 = (bf16[16,3584]{1,0:T(8,128)(2,1)S(1)}, bf16[16,3584]{1,0:T(8,128)(2,1)S(1)}, u32[]{:S(2)}, u32[]{:S(2)}) collective-permute-start(bf16[16,3584]{1,0:T(8,128)(2,1)S(1)} %collective-permute-done.7.refs_3_), channel_id=1, source_target_pairs={{0,1},{1,0},{2,3},{3,2},{4,5},{5,4},{6,7},{7,6},{8,9},{9,8},{10,11... | collective-permute-start | bytes 344072 | tf_op jit(solution)/shard_map/ppermute | solution.py:275
  54.9 1.3 %collective-permute-start.10 = (bf16[16,3584]{1,0:T(8,128)(2,1)S(1)}, bf16[16,3584]{1,0:T(8,128)(2,1)S(1)}, u32[]{:S(2)}, u32[]{:S(2)}) collective-permute-start(bf16[16,3584]{1,0:T(8,128)(2,1)S(1)} %collective-permute-done.6.refs_2_), channel_id=1, source_target_pairs={{0,1},{1,0},{2,3},{3,2},{4,5},{5,4},{6,7},{7,6},{8,9},{9,8},{10,11... | collective-permute-start | bytes 344072 | tf_op jit(solution)/shard_map/ppermute | solution.py:275
  55.0 1.4 %collective-permute-start.9 = (bf16[16,3584]{1,0:T(8,128)(2,1)S(1)}, bf16[16,3584]{1,0:T(8,128)(2,1)S(1)}, u32[]{:S(2)}, u32[]{:S(2)}) collective-permute-start(bf16[16,3584]{1,0:T(8,128)(2,1)S(1)} %collective-permute-done.5.refs_1_), channel_id=1, source_target_pairs={{0,1},{1,0},{2,3},{3,2},{4,5},{5,4},{6,7},{7,6},{8,9},{9,8},{10,11... | collective-permute-start | bytes 344072 | tf_op jit(solution)/shard_map/ppermute | solution.py:275
  66.0 1.9 %collective-permute-start.12 = (bf16[64,3584]{1,0:T(8,128)(2,1)S(1)}, bf16[64,3584]{1,0:T(8,128)(2,1)S(1)}, u32[]{:S(2)}, u32[]{:S(2)}) collective-permute-start(bf16[64,3584]{1,0:T(8,128)(2,1)S(1)} %get-tuple-element.56), channel_id=1, source_target_pairs={{0,1},{1,0},{2,3},{3,2},{4,5},{5,4},{6,7},{7,6},{8,9},{9,8},{10,11... | collective-permute-start | bytes 1376264 | tf_op jit(solution)/shard_map/ppermute | solution.py:275
  67.9 6.9 %collective-permute-start.13 = (bf16[16,3584]{1,0:T(8,128)(2,1)S(1)}, bf16[16,3584]{1,0:T(8,128)(2,1)S(1)}, u32[]{:S(2)}, u32[]{:S(2)}) collective-permute-start(bf16[16,3584]{1,0:T(8,128)(2,1)S(1)} %get-tuple-element.57), channel_id=1, source_target_pairs={{0,6},{1,7},{2,4},{3,5},{4,2},{5,3},{6,0},{7,1},{8,14},{9,15},{10,... | collective-permute-start | bytes 344072 | tf_op jit(solution)/shard_map/ppermute | solution.py:275
  69.0 7.3 %collective-permute-start.15 = (bf16[16,3584]{1,0:T(8,128)(2,1)S(1)}, bf16[16,3584]{1,0:T(8,128)(2,1)S(1)}, u32[]{:S(2)}, u32[]{:S(2)}) collective-permute-start(bf16[16,3584]{1,0:T(8,128)(2,1)S(1)} %get-tuple-element.58), channel_id=1, source_target_pairs={{0,4},{1,5},{2,6},{3,7},{4,0},{5,1},{6,2},{7,3},{8,12},{9,13},{10,... | collective-permute-start | bytes 344072 | tf_op jit(solution)/shard_map/ppermute | solution.py:275
  70.6 6.2 %collective-permute-start.14 = (bf16[16,3584]{1,0:T(8,128)(2,1)S(1)}, bf16[16,3584]{1,0:T(8,128)(2,1)S(1)}, u32[]{:S(2)}, u32[]{:S(2)}) collective-permute-start(bf16[16,3584]{1,0:T(8,128)(2,1)S(1)} %get-tuple-element.59), channel_id=1, source_target_pairs={{0,2},{1,3},{2,0},{3,1},{4,6},{5,7},{6,4},{7,5},{8,10},{9,11},{10,... | collective-permute-start | bytes 344072 | tf_op jit(solution)/shard_map/ppermute | solution.py:275
  76.9 5.7 %collective-permute-start.16 = (bf16[8,3584]{1,0:T(8,128)(2,1)S(1)}, bf16[8,3584]{1,0:T(8,128)(2,1)S(1)}, u32[]{:S(2)}, u32[]{:S(2)}) collective-permute-start(bf16[8,3584]{1,0:T(8,128)(2,1)S(1)} %slice.129), channel_id=1, source_target_pairs={{0,8},{1,9},{2,10},{3,11},{4,12},{5,13},{6,14},{7,15},{8,0},{9,1},... | collective-permute-start | bytes 172040 | tf_op jit(solution)/shard_map/ppermute | solution.py:275

commit v10 on v9

--- a/solution.py
+++ b/solution.py
@@ -175,10 +175,10 @@
 
 
 def expert_kernel(own_gates_ref, other_gates_ref, first_ref, second_ref, up_ref, low_ref, middle_ref, down_source, *refs):
-    pieces, (kept_ref, sent_ref, turned, hidden, down_ref, sems) = refs[:-6], refs[-6:]
+    pieces, results, (turned, hidden, down_ref, sems) = refs[:-8], refs[-8:-4], refs[-4:]
     half = turned.shape[1] // 2
     units, feature = up_ref.shape
-    wide = tile_of(feature, 1792)
+    wide = feature // 2
 
     first_unit = units - down_ref.shape[0]
     deep = tile_of(down_ref.shape[0], 128)
@@ -214,8 +214,9 @@
             term = jnp.dot(hidden[:, units_here], ref[:, columns], preferred_element_type=F32)
             total = term if total is None else total + term
             low += ref.shape[0]
-        kept_ref[:, columns] = total[:half]
-        sent_ref[:, columns] = total[half:].astype(BF16)
+        kept_ref, sent_ref = results[2 * (at // wide) : 2 * (at // wide) + 2]
+        kept_ref[...] = total[:half]
+        sent_ref[...] = total[half:].astype(BF16)
 
 
 def experts(pieces, gates, held, down_weight):
@@ -225,11 +226,12 @@
     return pl.pallas_call(
         expert_kernel,
         out_shape=(
-            jax.ShapeDtypeStruct((half, feature), F32),
-            jax.ShapeDtypeStruct((half, feature), BF16),
-        ),
+            jax.ShapeDtypeStruct((half, feature // 2), F32),
+            jax.ShapeDtypeStruct((half, feature // 2), BF16),
+        )
+        * 2,
         in_specs=[VMEM_SPEC] * 7 + [HBM_SPEC] + [VMEM_SPEC] * len(pieces),
-        out_specs=(VMEM_SPEC, VMEM_SPEC),
+        out_specs=(VMEM_SPEC,) * 4,
         scratch_shapes=[
             pltpu.VMEM((feature, 2 * half), BF16),
             pltpu.VMEM((2 * half, units), BF16),
@@ -325,10 +327,12 @@
     pieces = [own] + others
     pieces = pieces + [swap(piece, 1) for piece in pieces]
     held = (first_held, second_held, up_held, low_held, middle_held)
-    kept, sent = experts(pieces, (own_gates, other_gates), held, down_weight)
-    kept = sum_nearest(kept, swap(sent, 1))
-    combined = kept[:tok] + swap(kept[tok:].astype(BF16), chips).astype(F32)
-    return (middle + combined).astype(BF16)
+    results = experts(pieces, (own_gates, other_gates), held, down_weight)
+    combined = []
+    for kept, sent in (results[:2], results[2:]):
+        kept = sum_nearest(kept, swap(sent, 1))
+        combined.append(kept[:tok] + swap(kept[tok:].astype(BF16), chips).astype(F32))
+    return (middle + jnp.concatenate(combined, axis=1)).astype(BF16)
 
 
 def solution(mesh):

time: 83.6 us -> 82.6 us (0.988)
  starting transfers between devices: 25.2 us -> 30.4 us
  waiting for transfers between devices: 28.6 us -> 23.9 us
  Pallas kernels: 27.5 us -> 26.1 us
    ppermute x17 -> x22, starting transfers between devices: 14.3 us -> 19.5 us  [swap(): return lax.ppermute(x, 'ep', [(i, i ^ bit) for i in range(size)])]
    ppermute x17 -> x22, waiting for transfers between devices: 18.3 us -> 13.6 us  [swap(): return lax.ppermute(x, 'ep', [(i, i ^ bit) for i in range(size)])]
    pallas_call x1, Pallas kernels: 9.59 us -> 8.21 us  [experts(): pl.pallas_call(expert_kernel, out_shape=(jax.ShapeDtypeStruct((half, feat...]
  transfers between devices with their start and end apart: 19 -> 24, of which waited for: 16 -> 16; matrix products, arithmetic and copies ran while one was open for 1% -> 1% of each run, Pallas kernels for 18% -> 18%
where the time goes in v10:
time: 82.6 us; the launch traced here: 82.3 us
  starting transfers between devices  30.4 us (37%)
  Pallas kernels  26.1 us (32%)
  waiting for transfers between devices  23.9 us (29%)
  other arithmetic  1.74 us (2%)
    ppermute x22, starting transfers between devices, swap(): return lax.ppermute(x, 'ep', [(i, i ^ bit) for i in range(size)])  19.5 us
    pallas_call x4, Pallas kernels, fetch(): pl.pallas_call(functools.partial(fetch_kernel, count, carried, ranges), o...  13.6 us
    ppermute x22, waiting for transfers between devices, swap(): return lax.ppermute(x, 'ep', [(i, i ^ bit) for i in range(size)])  13.6 us
    pallas_call x1, Pallas kernels, experts(): pl.pallas_call(expert_kernel, out_shape=(jax.ShapeDtypeStruct((half, feat...  8.21 us
    all_to_all x1, starting transfers between devices, local(): lax.all_to_all(queries.reshape(size, tok, head_dim), 'ep', split_axis=0,...  7.38 us
    all_to_all x1, waiting for transfers between devices, local(): lax.all_to_all(attended, 'ep', split_axis=0, concat_axis=0, tiled=True)  5.76 us
    all_to_all x1, waiting for transfers between devices, local(): lax.all_to_all(queries.reshape(size, tok, head_dim), 'ep', split_axis=0,...  4.56 us
    all_to_all x1, starting transfers between devices, local(): lax.all_to_all(attended, 'ep', split_axis=0, concat_axis=0, tiled=True)  3.51 us
  transfers between devices with their start and end apart: 24, of which 16 were waited for; matrix products, arithmetic and copies ran while one was open for 1% of the time, Pallas kernels for 18%

profile of v10, /device:TPU:0, one launch (start us, length us, event | category | flops | bytes accessed | tf_op | source)
XLA Modules:
  0.0 82.3 jit_solution(16417452694640018957)
XLA Ops:
  0.0 7.4 %all-to-all-start = ((bf16[16,8,256]{2,1,0:T(8,128)(2,1)}), bf16[16,8,256]{2,1,0:T(8,128)(2,1)S(1)}, u32[]{:S(2)}, u32[]{:S(2)}) async-start(bf16[16,8,256]{2,1,0:T(8,128)(2,1)} %bitcast.17), calls=%async_computation | async-start | bytes 131072 | tf_op jit(solution)/shard_map/all_to_all | solution.py:298
  7.4 1.6 %shard_map.109 = (bf16[8,256,512]{2,1,0:T(8,128)(2,1)S(1)}, bf16[8,3584]{1,0:T(8,128)(2,1)S(1)}, f32[3584]{0:T(1024)S(1)}, s32[8]{0:T(128)S(1)}, s32[3,8]{1,0:T(4,128)S(1)}) custom-call(bf16[8,256,512]{2,1,0:T(8,128)(2,1)} %refs_0_.4, bf16[8,3584]{1,0:T(8,128)(2,1)} %refs_1_.3, f32[3584]{0:T(1024)} %refs_2_.2, s32[8]{0:T(128)} %refs_3_.1, s32[3,8]{1,0:T(4,128)} %bitcast.18), custom_call_target="tpu_custom_call" | custom-call | bytes 2161728 | tf_op jit(solution)/shard_map/pallas_call | solution.py:47
  9.0 0.7 convert_bitcast_fusion.shares_ref
  9.7 4.6 %all-to-all-done.query_ref = bf16[16,8,256]{2,1,0:T(8,128)(2,1)S(1)} async-done(((bf16[16,8,256]{2,1,0:T(8,128)(2,1)}), bf16[16,8,256]{2,1,0:T(8,128)(2,1)S(1)}, u32[]{:S(2)}, u32[]{:S(2)}) %all-to-all-start) | async-done | bytes 65568 | tf_op jit(solution)/shard_map/all_to_all | solution.py:298
  14.3 2.2 %shard_map.110.refs_1_ = bf16[16,8,384]{2,1,0:T(8,128)(2,1)} custom-call(s32[8]{0:T(128)S(1)} %get-tuple-element.39.lengths_ref, s32[3,8]{1,0:T(4,128)S(1)} %get-tuple-element.40.routes_ref, f32[3,8]{1,0:T(4,128)S(1)} %convert_bitcast_fusion.shares_ref, bf16[16,8,256]{2,1,0:T(8,128)(2,1)S(1)} %all-to-all-done.query_ref, ...), custom_call_target="tpu_custom_call" | custom-call | tf_op jit(solution)/shard_map/pallas_call | solution.py:100
  16.5 3.5 %all-to-all-start.1 = ((bf16[16,8,384]{2,1,0:T(8,128)(2,1)}), bf16[16,8,384]{2,1,0:T(8,128)(2,1)S(1)}, u32[]{:S(2)}, u32[]{:S(2)}) async-start(bf16[16,8,384]{2,1,0:T(8,128)(2,1)} %shard_map.110.refs_1_), calls=%async_computation.1 | async-start | bytes 196608 | tf_op jit(solution)/shard_map/all_to_all | solution.py:303
  20.1 1.5 %shard_map.111.weight_ref = bf16[256,3584]{1,0:T(8,128)(2,1)S(1)} custom-call(bf16[256,3584]{1,0:T(8,128)(2,1)} %refs_0_.5, bf16[16,8,384]{2,1,0:T(8,128)(2,1)} %shard_map.110.refs_1_), custom_call_target="tpu_custom_call" | custom-call | bytes 1835008 | tf_op jit(solution)/shard_map/pallas_call | solution.py:47
  21.6 5.8 %all-to-all-done.1 = bf16[16,8,384]{2,1,0:T(8,128)(2,1)S(1)} async-done(((bf16[16,8,384]{2,1,0:T(8,128)(2,1)}), bf16[16,8,384]{2,1,0:T(8,128)(2,1)S(1)}, u32[]{:S(2)}, u32[]{:S(2)}) %all-to-all-start.1) | async-done | bytes 98336 | tf_op jit(solution)/shard_map/all_to_all | solution.py:303
  27.3 1.0 %shard_map.113 = (bf16[64,3584]{1,0:T(8,128)(2,1)S(1)}, bf16[64,128]{1,0:T(8,128)(2,1)S(1)}) custom-call(s32[2]{0:T(128)S(1)} %get-tuple-element.71.place_ref, bf16[8,2,8,384]{3,2,1,0:T(8,128)(2,1)S(1)} %bitcast.10, bf16[256,3584]{1,0:T(8,128)(2,1)S(1)} %shard_map.111.weight_ref), custom_call_target="tpu_custom_call" | custom-call | flops 117440512 | bytes 1835008 | tf_op jit(solution)/shard_map/pallas_call | solution.py:133
  28.4 1.0 %shard_map.112 = (f32[64,3584]{1,0:T(8,128)S(1)}, bf16[64,128]{1,0:T(8,128)(2,1)S(1)}) custom-call(s32[2]{0:T(128)S(1)} %get-tuple-element.70.place_ref, bf16[8,2,8,384]{3,2,1,0:T(8,128)(2,1)S(1)} %bitcast.11, bf16[256,3584]{1,0:T(8,128)(2,1)S(1)} %shard_map.111.weight_ref), custom_call_target="tpu_custom_call" | custom-call | flops 117440512 | bytes 1835008 | tf_op jit(solution)/shard_map/pallas_call | solution.py:133
  29.4 0.8 collective-permute-done
  30.3 1.2 %collective-permute-start.3 = (bf16[16,3584]{1,0:T(8,128)(2,1)S(1)}, bf16[16,3584]{1,0:T(8,128)(2,1)S(1)}, u32[]{:S(2)}, u32[]{:S(2)}) collective-permute-start(bf16[16,3584]{1,0:T(8,128)(2,1)S(1)} %get-tuple-element.62), channel_id=1, source_target_pairs={{0,4},{1,5},{2,6},{3,7},{4,0},{5,1},{6,2},{7,3},{8,12},{9,13},{10,... | collective-permute-start | bytes 344072 | tf_op jit(solution)/shard_map/ppermute | solution.py:277
  31.5 2.3 %collective-permute-start.2 = (bf16[16,3584]{1,0:T(8,128)(2,1)S(1)}, bf16[16,3584]{1,0:T(8,128)(2,1)S(1)}, u32[]{:S(2)}, u32[]{:S(2)}) collective-permute-start(bf16[16,3584]{1,0:T(8,128)(2,1)S(1)} %get-tuple-element.63), channel_id=1, source_target_pairs={{0,2},{1,3},{2,0},{3,1},{4,6},{5,7},{6,4},{7,5},{8,10},{9,11},{10,... | collective-permute-start | bytes 344072 | tf_op jit(solution)/shard_map/ppermute | solution.py:277
  33.8 3.4 %collective-permute-done.1 = bf16[16,3584]{1,0:T(8,128)(2,1)S(1)} collective-permute-done((bf16[16,3584]{1,0:T(8,128)(2,1)S(1)}, bf16[16,3584]{1,0:T(8,128)(2,1)S(1)}, u32[]{:S(2)}, u32[]{:S(2)}) %collective-permute-start.1) | collective-permute-done | bytes 114720 | tf_op jit(solution)/shard_map/ppermute | solution.py:277
  37.2 0.2 collective-permute-done.3
  37.4 1.5 %collective-permute-done.2 = bf16[16,3584]{1,0:T(8,128)(2,1)S(1)} collective-permute-done((bf16[16,3584]{1,0:T(8,128)(2,1)S(1)}, bf16[16,3584]{1,0:T(8,128)(2,1)S(1)}, u32[]{:S(2)}, u32[]{:S(2)}) %collective-permute-start.2) | collective-permute-done | bytes 114720 | tf_op jit(solution)/shard_map/ppermute | solution.py:277
  39.0 0.2 collective-permute-start.4
  39.2 6.8 %shard_map.114 = (bf16[1536,3584]{1,0:T(8,128)(2,1)S(1)}, bf16[768,3584]{1,0:T(8,128)(2,1)S(1)}, bf16[512,3584]{1,0:T(8,128)(2,1)S(1)}, f32[3584]{0:T(1024)S(1)}) custom-call(bf16[1536,3584]{1,0:T(8,128)(2,1)} %refs_0_.6, bf16[1536,3584]{1,0:T(8,128)(2,1)} %refs_0_.7, bf16[1536,3584]{1,0:T(8,128)(2,1)} %down_source.1, f32[3584]{0:T(1024)S(1)} %get-tuple-element.45.refs_3_, ...), custom_call_target="tpu_custom_call" | custom-call | bytes 33030144 | tf_op jit(solution)/shard_map/pallas_call | solution.py:47
  46.0 0.9 %collective-permute-done.4 = bf16[16,3584]{1,0:T(8,128)(2,1)S(1)} collective-permute-done((bf16[16,3584]{1,0:T(8,128)(2,1)S(1)}, bf16[16,3584]{1,0:T(8,128)(2,1)S(1)}, u32[]{:S(2)}, u32[]{:S(2)}) %collective-permute-start.4) | collective-permute-done | bytes 114720 | tf_op jit(solution)/shard_map/ppermute | solution.py:277
  46.9 0.1 shard_map.115
  47.0 0.3 collective-permute-start.7
  47.3 1.3 %collective-permute-start.6 = (bf16[16,3584]{1,0:T(8,128)(2,1)S(1)}, bf16[16,3584]{1,0:T(8,128)(2,1)S(1)}, u32[]{:S(2)}, u32[]{:S(2)}) collective-permute-start(bf16[16,3584]{1,0:T(8,128)(2,1)S(1)} %bitcast.13), channel_id=1, source_target_pairs={{0,2},{1,3},{2,0},{3,1},{4,6},{5,7},{6,4},{7,5},{8,10},{9,11},{10,... | collective-permute-start | bytes 344072 | tf_op jit(solution)/shard_map/ppermute | solution.py:277
  48.7 1.9 %collective-permute-start.5 = (bf16[16,3584]{1,0:T(8,128)(2,1)S(1)}, bf16[16,3584]{1,0:T(8,128)(2,1)S(1)}, u32[]{:S(2)}, u32[]{:S(2)}) collective-permute-start(bf16[16,3584]{1,0:T(8,128)(2,1)S(1)} %bitcast.14), channel_id=1, source_target_pairs={{0,4},{1,5},{2,6},{3,7},{4,0},{5,1},{6,2},{7,3},{8,12},{9,13},{10,... | collective-permute-start | bytes 344072 | tf_op jit(solution)/shard_map/ppermute | solution.py:277
  50.6 3.7 %shard_map.116 = (bf16[768,3584]{1,0:T(8,128)(2,1)S(1)}, bf16[512,3584]{1,0:T(8,128)(2,1)S(1)}, bf16[16,3584]{1,0:T(8,128)(2,1)S(1)}) custom-call(bf16[1536,3584]{1,0:T(8,128)(2,1)} %refs_0_.7, bf16[1536,3584]{1,0:T(8,128)(2,1)} %down_source.1, bf16[16,3584]{1,0:T(8,128)(2,1)S(1)} %bitcast.15), custom_call_target="tpu_custom_call" | custom-call | bytes 22020096 | tf_op jit(solution)/shard_map/pallas_call | solution.py:47
  54.4 0.5 collective-permute-start.11
  54.9 0.1 collective-permute-start.10
  55.0 0.4 collective-permute-start.9
  55.4 0.3 collective-permute-done.8.refs_4_
  55.7 0.2 collective-permute-done.11.refs_7_
  55.9 0.4 collective-permute-done.10.refs_6_
  56.2 0.2 collective-permute-done.9.refs_5_
  56.4 8.2 %shard_map.117 = (f32[64,1792]{1,0:T(8,128)S(1)}, bf16[64,1792]{1,0:T(8,128)(2,1)S(1)}, f32[64,1792]{1,0:T(8,128)S(1)}, bf16[64,1792]{1,0:T(8,128)(2,1)S(1)}) custom-call(bf16[64,128]{1,0:T(8,128)(2,1)S(1)} %get-tuple-element.48.own_gates_ref, bf16[64,128]{1,0:T(8,128)(2,1)S(1)} %get-tuple-element.49.other_gates_ref, ...), custom_call_target="tpu_custom_call" | custom-call | flops 4227858432 | bytes 33030144 | tf_op jit(solution)/shard_map/pallas_call | solution.py:226
  64.6 0.4 collective-permute-start.12
  65.0 0.2 collective-permute-start.17
  65.2 1.0 %collective-permute-done.12 = bf16[64,1792]{1,0:T(8,128)(2,1)S(1)} collective-permute-done((bf16[64,1792]{1,0:T(8,128)(2,1)S(1)}, bf16[64,1792]{1,0:T(8,128)(2,1)S(1)}, u32[]{:S(2)}, u32[]{:S(2)}) %collective-permute-start.12) | collective-permute-done | bytes 229408 | tf_op jit(solution)/shard_map/ppermute | solution.py:277
  66.2 1.0 %collective-permute-start.13 = (bf16[16,1792]{1,0:T(8,128)(2,1)S(1)}, bf16[16,1792]{1,0:T(8,128)(2,1)S(1)}, u32[]{:S(2)}, u32[]{:S(2)}) collective-permute-start(bf16[16,1792]{1,0:T(8,128)(2,1)S(1)} %get-tuple-element.64), channel_id=1, source_target_pairs={{0,6},{1,7},{2,4},{3,5},{4,2},{5,3},{6,0},{7,1},{8,14},{9,15},{10,... | collective-permute-start | bytes 172040 | tf_op jit(solution)/shard_map/ppermute | solution.py:277
  67.2 1.6 %collective-permute-start.15 = (bf16[16,1792]{1,0:T(8,128)(2,1)S(1)}, bf16[16,1792]{1,0:T(8,128)(2,1)S(1)}, u32[]{:S(2)}, u32[]{:S(2)}) collective-permute-start(bf16[16,1792]{1,0:T(8,128)(2,1)S(1)} %get-tuple-element.65), channel_id=1, source_target_pairs={{0,4},{1,5},{2,6},{3,7},{4,0},{5,1},{6,2},{7,3},{8,12},{9,13},{10,... | collective-permute-start | bytes 172040 | tf_op jit(solution)/shard_map/ppermute | solution.py:277
  68.8 0.9 %collective-permute-start.14 = (bf16[16,1792]{1,0:T(8,128)(2,1)S(1)}, bf16[16,1792]{1,0:T(8,128)(2,1)S(1)}, u32[]{:S(2)}, u32[]{:S(2)}) collective-permute-start(bf16[16,1792]{1,0:T(8,128)(2,1)S(1)} %get-tuple-element.66), channel_id=1, source_target_pairs={{0,2},{1,3},{2,0},{3,1},{4,6},{5,7},{6,4},{7,5},{8,10},{9,11},{10,... | collective-permute-start | bytes 172040 | tf_op jit(solution)/shard_map/ppermute | solution.py:277
  69.8 1.0 %collective-permute-start.18 = (bf16[16,1792]{1,0:T(8,128)(2,1)S(1)}, bf16[16,1792]{1,0:T(8,128)(2,1)S(1)}, u32[]{:S(2)}, u32[]{:S(2)}) collective-permute-start(bf16[16,1792]{1,0:T(8,128)(2,1)S(1)} %get-tuple-element.67), channel_id=1, source_target_pairs={{0,6},{1,7},{2,4},{3,5},{4,2},{5,3},{6,0},{7,1},{8,14},{9,15},{10,... | collective-permute-start | bytes 172040 | tf_op jit(solution)/shard_map/ppermute | solution.py:277
  70.8 1.6 %collective-permute-start.20 = (bf16[16,1792]{1,0:T(8,128)(2,1)S(1)}, bf16[16,1792]{1,0:T(8,128)(2,1)S(1)}, u32[]{:S(2)}, u32[]{:S(2)}) collective-permute-start(bf16[16,1792]{1,0:T(8,128)(2,1)S(1)} %get-tuple-element.68), channel_id=1, source_target_pairs={{0,4},{1,5},{2,6},{3,7},{4,0},{5,1},{6,2},{7,3},{8,12},{9,13},{10,... | collective-permute-start | bytes 172040 | tf_op jit(solution)/shard_map/ppermute | solution.py:277
  72.4 0.9 %collective-permute-start.19 = (bf16[16,1792]{1,0:T(8,128)(2,1)S(1)}, bf16[16,1792]{1,0:T(8,128)(2,1)S(1)}, u32[]{:S(2)}, u32[]{:S(2)}) collective-permute-start(bf16[16,1792]{1,0:T(8,128)(2,1)S(1)} %get-tuple-element.69), channel_id=1, source_target_pairs={{0,2},{1,3},{2,0},{3,1},{4,6},{5,7},{6,4},{7,5},{8,10},{9,11},{10,... | collective-permute-start | bytes 172040 | tf_op jit(solution)/shard_map/ppermute | solution.py:277
  73.4 0.3 collective-permute-done.14
  73.7 1.7 %collective-permute-start.16 = (bf16[8,1792]{1,0:T(8,128)(2,1)S(1)}, bf16[8,1792]{1,0:T(8,128)(2,1)S(1)}, u32[]{:S(2)}, u32[]{:S(2)}) collective-permute-start(bf16[8,1792]{1,0:T(8,128)(2,1)S(1)} %slice.183), channel_id=1, source_target_pairs={{0,8},{1,9},{2,10},{3,11},{4,12},{5,13},{6,14},{7,15},{8,0},{9,1},... | collective-permute-start | bytes 86024 | tf_op jit(solution)/shard_map/ppermute | solution.py:277
  75.4 1.2 %collective-permute-done.19 = bf16[16,1792]{1,0:T(8,128)(2,1)S(1)} collective-permute-done((bf16[16,1792]{1,0:T(8,128)(2,1)S(1)}, bf16[16,1792]{1,0:T(8,128)(2,1)S(1)}, u32[]{:S(2)}, u32[]{:S(2)}) %collective-permute-start.19) | collective-permute-done | bytes 57376 | tf_op jit(solution)/shard_map/ppermute | solution.py:277
  76.7 1.7 %collective-permute-start.21 = (bf16[8,1792]{1,0:T(8,128)(2,1)S(1)}, bf16[8,1792]{1,0:T(8,128)(2,1)S(1)}, u32[]{:S(2)}, u32[]{:S(2)}) collective-permute-start(bf16[8,1792]{1,0:T(8,128)(2,1)S(1)} %slice.182), channel_id=1, source_target_pairs={{0,8},{1,9},{2,10},{3,11},{4,12},{5,13},{6,14},{7,15},{8,0},{9,1},... | collective-permute-start | bytes 86024 | tf_op jit(solution)/shard_map/ppermute | solution.py:277
  78.3 0.9 %collective-permute-done.16 = bf16[8,1792]{1,0:T(8,128)(2,1)S(1)} collective-permute-done((bf16[8,1792]{1,0:T(8,128)(2,1)S(1)}, bf16[8,1792]{1,0:T(8,128)(2,1)S(1)}, u32[]{:S(2)}, u32[]{:S(2)}) %collective-permute-start.16) | collective-permute-done | bytes 28704 | tf_op jit(solution)/shard_map/ppermute | solution.py:277
  79.2 2.4 %collective-permute-done.21 = bf16[8,1792]{1,0:T(8,128)(2,1)S(1)} collective-permute-done((bf16[8,1792]{1,0:T(8,128)(2,1)S(1)}, bf16[8,1792]{1,0:T(8,128)(2,1)S(1)}, u32[]{:S(2)}, u32[]{:S(2)}) %collective-permute-start.21) | collective-permute-done | bytes 28704 | tf_op jit(solution)/shard_map/ppermute | solution.py:277
  81.6 0.6 fusion.1
  (24 shorter events, 0.7 us)
Async XLA Ops:
  0.0 14.3 %all-to-all-start = ((bf16[16,8,256]{2,1,0:T(8,128)(2,1)}), bf16[16,8,256]{2,1,0:T(8,128)(2,1)S(1)}, u32[]{:S(2)}, u32[]{:S(2)}) async-start(bf16[16,8,256]{2,1,0:T(8,128)(2,1)} %bitcast.17), calls=%async_computation | async-start | bytes 131072 | tf_op jit(solution)/shard_map/all_to_all | solution.py:298
  16.5 10.9 %all-to-all-start.1 = ((bf16[16,8,384]{2,1,0:T(8,128)(2,1)}), bf16[16,8,384]{2,1,0:T(8,128)(2,1)S(1)}, u32[]{:S(2)}, u32[]{:S(2)}) async-start(bf16[16,8,384]{2,1,0:T(8,128)(2,1)} %shard_map.110.refs_1_), calls=%async_computation.1 | async-start | bytes 196608 | tf_op jit(solution)/shard_map/all_to_all | solution.py:303
  28.3 1.9 %collective-permute-start = (bf16[64,3584]{1,0:T(8,128)(2,1)S(1)}, bf16[64,3584]{1,0:T(8,128)(2,1)S(1)}, u32[]{:S(2)}, u32[]{:S(2)}) collective-permute-start(bf16[64,3584]{1,0:T(8,128)(2,1)S(1)} %get-tuple-element.43), channel_id=1, source_target_pairs={{0,1},{1,0},{2,3},{3,2},{4,5},{5,4},{6,7},{7,6},{8,9},{9,8},{10,11... | collective-permute-start | bytes 1376264 | tf_op jit(solution)/shard_map/ppermute | solution.py:277
  30.3 7.0 %collective-permute-start.1 = (bf16[16,3584]{1,0:T(8,128)(2,1)S(1)}, bf16[16,3584]{1,0:T(8,128)(2,1)S(1)}, u32[]{:S(2)}, u32[]{:S(2)}) collective-permute-start(bf16[16,3584]{1,0:T(8,128)(2,1)S(1)} %get-tuple-element.61), channel_id=1, source_target_pairs={{0,6},{1,7},{2,4},{3,5},{4,2},{5,3},{6,0},{7,1},{8,14},{9,15},{10,... | collective-permute-start | bytes 344072 | tf_op jit(solution)/shard_map/ppermute | solution.py:277
  30.3 7.0 %collective-permute-start.3 = (bf16[16,3584]{1,0:T(8,128)(2,1)S(1)}, bf16[16,3584]{1,0:T(8,128)(2,1)S(1)}, u32[]{:S(2)}, u32[]{:S(2)}) collective-permute-start(bf16[16,3584]{1,0:T(8,128)(2,1)S(1)} %get-tuple-element.62), channel_id=1, source_target_pairs={{0,4},{1,5},{2,6},{3,7},{4,0},{5,1},{6,2},{7,3},{8,12},{9,13},{10,... | collective-permute-start | bytes 344072 | tf_op jit(solution)/shard_map/ppermute | solution.py:277
  31.5 7.3 %collective-permute-start.2 = (bf16[16,3584]{1,0:T(8,128)(2,1)S(1)}, bf16[16,3584]{1,0:T(8,128)(2,1)S(1)}, u32[]{:S(2)}, u32[]{:S(2)}) collective-permute-start(bf16[16,3584]{1,0:T(8,128)(2,1)S(1)} %get-tuple-element.63), channel_id=1, source_target_pairs={{0,2},{1,3},{2,0},{3,1},{4,6},{5,7},{6,4},{7,5},{8,10},{9,11},{10,... | collective-permute-start | bytes 344072 | tf_op jit(solution)/shard_map/ppermute | solution.py:277
  39.0 7.9 %collective-permute-start.4 = (bf16[16,3584]{1,0:T(8,128)(2,1)S(1)}, bf16[16,3584]{1,0:T(8,128)(2,1)S(1)}, u32[]{:S(2)}, u32[]{:S(2)}) collective-permute-start(bf16[16,3584]{1,0:T(8,128)(2,1)S(1)} %convert_element_type.119.refs_4_.kept_ref), channel_id=1, source_target_pairs={{0,8},{1,9},{2,10},{3,11},{4,12},{5,13},{6,14},{7,15},{8,0},{9,1},... | collective-permute-start | bytes 344072 | tf_op jit(solution)/shard_map/ppermute | solution.py:277
  47.0 7.3 %collective-permute-start.7 = (bf16[16,3584]{1,0:T(8,128)(2,1)S(1)}, bf16[16,3584]{1,0:T(8,128)(2,1)S(1)}, u32[]{:S(2)}, u32[]{:S(2)}) collective-permute-start(bf16[16,3584]{1,0:T(8,128)(2,1)S(1)} %bitcast.12), channel_id=1, source_target_pairs={{0,6},{1,7},{2,4},{3,5},{4,2},{5,3},{6,0},{7,1},{8,14},{9,15},{10,... | collective-permute-start | bytes 344072 | tf_op jit(solution)/shard_map/ppermute | solution.py:277
  47.3 7.6 %collective-permute-start.6 = (bf16[16,3584]{1,0:T(8,128)(2,1)S(1)}, bf16[16,3584]{1,0:T(8,128)(2,1)S(1)}, u32[]{:S(2)}, u32[]{:S(2)}) collective-permute-start(bf16[16,3584]{1,0:T(8,128)(2,1)S(1)} %bitcast.13), channel_id=1, source_target_pairs={{0,2},{1,3},{2,0},{3,1},{4,6},{5,7},{6,4},{7,5},{8,10},{9,11},{10,... | collective-permute-start | bytes 344072 | tf_op jit(solution)/shard_map/ppermute | solution.py:277
  48.7 6.3 %collective-permute-start.5 = (bf16[16,3584]{1,0:T(8,128)(2,1)S(1)}, bf16[16,3584]{1,0:T(8,128)(2,1)S(1)}, u32[]{:S(2)}, u32[]{:S(2)}) collective-permute-start(bf16[16,3584]{1,0:T(8,128)(2,1)S(1)} %bitcast.14), channel_id=1, source_target_pairs={{0,4},{1,5},{2,6},{3,7},{4,0},{5,1},{6,2},{7,3},{8,12},{9,13},{10,... | collective-permute-start | bytes 344072 | tf_op jit(solution)/shard_map/ppermute | solution.py:277
  54.3 1.4 %collective-permute-start.8 = (bf16[16,3584]{1,0:T(8,128)(2,1)S(1)}, bf16[16,3584]{1,0:T(8,128)(2,1)S(1)}, u32[]{:S(2)}, u32[]{:S(2)}) collective-permute-start(bf16[16,3584]{1,0:T(8,128)(2,1)S(1)} %get-tuple-element.56.refs_0_), channel_id=1, source_target_pairs={{0,1},{1,0},{2,3},{3,2},{4,5},{5,4},{6,7},{7,6},{8,9},{9,8},{10,11... | collective-permute-start | bytes 344072 | tf_op jit(solution)/shard_map/ppermute | solution.py:277
  54.4 1.5 %collective-permute-start.11 = (bf16[16,3584]{1,0:T(8,128)(2,1)S(1)}, bf16[16,3584]{1,0:T(8,128)(2,1)S(1)}, u32[]{:S(2)}, u32[]{:S(2)}) collective-permute-start(bf16[16,3584]{1,0:T(8,128)(2,1)S(1)} %collective-permute-done.7.refs_3_), channel_id=1, source_target_pairs={{0,1},{1,0},{2,3},{3,2},{4,5},{5,4},{6,7},{7,6},{8,9},{9,8},{10,11... | collective-permute-start | bytes 344072 | tf_op jit(solution)/shard_map/ppermute | solution.py:277
  54.9 1.3 %collective-permute-start.10 = (bf16[16,3584]{1,0:T(8,128)(2,1)S(1)}, bf16[16,3584]{1,0:T(8,128)(2,1)S(1)}, u32[]{:S(2)}, u32[]{:S(2)}) collective-permute-start(bf16[16,3584]{1,0:T(8,128)(2,1)S(1)} %collective-permute-done.6.refs_2_), channel_id=1, source_target_pairs={{0,1},{1,0},{2,3},{3,2},{4,5},{5,4},{6,7},{7,6},{8,9},{9,8},{10,11... | collective-permute-start | bytes 344072 | tf_op jit(solution)/shard_map/ppermute | solution.py:277
  55.0 1.4 %collective-permute-start.9 = (bf16[16,3584]{1,0:T(8,128)(2,1)S(1)}, bf16[16,3584]{1,0:T(8,128)(2,1)S(1)}, u32[]{:S(2)}, u32[]{:S(2)}) collective-permute-start(bf16[16,3584]{1,0:T(8,128)(2,1)S(1)} %collective-permute-done.5.refs_1_), channel_id=1, source_target_pairs={{0,1},{1,0},{2,3},{3,2},{4,5},{5,4},{6,7},{7,6},{8,9},{9,8},{10,11... | collective-permute-start | bytes 344072 | tf_op jit(solution)/shard_map/ppermute | solution.py:277
  64.6 1.6 %collective-permute-start.12 = (bf16[64,1792]{1,0:T(8,128)(2,1)S(1)}, bf16[64,1792]{1,0:T(8,128)(2,1)S(1)}, u32[]{:S(2)}, u32[]{:S(2)}) collective-permute-start(bf16[64,1792]{1,0:T(8,128)(2,1)S(1)} %get-tuple-element.58), channel_id=1, source_target_pairs={{0,1},{1,0},{2,3},{3,2},{4,5},{5,4},{6,7},{7,6},{8,9},{9,8},{10,11... | collective-permute-start | bytes 688136 | tf_op jit(solution)/shard_map/ppermute | solution.py:277
  65.0 4.7 %collective-permute-start.17 = (bf16[64,1792]{1,0:T(8,128)(2,1)S(1)}, bf16[64,1792]{1,0:T(8,128)(2,1)S(1)}, u32[]{:S(2)}, u32[]{:S(2)}) collective-permute-start(bf16[64,1792]{1,0:T(8,128)(2,1)S(1)} %get-tuple-element.60), channel_id=1, source_target_pairs={{0,1},{1,0},{2,3},{3,2},{4,5},{5,4},{6,7},{7,6},{8,9},{9,8},{10,11... | collective-permute-start | bytes 688136 | tf_op jit(solution)/shard_map/ppermute | solution.py:277
  66.2 6.2 %collective-permute-start.13 = (bf16[16,1792]{1,0:T(8,128)(2,1)S(1)}, bf16[16,1792]{1,0:T(8,128)(2,1)S(1)}, u32[]{:S(2)}, u32[]{:S(2)}) collective-permute-start(bf16[16,1792]{1,0:T(8,128)(2,1)S(1)} %get-tuple-element.64), channel_id=1, source_target_pairs={{0,6},{1,7},{2,4},{3,5},{4,2},{5,3},{6,0},{7,1},{8,14},{9,15},{10,... | collective-permute-start | bytes 172040 | tf_op jit(solution)/shard_map/ppermute | solution.py:277
  67.2 6.2 %collective-permute-start.15 = (bf16[16,1792]{1,0:T(8,128)(2,1)S(1)}, bf16[16,1792]{1,0:T(8,128)(2,1)S(1)}, u32[]{:S(2)}, u32[]{:S(2)}) collective-permute-start(bf16[16,1792]{1,0:T(8,128)(2,1)S(1)} %get-tuple-element.65), channel_id=1, source_target_pairs={{0,4},{1,5},{2,6},{3,7},{4,0},{5,1},{6,2},{7,3},{8,12},{9,13},{10,... | collective-permute-start | bytes 172040 | tf_op jit(solution)/shard_map/ppermute | solution.py:277
  68.8 4.8 %collective-permute-start.14 = (bf16[16,1792]{1,0:T(8,128)(2,1)S(1)}, bf16[16,1792]{1,0:T(8,128)(2,1)S(1)}, u32[]{:S(2)}, u32[]{:S(2)}) collective-permute-start(bf16[16,1792]{1,0:T(8,128)(2,1)S(1)} %get-tuple-element.66), channel_id=1, source_target_pairs={{0,2},{1,3},{2,0},{3,1},{4,6},{5,7},{6,4},{7,5},{8,10},{9,11},{10,... | collective-permute-start | bytes 172040 | tf_op jit(solution)/shard_map/ppermute | solution.py:277
  69.8 5.6 %collective-permute-start.18 = (bf16[16,1792]{1,0:T(8,128)(2,1)S(1)}, bf16[16,1792]{1,0:T(8,128)(2,1)S(1)}, u32[]{:S(2)}, u32[]{:S(2)}) collective-permute-start(bf16[16,1792]{1,0:T(8,128)(2,1)S(1)} %get-tuple-element.67), channel_id=1, source_target_pairs={{0,6},{1,7},{2,4},{3,5},{4,2},{5,3},{6,0},{7,1},{8,14},{9,15},{10,... | collective-permute-start | bytes 172040 | tf_op jit(solution)/shard_map/ppermute | solution.py:277
  70.8 4.6 %collective-permute-start.20 = (bf16[16,1792]{1,0:T(8,128)(2,1)S(1)}, bf16[16,1792]{1,0:T(8,128)(2,1)S(1)}, u32[]{:S(2)}, u32[]{:S(2)}) collective-permute-start(bf16[16,1792]{1,0:T(8,128)(2,1)S(1)} %get-tuple-element.68), channel_id=1, source_target_pairs={{0,4},{1,5},{2,6},{3,7},{4,0},{5,1},{6,2},{7,3},{8,12},{9,13},{10,... | collective-permute-start | bytes 172040 | tf_op jit(solution)/shard_map/ppermute | solution.py:277
  72.4 4.2 %collective-permute-start.19 = (bf16[16,1792]{1,0:T(8,128)(2,1)S(1)}, bf16[16,1792]{1,0:T(8,128)(2,1)S(1)}, u32[]{:S(2)}, u32[]{:S(2)}) collective-permute-start(bf16[16,1792]{1,0:T(8,128)(2,1)S(1)} %get-tuple-element.69), channel_id=1, source_target_pairs={{0,2},{1,3},{2,0},{3,1},{4,6},{5,7},{6,4},{7,5},{8,10},{9,11},{10,... | collective-permute-start | bytes 172040 | tf_op jit(solution)/shard_map/ppermute | solution.py:277
  73.7 5.6 %collective-permute-start.16 = (bf16[8,1792]{1,0:T(8,128)(2,1)S(1)}, bf16[8,1792]{1,0:T(8,128)(2,1)S(1)}, u32[]{:S(2)}, u32[]{:S(2)}) collective-permute-start(bf16[8,1792]{1,0:T(8,128)(2,1)S(1)} %slice.183), channel_id=1, source_target_pairs={{0,8},{1,9},{2,10},{3,11},{4,12},{5,13},{6,14},{7,15},{8,0},{9,1},... | collective-permute-start | bytes 86024 | tf_op jit(solution)/shard_map/ppermute | solution.py:277
  76.7 5.0 %collective-permute-start.21 = (bf16[8,1792]{1,0:T(8,128)(2,1)S(1)}, bf16[8,1792]{1,0:T(8,128)(2,1)S(1)}, u32[]{:S(2)}, u32[]{:S(2)}) collective-permute-start(bf16[8,1792]{1,0:T(8,128)(2,1)S(1)} %slice.182), channel_id=1, source_target_pairs={{0,8},{1,9},{2,10},{3,11},{4,12},{5,13},{6,14},{7,15},{8,0},{9,1},... | collective-permute-start | bytes 86024 | tf_op jit(solution)/shard_map/ppermute | solution.py:277

commit v11 on v10

--- a/solution.py
+++ b/solution.py
@@ -277,9 +277,15 @@
         return lax.ppermute(x, "ep", [(i, i ^ bit) for i in range(size)])
 
     def sum_nearest(kept, arrived):
-        quarter = kept.shape[0] // 4
+        quarter = kept[0].shape[0] // 4
         parts = [
-            kept[at : at + quarter] + arrived[at : at + quarter].astype(F32)
+            jnp.concatenate(
+                [
+                    mine[at : at + quarter] + theirs[at : at + quarter].astype(F32)
+                    for mine, theirs in zip(kept, arrived)
+                ],
+                axis=1,
+            )
             for at in range(0, 4 * quarter, quarter)
         ]
         kept = parts[0]
@@ -305,7 +311,7 @@
     sent, other_gates = project(other_place, head_rows, output_held, BF16)
     arrived = swap(sent, 1)
     kept, own_gates = project(place, head_rows, output_held, F32)
-    kept = sum_nearest(kept, arrived)
+    kept = sum_nearest([kept], [arrived])
     summed = kept.at[:tok].add(residual_held.astype(F32)).astype(BF16)
     bit = chips
     units = gate_weight.shape[0]
@@ -328,11 +334,9 @@
     pieces = pieces + [swap(piece, 1) for piece in pieces]
     held = (first_held, second_held, up_held, low_held, middle_held)
     results = experts(pieces, (own_gates, other_gates), held, down_weight)
-    combined = []
-    for kept, sent in (results[:2], results[2:]):
-        kept = sum_nearest(kept, swap(sent, 1))
-        combined.append(kept[:tok] + swap(kept[tok:].astype(BF16), chips).astype(F32))
-    return (middle + jnp.concatenate(combined, axis=1)).astype(BF16)
+    kept = sum_nearest(results[::2], [swap(sent, 1) for sent in results[1::2]])
+    combined = kept[:tok] + swap(kept[tok:].astype(BF16), chips).astype(F32)
+    return (middle + combined).astype(BF16)
 
 
 def solution(mesh):

time: 82.6 us -> 82.3 us (level)
  starting transfers between devices: 30.4 us -> 25.5 us
  waiting for transfers between devices: 23.9 us -> 28.4 us
    ppermute x22 -> x18, starting transfers between devices: 19.5 us -> 14.6 us  [swap(): return lax.ppermute(x, 'ep', [(i, i ^ bit) for i in range(size)])]
    ppermute x22 -> x18, waiting for transfers between devices: 13.6 us -> 18.1 us  [swap(): return lax.ppermute(x, 'ep', [(i, i ^ bit) for i in range(size)])]
  transfers between devices with their start and end apart: 24 -> 20, of which waited for: 16 -> 17; matrix products, arithmetic and copies ran while one was open for 1% -> 1% of each run, Pallas kernels for 18% -> 18%
where the time goes in v11:
time: 82.3 us; the launch traced here: 82 us
  waiting for transfers between devices  28.4 us (35%)
  Pallas kernels  26.1 us (32%)
  starting transfers between devices  25.5 us (31%)
  other arithmetic  1.74 us (2%)
    ppermute x18, waiting for transfers between devices, swap(): return lax.ppermute(x, 'ep', [(i, i ^ bit) for i in range(size)])  18.1 us
    ppermute x18, starting transfers between devices, swap(): return lax.ppermute(x, 'ep', [(i, i ^ bit) for i in range(size)])  14.6 us
    pallas_call x4, Pallas kernels, fetch(): pl.pallas_call(functools.partial(fetch_kernel, count, carried, ranges), o...  13.6 us
    pallas_call x1, Pallas kernels, experts(): pl.pallas_call(expert_kernel, out_shape=(jax.ShapeDtypeStruct((half, feat...  8.2 us
    all_to_all x1, starting transfers between devices, local(): lax.all_to_all(queries.reshape(size, tok, head_dim), 'ep', split_axis=0,...  7.38 us
    all_to_all x1, waiting for transfers between devices, local(): lax.all_to_all(attended, 'ep', split_axis=0, concat_axis=0, tiled=True)  5.76 us
    all_to_all x1, waiting for transfers between devices, local(): lax.all_to_all(queries.reshape(size, tok, head_dim), 'ep', split_axis=0,...  4.56 us
    all_to_all x1, starting transfers between devices, local(): lax.all_to_all(attended, 'ep', split_axis=0, concat_axis=0, tiled=True)  3.51 us
  transfers between devices with their start and end apart: 20, of which 17 were waited for; matrix products, arithmetic and copies ran while one was open for 1% of the time, Pallas kernels for 18%

profile of v11, /device:TPU:0, one launch (start us, length us, event | category | flops | bytes accessed | tf_op | source)
XLA Modules:
  0.0 82.0 jit_solution(14128898409982441436)
XLA Ops:
  0.0 7.4 %all-to-all-start = ((bf16[16,8,256]{2,1,0:T(8,128)(2,1)}), bf16[16,8,256]{2,1,0:T(8,128)(2,1)S(1)}, u32[]{:S(2)}, u32[]{:S(2)}) async-start(bf16[16,8,256]{2,1,0:T(8,128)(2,1)} %bitcast.17), calls=%async_computation | async-start | bytes 131072 | tf_op jit(solution)/shard_map/all_to_all | solution.py:304
  7.4 1.6 %shard_map.109 = (bf16[8,256,512]{2,1,0:T(8,128)(2,1)S(1)}, bf16[8,3584]{1,0:T(8,128)(2,1)S(1)}, f32[3584]{0:T(1024)S(1)}, s32[8]{0:T(128)S(1)}, s32[3,8]{1,0:T(4,128)S(1)}) custom-call(bf16[8,256,512]{2,1,0:T(8,128)(2,1)} %refs_0_.4, bf16[8,3584]{1,0:T(8,128)(2,1)} %refs_1_.3, f32[3584]{0:T(1024)} %refs_2_.2, s32[8]{0:T(128)} %refs_3_.1, s32[3,8]{1,0:T(4,128)} %bitcast.18), custom_call_target="tpu_custom_call" | custom-call | bytes 2161728 | tf_op jit(solution)/shard_map/pallas_call | solution.py:47
  9.0 0.7 convert_bitcast_fusion.shares_ref
  9.7 4.6 %all-to-all-done.query_ref = bf16[16,8,256]{2,1,0:T(8,128)(2,1)S(1)} async-done(((bf16[16,8,256]{2,1,0:T(8,128)(2,1)}), bf16[16,8,256]{2,1,0:T(8,128)(2,1)S(1)}, u32[]{:S(2)}, u32[]{:S(2)}) %all-to-all-start) | async-done | bytes 65568 | tf_op jit(solution)/shard_map/all_to_all | solution.py:304
  14.3 2.2 %shard_map.110.refs_1_ = bf16[16,8,384]{2,1,0:T(8,128)(2,1)} custom-call(s32[8]{0:T(128)S(1)} %get-tuple-element.39.lengths_ref, s32[3,8]{1,0:T(4,128)S(1)} %get-tuple-element.40.routes_ref, f32[3,8]{1,0:T(4,128)S(1)} %convert_bitcast_fusion.shares_ref, bf16[16,8,256]{2,1,0:T(8,128)(2,1)S(1)} %all-to-all-done.query_ref, ...), custom_call_target="tpu_custom_call" | custom-call | tf_op jit(solution)/shard_map/pallas_call | solution.py:100
  16.5 3.5 %all-to-all-start.1 = ((bf16[16,8,384]{2,1,0:T(8,128)(2,1)}), bf16[16,8,384]{2,1,0:T(8,128)(2,1)S(1)}, u32[]{:S(2)}, u32[]{:S(2)}) async-start(bf16[16,8,384]{2,1,0:T(8,128)(2,1)} %shard_map.110.refs_1_), calls=%async_computation.1 | async-start | bytes 196608 | tf_op jit(solution)/shard_map/all_to_all | solution.py:309
  20.0 0.1 pad_add_fusion
  20.1 1.5 %shard_map.111.weight_ref = bf16[256,3584]{1,0:T(8,128)(2,1)S(1)} custom-call(bf16[256,3584]{1,0:T(8,128)(2,1)} %refs_0_.5, bf16[16,8,384]{2,1,0:T(8,128)(2,1)} %shard_map.110.refs_1_), custom_call_target="tpu_custom_call" | custom-call | bytes 1835008 | tf_op jit(solution)/shard_map/pallas_call | solution.py:47
  21.6 5.8 %all-to-all-done.1 = bf16[16,8,384]{2,1,0:T(8,128)(2,1)S(1)} async-done(((bf16[16,8,384]{2,1,0:T(8,128)(2,1)}), bf16[16,8,384]{2,1,0:T(8,128)(2,1)S(1)}, u32[]{:S(2)}, u32[]{:S(2)}) %all-to-all-start.1) | async-done | bytes 98336 | tf_op jit(solution)/shard_map/all_to_all | solution.py:309
  27.3 1.0 %shard_map.113 = (bf16[64,3584]{1,0:T(8,128)(2,1)S(1)}, bf16[64,128]{1,0:T(8,128)(2,1)S(1)}) custom-call(s32[2]{0:T(128)S(1)} %get-tuple-element.73.place_ref, bf16[8,2,8,384]{3,2,1,0:T(8,128)(2,1)S(1)} %bitcast.10, bf16[256,3584]{1,0:T(8,128)(2,1)S(1)} %shard_map.111.weight_ref), custom_call_target="tpu_custom_call" | custom-call | flops 117440512 | bytes 1835008 | tf_op jit(solution)/shard_map/pallas_call | solution.py:133
  28.4 1.0 %shard_map.112 = (f32[64,3584]{1,0:T(8,128)S(1)}, bf16[64,128]{1,0:T(8,128)(2,1)S(1)}) custom-call(s32[2]{0:T(128)S(1)} %get-tuple-element.72.place_ref, bf16[8,2,8,384]{3,2,1,0:T(8,128)(2,1)S(1)} %bitcast.11, bf16[256,3584]{1,0:T(8,128)(2,1)S(1)} %shard_map.111.weight_ref), custom_call_target="tpu_custom_call" | custom-call | flops 117440512 | bytes 1835008 | tf_op jit(solution)/shard_map/pallas_call | solution.py:133
  29.4 0.8 collective-permute-done
  30.3 0.1 collective-permute-start.1
  30.3 1.2 %collective-permute-start.3 = (bf16[16,3584]{1,0:T(8,128)(2,1)S(1)}, bf16[16,3584]{1,0:T(8,128)(2,1)S(1)}, u32[]{:S(2)}, u32[]{:S(2)}) collective-permute-start(bf16[16,3584]{1,0:T(8,128)(2,1)S(1)} %get-tuple-element.62), channel_id=1, source_target_pairs={{0,4},{1,5},{2,6},{3,7},{4,0},{5,1},{6,2},{7,3},{8,12},{9,13},{10,... | collective-permute-start | bytes 344072 | tf_op jit(solution)/shard_map/ppermute | solution.py:277
  31.5 2.3 %collective-permute-start.2 = (bf16[16,3584]{1,0:T(8,128)(2,1)S(1)}, bf16[16,3584]{1,0:T(8,128)(2,1)S(1)}, u32[]{:S(2)}, u32[]{:S(2)}) collective-permute-start(bf16[16,3584]{1,0:T(8,128)(2,1)S(1)} %get-tuple-element.63), channel_id=1, source_target_pairs={{0,2},{1,3},{2,0},{3,1},{4,6},{5,7},{6,4},{7,5},{8,10},{9,11},{10,... | collective-permute-start | bytes 344072 | tf_op jit(solution)/shard_map/ppermute | solution.py:277
  33.8 3.4 %collective-permute-done.1 = bf16[16,3584]{1,0:T(8,128)(2,1)S(1)} collective-permute-done((bf16[16,3584]{1,0:T(8,128)(2,1)S(1)}, bf16[16,3584]{1,0:T(8,128)(2,1)S(1)}, u32[]{:S(2)}, u32[]{:S(2)}) %collective-permute-start.1) | collective-permute-done | bytes 114720 | tf_op jit(solution)/shard_map/ppermute | solution.py:277
  37.2 0.2 collective-permute-done.3
  37.4 1.5 %collective-permute-done.2 = bf16[16,3584]{1,0:T(8,128)(2,1)S(1)} collective-permute-done((bf16[16,3584]{1,0:T(8,128)(2,1)S(1)}, bf16[16,3584]{1,0:T(8,128)(2,1)S(1)}, u32[]{:S(2)}, u32[]{:S(2)}) %collective-permute-start.2) | collective-permute-done | bytes 114720 | tf_op jit(solution)/shard_map/ppermute | solution.py:277
  39.0 0.2 collective-permute-start.4
  39.2 6.8 %shard_map.114 = (bf16[1536,3584]{1,0:T(8,128)(2,1)S(1)}, bf16[768,3584]{1,0:T(8,128)(2,1)S(1)}, bf16[512,3584]{1,0:T(8,128)(2,1)S(1)}, f32[3584]{0:T(1024)S(1)}) custom-call(bf16[1536,3584]{1,0:T(8,128)(2,1)} %refs_0_.6, bf16[1536,3584]{1,0:T(8,128)(2,1)} %refs_0_.7, bf16[1536,3584]{1,0:T(8,128)(2,1)} %down_source.1, f32[3584]{0:T(1024)S(1)} %get-tuple-element.45.refs_3_, ...), custom_call_target="tpu_custom_call" | custom-call | bytes 33030144 | tf_op jit(solution)/shard_map/pallas_call | solution.py:47
  46.0 0.9 %collective-permute-done.4 = bf16[16,3584]{1,0:T(8,128)(2,1)S(1)} collective-permute-done((bf16[16,3584]{1,0:T(8,128)(2,1)S(1)}, bf16[16,3584]{1,0:T(8,128)(2,1)S(1)}, u32[]{:S(2)}, u32[]{:S(2)}) %collective-permute-start.4) | collective-permute-done | bytes 114720 | tf_op jit(solution)/shard_map/ppermute | solution.py:277
  46.9 0.1 shard_map.115
  47.0 0.3 collective-permute-start.7
  47.3 1.3 %collective-permute-start.6 = (bf16[16,3584]{1,0:T(8,128)(2,1)S(1)}, bf16[16,3584]{1,0:T(8,128)(2,1)S(1)}, u32[]{:S(2)}, u32[]{:S(2)}) collective-permute-start(bf16[16,3584]{1,0:T(8,128)(2,1)S(1)} %bitcast.13), channel_id=1, source_target_pairs={{0,2},{1,3},{2,0},{3,1},{4,6},{5,7},{6,4},{7,5},{8,10},{9,11},{10,... | collective-permute-start | bytes 344072 | tf_op jit(solution)/shard_map/ppermute | solution.py:277
  48.7 1.9 %collective-permute-start.5 = (bf16[16,3584]{1,0:T(8,128)(2,1)S(1)}, bf16[16,3584]{1,0:T(8,128)(2,1)S(1)}, u32[]{:S(2)}, u32[]{:S(2)}) collective-permute-start(bf16[16,3584]{1,0:T(8,128)(2,1)S(1)} %bitcast.14), channel_id=1, source_target_pairs={{0,4},{1,5},{2,6},{3,7},{4,0},{5,1},{6,2},{7,3},{8,12},{9,13},{10,... | collective-permute-start | bytes 344072 | tf_op jit(solution)/shard_map/ppermute | solution.py:277
  50.6 3.7 %shard_map.116 = (bf16[768,3584]{1,0:T(8,128)(2,1)S(1)}, bf16[512,3584]{1,0:T(8,128)(2,1)S(1)}, bf16[16,3584]{1,0:T(8,128)(2,1)S(1)}) custom-call(bf16[1536,3584]{1,0:T(8,128)(2,1)} %refs_0_.7, bf16[1536,3584]{1,0:T(8,128)(2,1)} %down_source.1, bf16[16,3584]{1,0:T(8,128)(2,1)S(1)} %bitcast.15), custom_call_target="tpu_custom_call" | custom-call | bytes 22020096 | tf_op jit(solution)/shard_map/pallas_call | solution.py:47
  54.3 0.1 collective-permute-start.8
  54.4 0.5 collective-permute-start.11
  54.9 0.1 collective-permute-start.10
  55.0 0.4 collective-permute-start.9
  55.4 0.3 collective-permute-done.8.refs_4_
  55.7 0.2 collective-permute-done.11.refs_7_
  55.9 0.4 collective-permute-done.10.refs_6_
  56.2 0.2 collective-permute-done.9.refs_5_
  56.4 8.2 %shard_map.117 = (f32[64,1792]{1,0:T(8,128)S(1)}, bf16[64,1792]{1,0:T(8,128)(2,1)S(1)}, f32[64,1792]{1,0:T(8,128)S(1)}, bf16[64,1792]{1,0:T(8,128)(2,1)S(1)}) custom-call(bf16[64,128]{1,0:T(8,128)(2,1)S(1)} %get-tuple-element.48.own_gates_ref, bf16[64,128]{1,0:T(8,128)(2,1)S(1)} %get-tuple-element.49.other_gates_ref, ...), custom_call_target="tpu_custom_call" | custom-call | flops 4227858432 | bytes 33030144 | tf_op jit(solution)/shard_map/pallas_call | solution.py:226
  64.6 0.4 collective-permute-start.12
  65.0 0.2 collective-permute-start.13
  65.2 1.0 %collective-permute-done.12 = bf16[64,1792]{1,0:T(8,128)(2,1)S(1)} collective-permute-done((bf16[64,1792]{1,0:T(8,128)(2,1)S(1)}, bf16[64,1792]{1,0:T(8,128)(2,1)S(1)}, u32[]{:S(2)}, u32[]{:S(2)}) %collective-permute-start.12) | collective-permute-done | bytes 229408 | tf_op jit(solution)/shard_map/ppermute | solution.py:277
  66.2 0.3 collective-permute-done.13
  66.6 1.2 %collective-permute-start.15 = (bf16[16,3584]{1,0:T(8,128)(2,1)S(1)}, bf16[16,3584]{1,0:T(8,128)(2,1)S(1)}, u32[]{:S(2)}, u32[]{:S(2)}) collective-permute-start(bf16[16,3584]{1,0:T(8,128)(2,1)S(1)} %pad_maximum_fusion.1), channel_id=1, source_target_pairs={{0,2},{1,3},{2,0},{3,1},{4,6},{5,7},{6,4},{7,5},{8,10},{9,11},{10,... | collective-permute-start | bytes 344072 | tf_op jit(solution)/shard_map/ppermute | solution.py:277
  67.7 0.5 collective-permute-start.16
  68.2 2.0 %collective-permute-start.14 = (bf16[16,3584]{1,0:T(8,128)(2,1)S(1)}, bf16[16,3584]{1,0:T(8,128)(2,1)S(1)}, u32[]{:S(2)}, u32[]{:S(2)}) collective-permute-start(bf16[16,3584]{1,0:T(8,128)(2,1)S(1)} %pad_maximum_fusion), channel_id=1, source_target_pairs={{0,6},{1,7},{2,4},{3,5},{4,2},{5,3},{6,0},{7,1},{8,14},{9,15},{10,... | collective-permute-start | bytes 344072 | tf_op jit(solution)/shard_map/ppermute | solution.py:277
  70.3 1.7 %collective-permute-done.15 = bf16[16,3584]{1,0:T(8,128)(2,1)S(1)} collective-permute-done((bf16[16,3584]{1,0:T(8,128)(2,1)S(1)}, bf16[16,3584]{1,0:T(8,128)(2,1)S(1)}, u32[]{:S(2)}, u32[]{:S(2)}) %collective-permute-start.15) | collective-permute-done | bytes 114720 | tf_op jit(solution)/shard_map/ppermute | solution.py:277
  72.0 1.8 %collective-permute-done.16 = bf16[16,3584]{1,0:T(8,128)(2,1)S(1)} collective-permute-done((bf16[16,3584]{1,0:T(8,128)(2,1)S(1)}, bf16[16,3584]{1,0:T(8,128)(2,1)S(1)}, u32[]{:S(2)}, u32[]{:S(2)}) %collective-permute-start.16) | collective-permute-done | bytes 114720 | tf_op jit(solution)/shard_map/ppermute | solution.py:277
  73.8 1.9 %collective-permute-done.14 = bf16[16,3584]{1,0:T(8,128)(2,1)S(1)} collective-permute-done((bf16[16,3584]{1,0:T(8,128)(2,1)S(1)}, bf16[16,3584]{1,0:T(8,128)(2,1)S(1)}, u32[]{:S(2)}, u32[]{:S(2)}) %collective-permute-start.14) | collective-permute-done | bytes 114720 | tf_op jit(solution)/shard_map/ppermute | solution.py:277
  75.8 1.9 %collective-permute-start.17 = (bf16[8,3584]{1,0:T(8,128)(2,1)S(1)}, bf16[8,3584]{1,0:T(8,128)(2,1)S(1)}, u32[]{:S(2)}, u32[]{:S(2)}) collective-permute-start(bf16[8,3584]{1,0:T(8,128)(2,1)S(1)} %slice.173), channel_id=1, source_target_pairs={{0,8},{1,9},{2,10},{3,11},{4,12},{5,13},{6,14},{7,15},{8,0},{9,1},... | collective-permute-start | bytes 172040 | tf_op jit(solution)/shard_map/ppermute | solution.py:277
  77.7 3.6 %collective-permute-done.17 = bf16[8,3584]{1,0:T(8,128)(2,1)S(1)} collective-permute-done((bf16[8,3584]{1,0:T(8,128)(2,1)S(1)}, bf16[8,3584]{1,0:T(8,128)(2,1)S(1)}, u32[]{:S(2)}, u32[]{:S(2)}) %collective-permute-start.17) | collective-permute-done | bytes 57376 | tf_op jit(solution)/shard_map/ppermute | solution.py:277
  81.3 0.6 fusion.3
  (15 shorter events, 0.4 us)
Async XLA Ops:
  0.0 14.3 %all-to-all-start = ((bf16[16,8,256]{2,1,0:T(8,128)(2,1)}), bf16[16,8,256]{2,1,0:T(8,128)(2,1)S(1)}, u32[]{:S(2)}, u32[]{:S(2)}) async-start(bf16[16,8,256]{2,1,0:T(8,128)(2,1)} %bitcast.17), calls=%async_computation | async-start | bytes 131072 | tf_op jit(solution)/shard_map/all_to_all | solution.py:304
  16.5 10.9 %all-to-all-start.1 = ((bf16[16,8,384]{2,1,0:T(8,128)(2,1)}), bf16[16,8,384]{2,1,0:T(8,128)(2,1)S(1)}, u32[]{:S(2)}, u32[]{:S(2)}) async-start(bf16[16,8,384]{2,1,0:T(8,128)(2,1)} %shard_map.110.refs_1_), calls=%async_computation.1 | async-start | bytes 196608 | tf_op jit(solution)/shard_map/all_to_all | solution.py:309
  28.3 1.9 %collective-permute-start = (bf16[64,3584]{1,0:T(8,128)(2,1)S(1)}, bf16[64,3584]{1,0:T(8,128)(2,1)S(1)}, u32[]{:S(2)}, u32[]{:S(2)}) collective-permute-start(bf16[64,3584]{1,0:T(8,128)(2,1)S(1)} %get-tuple-element.43), channel_id=1, source_target_pairs={{0,1},{1,0},{2,3},{3,2},{4,5},{5,4},{6,7},{7,6},{8,9},{9,8},{10,11... | collective-permute-start | bytes 1376264 | tf_op jit(solution)/shard_map/ppermute | solution.py:277
  30.3 7.0 %collective-permute-start.1 = (bf16[16,3584]{1,0:T(8,128)(2,1)S(1)}, bf16[16,3584]{1,0:T(8,128)(2,1)S(1)}, u32[]{:S(2)}, u32[]{:S(2)}) collective-permute-start(bf16[16,3584]{1,0:T(8,128)(2,1)S(1)} %get-tuple-element.61), channel_id=1, source_target_pairs={{0,6},{1,7},{2,4},{3,5},{4,2},{5,3},{6,0},{7,1},{8,14},{9,15},{10,... | collective-permute-start | bytes 344072 | tf_op jit(solution)/shard_map/ppermute | solution.py:277
  30.3 7.0 %collective-permute-start.3 = (bf16[16,3584]{1,0:T(8,128)(2,1)S(1)}, bf16[16,3584]{1,0:T(8,128)(2,1)S(1)}, u32[]{:S(2)}, u32[]{:S(2)}) collective-permute-start(bf16[16,3584]{1,0:T(8,128)(2,1)S(1)} %get-tuple-element.62), channel_id=1, source_target_pairs={{0,4},{1,5},{2,6},{3,7},{4,0},{5,1},{6,2},{7,3},{8,12},{9,13},{10,... | collective-permute-start | bytes 344072 | tf_op jit(solution)/shard_map/ppermute | solution.py:277
  31.5 7.3 %collective-permute-start.2 = (bf16[16,3584]{1,0:T(8,128)(2,1)S(1)}, bf16[16,3584]{1,0:T(8,128)(2,1)S(1)}, u32[]{:S(2)}, u32[]{:S(2)}) collective-permute-start(bf16[16,3584]{1,0:T(8,128)(2,1)S(1)} %get-tuple-element.63), channel_id=1, source_target_pairs={{0,2},{1,3},{2,0},{3,1},{4,6},{5,7},{6,4},{7,5},{8,10},{9,11},{10,... | collective-permute-start | bytes 344072 | tf_op jit(solution)/shard_map/ppermute | solution.py:277
  39.0 7.9 %collective-permute-start.4 = (bf16[16,3584]{1,0:T(8,128)(2,1)S(1)}, bf16[16,3584]{1,0:T(8,128)(2,1)S(1)}, u32[]{:S(2)}, u32[]{:S(2)}) collective-permute-start(bf16[16,3584]{1,0:T(8,128)(2,1)S(1)} %convert_element_type.91.refs_4_.kept_ref), channel_id=1, source_target_pairs={{0,8},{1,9},{2,10},{3,11},{4,12},{5,13},{6,14},{7,15},{8,0},{9,1},... | collective-permute-start | bytes 344072 | tf_op jit(solution)/shard_map/ppermute | solution.py:277
  47.0 7.3 %collective-permute-start.7 = (bf16[16,3584]{1,0:T(8,128)(2,1)S(1)}, bf16[16,3584]{1,0:T(8,128)(2,1)S(1)}, u32[]{:S(2)}, u32[]{:S(2)}) collective-permute-start(bf16[16,3584]{1,0:T(8,128)(2,1)S(1)} %bitcast.12), channel_id=1, source_target_pairs={{0,6},{1,7},{2,4},{3,5},{4,2},{5,3},{6,0},{7,1},{8,14},{9,15},{10,... | collective-permute-start | bytes 344072 | tf_op jit(solution)/shard_map/ppermute | solution.py:277
  47.3 7.6 %collective-permute-start.6 = (bf16[16,3584]{1,0:T(8,128)(2,1)S(1)}, bf16[16,3584]{1,0:T(8,128)(2,1)S(1)}, u32[]{:S(2)}, u32[]{:S(2)}) collective-permute-start(bf16[16,3584]{1,0:T(8,128)(2,1)S(1)} %bitcast.13), channel_id=1, source_target_pairs={{0,2},{1,3},{2,0},{3,1},{4,6},{5,7},{6,4},{7,5},{8,10},{9,11},{10,... | collective-permute-start | bytes 344072 | tf_op jit(solution)/shard_map/ppermute | solution.py:277
  48.7 6.3 %collective-permute-start.5 = (bf16[16,3584]{1,0:T(8,128)(2,1)S(1)}, bf16[16,3584]{1,0:T(8,128)(2,1)S(1)}, u32[]{:S(2)}, u32[]{:S(2)}) collective-permute-start(bf16[16,3584]{1,0:T(8,128)(2,1)S(1)} %bitcast.14), channel_id=1, source_target_pairs={{0,4},{1,5},{2,6},{3,7},{4,0},{5,1},{6,2},{7,3},{8,12},{9,13},{10,... | collective-permute-start | bytes 344072 | tf_op jit(solution)/shard_map/ppermute | solution.py:277
  54.3 1.4 %collective-permute-start.8 = (bf16[16,3584]{1,0:T(8,128)(2,1)S(1)}, bf16[16,3584]{1,0:T(8,128)(2,1)S(1)}, u32[]{:S(2)}, u32[]{:S(2)}) collective-permute-start(bf16[16,3584]{1,0:T(8,128)(2,1)S(1)} %get-tuple-element.56.refs_0_), channel_id=1, source_target_pairs={{0,1},{1,0},{2,3},{3,2},{4,5},{5,4},{6,7},{7,6},{8,9},{9,8},{10,11... | collective-permute-start | bytes 344072 | tf_op jit(solution)/shard_map/ppermute | solution.py:277
  54.4 1.5 %collective-permute-start.11 = (bf16[16,3584]{1,0:T(8,128)(2,1)S(1)}, bf16[16,3584]{1,0:T(8,128)(2,1)S(1)}, u32[]{:S(2)}, u32[]{:S(2)}) collective-permute-start(bf16[16,3584]{1,0:T(8,128)(2,1)S(1)} %collective-permute-done.7.refs_3_), channel_id=1, source_target_pairs={{0,1},{1,0},{2,3},{3,2},{4,5},{5,4},{6,7},{7,6},{8,9},{9,8},{10,11... | collective-permute-start | bytes 344072 | tf_op jit(solution)/shard_map/ppermute | solution.py:277
  54.9 1.3 %collective-permute-start.10 = (bf16[16,3584]{1,0:T(8,128)(2,1)S(1)}, bf16[16,3584]{1,0:T(8,128)(2,1)S(1)}, u32[]{:S(2)}, u32[]{:S(2)}) collective-permute-start(bf16[16,3584]{1,0:T(8,128)(2,1)S(1)} %collective-permute-done.6.refs_2_), channel_id=1, source_target_pairs={{0,1},{1,0},{2,3},{3,2},{4,5},{5,4},{6,7},{7,6},{8,9},{9,8},{10,11... | collective-permute-start | bytes 344072 | tf_op jit(solution)/shard_map/ppermute | solution.py:277
  55.0 1.4 %collective-permute-start.9 = (bf16[16,3584]{1,0:T(8,128)(2,1)S(1)}, bf16[16,3584]{1,0:T(8,128)(2,1)S(1)}, u32[]{:S(2)}, u32[]{:S(2)}) collective-permute-start(bf16[16,3584]{1,0:T(8,128)(2,1)S(1)} %collective-permute-done.5.refs_1_), channel_id=1, source_target_pairs={{0,1},{1,0},{2,3},{3,2},{4,5},{5,4},{6,7},{7,6},{8,9},{9,8},{10,11... | collective-permute-start | bytes 344072 | tf_op jit(solution)/shard_map/ppermute | solution.py:277
  64.6 1.6 %collective-permute-start.12 = (bf16[64,1792]{1,0:T(8,128)(2,1)S(1)}, bf16[64,1792]{1,0:T(8,128)(2,1)S(1)}, u32[]{:S(2)}, u32[]{:S(2)}) collective-permute-start(bf16[64,1792]{1,0:T(8,128)(2,1)S(1)} %get-tuple-element.58), channel_id=1, source_target_pairs={{0,1},{1,0},{2,3},{3,2},{4,5},{5,4},{6,7},{7,6},{8,9},{9,8},{10,11... | collective-permute-start | bytes 688136 | tf_op jit(solution)/shard_map/ppermute | solution.py:277
  65.0 1.5 %collective-permute-start.13 = (bf16[64,1792]{1,0:T(8,128)(2,1)S(1)}, bf16[64,1792]{1,0:T(8,128)(2,1)S(1)}, u32[]{:S(2)}, u32[]{:S(2)}) collective-permute-start(bf16[64,1792]{1,0:T(8,128)(2,1)S(1)} %get-tuple-element.60), channel_id=1, source_target_pairs={{0,1},{1,0},{2,3},{3,2},{4,5},{5,4},{6,7},{7,6},{8,9},{9,8},{10,11... | collective-permute-start | bytes 688136 | tf_op jit(solution)/shard_map/ppermute | solution.py:277
  66.6 5.4 %collective-permute-start.15 = (bf16[16,3584]{1,0:T(8,128)(2,1)S(1)}, bf16[16,3584]{1,0:T(8,128)(2,1)S(1)}, u32[]{:S(2)}, u32[]{:S(2)}) collective-permute-start(bf16[16,3584]{1,0:T(8,128)(2,1)S(1)} %pad_maximum_fusion.1), channel_id=1, source_target_pairs={{0,2},{1,3},{2,0},{3,1},{4,6},{5,7},{6,4},{7,5},{8,10},{9,11},{10,... | collective-permute-start | bytes 344072 | tf_op jit(solution)/shard_map/ppermute | solution.py:277
  67.7 6.1 %collective-permute-start.16 = (bf16[16,3584]{1,0:T(8,128)(2,1)S(1)}, bf16[16,3584]{1,0:T(8,128)(2,1)S(1)}, u32[]{:S(2)}, u32[]{:S(2)}) collective-permute-start(bf16[16,3584]{1,0:T(8,128)(2,1)S(1)} %pad_maximum_fusion.2), channel_id=1, source_target_pairs={{0,4},{1,5},{2,6},{3,7},{4,0},{5,1},{6,2},{7,3},{8,12},{9,13},{10,... | collective-permute-start | bytes 344072 | tf_op jit(solution)/shard_map/ppermute | solution.py:277
  68.2 7.5 %collective-permute-start.14 = (bf16[16,3584]{1,0:T(8,128)(2,1)S(1)}, bf16[16,3584]{1,0:T(8,128)(2,1)S(1)}, u32[]{:S(2)}, u32[]{:S(2)}) collective-permute-start(bf16[16,3584]{1,0:T(8,128)(2,1)S(1)} %pad_maximum_fusion), channel_id=1, source_target_pairs={{0,6},{1,7},{2,4},{3,5},{4,2},{5,3},{6,0},{7,1},{8,14},{9,15},{10,... | collective-permute-start | bytes 344072 | tf_op jit(solution)/shard_map/ppermute | solution.py:277
  75.8 5.6 %collective-permute-start.17 = (bf16[8,3584]{1,0:T(8,128)(2,1)S(1)}, bf16[8,3584]{1,0:T(8,128)(2,1)S(1)}, u32[]{:S(2)}, u32[]{:S(2)}) collective-permute-start(bf16[8,3584]{1,0:T(8,128)(2,1)S(1)} %slice.173), channel_id=1, source_target_pairs={{0,8},{1,9},{2,10},{3,11},{4,12},{5,13},{6,14},{7,15},{8,0},{9,1},... | collective-permute-start | bytes 172040 | tf_op jit(solution)/shard_map/ppermute | solution.py:277

commit v12 on v11

--- a/solution.py
+++ b/solution.py
@@ -149,10 +149,8 @@
 
 
 def norm_kernel(kept_ref, arrived_ref, gain_ref, middle_ref, normed_ref):
-    tok = kept_ref.shape[0] // 2
     for block in range(2):
-        mine = pl.ds(block * tok, tok)
-        total = kept_ref[mine, :].astype(F32) + arrived_ref[1 - block].astype(F32)
+        total = kept_ref[block].astype(F32) + arrived_ref[1 - block].astype(F32)
         if block == 0:
             middle_ref[...] = total
         scale = lax.rsqrt(jnp.mean(total * total, axis=1, keepdims=True) + EPSILON)
@@ -171,7 +169,7 @@
         in_specs=[VMEM_SPEC] * 3,
         out_specs=(VMEM_SPEC, VMEM_SPEC),
         compiler_params=pltpu.CompilerParams(vmem_limit_bytes=4 << 20),
-    )(kept, arrived.reshape(2, tok, feature), gain)
+    )(kept.reshape(2, tok, feature), arrived.reshape(2, tok, feature), gain)
 
 
 def expert_kernel(own_gates_ref, other_gates_ref, first_ref, second_ref, up_ref, low_ref, middle_ref, down_source, *refs):

time: 82.3 us -> 82.3 us (level)
  no operation moved by 1% of the time
where the time goes in v12:
time: 82.3 us; the launch traced here: 82 us
  waiting for transfers between devices  28.4 us (35%)
  Pallas kernels  26.1 us (32%)
  starting transfers between devices  25.5 us (31%)
  other arithmetic  1.75 us (2%)
    ppermute x18, waiting for transfers between devices, swap(): return lax.ppermute(x, 'ep', [(i, i ^ bit) for i in range(size)])  18.1 us
    ppermute x18, starting transfers between devices, swap(): return lax.ppermute(x, 'ep', [(i, i ^ bit) for i in range(size)])  14.7 us
    pallas_call x4, Pallas kernels, fetch(): pl.pallas_call(functools.partial(fetch_kernel, count, carried, ranges), o...  13.6 us
    pallas_call x1, Pallas kernels, experts(): pl.pallas_call(expert_kernel, out_shape=(jax.ShapeDtypeStruct((half, feat...  8.2 us
    all_to_all x1, starting transfers between devices, local(): lax.all_to_all(queries.reshape(size, tok, head_dim), 'ep', split_axis=0,...  7.38 us
    all_to_all x1, waiting for transfers between devices, local(): lax.all_to_all(attended, 'ep', split_axis=0, concat_axis=0, tiled=True)  5.76 us
    all_to_all x1, waiting for transfers between devices, local(): lax.all_to_all(queries.reshape(size, tok, head_dim), 'ep', split_axis=0,...  4.56 us
    all_to_all x1, starting transfers between devices, local(): lax.all_to_all(attended, 'ep', split_axis=0, concat_axis=0, tiled=True)  3.51 us
  transfers between devices with their start and end apart: 20, of which 17 were waited for; matrix products, arithmetic and copies ran while one was open for 1% of the time, Pallas kernels for 18%

profile of v12, /device:TPU:0, one launch (start us, length us, event | category | flops | bytes accessed | tf_op | source)
XLA Modules:
  0.0 82.0 jit_solution(15385567188235577847)
XLA Ops:
  0.0 7.4 %all-to-all-start = ((bf16[16,8,256]{2,1,0:T(8,128)(2,1)}), bf16[16,8,256]{2,1,0:T(8,128)(2,1)S(1)}, u32[]{:S(2)}, u32[]{:S(2)}) async-start(bf16[16,8,256]{2,1,0:T(8,128)(2,1)} %bitcast.19), calls=%async_computation | async-start | bytes 131072 | tf_op jit(solution)/shard_map/all_to_all | solution.py:302
  7.4 1.6 %shard_map.109 = (bf16[8,256,512]{2,1,0:T(8,128)(2,1)S(1)}, bf16[8,3584]{1,0:T(8,128)(2,1)S(1)}, f32[3584]{0:T(1024)S(1)}, s32[8]{0:T(128)S(1)}, s32[3,8]{1,0:T(4,128)S(1)}) custom-call(bf16[8,256,512]{2,1,0:T(8,128)(2,1)} %refs_0_.4, bf16[8,3584]{1,0:T(8,128)(2,1)} %refs_1_.3, f32[3584]{0:T(1024)} %refs_2_.2, s32[8]{0:T(128)} %refs_3_.1, s32[3,8]{1,0:T(4,128)} %bitcast.20), custom_call_target="tpu_custom_call" | custom-call | bytes 2161728 | tf_op jit(solution)/shard_map/pallas_call | solution.py:47
  9.0 0.7 convert_bitcast_fusion.shares_ref
  9.7 4.6 %all-to-all-done.query_ref = bf16[16,8,256]{2,1,0:T(8,128)(2,1)S(1)} async-done(((bf16[16,8,256]{2,1,0:T(8,128)(2,1)}), bf16[16,8,256]{2,1,0:T(8,128)(2,1)S(1)}, u32[]{:S(2)}, u32[]{:S(2)}) %all-to-all-start) | async-done | bytes 65568 | tf_op jit(solution)/shard_map/all_to_all | solution.py:302
  14.3 2.2 %shard_map.110.refs_1_ = bf16[16,8,384]{2,1,0:T(8,128)(2,1)} custom-call(s32[8]{0:T(128)S(1)} %get-tuple-element.39.lengths_ref, s32[3,8]{1,0:T(4,128)S(1)} %get-tuple-element.40.routes_ref, f32[3,8]{1,0:T(4,128)S(1)} %convert_bitcast_fusion.shares_ref, bf16[16,8,256]{2,1,0:T(8,128)(2,1)S(1)} %all-to-all-done.query_ref, ...), custom_call_target="tpu_custom_call" | custom-call | tf_op jit(solution)/shard_map/pallas_call | solution.py:100
  16.5 3.5 %all-to-all-start.1 = ((bf16[16,8,384]{2,1,0:T(8,128)(2,1)}), bf16[16,8,384]{2,1,0:T(8,128)(2,1)S(1)}, u32[]{:S(2)}, u32[]{:S(2)}) async-start(bf16[16,8,384]{2,1,0:T(8,128)(2,1)} %shard_map.110.refs_1_), calls=%async_computation.1 | async-start | bytes 196608 | tf_op jit(solution)/shard_map/all_to_all | solution.py:307
  20.0 0.1 pad_add_fusion
  20.1 1.5 %shard_map.111.weight_ref = bf16[256,3584]{1,0:T(8,128)(2,1)S(1)} custom-call(bf16[256,3584]{1,0:T(8,128)(2,1)} %refs_0_.5, bf16[16,8,384]{2,1,0:T(8,128)(2,1)} %shard_map.110.refs_1_), custom_call_target="tpu_custom_call" | custom-call | bytes 1835008 | tf_op jit(solution)/shard_map/pallas_call | solution.py:47
  21.6 5.8 %all-to-all-done.1 = bf16[16,8,384]{2,1,0:T(8,128)(2,1)S(1)} async-done(((bf16[16,8,384]{2,1,0:T(8,128)(2,1)}), bf16[16,8,384]{2,1,0:T(8,128)(2,1)S(1)}, u32[]{:S(2)}, u32[]{:S(2)}) %all-to-all-start.1) | async-done | bytes 98336 | tf_op jit(solution)/shard_map/all_to_all | solution.py:307
  27.3 1.0 %shard_map.113 = (bf16[64,3584]{1,0:T(8,128)(2,1)S(1)}, bf16[64,128]{1,0:T(8,128)(2,1)S(1)}) custom-call(s32[2]{0:T(128)S(1)} %get-tuple-element.73.place_ref, bf16[8,2,8,384]{3,2,1,0:T(8,128)(2,1)S(1)} %bitcast.12, bf16[256,3584]{1,0:T(8,128)(2,1)S(1)} %shard_map.111.weight_ref), custom_call_target="tpu_custom_call" | custom-call | flops 117440512 | bytes 1835008 | tf_op jit(solution)/shard_map/pallas_call | solution.py:133
  28.4 1.0 %shard_map.112 = (f32[64,3584]{1,0:T(8,128)S(1)}, bf16[64,128]{1,0:T(8,128)(2,1)S(1)}) custom-call(s32[2]{0:T(128)S(1)} %get-tuple-element.72.place_ref, bf16[8,2,8,384]{3,2,1,0:T(8,128)(2,1)S(1)} %bitcast.13, bf16[256,3584]{1,0:T(8,128)(2,1)S(1)} %shard_map.111.weight_ref), custom_call_target="tpu_custom_call" | custom-call | flops 117440512 | bytes 1835008 | tf_op jit(solution)/shard_map/pallas_call | solution.py:133
  29.4 0.8 collective-permute-done
  30.3 0.1 collective-permute-start.1
  30.3 1.2 %collective-permute-start.3 = (bf16[16,3584]{1,0:T(8,128)(2,1)S(1)}, bf16[16,3584]{1,0:T(8,128)(2,1)S(1)}, u32[]{:S(2)}, u32[]{:S(2)}) collective-permute-start(bf16[16,3584]{1,0:T(8,128)(2,1)S(1)} %get-tuple-element.62), channel_id=1, source_target_pairs={{0,4},{1,5},{2,6},{3,7},{4,0},{5,1},{6,2},{7,3},{8,12},{9,13},{10,... | collective-permute-start | bytes 344072 | tf_op jit(solution)/shard_map/ppermute | solution.py:275
  31.5 2.3 %collective-permute-start.2 = (bf16[16,3584]{1,0:T(8,128)(2,1)S(1)}, bf16[16,3584]{1,0:T(8,128)(2,1)S(1)}, u32[]{:S(2)}, u32[]{:S(2)}) collective-permute-start(bf16[16,3584]{1,0:T(8,128)(2,1)S(1)} %get-tuple-element.63), channel_id=1, source_target_pairs={{0,2},{1,3},{2,0},{3,1},{4,6},{5,7},{6,4},{7,5},{8,10},{9,11},{10,... | collective-permute-start | bytes 344072 | tf_op jit(solution)/shard_map/ppermute | solution.py:275
  33.8 3.4 %collective-permute-done.1 = bf16[16,3584]{1,0:T(8,128)(2,1)S(1)} collective-permute-done((bf16[16,3584]{1,0:T(8,128)(2,1)S(1)}, bf16[16,3584]{1,0:T(8,128)(2,1)S(1)}, u32[]{:S(2)}, u32[]{:S(2)}) %collective-permute-start.1) | collective-permute-done | bytes 114720 | tf_op jit(solution)/shard_map/ppermute | solution.py:275
  37.2 0.2 collective-permute-done.3
  37.4 1.5 %collective-permute-done.2 = bf16[16,3584]{1,0:T(8,128)(2,1)S(1)} collective-permute-done((bf16[16,3584]{1,0:T(8,128)(2,1)S(1)}, bf16[16,3584]{1,0:T(8,128)(2,1)S(1)}, u32[]{:S(2)}, u32[]{:S(2)}) %collective-permute-start.2) | collective-permute-done | bytes 114720 | tf_op jit(solution)/shard_map/ppermute | solution.py:275
  39.0 0.2 collective-permute-start.4
  39.2 6.8 %shard_map.114 = (bf16[1536,3584]{1,0:T(8,128)(2,1)S(1)}, bf16[768,3584]{1,0:T(8,128)(2,1)S(1)}, bf16[512,3584]{1,0:T(8,128)(2,1)S(1)}, f32[3584]{0:T(1024)S(1)}) custom-call(bf16[1536,3584]{1,0:T(8,128)(2,1)} %refs_0_.6, bf16[1536,3584]{1,0:T(8,128)(2,1)} %refs_0_.7, bf16[1536,3584]{1,0:T(8,128)(2,1)} %down_source.1, f32[3584]{0:T(1024)S(1)} %get-tuple-element.45.refs_3_, ...), custom_call_target="tpu_custom_call" | custom-call | bytes 33030144 | tf_op jit(solution)/shard_map/pallas_call | solution.py:47
  46.0 0.9 %collective-permute-done.4 = bf16[16,3584]{1,0:T(8,128)(2,1)S(1)} collective-permute-done((bf16[16,3584]{1,0:T(8,128)(2,1)S(1)}, bf16[16,3584]{1,0:T(8,128)(2,1)S(1)}, u32[]{:S(2)}, u32[]{:S(2)}) %collective-permute-start.4) | collective-permute-done | bytes 114720 | tf_op jit(solution)/shard_map/ppermute | solution.py:275
  46.9 0.1 shard_map.115
  47.0 0.3 collective-permute-start.7
  47.3 1.3 %collective-permute-start.6 = (bf16[16,3584]{1,0:T(8,128)(2,1)S(1)}, bf16[16,3584]{1,0:T(8,128)(2,1)S(1)}, u32[]{:S(2)}, u32[]{:S(2)}) collective-permute-start(bf16[16,3584]{1,0:T(8,128)(2,1)S(1)} %bitcast.15), channel_id=1, source_target_pairs={{0,2},{1,3},{2,0},{3,1},{4,6},{5,7},{6,4},{7,5},{8,10},{9,11},{10,... | collective-permute-start | bytes 344072 | tf_op jit(solution)/shard_map/ppermute | solution.py:275
  48.7 1.9 %collective-permute-start.5 = (bf16[16,3584]{1,0:T(8,128)(2,1)S(1)}, bf16[16,3584]{1,0:T(8,128)(2,1)S(1)}, u32[]{:S(2)}, u32[]{:S(2)}) collective-permute-start(bf16[16,3584]{1,0:T(8,128)(2,1)S(1)} %bitcast.16), channel_id=1, source_target_pairs={{0,4},{1,5},{2,6},{3,7},{4,0},{5,1},{6,2},{7,3},{8,12},{9,13},{10,... | collective-permute-start | bytes 344072 | tf_op jit(solution)/shard_map/ppermute | solution.py:275
  50.6 3.7 %shard_map.116 = (bf16[768,3584]{1,0:T(8,128)(2,1)S(1)}, bf16[512,3584]{1,0:T(8,128)(2,1)S(1)}, bf16[16,3584]{1,0:T(8,128)(2,1)S(1)}) custom-call(bf16[1536,3584]{1,0:T(8,128)(2,1)} %refs_0_.7, bf16[1536,3584]{1,0:T(8,128)(2,1)} %down_source.1, bf16[16,3584]{1,0:T(8,128)(2,1)S(1)} %bitcast.17), custom_call_target="tpu_custom_call" | custom-call | bytes 22020096 | tf_op jit(solution)/shard_map/pallas_call | solution.py:47
  54.3 0.1 collective-permute-start.8
  54.4 0.5 collective-permute-start.11
  54.9 0.1 collective-permute-start.10
  55.0 0.4 collective-permute-start.9
  55.4 0.3 collective-permute-done.8.refs_4_
  55.7 0.2 collective-permute-done.11.refs_7_
  55.9 0.4 collective-permute-done.10.refs_6_
  56.2 0.2 collective-permute-done.9.refs_5_
  56.4 8.2 %shard_map.117 = (f32[64,1792]{1,0:T(8,128)S(1)}, bf16[64,1792]{1,0:T(8,128)(2,1)S(1)}, f32[64,1792]{1,0:T(8,128)S(1)}, bf16[64,1792]{1,0:T(8,128)(2,1)S(1)}) custom-call(bf16[64,128]{1,0:T(8,128)(2,1)S(1)} %get-tuple-element.48.own_gates_ref, bf16[64,128]{1,0:T(8,128)(2,1)S(1)} %get-tuple-element.49.other_gates_ref, ...), custom_call_target="tpu_custom_call" | custom-call | flops 4227858432 | bytes 33030144 | tf_op jit(solution)/shard_map/pallas_call | solution.py:224
  64.6 0.4 collective-permute-start.12
  65.0 0.2 collective-permute-start.13
  65.2 1.0 %collective-permute-done.12 = bf16[64,1792]{1,0:T(8,128)(2,1)S(1)} collective-permute-done((bf16[64,1792]{1,0:T(8,128)(2,1)S(1)}, bf16[64,1792]{1,0:T(8,128)(2,1)S(1)}, u32[]{:S(2)}, u32[]{:S(2)}) %collective-permute-start.12) | collective-permute-done | bytes 229408 | tf_op jit(solution)/shard_map/ppermute | solution.py:275
  66.2 0.3 collective-permute-done.13
  66.6 1.2 %collective-permute-start.15 = (bf16[16,3584]{1,0:T(8,128)(2,1)S(1)}, bf16[16,3584]{1,0:T(8,128)(2,1)S(1)}, u32[]{:S(2)}, u32[]{:S(2)}) collective-permute-start(bf16[16,3584]{1,0:T(8,128)(2,1)S(1)} %pad_maximum_fusion.1), channel_id=1, source_target_pairs={{0,2},{1,3},{2,0},{3,1},{4,6},{5,7},{6,4},{7,5},{8,10},{9,11},{10,... | collective-permute-start | bytes 344072 | tf_op jit(solution)/shard_map/ppermute | solution.py:275
  67.7 0.5 collective-permute-start.16
  68.2 2.0 %collective-permute-start.14 = (bf16[16,3584]{1,0:T(8,128)(2,1)S(1)}, bf16[16,3584]{1,0:T(8,128)(2,1)S(1)}, u32[]{:S(2)}, u32[]{:S(2)}) collective-permute-start(bf16[16,3584]{1,0:T(8,128)(2,1)S(1)} %pad_maximum_fusion), channel_id=1, source_target_pairs={{0,6},{1,7},{2,4},{3,5},{4,2},{5,3},{6,0},{7,1},{8,14},{9,15},{10,... | collective-permute-start | bytes 344072 | tf_op jit(solution)/shard_map/ppermute | solution.py:275
  70.3 1.7 %collective-permute-done.15 = bf16[16,3584]{1,0:T(8,128)(2,1)S(1)} collective-permute-done((bf16[16,3584]{1,0:T(8,128)(2,1)S(1)}, bf16[16,3584]{1,0:T(8,128)(2,1)S(1)}, u32[]{:S(2)}, u32[]{:S(2)}) %collective-permute-start.15) | collective-permute-done | bytes 114720 | tf_op jit(solution)/shard_map/ppermute | solution.py:275
  72.0 1.8 %collective-permute-done.16 = bf16[16,3584]{1,0:T(8,128)(2,1)S(1)} collective-permute-done((bf16[16,3584]{1,0:T(8,128)(2,1)S(1)}, bf16[16,3584]{1,0:T(8,128)(2,1)S(1)}, u32[]{:S(2)}, u32[]{:S(2)}) %collective-permute-start.16) | collective-permute-done | bytes 114720 | tf_op jit(solution)/shard_map/ppermute | solution.py:275
  73.8 1.9 %collective-permute-done.14 = bf16[16,3584]{1,0:T(8,128)(2,1)S(1)} collective-permute-done((bf16[16,3584]{1,0:T(8,128)(2,1)S(1)}, bf16[16,3584]{1,0:T(8,128)(2,1)S(1)}, u32[]{:S(2)}, u32[]{:S(2)}) %collective-permute-start.14) | collective-permute-done | bytes 114720 | tf_op jit(solution)/shard_map/ppermute | solution.py:275
  75.8 2.0 %collective-permute-start.17 = (bf16[8,3584]{1,0:T(8,128)(2,1)S(1)}, bf16[8,3584]{1,0:T(8,128)(2,1)S(1)}, u32[]{:S(2)}, u32[]{:S(2)}) collective-permute-start(bf16[8,3584]{1,0:T(8,128)(2,1)S(1)} %slice.173), channel_id=1, source_target_pairs={{0,8},{1,9},{2,10},{3,11},{4,12},{5,13},{6,14},{7,15},{8,0},{9,1},... | collective-permute-start | bytes 172040 | tf_op jit(solution)/shard_map/ppermute | solution.py:275
  77.7 3.6 %collective-permute-done.17 = bf16[8,3584]{1,0:T(8,128)(2,1)S(1)} collective-permute-done((bf16[8,3584]{1,0:T(8,128)(2,1)S(1)}, bf16[8,3584]{1,0:T(8,128)(2,1)S(1)}, u32[]{:S(2)}, u32[]{:S(2)}) %collective-permute-start.17) | collective-permute-done | bytes 57376 | tf_op jit(solution)/shard_map/ppermute | solution.py:275
  81.4 0.6 fusion.3
  (16 shorter events, 0.4 us)
Async XLA Ops:
  0.0 14.3 %all-to-all-start = ((bf16[16,8,256]{2,1,0:T(8,128)(2,1)}), bf16[16,8,256]{2,1,0:T(8,128)(2,1)S(1)}, u32[]{:S(2)}, u32[]{:S(2)}) async-start(bf16[16,8,256]{2,1,0:T(8,128)(2,1)} %bitcast.19), calls=%async_computation | async-start | bytes 131072 | tf_op jit(solution)/shard_map/all_to_all | solution.py:302
  16.5 10.9 %all-to-all-start.1 = ((bf16[16,8,384]{2,1,0:T(8,128)(2,1)}), bf16[16,8,384]{2,1,0:T(8,128)(2,1)S(1)}, u32[]{:S(2)}, u32[]{:S(2)}) async-start(bf16[16,8,384]{2,1,0:T(8,128)(2,1)} %shard_map.110.refs_1_), calls=%async_computation.1 | async-start | bytes 196608 | tf_op jit(solution)/shard_map/all_to_all | solution.py:307
  28.3 1.9 %collective-permute-start = (bf16[64,3584]{1,0:T(8,128)(2,1)S(1)}, bf16[64,3584]{1,0:T(8,128)(2,1)S(1)}, u32[]{:S(2)}, u32[]{:S(2)}) collective-permute-start(bf16[64,3584]{1,0:T(8,128)(2,1)S(1)} %get-tuple-element.43), channel_id=1, source_target_pairs={{0,1},{1,0},{2,3},{3,2},{4,5},{5,4},{6,7},{7,6},{8,9},{9,8},{10,11... | collective-permute-start | bytes 1376264 | tf_op jit(solution)/shard_map/ppermute | solution.py:275
  30.3 7.0 %collective-permute-start.1 = (bf16[16,3584]{1,0:T(8,128)(2,1)S(1)}, bf16[16,3584]{1,0:T(8,128)(2,1)S(1)}, u32[]{:S(2)}, u32[]{:S(2)}) collective-permute-start(bf16[16,3584]{1,0:T(8,128)(2,1)S(1)} %get-tuple-element.61), channel_id=1, source_target_pairs={{0,6},{1,7},{2,4},{3,5},{4,2},{5,3},{6,0},{7,1},{8,14},{9,15},{10,... | collective-permute-start | bytes 344072 | tf_op jit(solution)/shard_map/ppermute | solution.py:275
  30.3 7.0 %collective-permute-start.3 = (bf16[16,3584]{1,0:T(8,128)(2,1)S(1)}, bf16[16,3584]{1,0:T(8,128)(2,1)S(1)}, u32[]{:S(2)}, u32[]{:S(2)}) collective-permute-start(bf16[16,3584]{1,0:T(8,128)(2,1)S(1)} %get-tuple-element.62), channel_id=1, source_target_pairs={{0,4},{1,5},{2,6},{3,7},{4,0},{5,1},{6,2},{7,3},{8,12},{9,13},{10,... | collective-permute-start | bytes 344072 | tf_op jit(solution)/shard_map/ppermute | solution.py:275
  31.5 7.3 %collective-permute-start.2 = (bf16[16,3584]{1,0:T(8,128)(2,1)S(1)}, bf16[16,3584]{1,0:T(8,128)(2,1)S(1)}, u32[]{:S(2)}, u32[]{:S(2)}) collective-permute-start(bf16[16,3584]{1,0:T(8,128)(2,1)S(1)} %get-tuple-element.63), channel_id=1, source_target_pairs={{0,2},{1,3},{2,0},{3,1},{4,6},{5,7},{6,4},{7,5},{8,10},{9,11},{10,... | collective-permute-start | bytes 344072 | tf_op jit(solution)/shard_map/ppermute | solution.py:275
  39.0 7.9 %collective-permute-start.4 = (bf16[16,3584]{1,0:T(8,128)(2,1)S(1)}, bf16[16,3584]{1,0:T(8,128)(2,1)S(1)}, u32[]{:S(2)}, u32[]{:S(2)}) collective-permute-start(bf16[16,3584]{1,0:T(8,128)(2,1)S(1)} %convert_element_type.91.refs_4_), channel_id=1, source_target_pairs={{0,8},{1,9},{2,10},{3,11},{4,12},{5,13},{6,14},{7,15},{8,0},{9,1},... | collective-permute-start | bytes 344072 | tf_op jit(solution)/shard_map/ppermute | solution.py:275
  47.0 7.3 %collective-permute-start.7 = (bf16[16,3584]{1,0:T(8,128)(2,1)S(1)}, bf16[16,3584]{1,0:T(8,128)(2,1)S(1)}, u32[]{:S(2)}, u32[]{:S(2)}) collective-permute-start(bf16[16,3584]{1,0:T(8,128)(2,1)S(1)} %bitcast.14), channel_id=1, source_target_pairs={{0,6},{1,7},{2,4},{3,5},{4,2},{5,3},{6,0},{7,1},{8,14},{9,15},{10,... | collective-permute-start | bytes 344072 | tf_op jit(solution)/shard_map/ppermute | solution.py:275
  47.3 7.5 %collective-permute-start.6 = (bf16[16,3584]{1,0:T(8,128)(2,1)S(1)}, bf16[16,3584]{1,0:T(8,128)(2,1)S(1)}, u32[]{:S(2)}, u32[]{:S(2)}) collective-permute-start(bf16[16,3584]{1,0:T(8,128)(2,1)S(1)} %bitcast.15), channel_id=1, source_target_pairs={{0,2},{1,3},{2,0},{3,1},{4,6},{5,7},{6,4},{7,5},{8,10},{9,11},{10,... | collective-permute-start | bytes 344072 | tf_op jit(solution)/shard_map/ppermute | solution.py:275
  48.7 6.3 %collective-permute-start.5 = (bf16[16,3584]{1,0:T(8,128)(2,1)S(1)}, bf16[16,3584]{1,0:T(8,128)(2,1)S(1)}, u32[]{:S(2)}, u32[]{:S(2)}) collective-permute-start(bf16[16,3584]{1,0:T(8,128)(2,1)S(1)} %bitcast.16), channel_id=1, source_target_pairs={{0,4},{1,5},{2,6},{3,7},{4,0},{5,1},{6,2},{7,3},{8,12},{9,13},{10,... | collective-permute-start | bytes 344072 | tf_op jit(solution)/shard_map/ppermute | solution.py:275
  54.3 1.4 %collective-permute-start.8 = (bf16[16,3584]{1,0:T(8,128)(2,1)S(1)}, bf16[16,3584]{1,0:T(8,128)(2,1)S(1)}, u32[]{:S(2)}, u32[]{:S(2)}) collective-permute-start(bf16[16,3584]{1,0:T(8,128)(2,1)S(1)} %get-tuple-element.56.refs_0_), channel_id=1, source_target_pairs={{0,1},{1,0},{2,3},{3,2},{4,5},{5,4},{6,7},{7,6},{8,9},{9,8},{10,11... | collective-permute-start | bytes 344072 | tf_op jit(solution)/shard_map/ppermute | solution.py:275
  54.4 1.5 %collective-permute-start.11 = (bf16[16,3584]{1,0:T(8,128)(2,1)S(1)}, bf16[16,3584]{1,0:T(8,128)(2,1)S(1)}, u32[]{:S(2)}, u32[]{:S(2)}) collective-permute-start(bf16[16,3584]{1,0:T(8,128)(2,1)S(1)} %collective-permute-done.7.refs_3_), channel_id=1, source_target_pairs={{0,1},{1,0},{2,3},{3,2},{4,5},{5,4},{6,7},{7,6},{8,9},{9,8},{10,11... | collective-permute-start | bytes 344072 | tf_op jit(solution)/shard_map/ppermute | solution.py:275
  54.9 1.3 %collective-permute-start.10 = (bf16[16,3584]{1,0:T(8,128)(2,1)S(1)}, bf16[16,3584]{1,0:T(8,128)(2,1)S(1)}, u32[]{:S(2)}, u32[]{:S(2)}) collective-permute-start(bf16[16,3584]{1,0:T(8,128)(2,1)S(1)} %collective-permute-done.6.refs_2_), channel_id=1, source_target_pairs={{0,1},{1,0},{2,3},{3,2},{4,5},{5,4},{6,7},{7,6},{8,9},{9,8},{10,11... | collective-permute-start | bytes 344072 | tf_op jit(solution)/shard_map/ppermute | solution.py:275
  55.0 1.4 %collective-permute-start.9 = (bf16[16,3584]{1,0:T(8,128)(2,1)S(1)}, bf16[16,3584]{1,0:T(8,128)(2,1)S(1)}, u32[]{:S(2)}, u32[]{:S(2)}) collective-permute-start(bf16[16,3584]{1,0:T(8,128)(2,1)S(1)} %collective-permute-done.5.refs_1_), channel_id=1, source_target_pairs={{0,1},{1,0},{2,3},{3,2},{4,5},{5,4},{6,7},{7,6},{8,9},{9,8},{10,11... | collective-permute-start | bytes 344072 | tf_op jit(solution)/shard_map/ppermute | solution.py:275
  64.6 1.6 %collective-permute-start.12 = (bf16[64,1792]{1,0:T(8,128)(2,1)S(1)}, bf16[64,1792]{1,0:T(8,128)(2,1)S(1)}, u32[]{:S(2)}, u32[]{:S(2)}) collective-permute-start(bf16[64,1792]{1,0:T(8,128)(2,1)S(1)} %get-tuple-element.58), channel_id=1, source_target_pairs={{0,1},{1,0},{2,3},{3,2},{4,5},{5,4},{6,7},{7,6},{8,9},{9,8},{10,11... | collective-permute-start | bytes 688136 | tf_op jit(solution)/shard_map/ppermute | solution.py:275
  65.0 1.5 %collective-permute-start.13 = (bf16[64,1792]{1,0:T(8,128)(2,1)S(1)}, bf16[64,1792]{1,0:T(8,128)(2,1)S(1)}, u32[]{:S(2)}, u32[]{:S(2)}) collective-permute-start(bf16[64,1792]{1,0:T(8,128)(2,1)S(1)} %get-tuple-element.60), channel_id=1, source_target_pairs={{0,1},{1,0},{2,3},{3,2},{4,5},{5,4},{6,7},{7,6},{8,9},{9,8},{10,11... | collective-permute-start | bytes 688136 | tf_op jit(solution)/shard_map/ppermute | solution.py:275
  66.6 5.4 %collective-permute-start.15 = (bf16[16,3584]{1,0:T(8,128)(2,1)S(1)}, bf16[16,3584]{1,0:T(8,128)(2,1)S(1)}, u32[]{:S(2)}, u32[]{:S(2)}) collective-permute-start(bf16[16,3584]{1,0:T(8,128)(2,1)S(1)} %pad_maximum_fusion.1), channel_id=1, source_target_pairs={{0,2},{1,3},{2,0},{3,1},{4,6},{5,7},{6,4},{7,5},{8,10},{9,11},{10,... | collective-permute-start | bytes 344072 | tf_op jit(solution)/shard_map/ppermute | solution.py:275
  67.7 6.1 %collective-permute-start.16 = (bf16[16,3584]{1,0:T(8,128)(2,1)S(1)}, bf16[16,3584]{1,0:T(8,128)(2,1)S(1)}, u32[]{:S(2)}, u32[]{:S(2)}) collective-permute-start(bf16[16,3584]{1,0:T(8,128)(2,1)S(1)} %pad_maximum_fusion.2), channel_id=1, source_target_pairs={{0,4},{1,5},{2,6},{3,7},{4,0},{5,1},{6,2},{7,3},{8,12},{9,13},{10,... | collective-permute-start | bytes 344072 | tf_op jit(solution)/shard_map/ppermute | solution.py:275
  68.2 7.5 %collective-permute-start.14 = (bf16[16,3584]{1,0:T(8,128)(2,1)S(1)}, bf16[16,3584]{1,0:T(8,128)(2,1)S(1)}, u32[]{:S(2)}, u32[]{:S(2)}) collective-permute-start(bf16[16,3584]{1,0:T(8,128)(2,1)S(1)} %pad_maximum_fusion), channel_id=1, source_target_pairs={{0,6},{1,7},{2,4},{3,5},{4,2},{5,3},{6,0},{7,1},{8,14},{9,15},{10,... | collective-permute-start | bytes 344072 | tf_op jit(solution)/shard_map/ppermute | solution.py:275
  75.8 5.6 %collective-permute-start.17 = (bf16[8,3584]{1,0:T(8,128)(2,1)S(1)}, bf16[8,3584]{1,0:T(8,128)(2,1)S(1)}, u32[]{:S(2)}, u32[]{:S(2)}) collective-permute-start(bf16[8,3584]{1,0:T(8,128)(2,1)S(1)} %slice.173), channel_id=1, source_target_pairs={{0,8},{1,9},{2,10},{3,11},{4,12},{5,13},{6,14},{7,15},{8,0},{9,1},... | collective-permute-start | bytes 172040 | tf_op jit(solution)/shard_map/ppermute | solution.py:275

commit v13 on v12

--- a/solution.py
+++ b/solution.py
@@ -60,10 +60,33 @@
     )(*[pltpu.with_memory_space_constraint(a, pltpu.HBM) for a in arrays], *carries, *after)
 
 
-def attend_kernel(lengths_ref, routes_ref, shares_ref, query_ref, cache_ref, out_ref):
+def gate_kernel(tok, span, routes_ref, shares_ref, out_ref):
+    rows = out_ref.shape[0]
+    place = lax.broadcasted_iota(jnp.int32, (rows, 1), 0)
+    place_row = lax.rem(place, tok)
+    expert = place // (tok * span)
+    gates = jnp.zeros((rows, 1), F32)
+    for row in range(tok):
+        for k in range(shares_ref.shape[0]):
+            named = (place_row == row) & (expert == routes_ref[k, row])
+            gates = gates + jnp.where(named, shares_ref[k, row], 0.0)
+    out_ref[...] = jnp.broadcast_to(gates, (rows, LANES)).astype(BF16)
+
+
+def gate_table(size, routes, shares):
+    tok = routes.shape[1]
+    return pl.pallas_call(
+        functools.partial(gate_kernel, tok, size // EXPERTS),
+        out_shape=jax.ShapeDtypeStruct((size * tok, LANES), BF16),
+        in_specs=[SMEM_SPEC] * 2,
+        out_specs=VMEM_SPEC,
+        compiler_params=pltpu.CompilerParams(vmem_limit_bytes=4 << 20),
+    )(routes, shares)
+
+
+def attend_kernel(lengths_ref, gates_ref, query_ref, cache_ref, out_ref):
     heads, tok, head_dim = query_ref.shape
     context = cache_ref.shape[1]
-    span = heads // EXPERTS
     rows = heads * tok
     turned = query_ref[...].reshape(rows, head_dim).T
     lane_row = lax.rem(lax.broadcasted_iota(jnp.int32, (1, rows), 1), tok)
@@ -84,26 +107,18 @@
         found = jnp.dot(prob, cache_ref[row, :, head_dim:], preferred_element_type=F32)
         attended = jnp.where(place_row == row, found, attended)
     out_ref[:, :, :head_dim] = attended.astype(BF16).reshape(heads, tok, head_dim)
-    expert = place // (tok * span)
-    gates = jnp.zeros((rows, 1), F32)
-    for row in range(tok):
-        for k in range(shares_ref.shape[0]):
-            named = (place_row == row) & (expert == routes_ref[k, row])
-            gates = gates + jnp.where(named, shares_ref[k, row], 0.0)
-    out_ref[:, :, head_dim:] = (
-        jnp.broadcast_to(gates, (rows, LANES)).astype(BF16).reshape(heads, tok, LANES)
-    )
-
-
-def attend(lengths, routes, shares, query_rows, cache):
+    out_ref[:, :, head_dim:] = gates_ref[...].reshape(heads, tok, LANES)
+
+
+def attend(lengths, gates, query_rows, cache):
     heads, tok, head_dim = query_rows.shape
     return pl.pallas_call(
         attend_kernel,
         out_shape=jax.ShapeDtypeStruct((heads, tok, head_dim + LANES), BF16),
-        in_specs=[SMEM_SPEC] * 3 + [VMEM_SPEC] * 2,
+        in_specs=[SMEM_SPEC] + [VMEM_SPEC] * 3,
         out_specs=VMEM_SPEC,
         compiler_params=pltpu.CompilerParams(vmem_limit_bytes=8 << 20),
-    )(lengths, routes, shares, query_rows, cache)
+    )(lengths, gates, query_rows, cache)
 
 
 def relative_order(chips):
@@ -299,10 +314,11 @@
     cache, residual_held, gain_held, lengths_held, routes_held = fetch(
         key_values, residual, norm_gain, lengths, routes.T
     )
+    gates = gate_table(size, routes_held, gate_weights.astype(F32).T)
     query_rows = lax.all_to_all(
         queries.reshape(size, tok, head_dim), "ep", split_axis=0, concat_axis=0, tiled=True
     )
-    attended = attend(lengths_held, routes_held, gate_weights.astype(F32).T, query_rows, cache)
+    attended = attend(lengths_held, gates, query_rows, cache)
     (output_held,) = fetch(output_weight, after=(attended,))
     head_rows = lax.all_to_all(attended, "ep", split_axis=0, concat_axis=0, tiled=True)
     head_rows = head_rows.reshape(chips, 2, tok, head_dim + LANES)

time: 82.3 us -> 82.2 us (level)
    all_to_all x1, waiting for transfers between devices: 4.56 us -> 3.72 us  [local(): lax.all_to_all(queries.reshape(size, tok, head_dim), 'ep', split_axis=0,...]
    pallas_call x0 -> x1, Pallas kernels: none -> 0.83 us  [gate_table(): pl.pallas_call(functools.partial(gate_kernel, tok, size // EXPERTS), out_...]
  transfers between devices with their start and end apart: 20 -> 20, of which waited for: 17 -> 17; matrix products, arithmetic and copies ran while one was open for 1% -> 1% of each run, Pallas kernels for 18% -> 19%
where the time goes in v13:
time: 82.2 us; the launch traced here: 81.9 us
  waiting for transfers between devices  27.6 us (34%)
  Pallas kernels  26.8 us (33%)
  starting transfers between devices  25.5 us (31%)
  other arithmetic  1.75 us (2%)
    ppermute x18, waiting for transfers between devices, swap(): return lax.ppermute(x, 'ep', [(i, i ^ bit) for i in range(size)])  18.1 us
    ppermute x18, starting transfers between devices, swap(): return lax.ppermute(x, 'ep', [(i, i ^ bit) for i in range(size)])  14.7 us
    pallas_call x4, Pallas kernels, fetch(): pl.pallas_call(functools.partial(fetch_kernel, count, carried, ranges), o...  13.6 us
    pallas_call x1, Pallas kernels, experts(): pl.pallas_call(expert_kernel, out_shape=(jax.ShapeDtypeStruct((half, feat...  8.2 us
    all_to_all x1, starting transfers between devices, local(): lax.all_to_all(queries.reshape(size, tok, head_dim), 'ep', split_axis=0,...  7.38 us
    all_to_all x1, waiting for transfers between devices, local(): lax.all_to_all(attended, 'ep', split_axis=0, concat_axis=0, tiled=True)  5.76 us
    all_to_all x1, waiting for transfers between devices, local(): lax.all_to_all(queries.reshape(size, tok, head_dim), 'ep', split_axis=0,...  3.72 us
    all_to_all x1, starting transfers between devices, local(): lax.all_to_all(attended, 'ep', split_axis=0, concat_axis=0, tiled=True)  3.51 us
  transfers between devices with their start and end apart: 20, of which 17 were waited for; matrix products, arithmetic and copies ran while one was open for 1% of the time, Pallas kernels for 19%

profile of v13, /device:TPU:0, one launch (start us, length us, event | category | flops | bytes accessed | tf_op | source)
XLA Modules:
  0.0 81.9 jit_solution(14679160842828340581)
XLA Ops:
  0.0 7.4 %all-to-all-start = ((bf16[16,8,256]{2,1,0:T(8,128)(2,1)}), bf16[16,8,256]{2,1,0:T(8,128)(2,1)S(1)}, u32[]{:S(2)}, u32[]{:S(2)}) async-start(bf16[16,8,256]{2,1,0:T(8,128)(2,1)} %bitcast.19), calls=%async_computation | async-start | bytes 131072 | tf_op jit(solution)/shard_map/all_to_all | solution.py:318
  7.4 1.6 %shard_map.109 = (bf16[8,256,512]{2,1,0:T(8,128)(2,1)S(1)}, bf16[8,3584]{1,0:T(8,128)(2,1)S(1)}, f32[3584]{0:T(1024)S(1)}, s32[8]{0:T(128)S(1)}, s32[3,8]{1,0:T(4,128)S(1)}) custom-call(bf16[8,256,512]{2,1,0:T(8,128)(2,1)} %refs_0_.4, bf16[8,3584]{1,0:T(8,128)(2,1)} %refs_1_.3, f32[3584]{0:T(1024)} %refs_2_.2, s32[8]{0:T(128)} %refs_3_.1, s32[3,8]{1,0:T(4,128)} %bitcast.20), custom_call_target="tpu_custom_call" | custom-call | bytes 2161728 | tf_op jit(solution)/shard_map/pallas_call | solution.py:47
  9.0 0.7 convert_bitcast_fusion.shares_ref
  9.7 0.8 %shard_map.110.gates_ref = bf16[128,128]{1,0:T(8,128)(2,1)S(1)} custom-call(s32[3,8]{1,0:T(4,128)S(1)} %get-tuple-element.40.routes_ref, f32[3,8]{1,0:T(4,128)S(1)} %convert_bitcast_fusion.shares_ref), custom_call_target="tpu_custom_call" | custom-call | tf_op jit(solution)/shard_map/pallas_call | solution.py:78
  10.6 3.7 %all-to-all-done.query_ref = bf16[16,8,256]{2,1,0:T(8,128)(2,1)S(1)} async-done(((bf16[16,8,256]{2,1,0:T(8,128)(2,1)}), bf16[16,8,256]{2,1,0:T(8,128)(2,1)S(1)}, u32[]{:S(2)}, u32[]{:S(2)}) %all-to-all-start) | async-done | bytes 65568 | tf_op jit(solution)/shard_map/all_to_all | solution.py:318
  14.3 2.0 %shard_map.111.refs_1_ = bf16[16,8,384]{2,1,0:T(8,128)(2,1)} custom-call(s32[8]{0:T(128)S(1)} %get-tuple-element.39.lengths_ref, bf16[128,128]{1,0:T(8,128)(2,1)S(1)} %shard_map.110.gates_ref, bf16[16,8,256]{2,1,0:T(8,128)(2,1)S(1)} %all-to-all-done.query_ref, bf16[8,256,512]{2,1,0:T(8,128)(2,1)S(1)} %get-tuple-element.41.cache_ref), custom_call_target="tpu_custom_call" | custom-call | tf_op jit(solution)/shard_map/pallas_call | solution.py:115
  16.3 3.5 %all-to-all-start.1 = ((bf16[16,8,384]{2,1,0:T(8,128)(2,1)}), bf16[16,8,384]{2,1,0:T(8,128)(2,1)S(1)}, u32[]{:S(2)}, u32[]{:S(2)}) async-start(bf16[16,8,384]{2,1,0:T(8,128)(2,1)} %shard_map.111.refs_1_), calls=%async_computation.1 | async-start | bytes 196608 | tf_op jit(solution)/shard_map/all_to_all | solution.py:323
  19.9 0.1 pad_add_fusion
  19.9 1.5 %shard_map.112.weight_ref = bf16[256,3584]{1,0:T(8,128)(2,1)S(1)} custom-call(bf16[256,3584]{1,0:T(8,128)(2,1)} %refs_0_.5, bf16[16,8,384]{2,1,0:T(8,128)(2,1)} %shard_map.111.refs_1_), custom_call_target="tpu_custom_call" | custom-call | bytes 1835008 | tf_op jit(solution)/shard_map/pallas_call | solution.py:47
  21.4 5.8 %all-to-all-done.1 = bf16[16,8,384]{2,1,0:T(8,128)(2,1)S(1)} async-done(((bf16[16,8,384]{2,1,0:T(8,128)(2,1)}), bf16[16,8,384]{2,1,0:T(8,128)(2,1)S(1)}, u32[]{:S(2)}, u32[]{:S(2)}) %all-to-all-start.1) | async-done | bytes 98336 | tf_op jit(solution)/shard_map/all_to_all | solution.py:323
  27.2 1.0 %shard_map.114 = (bf16[64,3584]{1,0:T(8,128)(2,1)S(1)}, bf16[64,128]{1,0:T(8,128)(2,1)S(1)}) custom-call(s32[2]{0:T(128)S(1)} %get-tuple-element.73.place_ref, bf16[8,2,8,384]{3,2,1,0:T(8,128)(2,1)S(1)} %bitcast.12, bf16[256,3584]{1,0:T(8,128)(2,1)S(1)} %shard_map.112.weight_ref), custom_call_target="tpu_custom_call" | custom-call | flops 117440512 | bytes 1835008 | tf_op jit(solution)/shard_map/pallas_call | solution.py:148
  28.3 1.0 %shard_map.113 = (f32[64,3584]{1,0:T(8,128)S(1)}, bf16[64,128]{1,0:T(8,128)(2,1)S(1)}) custom-call(s32[2]{0:T(128)S(1)} %get-tuple-element.72.place_ref, bf16[8,2,8,384]{3,2,1,0:T(8,128)(2,1)S(1)} %bitcast.13, bf16[256,3584]{1,0:T(8,128)(2,1)S(1)} %shard_map.112.weight_ref), custom_call_target="tpu_custom_call" | custom-call | flops 117440512 | bytes 1835008 | tf_op jit(solution)/shard_map/pallas_call | solution.py:148
  29.3 0.8 collective-permute-done
  30.1 0.1 collective-permute-start.1
  30.2 1.2 %collective-permute-start.3 = (bf16[16,3584]{1,0:T(8,128)(2,1)S(1)}, bf16[16,3584]{1,0:T(8,128)(2,1)S(1)}, u32[]{:S(2)}, u32[]{:S(2)}) collective-permute-start(bf16[16,3584]{1,0:T(8,128)(2,1)S(1)} %get-tuple-element.62), channel_id=1, source_target_pairs={{0,4},{1,5},{2,6},{3,7},{4,0},{5,1},{6,2},{7,3},{8,12},{9,13},{10,... | collective-permute-start | bytes 344072 | tf_op jit(solution)/shard_map/ppermute | solution.py:290
  31.4 2.3 %collective-permute-start.2 = (bf16[16,3584]{1,0:T(8,128)(2,1)S(1)}, bf16[16,3584]{1,0:T(8,128)(2,1)S(1)}, u32[]{:S(2)}, u32[]{:S(2)}) collective-permute-start(bf16[16,3584]{1,0:T(8,128)(2,1)S(1)} %get-tuple-element.63), channel_id=1, source_target_pairs={{0,2},{1,3},{2,0},{3,1},{4,6},{5,7},{6,4},{7,5},{8,10},{9,11},{10,... | collective-permute-start | bytes 344072 | tf_op jit(solution)/shard_map/ppermute | solution.py:290
  33.7 3.4 %collective-permute-done.1 = bf16[16,3584]{1,0:T(8,128)(2,1)S(1)} collective-permute-done((bf16[16,3584]{1,0:T(8,128)(2,1)S(1)}, bf16[16,3584]{1,0:T(8,128)(2,1)S(1)}, u32[]{:S(2)}, u32[]{:S(2)}) %collective-permute-start.1) | collective-permute-done | bytes 114720 | tf_op jit(solution)/shard_map/ppermute | solution.py:290
  37.1 0.2 collective-permute-done.3
  37.2 1.5 %collective-permute-done.2 = bf16[16,3584]{1,0:T(8,128)(2,1)S(1)} collective-permute-done((bf16[16,3584]{1,0:T(8,128)(2,1)S(1)}, bf16[16,3584]{1,0:T(8,128)(2,1)S(1)}, u32[]{:S(2)}, u32[]{:S(2)}) %collective-permute-start.2) | collective-permute-done | bytes 114720 | tf_op jit(solution)/shard_map/ppermute | solution.py:290
  38.9 0.2 collective-permute-start.4
  39.1 6.8 %shard_map.115 = (bf16[1536,3584]{1,0:T(8,128)(2,1)S(1)}, bf16[768,3584]{1,0:T(8,128)(2,1)S(1)}, bf16[512,3584]{1,0:T(8,128)(2,1)S(1)}, f32[3584]{0:T(1024)S(1)}) custom-call(bf16[1536,3584]{1,0:T(8,128)(2,1)} %refs_0_.6, bf16[1536,3584]{1,0:T(8,128)(2,1)} %refs_0_.7, bf16[1536,3584]{1,0:T(8,128)(2,1)} %down_source.1, f32[3584]{0:T(1024)S(1)} %get-tuple-element.45.refs_3_, ...), custom_call_target="tpu_custom_call" | custom-call | bytes 33030144 | tf_op jit(solution)/shard_map/pallas_call | solution.py:47
  45.9 0.9 %collective-permute-done.4 = bf16[16,3584]{1,0:T(8,128)(2,1)S(1)} collective-permute-done((bf16[16,3584]{1,0:T(8,128)(2,1)S(1)}, bf16[16,3584]{1,0:T(8,128)(2,1)S(1)}, u32[]{:S(2)}, u32[]{:S(2)}) %collective-permute-start.4) | collective-permute-done | bytes 114720 | tf_op jit(solution)/shard_map/ppermute | solution.py:290
  46.8 0.1 shard_map.116
  46.9 0.3 collective-permute-start.7
  47.2 1.3 %collective-permute-start.6 = (bf16[16,3584]{1,0:T(8,128)(2,1)S(1)}, bf16[16,3584]{1,0:T(8,128)(2,1)S(1)}, u32[]{:S(2)}, u32[]{:S(2)}) collective-permute-start(bf16[16,3584]{1,0:T(8,128)(2,1)S(1)} %bitcast.15), channel_id=1, source_target_pairs={{0,2},{1,3},{2,0},{3,1},{4,6},{5,7},{6,4},{7,5},{8,10},{9,11},{10,... | collective-permute-start | bytes 344072 | tf_op jit(solution)/shard_map/ppermute | solution.py:290
  48.6 1.9 %collective-permute-start.5 = (bf16[16,3584]{1,0:T(8,128)(2,1)S(1)}, bf16[16,3584]{1,0:T(8,128)(2,1)S(1)}, u32[]{:S(2)}, u32[]{:S(2)}) collective-permute-start(bf16[16,3584]{1,0:T(8,128)(2,1)S(1)} %bitcast.16), channel_id=1, source_target_pairs={{0,4},{1,5},{2,6},{3,7},{4,0},{5,1},{6,2},{7,3},{8,12},{9,13},{10,... | collective-permute-start | bytes 344072 | tf_op jit(solution)/shard_map/ppermute | solution.py:290
  50.5 3.7 %shard_map.117 = (bf16[768,3584]{1,0:T(8,128)(2,1)S(1)}, bf16[512,3584]{1,0:T(8,128)(2,1)S(1)}, bf16[16,3584]{1,0:T(8,128)(2,1)S(1)}) custom-call(bf16[1536,3584]{1,0:T(8,128)(2,1)} %refs_0_.7, bf16[1536,3584]{1,0:T(8,128)(2,1)} %down_source.1, bf16[16,3584]{1,0:T(8,128)(2,1)S(1)} %bitcast.17), custom_call_target="tpu_custom_call" | custom-call | bytes 22020096 | tf_op jit(solution)/shard_map/pallas_call | solution.py:47
  54.3 0.5 collective-permute-start.11
  54.8 0.1 collective-permute-start.10
  54.8 0.4 collective-permute-start.9
  55.3 0.3 collective-permute-done.8.refs_4_
  55.6 0.2 collective-permute-done.11.refs_7_
  55.7 0.4 collective-permute-done.10.refs_6_
  56.1 0.2 collective-permute-done.9.refs_5_
  56.2 8.2 %shard_map.118 = (f32[64,1792]{1,0:T(8,128)S(1)}, bf16[64,1792]{1,0:T(8,128)(2,1)S(1)}, f32[64,1792]{1,0:T(8,128)S(1)}, bf16[64,1792]{1,0:T(8,128)(2,1)S(1)}) custom-call(bf16[64,128]{1,0:T(8,128)(2,1)S(1)} %get-tuple-element.48.own_gates_ref, bf16[64,128]{1,0:T(8,128)(2,1)S(1)} %get-tuple-element.49.other_gates_ref, ...), custom_call_target="tpu_custom_call" | custom-call | flops 4227858432 | bytes 33030144 | tf_op jit(solution)/shard_map/pallas_call | solution.py:239
  64.5 0.4 collective-permute-start.12
  64.9 0.2 collective-permute-start.13
  65.0 1.0 %collective-permute-done.12 = bf16[64,1792]{1,0:T(8,128)(2,1)S(1)} collective-permute-done((bf16[64,1792]{1,0:T(8,128)(2,1)S(1)}, bf16[64,1792]{1,0:T(8,128)(2,1)S(1)}, u32[]{:S(2)}, u32[]{:S(2)}) %collective-permute-start.12) | collective-permute-done | bytes 229408 | tf_op jit(solution)/shard_map/ppermute | solution.py:290
  66.1 0.3 collective-permute-done.13
  66.4 1.1 %collective-permute-start.15 = (bf16[16,3584]{1,0:T(8,128)(2,1)S(1)}, bf16[16,3584]{1,0:T(8,128)(2,1)S(1)}, u32[]{:S(2)}, u32[]{:S(2)}) collective-permute-start(bf16[16,3584]{1,0:T(8,128)(2,1)S(1)} %pad_maximum_fusion.1), channel_id=1, source_target_pairs={{0,2},{1,3},{2,0},{3,1},{4,6},{5,7},{6,4},{7,5},{8,10},{9,11},{10,... | collective-permute-start | bytes 344072 | tf_op jit(solution)/shard_map/ppermute | solution.py:290
  67.6 0.5 collective-permute-start.16
  68.1 2.0 %collective-permute-start.14 = (bf16[16,3584]{1,0:T(8,128)(2,1)S(1)}, bf16[16,3584]{1,0:T(8,128)(2,1)S(1)}, u32[]{:S(2)}, u32[]{:S(2)}) collective-permute-start(bf16[16,3584]{1,0:T(8,128)(2,1)S(1)} %pad_maximum_fusion), channel_id=1, source_target_pairs={{0,6},{1,7},{2,4},{3,5},{4,2},{5,3},{6,0},{7,1},{8,14},{9,15},{10,... | collective-permute-start | bytes 344072 | tf_op jit(solution)/shard_map/ppermute | solution.py:290
  70.1 1.7 %collective-permute-done.15 = bf16[16,3584]{1,0:T(8,128)(2,1)S(1)} collective-permute-done((bf16[16,3584]{1,0:T(8,128)(2,1)S(1)}, bf16[16,3584]{1,0:T(8,128)(2,1)S(1)}, u32[]{:S(2)}, u32[]{:S(2)}) %collective-permute-start.15) | collective-permute-done | bytes 114720 | tf_op jit(solution)/shard_map/ppermute | solution.py:290
  71.9 1.8 %collective-permute-done.16 = bf16[16,3584]{1,0:T(8,128)(2,1)S(1)} collective-permute-done((bf16[16,3584]{1,0:T(8,128)(2,1)S(1)}, bf16[16,3584]{1,0:T(8,128)(2,1)S(1)}, u32[]{:S(2)}, u32[]{:S(2)}) %collective-permute-start.16) | collective-permute-done | bytes 114720 | tf_op jit(solution)/shard_map/ppermute | solution.py:290
  73.7 1.9 %collective-permute-done.14 = bf16[16,3584]{1,0:T(8,128)(2,1)S(1)} collective-permute-done((bf16[16,3584]{1,0:T(8,128)(2,1)S(1)}, bf16[16,3584]{1,0:T(8,128)(2,1)S(1)}, u32[]{:S(2)}, u32[]{:S(2)}) %collective-permute-start.14) | collective-permute-done | bytes 114720 | tf_op jit(solution)/shard_map/ppermute | solution.py:290
  75.7 1.9 %collective-permute-start.17 = (bf16[8,3584]{1,0:T(8,128)(2,1)S(1)}, bf16[8,3584]{1,0:T(8,128)(2,1)S(1)}, u32[]{:S(2)}, u32[]{:S(2)}) collective-permute-start(bf16[8,3584]{1,0:T(8,128)(2,1)S(1)} %slice.173), channel_id=1, source_target_pairs={{0,8},{1,9},{2,10},{3,11},{4,12},{5,13},{6,14},{7,15},{8,0},{9,1},... | collective-permute-start | bytes 172040 | tf_op jit(solution)/shard_map/ppermute | solution.py:290
  77.6 3.6 %collective-permute-done.17 = bf16[8,3584]{1,0:T(8,128)(2,1)S(1)} collective-permute-done((bf16[8,3584]{1,0:T(8,128)(2,1)S(1)}, bf16[8,3584]{1,0:T(8,128)(2,1)S(1)}, u32[]{:S(2)}, u32[]{:S(2)}) %collective-permute-start.17) | collective-permute-done | bytes 57376 | tf_op jit(solution)/shard_map/ppermute | solution.py:290
  81.2 0.6 fusion.3
  (17 shorter events, 0.5 us)
Async XLA Ops:
  0.0 14.3 %all-to-all-start = ((bf16[16,8,256]{2,1,0:T(8,128)(2,1)}), bf16[16,8,256]{2,1,0:T(8,128)(2,1)S(1)}, u32[]{:S(2)}, u32[]{:S(2)}) async-start(bf16[16,8,256]{2,1,0:T(8,128)(2,1)} %bitcast.19), calls=%async_computation | async-start | bytes 131072 | tf_op jit(solution)/shard_map/all_to_all | solution.py:318
  16.3 10.9 %all-to-all-start.1 = ((bf16[16,8,384]{2,1,0:T(8,128)(2,1)}), bf16[16,8,384]{2,1,0:T(8,128)(2,1)S(1)}, u32[]{:S(2)}, u32[]{:S(2)}) async-start(bf16[16,8,384]{2,1,0:T(8,128)(2,1)} %shard_map.111.refs_1_), calls=%async_computation.1 | async-start | bytes 196608 | tf_op jit(solution)/shard_map/all_to_all | solution.py:323
  28.2 1.9 %collective-permute-start = (bf16[64,3584]{1,0:T(8,128)(2,1)S(1)}, bf16[64,3584]{1,0:T(8,128)(2,1)S(1)}, u32[]{:S(2)}, u32[]{:S(2)}) collective-permute-start(bf16[64,3584]{1,0:T(8,128)(2,1)S(1)} %get-tuple-element.43), channel_id=1, source_target_pairs={{0,1},{1,0},{2,3},{3,2},{4,5},{5,4},{6,7},{7,6},{8,9},{9,8},{10,11... | collective-permute-start | bytes 1376264 | tf_op jit(solution)/shard_map/ppermute | solution.py:290
  30.1 7.0 %collective-permute-start.1 = (bf16[16,3584]{1,0:T(8,128)(2,1)S(1)}, bf16[16,3584]{1,0:T(8,128)(2,1)S(1)}, u32[]{:S(2)}, u32[]{:S(2)}) collective-permute-start(bf16[16,3584]{1,0:T(8,128)(2,1)S(1)} %get-tuple-element.61), channel_id=1, source_target_pairs={{0,6},{1,7},{2,4},{3,5},{4,2},{5,3},{6,0},{7,1},{8,14},{9,15},{10,... | collective-permute-start | bytes 344072 | tf_op jit(solution)/shard_map/ppermute | solution.py:290
  30.2 7.0 %collective-permute-start.3 = (bf16[16,3584]{1,0:T(8,128)(2,1)S(1)}, bf16[16,3584]{1,0:T(8,128)(2,1)S(1)}, u32[]{:S(2)}, u32[]{:S(2)}) collective-permute-start(bf16[16,3584]{1,0:T(8,128)(2,1)S(1)} %get-tuple-element.62), channel_id=1, source_target_pairs={{0,4},{1,5},{2,6},{3,7},{4,0},{5,1},{6,2},{7,3},{8,12},{9,13},{10,... | collective-permute-start | bytes 344072 | tf_op jit(solution)/shard_map/ppermute | solution.py:290
  31.4 7.3 %collective-permute-start.2 = (bf16[16,3584]{1,0:T(8,128)(2,1)S(1)}, bf16[16,3584]{1,0:T(8,128)(2,1)S(1)}, u32[]{:S(2)}, u32[]{:S(2)}) collective-permute-start(bf16[16,3584]{1,0:T(8,128)(2,1)S(1)} %get-tuple-element.63), channel_id=1, source_target_pairs={{0,2},{1,3},{2,0},{3,1},{4,6},{5,7},{6,4},{7,5},{8,10},{9,11},{10,... | collective-permute-start | bytes 344072 | tf_op jit(solution)/shard_map/ppermute | solution.py:290
  38.9 7.9 %collective-permute-start.4 = (bf16[16,3584]{1,0:T(8,128)(2,1)S(1)}, bf16[16,3584]{1,0:T(8,128)(2,1)S(1)}, u32[]{:S(2)}, u32[]{:S(2)}) collective-permute-start(bf16[16,3584]{1,0:T(8,128)(2,1)S(1)} %convert_element_type.91.refs_4_), channel_id=1, source_target_pairs={{0,8},{1,9},{2,10},{3,11},{4,12},{5,13},{6,14},{7,15},{8,0},{9,1},... | collective-permute-start | bytes 344072 | tf_op jit(solution)/shard_map/ppermute | solution.py:290
  46.9 7.3 %collective-permute-start.7 = (bf16[16,3584]{1,0:T(8,128)(2,1)S(1)}, bf16[16,3584]{1,0:T(8,128)(2,1)S(1)}, u32[]{:S(2)}, u32[]{:S(2)}) collective-permute-start(bf16[16,3584]{1,0:T(8,128)(2,1)S(1)} %bitcast.14), channel_id=1, source_target_pairs={{0,6},{1,7},{2,4},{3,5},{4,2},{5,3},{6,0},{7,1},{8,14},{9,15},{10,... | collective-permute-start | bytes 344072 | tf_op jit(solution)/shard_map/ppermute | solution.py:290
  47.2 7.5 %collective-permute-start.6 = (bf16[16,3584]{1,0:T(8,128)(2,1)S(1)}, bf16[16,3584]{1,0:T(8,128)(2,1)S(1)}, u32[]{:S(2)}, u32[]{:S(2)}) collective-permute-start(bf16[16,3584]{1,0:T(8,128)(2,1)S(1)} %bitcast.15), channel_id=1, source_target_pairs={{0,2},{1,3},{2,0},{3,1},{4,6},{5,7},{6,4},{7,5},{8,10},{9,11},{10,... | collective-permute-start | bytes 344072 | tf_op jit(solution)/shard_map/ppermute | solution.py:290
  48.6 6.3 %collective-permute-start.5 = (bf16[16,3584]{1,0:T(8,128)(2,1)S(1)}, bf16[16,3584]{1,0:T(8,128)(2,1)S(1)}, u32[]{:S(2)}, u32[]{:S(2)}) collective-permute-start(bf16[16,3584]{1,0:T(8,128)(2,1)S(1)} %bitcast.16), channel_id=1, source_target_pairs={{0,4},{1,5},{2,6},{3,7},{4,0},{5,1},{6,2},{7,3},{8,12},{9,13},{10,... | collective-permute-start | bytes 344072 | tf_op jit(solution)/shard_map/ppermute | solution.py:290
  54.2 1.4 %collective-permute-start.8 = (bf16[16,3584]{1,0:T(8,128)(2,1)S(1)}, bf16[16,3584]{1,0:T(8,128)(2,1)S(1)}, u32[]{:S(2)}, u32[]{:S(2)}) collective-permute-start(bf16[16,3584]{1,0:T(8,128)(2,1)S(1)} %get-tuple-element.56.refs_0_), channel_id=1, source_target_pairs={{0,1},{1,0},{2,3},{3,2},{4,5},{5,4},{6,7},{7,6},{8,9},{9,8},{10,11... | collective-permute-start | bytes 344072 | tf_op jit(solution)/shard_map/ppermute | solution.py:290
  54.3 1.5 %collective-permute-start.11 = (bf16[16,3584]{1,0:T(8,128)(2,1)S(1)}, bf16[16,3584]{1,0:T(8,128)(2,1)S(1)}, u32[]{:S(2)}, u32[]{:S(2)}) collective-permute-start(bf16[16,3584]{1,0:T(8,128)(2,1)S(1)} %collective-permute-done.7.refs_3_), channel_id=1, source_target_pairs={{0,1},{1,0},{2,3},{3,2},{4,5},{5,4},{6,7},{7,6},{8,9},{9,8},{10,11... | collective-permute-start | bytes 344072 | tf_op jit(solution)/shard_map/ppermute | solution.py:290
  54.8 1.3 %collective-permute-start.10 = (bf16[16,3584]{1,0:T(8,128)(2,1)S(1)}, bf16[16,3584]{1,0:T(8,128)(2,1)S(1)}, u32[]{:S(2)}, u32[]{:S(2)}) collective-permute-start(bf16[16,3584]{1,0:T(8,128)(2,1)S(1)} %collective-permute-done.6.refs_2_), channel_id=1, source_target_pairs={{0,1},{1,0},{2,3},{3,2},{4,5},{5,4},{6,7},{7,6},{8,9},{9,8},{10,11... | collective-permute-start | bytes 344072 | tf_op jit(solution)/shard_map/ppermute | solution.py:290
  54.8 1.4 %collective-permute-start.9 = (bf16[16,3584]{1,0:T(8,128)(2,1)S(1)}, bf16[16,3584]{1,0:T(8,128)(2,1)S(1)}, u32[]{:S(2)}, u32[]{:S(2)}) collective-permute-start(bf16[16,3584]{1,0:T(8,128)(2,1)S(1)} %collective-permute-done.5.refs_1_), channel_id=1, source_target_pairs={{0,1},{1,0},{2,3},{3,2},{4,5},{5,4},{6,7},{7,6},{8,9},{9,8},{10,11... | collective-permute-start | bytes 344072 | tf_op jit(solution)/shard_map/ppermute | solution.py:290
  64.5 1.6 %collective-permute-start.12 = (bf16[64,1792]{1,0:T(8,128)(2,1)S(1)}, bf16[64,1792]{1,0:T(8,128)(2,1)S(1)}, u32[]{:S(2)}, u32[]{:S(2)}) collective-permute-start(bf16[64,1792]{1,0:T(8,128)(2,1)S(1)} %get-tuple-element.58), channel_id=1, source_target_pairs={{0,1},{1,0},{2,3},{3,2},{4,5},{5,4},{6,7},{7,6},{8,9},{9,8},{10,11... | collective-permute-start | bytes 688136 | tf_op jit(solution)/shard_map/ppermute | solution.py:290
  64.9 1.5 %collective-permute-start.13 = (bf16[64,1792]{1,0:T(8,128)(2,1)S(1)}, bf16[64,1792]{1,0:T(8,128)(2,1)S(1)}, u32[]{:S(2)}, u32[]{:S(2)}) collective-permute-start(bf16[64,1792]{1,0:T(8,128)(2,1)S(1)} %get-tuple-element.60), channel_id=1, source_target_pairs={{0,1},{1,0},{2,3},{3,2},{4,5},{5,4},{6,7},{7,6},{8,9},{9,8},{10,11... | collective-permute-start | bytes 688136 | tf_op jit(solution)/shard_map/ppermute | solution.py:290
  66.4 5.4 %collective-permute-start.15 = (bf16[16,3584]{1,0:T(8,128)(2,1)S(1)}, bf16[16,3584]{1,0:T(8,128)(2,1)S(1)}, u32[]{:S(2)}, u32[]{:S(2)}) collective-permute-start(bf16[16,3584]{1,0:T(8,128)(2,1)S(1)} %pad_maximum_fusion.1), channel_id=1, source_target_pairs={{0,2},{1,3},{2,0},{3,1},{4,6},{5,7},{6,4},{7,5},{8,10},{9,11},{10,... | collective-permute-start | bytes 344072 | tf_op jit(solution)/shard_map/ppermute | solution.py:290
  67.6 6.1 %collective-permute-start.16 = (bf16[16,3584]{1,0:T(8,128)(2,1)S(1)}, bf16[16,3584]{1,0:T(8,128)(2,1)S(1)}, u32[]{:S(2)}, u32[]{:S(2)}) collective-permute-start(bf16[16,3584]{1,0:T(8,128)(2,1)S(1)} %pad_maximum_fusion.2), channel_id=1, source_target_pairs={{0,4},{1,5},{2,6},{3,7},{4,0},{5,1},{6,2},{7,3},{8,12},{9,13},{10,... | collective-permute-start | bytes 344072 | tf_op jit(solution)/shard_map/ppermute | solution.py:290
  68.1 7.5 %collective-permute-start.14 = (bf16[16,3584]{1,0:T(8,128)(2,1)S(1)}, bf16[16,3584]{1,0:T(8,128)(2,1)S(1)}, u32[]{:S(2)}, u32[]{:S(2)}) collective-permute-start(bf16[16,3584]{1,0:T(8,128)(2,1)S(1)} %pad_maximum_fusion), channel_id=1, source_target_pairs={{0,6},{1,7},{2,4},{3,5},{4,2},{5,3},{6,0},{7,1},{8,14},{9,15},{10,... | collective-permute-start | bytes 344072 | tf_op jit(solution)/shard_map/ppermute | solution.py:290
  75.7 5.6 %collective-permute-start.17 = (bf16[8,3584]{1,0:T(8,128)(2,1)S(1)}, bf16[8,3584]{1,0:T(8,128)(2,1)S(1)}, u32[]{:S(2)}, u32[]{:S(2)}) collective-permute-start(bf16[8,3584]{1,0:T(8,128)(2,1)S(1)} %slice.173), channel_id=1, source_target_pairs={{0,8},{1,9},{2,10},{3,11},{4,12},{5,13},{6,14},{7,15},{8,0},{9,1},... | collective-permute-start | bytes 172040 | tf_op jit(solution)/shard_map/ppermute | solution.py:290

commit v14 on v12

--- a/solution.py
+++ b/solution.py
@@ -114,15 +114,19 @@
     return order
 
 
-def project_kernel(place_ref, rows_ref, weight_ref, terms_ref, gates_ref, ordered):
+def project_kernel(place_ref, rows_ref, weight_ref, left_ref, right_ref, gates_ref, ordered):
     chips, _, tok, _ = rows_ref.shape
     head_dim = weight_ref.shape[0]
     for at, bits in enumerate(relative_order(chips)):
         ordered[at] = rows_ref[place_ref[0] ^ bits, place_ref[1]]
     block = ordered[...].reshape(chips * tok, head_dim + LANES)
-    terms_ref[...] = jnp.dot(
-        block[:, :head_dim], weight_ref[...], preferred_element_type=F32
-    ).astype(terms_ref.dtype)
+    wide = left_ref.shape[1]
+    for at, terms_ref in enumerate((left_ref, right_ref)):
+        terms_ref[...] = jnp.dot(
+            block[:, :head_dim],
+            weight_ref[:, pl.ds(at * wide, wide)],
+            preferred_element_type=F32,
+        ).astype(terms_ref.dtype)
     gates_ref[...] = block[:, head_dim:]
 
 
@@ -133,11 +137,12 @@
     return pl.pallas_call(
         project_kernel,
         out_shape=(
-            jax.ShapeDtypeStruct((half, feature), dtype),
+            jax.ShapeDtypeStruct((half, feature // 2), dtype),
+            jax.ShapeDtypeStruct((half, feature // 2), dtype),
             jax.ShapeDtypeStruct((half, LANES), BF16),
         ),
         in_specs=[SMEM_SPEC, VMEM_SPEC, VMEM_SPEC],
-        out_specs=(VMEM_SPEC, VMEM_SPEC),
+        out_specs=(VMEM_SPEC,) * 3,
         scratch_shapes=[pltpu.VMEM((chips, tok, width), BF16)],
         compiler_params=pltpu.CompilerParams(vmem_limit_bytes=8 << 20),
         cost_estimate=pl.CostEstimate(
@@ -306,10 +311,10 @@
     (output_held,) = fetch(output_weight, after=(attended,))
     head_rows = lax.all_to_all(attended, "ep", split_axis=0, concat_axis=0, tiled=True)
     head_rows = head_rows.reshape(chips, 2, tok, head_dim + LANES)
-    sent, other_gates = project(other_place, head_rows, output_held, BF16)
-    arrived = swap(sent, 1)
-    kept, own_gates = project(place, head_rows, output_held, F32)
-    kept = sum_nearest([kept], [arrived])
+    *sent, other_gates = project(other_place, head_rows, output_held, BF16)
+    arrived = [swap(terms, 1) for terms in sent]
+    *kept, own_gates = project(place, head_rows, output_held, F32)
+    kept = sum_nearest(kept, arrived)
     summed = kept.at[:tok].add(residual_held.astype(F32)).astype(BF16)
     bit = chips
     units = gate_weight.shape[0]

time: 82.3 us -> 82.5 us (level)
  starting transfers between devices: 25.5 us -> 26.6 us
  waiting for transfers between devices: 28.4 us -> 27.5 us
    ppermute x18 -> x19, starting transfers between devices: 14.7 us -> 15.7 us  [swap(): return lax.ppermute(x, 'ep', [(i, i ^ bit) for i in range(size)])]
    ppermute x18 -> x19, waiting for transfers between devices: 18.1 us -> 17.1 us  [swap(): return lax.ppermute(x, 'ep', [(i, i ^ bit) for i in range(size)])]
  transfers between devices with their start and end apart: 20 -> 21, of which waited for: 17 -> 17; matrix products, arithmetic and copies ran while one was open for 1% -> 1% of each run, Pallas kernels for 18% -> 18%
where the time goes in v14:
time: 82.5 us; the launch traced here: 82.1 us
  waiting for transfers between devices  27.5 us (33%)
  starting transfers between devices  26.6 us (32%)
  Pallas kernels  26.1 us (32%)
  other arithmetic  1.79 us (2%)
    ppermute x19, waiting for transfers between devices, swap(): return lax.ppermute(x, 'ep', [(i, i ^ bit) for i in range(size)])  17.1 us
    ppermute x19, starting transfers between devices, swap(): return lax.ppermute(x, 'ep', [(i, i ^ bit) for i in range(size)])  15.7 us
    pallas_call x4, Pallas kernels, fetch(): pl.pallas_call(functools.partial(fetch_kernel, count, carried, ranges), o...  13.6 us
    pallas_call x1, Pallas kernels, experts(): pl.pallas_call(expert_kernel, out_shape=(jax.ShapeDtypeStruct((half, feat...  8.2 us
    all_to_all x1, starting transfers between devices, local(): lax.all_to_all(queries.reshape(size, tok, head_dim), 'ep', split_axis=0,...  7.38 us
    all_to_all x1, waiting for transfers between devices, local(): lax.all_to_all(attended, 'ep', split_axis=0, concat_axis=0, tiled=True)  5.76 us
    all_to_all x1, waiting for transfers between devices, local(): lax.all_to_all(queries.reshape(size, tok, head_dim), 'ep', split_axis=0,...  4.56 us
    all_to_all x1, starting transfers between devices, local(): lax.all_to_all(attended, 'ep', split_axis=0, concat_axis=0, tiled=True)  3.51 us
  transfers between devices with their start and end apart: 21, of which 17 were waited for; matrix products, arithmetic and copies ran while one was open for 1% of the time, Pallas kernels for 18%

profile of v14, /device:TPU:0, one launch (start us, length us, event | category | flops | bytes accessed | tf_op | source)
XLA Modules:
  0.0 82.1 jit_solution(16885096210980393326)
XLA Ops:
  0.0 7.4 %all-to-all-start = ((bf16[16,8,256]{2,1,0:T(8,128)(2,1)}), bf16[16,8,256]{2,1,0:T(8,128)(2,1)S(1)}, u32[]{:S(2)}, u32[]{:S(2)}) async-start(bf16[16,8,256]{2,1,0:T(8,128)(2,1)} %bitcast.19), calls=%async_computation | async-start | bytes 131072 | tf_op jit(solution)/shard_map/all_to_all | solution.py:307
  7.4 1.6 %shard_map.109 = (bf16[8,256,512]{2,1,0:T(8,128)(2,1)S(1)}, bf16[8,3584]{1,0:T(8,128)(2,1)S(1)}, f32[3584]{0:T(1024)S(1)}, s32[8]{0:T(128)S(1)}, s32[3,8]{1,0:T(4,128)S(1)}) custom-call(bf16[8,256,512]{2,1,0:T(8,128)(2,1)} %refs_0_.4, bf16[8,3584]{1,0:T(8,128)(2,1)} %refs_1_.3, f32[3584]{0:T(1024)} %refs_2_.2, s32[8]{0:T(128)} %refs_3_.1, s32[3,8]{1,0:T(4,128)} %bitcast.20), custom_call_target="tpu_custom_call" | custom-call | bytes 2161728 | tf_op jit(solution)/shard_map/pallas_call | solution.py:47
  9.0 0.7 convert_bitcast_fusion.shares_ref
  9.7 4.6 %all-to-all-done.query_ref = bf16[16,8,256]{2,1,0:T(8,128)(2,1)S(1)} async-done(((bf16[16,8,256]{2,1,0:T(8,128)(2,1)}), bf16[16,8,256]{2,1,0:T(8,128)(2,1)S(1)}, u32[]{:S(2)}, u32[]{:S(2)}) %all-to-all-start) | async-done | bytes 65568 | tf_op jit(solution)/shard_map/all_to_all | solution.py:307
  14.3 2.2 %shard_map.110.refs_1_ = bf16[16,8,384]{2,1,0:T(8,128)(2,1)} custom-call(s32[8]{0:T(128)S(1)} %get-tuple-element.41.lengths_ref, s32[3,8]{1,0:T(4,128)S(1)} %get-tuple-element.42.routes_ref, f32[3,8]{1,0:T(4,128)S(1)} %convert_bitcast_fusion.shares_ref, bf16[16,8,256]{2,1,0:T(8,128)(2,1)S(1)} %all-to-all-done.query_ref, ...), custom_call_target="tpu_custom_call" | custom-call | tf_op jit(solution)/shard_map/pallas_call | solution.py:100
  16.5 3.5 %all-to-all-start.1 = ((bf16[16,8,384]{2,1,0:T(8,128)(2,1)}), bf16[16,8,384]{2,1,0:T(8,128)(2,1)S(1)}, u32[]{:S(2)}, u32[]{:S(2)}) async-start(bf16[16,8,384]{2,1,0:T(8,128)(2,1)} %shard_map.110.refs_1_), calls=%async_computation.1 | async-start | bytes 196608 | tf_op jit(solution)/shard_map/all_to_all | solution.py:312
  20.0 0.1 pad_add_fusion
  20.1 1.5 %shard_map.111.weight_ref = bf16[256,3584]{1,0:T(8,128)(2,1)S(1)} custom-call(bf16[256,3584]{1,0:T(8,128)(2,1)} %refs_0_.5, bf16[16,8,384]{2,1,0:T(8,128)(2,1)} %shard_map.110.refs_1_), custom_call_target="tpu_custom_call" | custom-call | bytes 1835008 | tf_op jit(solution)/shard_map/pallas_call | solution.py:47
  21.6 5.8 %all-to-all-done.1 = bf16[16,8,384]{2,1,0:T(8,128)(2,1)S(1)} async-done(((bf16[16,8,384]{2,1,0:T(8,128)(2,1)}), bf16[16,8,384]{2,1,0:T(8,128)(2,1)S(1)}, u32[]{:S(2)}, u32[]{:S(2)}) %all-to-all-start.1) | async-done | bytes 98336 | tf_op jit(solution)/shard_map/all_to_all | solution.py:312
  27.3 1.0 %shard_map.113 = (bf16[64,1792]{1,0:T(8,128)(2,1)S(1)}, bf16[64,1792]{1,0:T(8,128)(2,1)S(1)}, bf16[64,128]{1,0:T(8,128)(2,1)S(1)}) custom-call(s32[2]{0:T(128)S(1)} %get-tuple-element.82.place_ref, bf16[8,2,8,384]{3,2,1,0:T(8,128)(2,1)S(1)} %bitcast.12, bf16[256,3584]{1,0:T(8,128)(2,1)S(1)} %shard_map.111.weight_ref), custom_call_target="tpu_custom_call" | custom-call | flops 117440512 | bytes 1835008 | tf_op jit(solution)/shard_map/pallas_call | solution.py:137
  28.4 0.5 collective-permute-start.1
  28.9 1.0 %shard_map.112 = (f32[64,1792]{1,0:T(8,128)S(1)}, f32[64,1792]{1,0:T(8,128)S(1)}, bf16[64,128]{1,0:T(8,128)(2,1)S(1)}) custom-call(s32[2]{0:T(128)S(1)} %get-tuple-element.81.place_ref, bf16[8,2,8,384]{3,2,1,0:T(8,128)(2,1)S(1)} %bitcast.13, bf16[256,3584]{1,0:T(8,128)(2,1)S(1)} %shard_map.111.weight_ref), custom_call_target="tpu_custom_call" | custom-call | flops 117440512 | bytes 1835008 | tf_op jit(solution)/shard_map/pallas_call | solution.py:137
  29.9 0.3 collective-permute-done.1
  30.3 0.1 collective-permute-start.3
  30.4 0.6 collective-permute-start.4
  30.9 3.0 %collective-permute-start.2 = (bf16[16,3584]{1,0:T(8,128)(2,1)S(1)}, bf16[16,3584]{1,0:T(8,128)(2,1)S(1)}, u32[]{:S(2)}, u32[]{:S(2)}) collective-permute-start(bf16[16,3584]{1,0:T(8,128)(2,1)S(1)} %pad_maximum_fusion), channel_id=1, source_target_pairs={{0,6},{1,7},{2,4},{3,5},{4,2},{5,3},{6,0},{7,1},{8,14},{9,15},{10,... | collective-permute-start | bytes 344072 | tf_op jit(solution)/shard_map/ppermute | solution.py:280
  34.0 1.6 %collective-permute-done.3 = bf16[16,3584]{1,0:T(8,128)(2,1)S(1)} collective-permute-done((bf16[16,3584]{1,0:T(8,128)(2,1)S(1)}, bf16[16,3584]{1,0:T(8,128)(2,1)S(1)}, u32[]{:S(2)}, u32[]{:S(2)}) %collective-permute-start.3) | collective-permute-done | bytes 114720 | tf_op jit(solution)/shard_map/ppermute | solution.py:280
  35.6 0.8 %collective-permute-done.4 = bf16[16,3584]{1,0:T(8,128)(2,1)S(1)} collective-permute-done((bf16[16,3584]{1,0:T(8,128)(2,1)S(1)}, bf16[16,3584]{1,0:T(8,128)(2,1)S(1)}, u32[]{:S(2)}, u32[]{:S(2)}) %collective-permute-start.4) | collective-permute-done | bytes 114720 | tf_op jit(solution)/shard_map/ppermute | solution.py:280
  36.4 2.9 %collective-permute-done.2 = bf16[16,3584]{1,0:T(8,128)(2,1)S(1)} collective-permute-done((bf16[16,3584]{1,0:T(8,128)(2,1)S(1)}, bf16[16,3584]{1,0:T(8,128)(2,1)S(1)}, u32[]{:S(2)}, u32[]{:S(2)}) %collective-permute-start.2) | collective-permute-done | bytes 114720 | tf_op jit(solution)/shard_map/ppermute | solution.py:280
  39.4 0.2 collective-permute-start.5
  39.6 6.8 %shard_map.114 = (bf16[1536,3584]{1,0:T(8,128)(2,1)S(1)}, bf16[768,3584]{1,0:T(8,128)(2,1)S(1)}, bf16[512,3584]{1,0:T(8,128)(2,1)S(1)}, f32[3584]{0:T(1024)S(1)}) custom-call(bf16[1536,3584]{1,0:T(8,128)(2,1)} %refs_0_.6, bf16[1536,3584]{1,0:T(8,128)(2,1)} %refs_0_.7, bf16[1536,3584]{1,0:T(8,128)(2,1)} %down_source.1, f32[3584]{0:T(1024)S(1)} %get-tuple-element.49.refs_3_, ...), custom_call_target="tpu_custom_call" | custom-call | bytes 33030144 | tf_op jit(solution)/shard_map/pallas_call | solution.py:47
  46.4 0.5 collective-permute-done.5
  46.9 0.1 shard_map.115
  47.0 0.7 collective-permute-start.8
  47.7 1.3 %collective-permute-start.7 = (bf16[16,3584]{1,0:T(8,128)(2,1)S(1)}, bf16[16,3584]{1,0:T(8,128)(2,1)S(1)}, u32[]{:S(2)}, u32[]{:S(2)}) collective-permute-start(bf16[16,3584]{1,0:T(8,128)(2,1)S(1)} %bitcast.15), channel_id=1, source_target_pairs={{0,2},{1,3},{2,0},{3,1},{4,6},{5,7},{6,4},{7,5},{8,10},{9,11},{10,... | collective-permute-start | bytes 344072 | tf_op jit(solution)/shard_map/ppermute | solution.py:280
  49.1 1.5 %collective-permute-start.6 = (bf16[16,3584]{1,0:T(8,128)(2,1)S(1)}, bf16[16,3584]{1,0:T(8,128)(2,1)S(1)}, u32[]{:S(2)}, u32[]{:S(2)}) collective-permute-start(bf16[16,3584]{1,0:T(8,128)(2,1)S(1)} %bitcast.16), channel_id=1, source_target_pairs={{0,4},{1,5},{2,6},{3,7},{4,0},{5,1},{6,2},{7,3},{8,12},{9,13},{10,... | collective-permute-start | bytes 344072 | tf_op jit(solution)/shard_map/ppermute | solution.py:280
  50.6 3.7 %shard_map.116 = (bf16[768,3584]{1,0:T(8,128)(2,1)S(1)}, bf16[512,3584]{1,0:T(8,128)(2,1)S(1)}, bf16[16,3584]{1,0:T(8,128)(2,1)S(1)}) custom-call(bf16[1536,3584]{1,0:T(8,128)(2,1)} %refs_0_.7, bf16[1536,3584]{1,0:T(8,128)(2,1)} %down_source.1, bf16[16,3584]{1,0:T(8,128)(2,1)S(1)} %bitcast.17), custom_call_target="tpu_custom_call" | custom-call | bytes 22020096 | tf_op jit(solution)/shard_map/pallas_call | solution.py:47
  54.4 0.5 collective-permute-start.12
  54.9 0.1 collective-permute-start.11
  55.0 0.4 collective-permute-start.10
  55.4 0.3 collective-permute-done.9.refs_4_
  55.7 0.2 collective-permute-done.12.refs_7_
  55.9 0.4 collective-permute-done.11.refs_6_
  56.2 0.2 collective-permute-done.10.refs_5_
  56.4 8.2 %shard_map.117 = (f32[64,1792]{1,0:T(8,128)S(1)}, bf16[64,1792]{1,0:T(8,128)(2,1)S(1)}, f32[64,1792]{1,0:T(8,128)S(1)}, bf16[64,1792]{1,0:T(8,128)(2,1)S(1)}) custom-call(bf16[64,128]{1,0:T(8,128)(2,1)S(1)} %get-tuple-element.52.own_gates_ref, bf16[64,128]{1,0:T(8,128)(2,1)S(1)} %get-tuple-element.53.other_gates_ref, ...), custom_call_target="tpu_custom_call" | custom-call | flops 4227858432 | bytes 33030144 | tf_op jit(solution)/shard_map/pallas_call | solution.py:229
  64.6 0.4 collective-permute-start.13
  65.0 0.2 collective-permute-start.14
  65.2 1.0 %collective-permute-done.13 = bf16[64,1792]{1,0:T(8,128)(2,1)S(1)} collective-permute-done((bf16[64,1792]{1,0:T(8,128)(2,1)S(1)}, bf16[64,1792]{1,0:T(8,128)(2,1)S(1)}, u32[]{:S(2)}, u32[]{:S(2)}) %collective-permute-start.13) | collective-permute-done | bytes 229408 | tf_op jit(solution)/shard_map/ppermute | solution.py:280
  66.2 0.3 collective-permute-done.14
  66.6 0.8 collective-permute-start.16
  67.3 0.7 collective-permute-start.17
  68.1 2.2 %collective-permute-start.15 = (bf16[16,3584]{1,0:T(8,128)(2,1)S(1)}, bf16[16,3584]{1,0:T(8,128)(2,1)S(1)}, u32[]{:S(2)}, u32[]{:S(2)}) collective-permute-start(bf16[16,3584]{1,0:T(8,128)(2,1)S(1)} %pad_maximum_fusion.3), channel_id=1, source_target_pairs={{0,6},{1,7},{2,4},{3,5},{4,2},{5,3},{6,0},{7,1},{8,14},{9,15},{10,... | collective-permute-start | bytes 344072 | tf_op jit(solution)/shard_map/ppermute | solution.py:280
  70.3 1.7 %collective-permute-done.16 = bf16[16,3584]{1,0:T(8,128)(2,1)S(1)} collective-permute-done((bf16[16,3584]{1,0:T(8,128)(2,1)S(1)}, bf16[16,3584]{1,0:T(8,128)(2,1)S(1)}, u32[]{:S(2)}, u32[]{:S(2)}) %collective-permute-start.16) | collective-permute-done | bytes 114720 | tf_op jit(solution)/shard_map/ppermute | solution.py:280
  72.0 1.4 %collective-permute-done.17 = bf16[16,3584]{1,0:T(8,128)(2,1)S(1)} collective-permute-done((bf16[16,3584]{1,0:T(8,128)(2,1)S(1)}, bf16[16,3584]{1,0:T(8,128)(2,1)S(1)}, u32[]{:S(2)}, u32[]{:S(2)}) %collective-permute-start.17) | collective-permute-done | bytes 114720 | tf_op jit(solution)/shard_map/ppermute | solution.py:280
  73.4 2.3 %collective-permute-done.15 = bf16[16,3584]{1,0:T(8,128)(2,1)S(1)} collective-permute-done((bf16[16,3584]{1,0:T(8,128)(2,1)S(1)}, bf16[16,3584]{1,0:T(8,128)(2,1)S(1)}, u32[]{:S(2)}, u32[]{:S(2)}) %collective-permute-start.15) | collective-permute-done | bytes 114720 | tf_op jit(solution)/shard_map/ppermute | solution.py:280
  75.8 2.4 %collective-permute-start.18 = (bf16[8,3584]{1,0:T(8,128)(2,1)S(1)}, bf16[8,3584]{1,0:T(8,128)(2,1)S(1)}, u32[]{:S(2)}, u32[]{:S(2)}) collective-permute-start(bf16[8,3584]{1,0:T(8,128)(2,1)S(1)} %slice.217), channel_id=1, source_target_pairs={{0,8},{1,9},{2,10},{3,11},{4,12},{5,13},{6,14},{7,15},{8,0},{9,1},... | collective-permute-start | bytes 172040 | tf_op jit(solution)/shard_map/ppermute | solution.py:280
  78.1 3.3 %collective-permute-done.18 = bf16[8,3584]{1,0:T(8,128)(2,1)S(1)} collective-permute-done((bf16[8,3584]{1,0:T(8,128)(2,1)S(1)}, bf16[8,3584]{1,0:T(8,128)(2,1)S(1)}, u32[]{:S(2)}, u32[]{:S(2)}) %collective-permute-start.18) | collective-permute-done | bytes 57376 | tf_op jit(solution)/shard_map/ppermute | solution.py:280
  81.5 0.6 fusion.5
  (22 shorter events, 0.5 us)
Async XLA Ops:
  0.0 14.3 %all-to-all-start = ((bf16[16,8,256]{2,1,0:T(8,128)(2,1)}), bf16[16,8,256]{2,1,0:T(8,128)(2,1)S(1)}, u32[]{:S(2)}, u32[]{:S(2)}) async-start(bf16[16,8,256]{2,1,0:T(8,128)(2,1)} %bitcast.19), calls=%async_computation | async-start | bytes 131072 | tf_op jit(solution)/shard_map/all_to_all | solution.py:307
  16.5 10.9 %all-to-all-start.1 = ((bf16[16,8,384]{2,1,0:T(8,128)(2,1)}), bf16[16,8,384]{2,1,0:T(8,128)(2,1)S(1)}, u32[]{:S(2)}, u32[]{:S(2)}) async-start(bf16[16,8,384]{2,1,0:T(8,128)(2,1)} %shard_map.110.refs_1_), calls=%async_computation.1 | async-start | bytes 196608 | tf_op jit(solution)/shard_map/all_to_all | solution.py:312
  28.3 1.6 %collective-permute-start = (bf16[64,1792]{1,0:T(8,128)(2,1)S(1)}, bf16[64,1792]{1,0:T(8,128)(2,1)S(1)}, u32[]{:S(2)}, u32[]{:S(2)}) collective-permute-start(bf16[64,1792]{1,0:T(8,128)(2,1)S(1)} %get-tuple-element.45), channel_id=1, source_target_pairs={{0,1},{1,0},{2,3},{3,2},{4,5},{5,4},{6,7},{7,6},{8,9},{9,8},{10,11... | collective-permute-start | bytes 688136 | tf_op jit(solution)/shard_map/ppermute | solution.py:280
  28.4 1.8 %collective-permute-start.1 = (bf16[64,1792]{1,0:T(8,128)(2,1)S(1)}, bf16[64,1792]{1,0:T(8,128)(2,1)S(1)}, u32[]{:S(2)}, u32[]{:S(2)}) collective-permute-start(bf16[64,1792]{1,0:T(8,128)(2,1)S(1)} %get-tuple-element.47), channel_id=1, source_target_pairs={{0,1},{1,0},{2,3},{3,2},{4,5},{5,4},{6,7},{7,6},{8,9},{9,8},{10,11... | collective-permute-start | bytes 688136 | tf_op jit(solution)/shard_map/ppermute | solution.py:280
  30.3 5.3 %collective-permute-start.3 = (bf16[16,3584]{1,0:T(8,128)(2,1)S(1)}, bf16[16,3584]{1,0:T(8,128)(2,1)S(1)}, u32[]{:S(2)}, u32[]{:S(2)}) collective-permute-start(bf16[16,3584]{1,0:T(8,128)(2,1)S(1)} %pad_maximum_fusion.1), channel_id=1, source_target_pairs={{0,2},{1,3},{2,0},{3,1},{4,6},{5,7},{6,4},{7,5},{8,10},{9,11},{10,... | collective-permute-start | bytes 344072 | tf_op jit(solution)/shard_map/ppermute | solution.py:280
  30.4 6.1 %collective-permute-start.4 = (bf16[16,3584]{1,0:T(8,128)(2,1)S(1)}, bf16[16,3584]{1,0:T(8,128)(2,1)S(1)}, u32[]{:S(2)}, u32[]{:S(2)}) collective-permute-start(bf16[16,3584]{1,0:T(8,128)(2,1)S(1)} %pad_maximum_fusion.2), channel_id=1, source_target_pairs={{0,4},{1,5},{2,6},{3,7},{4,0},{5,1},{6,2},{7,3},{8,12},{9,13},{10,... | collective-permute-start | bytes 344072 | tf_op jit(solution)/shard_map/ppermute | solution.py:280
  30.9 8.3 %collective-permute-start.2 = (bf16[16,3584]{1,0:T(8,128)(2,1)S(1)}, bf16[16,3584]{1,0:T(8,128)(2,1)S(1)}, u32[]{:S(2)}, u32[]{:S(2)}) collective-permute-start(bf16[16,3584]{1,0:T(8,128)(2,1)S(1)} %pad_maximum_fusion), channel_id=1, source_target_pairs={{0,6},{1,7},{2,4},{3,5},{4,2},{5,3},{6,0},{7,1},{8,14},{9,15},{10,... | collective-permute-start | bytes 344072 | tf_op jit(solution)/shard_map/ppermute | solution.py:280
  39.4 7.5 %collective-permute-start.5 = (bf16[16,3584]{1,0:T(8,128)(2,1)S(1)}, bf16[16,3584]{1,0:T(8,128)(2,1)S(1)}, u32[]{:S(2)}, u32[]{:S(2)}) collective-permute-start(bf16[16,3584]{1,0:T(8,128)(2,1)S(1)} %convert_element_type.98.refs_4_), channel_id=1, source_target_pairs={{0,8},{1,9},{2,10},{3,11},{4,12},{5,13},{6,14},{7,15},{8,0},{9,1},... | collective-permute-start | bytes 344072 | tf_op jit(solution)/shard_map/ppermute | solution.py:280
  47.0 7.3 %collective-permute-start.8 = (bf16[16,3584]{1,0:T(8,128)(2,1)S(1)}, bf16[16,3584]{1,0:T(8,128)(2,1)S(1)}, u32[]{:S(2)}, u32[]{:S(2)}) collective-permute-start(bf16[16,3584]{1,0:T(8,128)(2,1)S(1)} %bitcast.14), channel_id=1, source_target_pairs={{0,6},{1,7},{2,4},{3,5},{4,2},{5,3},{6,0},{7,1},{8,14},{9,15},{10,... | collective-permute-start | bytes 344072 | tf_op jit(solution)/shard_map/ppermute | solution.py:280
  47.7 7.1 %collective-permute-start.7 = (bf16[16,3584]{1,0:T(8,128)(2,1)S(1)}, bf16[16,3584]{1,0:T(8,128)(2,1)S(1)}, u32[]{:S(2)}, u32[]{:S(2)}) collective-permute-start(bf16[16,3584]{1,0:T(8,128)(2,1)S(1)} %bitcast.15), channel_id=1, source_target_pairs={{0,2},{1,3},{2,0},{3,1},{4,6},{5,7},{6,4},{7,5},{8,10},{9,11},{10,... | collective-permute-start | bytes 344072 | tf_op jit(solution)/shard_map/ppermute | solution.py:280
  49.1 5.9 %collective-permute-start.6 = (bf16[16,3584]{1,0:T(8,128)(2,1)S(1)}, bf16[16,3584]{1,0:T(8,128)(2,1)S(1)}, u32[]{:S(2)}, u32[]{:S(2)}) collective-permute-start(bf16[16,3584]{1,0:T(8,128)(2,1)S(1)} %bitcast.16), channel_id=1, source_target_pairs={{0,4},{1,5},{2,6},{3,7},{4,0},{5,1},{6,2},{7,3},{8,12},{9,13},{10,... | collective-permute-start | bytes 344072 | tf_op jit(solution)/shard_map/ppermute | solution.py:280
  54.3 1.4 %collective-permute-start.9 = (bf16[16,3584]{1,0:T(8,128)(2,1)S(1)}, bf16[16,3584]{1,0:T(8,128)(2,1)S(1)}, u32[]{:S(2)}, u32[]{:S(2)}) collective-permute-start(bf16[16,3584]{1,0:T(8,128)(2,1)S(1)} %get-tuple-element.60.refs_0_), channel_id=1, source_target_pairs={{0,1},{1,0},{2,3},{3,2},{4,5},{5,4},{6,7},{7,6},{8,9},{9,8},{10,11... | collective-permute-start | bytes 344072 | tf_op jit(solution)/shard_map/ppermute | solution.py:280
  54.4 1.5 %collective-permute-start.12 = (bf16[16,3584]{1,0:T(8,128)(2,1)S(1)}, bf16[16,3584]{1,0:T(8,128)(2,1)S(1)}, u32[]{:S(2)}, u32[]{:S(2)}) collective-permute-start(bf16[16,3584]{1,0:T(8,128)(2,1)S(1)} %collective-permute-done.8.refs_3_), channel_id=1, source_target_pairs={{0,1},{1,0},{2,3},{3,2},{4,5},{5,4},{6,7},{7,6},{8,9},{9,8},{10,11... | collective-permute-start | bytes 344072 | tf_op jit(solution)/shard_map/ppermute | solution.py:280
  54.9 1.3 %collective-permute-start.11 = (bf16[16,3584]{1,0:T(8,128)(2,1)S(1)}, bf16[16,3584]{1,0:T(8,128)(2,1)S(1)}, u32[]{:S(2)}, u32[]{:S(2)}) collective-permute-start(bf16[16,3584]{1,0:T(8,128)(2,1)S(1)} %collective-permute-done.7.refs_2_), channel_id=1, source_target_pairs={{0,1},{1,0},{2,3},{3,2},{4,5},{5,4},{6,7},{7,6},{8,9},{9,8},{10,11... | collective-permute-start | bytes 344072 | tf_op jit(solution)/shard_map/ppermute | solution.py:280
  55.0 1.4 %collective-permute-start.10 = (bf16[16,3584]{1,0:T(8,128)(2,1)S(1)}, bf16[16,3584]{1,0:T(8,128)(2,1)S(1)}, u32[]{:S(2)}, u32[]{:S(2)}) collective-permute-start(bf16[16,3584]{1,0:T(8,128)(2,1)S(1)} %collective-permute-done.6.refs_1_), channel_id=1, source_target_pairs={{0,1},{1,0},{2,3},{3,2},{4,5},{5,4},{6,7},{7,6},{8,9},{9,8},{10,11... | collective-permute-start | bytes 344072 | tf_op jit(solution)/shard_map/ppermute | solution.py:280
  64.6 1.6 %collective-permute-start.13 = (bf16[64,1792]{1,0:T(8,128)(2,1)S(1)}, bf16[64,1792]{1,0:T(8,128)(2,1)S(1)}, u32[]{:S(2)}, u32[]{:S(2)}) collective-permute-start(bf16[64,1792]{1,0:T(8,128)(2,1)S(1)} %get-tuple-element.62), channel_id=1, source_target_pairs={{0,1},{1,0},{2,3},{3,2},{4,5},{5,4},{6,7},{7,6},{8,9},{9,8},{10,11... | collective-permute-start | bytes 688136 | tf_op jit(solution)/shard_map/ppermute | solution.py:280
  65.0 1.5 %collective-permute-start.14 = (bf16[64,1792]{1,0:T(8,128)(2,1)S(1)}, bf16[64,1792]{1,0:T(8,128)(2,1)S(1)}, u32[]{:S(2)}, u32[]{:S(2)}) collective-permute-start(bf16[64,1792]{1,0:T(8,128)(2,1)S(1)} %get-tuple-element.64), channel_id=1, source_target_pairs={{0,1},{1,0},{2,3},{3,2},{4,5},{5,4},{6,7},{7,6},{8,9},{9,8},{10,11... | collective-permute-start | bytes 688136 | tf_op jit(solution)/shard_map/ppermute | solution.py:280
  66.6 5.4 %collective-permute-start.16 = (bf16[16,3584]{1,0:T(8,128)(2,1)S(1)}, bf16[16,3584]{1,0:T(8,128)(2,1)S(1)}, u32[]{:S(2)}, u32[]{:S(2)}) collective-permute-start(bf16[16,3584]{1,0:T(8,128)(2,1)S(1)} %pad_maximum_fusion.4), channel_id=1, source_target_pairs={{0,2},{1,3},{2,0},{3,1},{4,6},{5,7},{6,4},{7,5},{8,10},{9,11},{10,... | collective-permute-start | bytes 344072 | tf_op jit(solution)/shard_map/ppermute | solution.py:280
  67.3 6.1 %collective-permute-start.17 = (bf16[16,3584]{1,0:T(8,128)(2,1)S(1)}, bf16[16,3584]{1,0:T(8,128)(2,1)S(1)}, u32[]{:S(2)}, u32[]{:S(2)}) collective-permute-start(bf16[16,3584]{1,0:T(8,128)(2,1)S(1)} %pad_maximum_fusion.5), channel_id=1, source_target_pairs={{0,4},{1,5},{2,6},{3,7},{4,0},{5,1},{6,2},{7,3},{8,12},{9,13},{10,... | collective-permute-start | bytes 344072 | tf_op jit(solution)/shard_map/ppermute | solution.py:280
  68.1 7.7 %collective-permute-start.15 = (bf16[16,3584]{1,0:T(8,128)(2,1)S(1)}, bf16[16,3584]{1,0:T(8,128)(2,1)S(1)}, u32[]{:S(2)}, u32[]{:S(2)}) collective-permute-start(bf16[16,3584]{1,0:T(8,128)(2,1)S(1)} %pad_maximum_fusion.3), channel_id=1, source_target_pairs={{0,6},{1,7},{2,4},{3,5},{4,2},{5,3},{6,0},{7,1},{8,14},{9,15},{10,... | collective-permute-start | bytes 344072 | tf_op jit(solution)/shard_map/ppermute | solution.py:280
  75.8 5.7 %collective-permute-start.18 = (bf16[8,3584]{1,0:T(8,128)(2,1)S(1)}, bf16[8,3584]{1,0:T(8,128)(2,1)S(1)}, u32[]{:S(2)}, u32[]{:S(2)}) collective-permute-start(bf16[8,3584]{1,0:T(8,128)(2,1)S(1)} %slice.217), channel_id=1, source_target_pairs={{0,8},{1,9},{2,10},{3,11},{4,12},{5,13},{6,14},{7,15},{8,0},{9,1},... | collective-permute-start | bytes 172040 | tf_op jit(solution)/shard_map/ppermute | solution.py:280
